TPU v7x, 32 devices: a whole 2x2x4 slice. The times are simulated.
32 devices in a mesh: ctx: 8 (over z, y), ep: 4 (over x, core).
Axes of the slice: x: 2, y: 2, z: 4, core: 2. Of those that a mesh axis runs over, the one named last changes fastest.
Arguments:
- q_nope: bfloat16 [1024, 8192], P('ctx', 'ep'), may hold values from -6 to 6
- q_rope: bfloat16 [1024, 4096], P('ctx', 'ep'), may hold values from -300 to 300
- latent: bfloat16 [1024, 512], P('ctx'), may hold values from -6 to 6
- k_rope: bfloat16 [1024, 64], P('ctx'), may hold values from -5 to 5
- w_uk: bfloat16 [512, 8192], P(None, 'ep'), may hold values from -0.25 to 0.25
- w_uv: bfloat16 [512, 8192], P(None, 'ep'), may hold values from -0.25 to 0.25
- positions: int32 [1024], replicated, may hold values from 0 to 1023, as said below
- moe_rows: bfloat16 [1024, 7168], P('ctx', 'ep'), may hold values from -6 to 6
- expert_ids: int32 [1024, 8], P('ctx'), may hold values from 0 to 255, all different within a row; in each aligned block of 128 rows (0 to 127, 128 to 255, ...) at most 8 rows name the same one
- expert_weights: float32 [1024, 8], P('ctx'), may hold values from 0.05 to 0.5
- w_gate: bfloat16 [8, 7168, 1024], P('ctx', None, 'ep'), may hold values from -0.0625 to 0.0625
- w_up: bfloat16 [8, 7168, 1024], P('ctx', None, 'ep'), may hold values from -0.0625 to 0.0625
- w_down: bfloat16 [8, 1024, 7168], P('ctx', 'ep'), may hold values from -0.1875 to 0.1875
Outputs:
- attention: bfloat16 [1024, 8192], P('ctx', 'ep')
- moe_out: bfloat16 [1024, 7168], P('ctx', 'ep')
Inputs may be any that keep to these rules, and one draw needn't show every extreme that they name: `expert_ids`: each row names 8 different experts; in each aligned block of 128 rows (the rows of one index of ctx) no expert is named by more than 8 rows. A permutation of the positions; the 128 rows of each index of ctx are two runs of 64 consecutive positions, run j and run 2 * 8 - 1 - j of the prompt for some j.
All inputs are finite; a program needn't handle non-finite values.
Results may differ from a plain program's by a relative error of at most 0.017.
Values may be sent and summed in bfloat16 or wider, within the bound.
No kernel may reach another device: no remote copies, remote signals or barrier semaphores. Data moves between devices by JAX's collectives and lax.ppermute only.
A program may use at most 192 MiB of HBM per device.

v0:
```python
import math

import jax
import jax.numpy as jnp
from jax import lax
from jax.experimental import pallas as pl
from jax.experimental.pallas import tpu as pltpu
from jax.sharding import PartitionSpec as P

NOPE = 128
ROPE = 64
VDIM = 128
TOP = 8
CAP = 8
HALF = 64
GROUP = 4
MIB = 1 << 20
LIMIT = 52 * MIB
FULL = 60 * MIB

NT = (((1,), (1,)), ((), ()))
TN = (((0,), (0,)), ((), ()))
VMEM = pltpu.VMEM
SMEM_SPEC = pl.BlockSpec(memory_space=pltpu.SMEM)
VMEM_SPEC = pl.BlockSpec(memory_space=pltpu.VMEM)
HBM_SPEC = pl.BlockSpec(memory_space=pltpu.HBM)


def route_kernel(
    ep_ref,
    ids_ref,
    weights_ref,
    rope_ref,
    rows_ref,
    latent_ref,
    sent_ref,
    high_ref,
    low_ref,
    packed_ref,
):
    quarter = packed_ref.shape[0]
    latent_width = latent_ref.shape[1]
    place = pl.multiple_of(ep_ref[0] * quarter, quarter)
    row_count = ids_ref.shape[1]
    slots = sent_ref.shape[0] * CAP
    slot = lax.broadcasted_iota(jnp.int32, (slots, row_count), 0)
    expert = slot // CAP
    named = jnp.zeros((slots, row_count), jnp.float32)
    gate = jnp.zeros((slots, row_count), jnp.float32)
    for choice in range(TOP):
        match = ids_ref[choice : choice + 1, :] == expert
        named = jnp.where(match, 1.0, named)
        gate = jnp.where(match, weights_ref[choice : choice + 1, :], gate)
    row = lax.broadcasted_iota(jnp.int32, (row_count, row_count), 0)
    other = lax.broadcasted_iota(jnp.int32, (row_count, row_count), 1)
    before = jnp.where(row < other, 1.0, 0.0).astype(jnp.bfloat16)
    rank = jnp.dot(named.astype(jnp.bfloat16), before, preferred_element_type=jnp.float32)
    taken = (named > 0.0) & (rank == (slot % CAP).astype(jnp.float32))
    select = jnp.where(taken, 1.0, 0.0).astype(jnp.bfloat16)
    gate = jnp.where(taken, gate, 0.0)
    high = gate.astype(jnp.bfloat16)
    high_ref[...] = high
    low_ref[...] = (gate - high.astype(jnp.float32)).astype(jnp.bfloat16)
    rope = rope_ref[...].astype(jnp.float32).T
    packed_ref[:, :latent_width] = latent_ref[pl.ds(place, quarter), :]
    for part in range(row_count // quarter):

        @pl.when(ep_ref[0] == part)
        def _():
            packed_ref[:, latent_width:] = rope[part * quarter : (part + 1) * quarter].astype(
                jnp.bfloat16
            )

    sent = jnp.dot(select, rows_ref[...], preferred_element_type=jnp.float32)
    for index in range(slots // CAP):
        sent_ref[index] = sent[index * CAP : (index + 1) * CAP].astype(jnp.bfloat16)


def route(ep, expert_ids, expert_weights, k_rope, moe_rows, latent, ctx):
    row_count, features = moe_rows.shape
    quarter = row_count // 4
    latent_width = latent.shape[1]
    slots = ctx * CAP
    return pl.pallas_call(
        route_kernel,
        out_shape=[
            jax.ShapeDtypeStruct((ctx, CAP, features), jnp.bfloat16),
            jax.ShapeDtypeStruct((slots, row_count), jnp.bfloat16),
            jax.ShapeDtypeStruct((slots, row_count), jnp.bfloat16),
            jax.ShapeDtypeStruct((quarter, latent_width + ROPE), jnp.bfloat16),
        ],
        in_specs=[SMEM_SPEC] + [VMEM_SPEC] * 5,
        out_specs=[VMEM_SPEC] * 4,
        compiler_params=pltpu.CompilerParams(vmem_limit_bytes=FULL),
        cost_estimate=pl.CostEstimate(
            flops=2 * row_count * slots * features, bytes_accessed=1 * MIB, transcendentals=0
        ),
        name="route",
    )(ep, expert_ids.T, expert_weights.T, k_rope.T, moe_rows, latent)


def weight_copies(ep_ref, flips, gate_hbm, up_hbm, gate, up, semaphores):
    features = gate.shape[1]
    copies = []
    for index, flip in enumerate(flips):
        place = pl.multiple_of((ep_ref[0] ^ flip) * features, features)
        for which, (source, target) in enumerate(((gate_hbm, gate), (up_hbm, up))):
            copy = pltpu.make_async_copy(
                source.at[0, pl.ds(place, features)], target.at[index], semaphores.at[index, which]
            )
            copy.start()
            copies.append(copy)
    return copies


def near_kernel(
    ep_ref, own_ref, core_ref, gate_hbm, up_hbm, gate_out, up_out, gate, up, semaphores
):
    copies = weight_copies(ep_ref, (0, 1), gate_hbm, up_hbm, gate, up, semaphores)
    gate_sum, up_sum = None, None
    for index, x_ref in enumerate((own_ref, core_ref)):
        rows = x_ref[...]
        copies[2 * index].wait()
        part = jnp.dot(rows, gate[index], preferred_element_type=jnp.float32)
        gate_sum = part if gate_sum is None else gate_sum + part
        copies[2 * index + 1].wait()
        part = jnp.dot(rows, up[index], preferred_element_type=jnp.float32)
        up_sum = part if up_sum is None else up_sum + part
    gate_out[...] = gate_sum
    up_out[...] = up_sum


def near_experts(ep, own, core, w_gate, w_up):
    slots, features = own.shape
    units = w_gate.shape[2]
    return pl.pallas_call(
        near_kernel,
        out_shape=[jax.ShapeDtypeStruct((slots, units), jnp.float32)] * 2,
        in_specs=[SMEM_SPEC] + [VMEM_SPEC] * 2 + [HBM_SPEC] * 2,
        out_specs=[VMEM_SPEC] * 2,
        scratch_shapes=[
            VMEM((2, features, units), jnp.bfloat16),
            VMEM((2, features, units), jnp.bfloat16),
            pltpu.SemaphoreType.DMA((2, 2)),
        ],
        compiler_params=pltpu.CompilerParams(vmem_limit_bytes=LIMIT),
        cost_estimate=pl.CostEstimate(
            flops=8 * slots * features * units,
            bytes_accessed=8 * features * units,
            transcendentals=0,
        ),
        name="near_experts",
    )(ep, own, core, w_gate, w_up)


def far_kernel(
    ep_ref,
    far_ref,
    core_far_ref,
    gate_part,
    up_part,
    gate_hbm,
    up_hbm,
    down_hbm,
    own_out,
    core_out,
    far_out,
    core_far_out,
    gate,
    up,
    down,
    semaphores,
    down_semaphores,
):
    features = gate.shape[1]
    copies = weight_copies(ep_ref, (2, 3), gate_hbm, up_hbm, gate, up, semaphores)
    down_copies = []
    for flip in (3, 1, 2, 0):
        place = pl.multiple_of((ep_ref[0] ^ flip) * features, features)
        copy = pltpu.make_async_copy(
            down_hbm.at[0, :, pl.ds(place, features)], down.at[flip], down_semaphores.at[flip]
        )
        copy.start()
        down_copies.append(copy)
    gate_sum, up_sum = gate_part[...], up_part[...]
    for index, x_ref in enumerate((far_ref, core_far_ref)):
        rows = x_ref[...]
        copies[2 * index].wait()
        gate_sum = gate_sum + jnp.dot(rows, gate[index], preferred_element_type=jnp.float32)
        copies[2 * index + 1].wait()
        up_sum = up_sum + jnp.dot(rows, up[index], preferred_element_type=jnp.float32)
    hidden = (gate_sum / (1.0 + jnp.exp(-gate_sum)) * up_sum).astype(jnp.bfloat16)
    outs = (own_out, core_out, far_out, core_far_out)
    for copy, flip in zip(down_copies, (3, 1, 2, 0)):
        copy.wait()
        outs[flip][...] = jnp.dot(
            hidden, down[flip], preferred_element_type=jnp.float32
        ).astype(jnp.bfloat16)


def far_experts(ep, far, core_far, gate_part, up_part, w_gate, w_up, w_down):
    slots, features = far.shape
    units = w_gate.shape[2]
    return pl.pallas_call(
        far_kernel,
        out_shape=[jax.ShapeDtypeStruct((slots, features), jnp.bfloat16)] * 4,
        in_specs=[SMEM_SPEC] + [VMEM_SPEC] * 4 + [HBM_SPEC] * 3,
        out_specs=[VMEM_SPEC] * 4,
        scratch_shapes=[
            VMEM((2, features, units), jnp.bfloat16),
            VMEM((2, features, units), jnp.bfloat16),
            VMEM((4, units, features), jnp.bfloat16),
            pltpu.SemaphoreType.DMA((2, 2)),
            pltpu.SemaphoreType.DMA((4,)),
        ],
        compiler_params=pltpu.CompilerParams(vmem_limit_bytes=LIMIT),
        cost_estimate=pl.CostEstimate(
            flops=16 * slots * features * units,
            bytes_accessed=16 * features * units,
            transcendentals=slots * units,
        ),
        name="far_experts",
    )(ep, far, core_far, gate_part, up_part, w_gate, w_up, w_down)


def add_kernel(*refs):
    total = refs[0][...].astype(jnp.float32)
    for ref in refs[1:-1]:
        total = total + ref[...].astype(jnp.float32)
    refs[-1][...] = total.astype(jnp.bfloat16)


def add(*parts):
    return pl.pallas_call(
        add_kernel,
        out_shape=jax.ShapeDtypeStruct(parts[0].shape, jnp.bfloat16),
        in_specs=[VMEM_SPEC] * len(parts),
        out_specs=VMEM_SPEC,
        compiler_params=pltpu.CompilerParams(vmem_limit_bytes=8 * MIB),
        cost_estimate=pl.CostEstimate(flops=0, bytes_accessed=MIB, transcendentals=0),
        name="add",
    )(*parts)


def combine_kernel(high_ref, low_ref, returned_ref, out_ref):
    returned = returned_ref[...]
    total = lax.dot_general(high_ref[...], returned, TN, preferred_element_type=jnp.float32)
    total = total + lax.dot_general(
        low_ref[...], returned, TN, preferred_element_type=jnp.float32
    )
    out_ref[...] = total.astype(jnp.bfloat16)


def combine(high, low, returned):
    slots, row_count = high.shape
    features = returned.shape[1]
    return pl.pallas_call(
        combine_kernel,
        out_shape=jax.ShapeDtypeStruct((row_count, features), jnp.bfloat16),
        in_specs=[VMEM_SPEC] * 3,
        out_specs=VMEM_SPEC,
        compiler_params=pltpu.CompilerParams(vmem_limit_bytes=LIMIT),
        cost_estimate=pl.CostEstimate(
            flops=4 * row_count * slots * features, bytes_accessed=MIB, transcendentals=0
        ),
        name="combine",
    )(high, low, returned)


def fold_kernel(q_nope_ref, q_rope_ref, w_uk_ref, out_ref):
    latent_width = w_uk_ref.shape[0]
    for head in range(GROUP):
        columns = slice(head * NOPE, (head + 1) * NOPE)
        folded = lax.dot_general(
            q_nope_ref[:, columns], w_uk_ref[:, columns], NT, preferred_element_type=jnp.float32
        ).astype(jnp.bfloat16)
        rotated = q_rope_ref[:, head * ROPE : (head + 1) * ROPE]
        for run in range(2):
            rows = slice(run * HALF, (run + 1) * HALF)
            place = slice(head * HALF, (head + 1) * HALF)
            out_ref[run, place, :latent_width] = folded[rows]
            out_ref[run, place, latent_width:] = rotated[rows]


def fold(q_nope, q_rope, w_uk):
    query_count, columns = q_nope.shape
    heads = columns // NOPE
    latent_width = w_uk.shape[0]
    width = latent_width + ROPE
    return pl.pallas_call(
        fold_kernel,
        out_shape=jax.ShapeDtypeStruct((2, heads * HALF, width), jnp.bfloat16),
        grid=(heads // GROUP,),
        in_specs=[
            pl.BlockSpec((query_count, GROUP * NOPE), lambda step: (0, step)),
            pl.BlockSpec((query_count, GROUP * ROPE), lambda step: (0, step)),
            pl.BlockSpec((latent_width, GROUP * NOPE), lambda step: (0, step)),
        ],
        out_specs=pl.BlockSpec((2, GROUP * HALF, width), lambda step: (0, step, 0)),
        compiler_params=pltpu.CompilerParams(vmem_limit_bytes=FULL),
        cost_estimate=pl.CostEstimate(
            flops=2 * query_count * columns * latent_width,
            bytes_accessed=6 * MIB,
            transcendentals=0,
        ),
        name="fold",
    )(q_nope, q_rope, w_uk)


def attend_run(run, base, seen, queries_ref, keys_ref, w_uv_ref, w_uv_copy, store):
    latent_width = w_uv_ref.shape[0]
    heads = w_uv_ref.shape[1] // VDIM
    count = GROUP * HALF
    factor = math.log2(math.e) / math.sqrt(NOPE + ROPE)
    query_position = base + lax.rem(lax.broadcasted_iota(jnp.int32, (count, seen), 0), HALF)
    visible = lax.broadcasted_iota(jnp.int32, (count, seen), 1) <= query_position
    for group in range(heads // GROUP):
        scores = lax.dot_general(
            queries_ref[run, group * count : (group + 1) * count, :],
            keys_ref[:seen, :],
            NT,
            preferred_element_type=jnp.float32,
        )
        scores = jnp.where(visible, scores, -jnp.inf)
        top = jnp.max(scores, axis=1, keepdims=True)
        part = jnp.exp2((scores - top) * factor)
        total = jnp.sum(part, axis=1, keepdims=True)
        summed = jnp.dot(
            part.astype(jnp.bfloat16),
            keys_ref[:seen, :latent_width],
            preferred_element_type=jnp.float32,
        )
        mixed = (summed / total).astype(jnp.bfloat16)
        if not group:
            w_uv_copy.wait()
        for index in range(GROUP):
            head = group * GROUP + index
            columns = slice(head * VDIM, (head + 1) * VDIM)
            store(
                columns,
                jnp.dot(
                    mixed[index * HALF : (index + 1) * HALF],
                    w_uv_ref[:, columns],
                    preferred_element_type=jnp.float32,
                ).astype(jnp.bfloat16),
            )


def runs_of(my_ctx, positions_ref):
    first = my_ctx * (2 * HALF)
    low = jnp.where(positions_ref[first] < positions_ref[first + HALF], 0, 1)
    return low, positions_ref[first + low * HALF], positions_ref[first + (1 - low) * HALF]


def low_kernel(
    own_ref,
    positions_ref,
    queries_ref,
    w_uv_hbm,
    own_keys,
    core_own_keys,
    far_keys,
    core_far_keys,
    keys_ref,
    out_ref,
    w_uv_ref,
    semaphore,
):
    w_uv_copy = pltpu.make_async_copy(w_uv_hbm, w_uv_ref, semaphore)
    w_uv_copy.start()
    blocks, block_rows, width = own_keys.shape
    my_ctx, my_ep = own_ref[0], own_ref[1]
    for flip, source in enumerate((own_keys, core_own_keys, far_keys, core_far_keys)):
        for index in range(blocks):
            start = (index ^ my_ctx) * (4 * block_rows) + (my_ep ^ flip) * block_rows
            place = pl.multiple_of(positions_ref[start], block_rows)
            keys_ref[pl.ds(place, block_rows), :] = source[index]
    run, base, _ = runs_of(my_ctx, positions_ref)

    def store(columns, value):
        out_ref[:, columns] = value

    seen = keys_ref.shape[0] // 2
    attend_run(run, base, seen, queries_ref, keys_ref, w_uv_ref, w_uv_copy, store)


def high_kernel(
    own_ref,
    positions_ref,
    queries_ref,
    w_uv_hbm,
    keys_ref,
    low_ref,
    out_ref,
    w_uv_ref,
    semaphore,
):
    w_uv_copy = pltpu.make_async_copy(w_uv_hbm, w_uv_ref, semaphore)
    w_uv_copy.start()
    low, _, base = runs_of(own_ref[0], positions_ref)
    run = 1 - low
    out_ref[pl.ds(pl.multiple_of(low * HALF, HALF), HALF), :] = low_ref[...]
    rows = pl.ds(pl.multiple_of(run * HALF, HALF), HALF)

    def store(columns, value):
        out_ref[rows, columns] = value

    seen = keys_ref.shape[0]
    attend_run(run, base, seen, queries_ref, keys_ref, w_uv_ref, w_uv_copy, store)


def attend_low(own, positions, queries, w_uv, pieces):
    columns = w_uv.shape[1]
    key_count = positions.shape[0]
    width = pieces[0].shape[-1]
    count = queries.shape[1]
    return pl.pallas_call(
        low_kernel,
        out_shape=[
            jax.ShapeDtypeStruct((key_count, width), jnp.bfloat16),
            jax.ShapeDtypeStruct((HALF, columns), jnp.bfloat16),
        ],
        in_specs=[SMEM_SPEC] * 2 + [VMEM_SPEC, HBM_SPEC] + [VMEM_SPEC] * 4,
        out_specs=[VMEM_SPEC] * 2,
        scratch_shapes=[VMEM(w_uv.shape, jnp.bfloat16), pltpu.SemaphoreType.DMA(())],
        compiler_params=pltpu.CompilerParams(vmem_limit_bytes=LIMIT),
        cost_estimate=pl.CostEstimate(
            flops=2 * count * key_count * width,
            bytes_accessed=6 * MIB,
            transcendentals=count * key_count // 2,
        ),
        name="attention_low",
    )(own, positions, queries, w_uv, *pieces)


def attend_high(own, positions, queries, w_uv, keys, low):
    columns = w_uv.shape[1]
    key_count = positions.shape[0]
    width = keys.shape[1]
    count = queries.shape[1]
    return pl.pallas_call(
        high_kernel,
        out_shape=jax.ShapeDtypeStruct((2 * HALF, columns), jnp.bfloat16),
        in_specs=[SMEM_SPEC] * 2 + [VMEM_SPEC, HBM_SPEC] + [VMEM_SPEC] * 2,
        out_specs=VMEM_SPEC,
        scratch_shapes=[VMEM(w_uv.shape, jnp.bfloat16), pltpu.SemaphoreType.DMA(())],
        compiler_params=pltpu.CompilerParams(vmem_limit_bytes=LIMIT),
        cost_estimate=pl.CostEstimate(
            flops=4 * count * key_count * width,
            bytes_accessed=6 * MIB,
            transcendentals=count * key_count,
        ),
        name="attention_high",
    )(own, positions, queries, w_uv, keys, low)


def shards(
    q_nope,
    q_rope,
    latent,
    k_rope,
    w_uk,
    w_uv,
    positions,
    moe_rows,
    expert_ids,
    expert_weights,
    w_gate,
    w_up,
    w_down,
):
    ctx = lax.axis_size("ctx")
    me = lax.axis_index("ctx").astype(jnp.int32).reshape(1)
    ep = lax.axis_index("ep").astype(jnp.int32).reshape(1)

    def over_ctx(value, flip):
        return lax.ppermute(value, "ctx", [(i, i ^ flip) for i in range(ctx)])

    def over_ep(value, flip):
        return lax.ppermute(value, "ep", [(i, i ^ flip) for i in range(4)])

    def exchange(value):
        return lax.all_to_all(value, "ctx", split_axis=0, concat_axis=0, tiled=True)

    outgoing, high, low, packed = route(
        ep, expert_ids, expert_weights, k_rope, moe_rows, latent, ctx
    )
    arrived = exchange(outgoing)
    packed, q_nope = lax.optimization_barrier((packed, q_nope))
    queries = fold(q_nope, q_rope, w_uk)
    own_keys = packed[None]
    step = 1
    while step < ctx // 2:
        own_keys = jnp.concatenate([own_keys, over_ctx(own_keys, step)], axis=0)
        step *= 2
    arrived, queries, own_keys = lax.optimization_barrier((arrived, queries, own_keys))

    own = arrived.reshape(ctx * CAP, arrived.shape[2])
    far = over_ep(own, 2)
    core = over_ep(own, 1)
    gate_part, up_part = near_experts(ep, own, core, w_gate, w_up)
    received = over_ctx(own_keys, step)
    received, far, gate_part = lax.optimization_barrier((received, far, gate_part))
    core_far = over_ep(far, 1)
    own_keys = jnp.concatenate([own_keys, received], axis=0)
    far_keys = over_ep(own_keys, 2)
    own_out, core_out, far_out, core_far_out = far_experts(
        ep, far, core_far, gate_part, up_part, w_gate, w_up, w_down
    )
    from_core_far = over_ep(core_far_out, 1)
    from_core = over_ep(core_out, 1)
    core_own_keys = over_ep(own_keys, 1)
    from_core_far, far_keys = lax.optimization_barrier((from_core_far, far_keys))
    to_far = add(far_out, from_core_far)
    from_far = over_ep(to_far, 2)
    core_far_keys = over_ep(far_keys, 1)
    place = jnp.concatenate([me, ep])
    keys, low_out = attend_low(
        place, positions, queries, w_uv, (own_keys, core_own_keys, far_keys, core_far_keys)
    )
    from_far, keys, low_out = lax.optimization_barrier((from_far, keys, low_out))
    returning = add(own_out, from_core, from_far)
    returned = exchange(returning.reshape(arrived.shape))
    attention = attend_high(place, positions, queries, w_uv, keys, low_out)
    moe_out = combine(high, low, returned.reshape(own.shape))
    return (attention, moe_out)


def solution(mesh):
    return jax.shard_map(
        shards,
        mesh=mesh,
        in_specs=(
            P("ctx", "ep"),
            P("ctx", "ep"),
            P("ctx", None),
            P("ctx", None),
            P(None, "ep"),
            P(None, "ep"),
            P(),
            P("ctx", "ep"),
            P("ctx", None),
            P("ctx", None),
            P("ctx", None, "ep"),
            P("ctx", None, "ep"),
            P("ctx", "ep", None),
        ),
        out_specs=(P("ctx", "ep"), P("ctx", "ep")),
        check_vma=False,
    )
```

profile of v0, /device:TPU:0, one launch (start us, length us, event | category | flops | bytes accessed | tf_op | source)
XLA Modules:
  0.0 68.8 jit_solution(6483403618162500742)
XLA Ops:
  0.6 2.2 %route.1 = (bf16[8,8,1792]{2,1,0:T(8,128)(2,1)}, bf16[64,128]{1,0:T(8,128)(2,1)}, bf16[64,128]{1,0:T(8,128)(2,1)}, bf16[32,576]{1,0:T(8,128)(2,1)}) custom-call(s32[1]{0:T(128)} %bitcast.1.ep_ref, s32[8,128]{1,0:T(8,128)} %bitcast.17, f32[8,128]{1,0:T(8,128)} %bitcast.18, bf16[64,128]{1,0:T(8,128)(2,1)} %bitcast.16, bf16[128,1792]{1,0:T(8,128)(2,1)} %rows_ref.1, ...), custom_call_target="tpu_custom_call" | custom-call | flops 29360128 | bytes 1048576 | tf_op jit(solution)/shard_map/route/pallas_call | solution.py:84
  2.8 7.3 %all-to-all-start = ((bf16[8,8,1792]{2,1,0:T(8,128)(2,1)}), bf16[8,8,1792]{2,1,0:T(8,128)(2,1)S(1)}, u32[]{:S(2)}, u32[]{:S(2)}) async-start(bf16[8,8,1792]{2,1,0:T(8,128)(2,1)} %get-tuple-element.27), calls=%async_computation | async-start | bytes 458752 | tf_op jit(solution)/shard_map/all_to_all | solution.py:483
  10.1 2.0 %collective-permute-start = (bf16[1,32,576]{2,1,0:T(8,128)(2,1)}, bf16[1,32,576]{2,1,0:T(8,128)(2,1)S(1)}, u32[]{:S(2)}, u32[]{:S(2)}) collective-permute-start(bf16[1,32,576]{2,1,0:T(8,128)(2,1)} %bitcast.13), channel_id=1, source_target_pairs={{0,4},{4,0},{8,12},{12,8},{16,20},{20,16},{24,28},{28,24},{1,5},{5... | collective-permute-start | bytes 110600 | tf_op jit(solution)/shard_map/ppermute | solution.py:477
  12.1 2.9 %collective-permute-done = bf16[1,32,576]{2,1,0:T(8,128)(2,1)S(1)} collective-permute-done((bf16[1,32,576]{2,1,0:T(8,128)(2,1)}, bf16[1,32,576]{2,1,0:T(8,128)(2,1)S(1)}, u32[]{:S(2)}, u32[]{:S(2)}) %collective-permute-start) | collective-permute-done | bytes 36896 | tf_op jit(solution)/shard_map/ppermute | solution.py:477
  15.0 0.8 %pad_maximum_fusion.1 = bf16[2,32,576]{2,1,0:T(8,128)(2,1)S(1)} fusion(bf16[1,32,576]{2,1,0:T(8,128)(2,1)S(1)} %collective-permute-done, bf16[1,32,576]{2,1,0:T(8,128)(2,1)} %bitcast.14), kind=kLoop, calls=%fused_computation.1 | loop fusion | flops 36864 | bytes 147456 | tf_op jit(solution)/shard_map/concatenate | solution.py:494
  15.8 0.0 copy-start.4
  15.8 1.9 %collective-permute-start.1 = (bf16[2,32,576]{2,1,0:T(8,128)(2,1)S(1)}, bf16[2,32,576]{2,1,0:T(8,128)(2,1)S(1)}, u32[]{:S(2)}, u32[]{:S(2)}) collective-permute-start(bf16[2,32,576]{2,1,0:T(8,128)(2,1)S(1)} %pad_maximum_fusion.1), channel_id=1, source_target_pairs={{0,8},{4,12},{8,0},{12,4},{16,24},{20,28},{24,16},{28,20},{1,9},{5... | collective-permute-start | bytes 221192 | tf_op jit(solution)/shard_map/ppermute | solution.py:477
  17.7 4.6 %fold.1.queries_ref = bf16[2,1024,576]{2,1,0:T(8,128)(2,1)} custom-call(bf16[128,2048]{1,0:T(8,128)(2,1)} %q_nope_ref, bf16[128,1024]{1,0:T(8,128)(2,1)} %q_rope_ref.1, bf16[512,2048]{1,0:T(8,128)(2,1)} %w_uk_ref.1), custom_call_target="tpu_custom_call" | custom-call | flops 268435456 | bytes 6291456 | tf_op jit(solution)/shard_map/fold/pallas_call | solution.py:290
  22.3 0.0 collective-permute-done.1
  22.3 0.0 copy-done.4
  22.4 0.0 all-to-all-done
  22.4 0.1 collective-permute-start.4
  22.4 1.6 %collective-permute-start.3 = (bf16[64,1792]{1,0:T(8,128)(2,1)S(1)}, bf16[64,1792]{1,0:T(8,128)(2,1)S(1)}, u32[]{:S(2)}, u32[]{:S(2)}) collective-permute-start(bf16[64,1792]{1,0:T(8,128)(2,1)S(1)} %bitcast.11), channel_id=1, source_target_pairs={{0,2},{1,3},{2,0},{3,1},{4,6},{5,7},{6,4},{7,5},{8,10},{9,11},{10,... | collective-permute-start | bytes 688136 | tf_op jit(solution)/shard_map/ppermute | solution.py:480
  24.0 2.8 %collective-permute-start.2 = (bf16[4,32,576]{2,1,0:T(8,128)(2,1)S(1)}, bf16[4,32,576]{2,1,0:T(8,128)(2,1)S(1)}, u32[]{:S(2)}, u32[]{:S(2)}) collective-permute-start(bf16[4,32,576]{2,1,0:T(8,128)(2,1)S(1)} %pad_maximum_fusion), channel_id=1, source_target_pairs={{0,16},{4,20},{8,24},{12,28},{16,0},{20,4},{24,8},{28,12},{1,17},{... | collective-permute-start | bytes 442376 | tf_op jit(solution)/shard_map/ppermute | solution.py:477
  26.8 0.0 collective-permute-done.4.core_ref
  26.8 3.1 %near_experts.1 = (f32[64,256]{1,0:T(8,128)S(1)}, f32[64,256]{1,0:T(8,128)S(1)}) custom-call(s32[1]{0:T(128)} %bitcast.1.ep_ref, bf16[64,1792]{1,0:T(8,128)(2,1)S(1)} %bitcast.12, bf16[64,1792]{1,0:T(8,128)(2,1)S(1)} %collective-permute-done.4.core_ref, bf16[1,7168,256]{2,1,0:T(8,128)(2,1)} %gate_hbm.3, bf16[1,7168,256]{2,1,0:T(8,128)(2,1)} %up_hbm.3), custom_call_target="tpu_custom_call" | custom-call | flops 234881024 | bytes 3670016 | tf_op jit(solution)/shard_map/near_experts/pallas_call | solution.py:136
  29.9 4.5 %collective-permute-done.2 = bf16[4,32,576]{2,1,0:T(8,128)(2,1)S(1)} collective-permute-done((bf16[4,32,576]{2,1,0:T(8,128)(2,1)S(1)}, bf16[4,32,576]{2,1,0:T(8,128)(2,1)S(1)}, u32[]{:S(2)}, u32[]{:S(2)}) %collective-permute-start.2) | collective-permute-done | bytes 147488 | tf_op jit(solution)/shard_map/ppermute | solution.py:477
  34.4 0.0 collective-permute-done.3.far_ref
  34.4 0.1 collective-permute-start.5
  34.5 0.6 collective-permute-start.7
  35.1 0.8 %collective-permute-done.5.core_far_ref = bf16[64,1792]{1,0:T(8,128)(2,1)S(1)} collective-permute-done((bf16[64,1792]{1,0:T(8,128)(2,1)S(1)}, bf16[64,1792]{1,0:T(8,128)(2,1)S(1)}, u32[]{:S(2)}, u32[]{:S(2)}) %collective-permute-start.5) | collective-permute-done | bytes 229408 | tf_op jit(solution)/shard_map/ppermute | solution.py:480
  35.9 0.0 copy-start.2
  35.9 4.5 %far_experts.1 = (bf16[64,1792]{1,0:T(8,128)(2,1)S(1)}, bf16[64,1792]{1,0:T(8,128)(2,1)S(1)}, bf16[64,1792]{1,0:T(8,128)(2,1)S(1)}, bf16[64,1792]{1,0:T(8,128)(2,1)S(1)}) custom-call(s32[1]{0:T(128)} %bitcast.1.ep_ref, bf16[64,1792]{1,0:T(8,128)(2,1)S(1)} %collective-permute-done.3.far_ref, bf16[64,1792]{1,0:T(8,128)(2,1)S(1)} %collective-permute-done.5.core_far_ref, ...), custom_call_target="tpu_custom_call" | custom-call | flops 469762048 | bytes 7340032 | tf_op jit(solution)/shard_map/far_experts/pallas_call | solution.py:204
  40.4 0.2 collective-permute-start.6
  40.6 0.4 collective-permute-start.9
  41.0 3.7 %collective-permute-done.7.far_keys = bf16[8,32,576]{2,1,0:T(8,128)(2,1)S(1)} collective-permute-done((bf16[8,32,576]{2,1,0:T(8,128)(2,1)S(1)}, bf16[8,32,576]{2,1,0:T(8,128)(2,1)S(1)}, u32[]{:S(2)}, u32[]{:S(2)}) %collective-permute-start.7) | collective-permute-done | bytes 294944 | tf_op jit(solution)/shard_map/ppermute | solution.py:480
  44.6 0.0 collective-permute-done.6.refs_1_
  44.6 0.0 collective-permute-start.10
  44.7 0.1 add.4
  44.7 0.6 collective-permute-start.8
  45.3 0.2 collective-permute-start.11
  45.5 0.1 pad_add_fusion.own_ref
  45.6 0.0 collective-permute-done.9.core_own_keys
  45.6 0.7 collective-permute-done.10.core_far_keys
  46.3 0.0 copy-done.2
  46.3 6.3 %attention_low.1 = (bf16[1024,576]{1,0:T(8,128)(2,1)}, bf16[64,2048]{1,0:T(8,128)(2,1)S(1)}) custom-call(s32[2]{0:T(128)S(1)} %pad_add_fusion.own_ref, s32[1024]{0:T(1024)S(1)} %copy-done.2, bf16[2,1024,576]{2,1,0:T(8,128)(2,1)} %fold.1.queries_ref, bf16[512,2048]{1,0:T(8,128)(2,1)} %w_uv_hbm.3, ...), custom_call_target="tpu_custom_call" | custom-call | flops 1207959552 | bytes 6291456 | tf_op jit(solution)/shard_map/attention_low/pallas_call | solution.py:417
  52.6 0.2 collective-permute-done.8.refs_2_
  52.8 0.0 collective-permute-done.11.refs_1_
  52.8 0.8 %add.5 = bf16[64,1792]{1,0:T(8,128)(2,1)} custom-call(bf16[64,1792]{1,0:T(8,128)(2,1)S(1)} %get-tuple-element.49.refs_0_, bf16[64,1792]{1,0:T(8,128)(2,1)S(1)} %collective-permute-done.11.refs_1_, bf16[64,1792]{1,0:T(8,128)(2,1)S(1)} %collective-permute-done.8.refs_2_), custom_call_target="tpu_custom_call" | custom-call | bytes 1048576 | tf_op jit(solution)/shard_map/add/pallas_call | solution.py:234
  53.6 4.7 %all-to-all-start.1 = ((bf16[8,8,1792]{2,1,0:T(8,128)(2,1)}), bf16[8,8,1792]{2,1,0:T(8,128)(2,1)S(1)}, u32[]{:S(2)}, u32[]{:S(2)}) async-start(bf16[8,8,1792]{2,1,0:T(8,128)(2,1)} %bitcast.7), calls=%async_computation.1 | async-start | bytes 458752 | tf_op jit(solution)/shard_map/all_to_all | solution.py:483
  58.3 0.0 copy-start.3
  58.3 1.3 %copy-done.3 = bf16[1024,576]{1,0:T(8,128)(2,1)S(1)} copy-done((bf16[1024,576]{1,0:T(8,128)(2,1)S(1)}, bf16[1024,576]{1,0:T(8,128)(2,1)}, u32[]{:S(2)}) %copy-start.3) | copy-done | bytes 1179672
  59.6 0.0 copy-start
  59.6 0.0 copy-start.1
  59.6 8.0 %attention_high.1 = bf16[128,2048]{1,0:T(8,128)(2,1)} custom-call(s32[2]{0:T(128)S(1)} %pad_add_fusion.own_ref, s32[1024]{0:T(1024)S(1)} %copy-done.2, bf16[2,1024,576]{2,1,0:T(8,128)(2,1)} %fold.1.queries_ref, bf16[512,2048]{1,0:T(8,128)(2,1)} %w_uv_hbm.3, bf16[1024,576]{1,0:T(8,128)(2,1)S(1)} %copy-done.3, bf16[64,2048]{1,0:T(8,128)(2,1)S(1)} %get-tuple-element.46.low_ref), custom_call_target="tpu_custom_call" | custom-call | flops 2415919104 | bytes 6291456 | tf_op jit(solution)/shard_map/attention_high/pallas_call | solution.py:441
  67.6 0.0 all-to-all-done.1
  67.6 0.0 copy-done
  67.6 0.0 copy-done.1
  67.6 1.2 %combine.1 = bf16[128,1792]{1,0:T(8,128)(2,1)} custom-call(bf16[64,128]{1,0:T(8,128)(2,1)S(1)} %copy-done, bf16[64,128]{1,0:T(8,128)(2,1)S(1)} %copy-done.1, bf16[64,1792]{1,0:T(8,128)(2,1)S(1)} %bitcast.9), custom_call_target="tpu_custom_call" | custom-call | flops 58720256 | bytes 1048576 | tf_op jit(solution)/shard_map/combine/pallas_call | solution.py:257
  (3 shorter events, 0.1 us)
Async XLA Ops:
  2.8 19.5 %all-to-all-start = ((bf16[8,8,1792]{2,1,0:T(8,128)(2,1)}), bf16[8,8,1792]{2,1,0:T(8,128)(2,1)S(1)}, u32[]{:S(2)}, u32[]{:S(2)}) async-start(bf16[8,8,1792]{2,1,0:T(8,128)(2,1)} %get-tuple-element.27), calls=%async_computation | async-start | bytes 458752 | tf_op jit(solution)/shard_map/all_to_all | solution.py:483
  10.1 4.9 %collective-permute-start = (bf16[1,32,576]{2,1,0:T(8,128)(2,1)}, bf16[1,32,576]{2,1,0:T(8,128)(2,1)S(1)}, u32[]{:S(2)}, u32[]{:S(2)}) collective-permute-start(bf16[1,32,576]{2,1,0:T(8,128)(2,1)} %bitcast.13), channel_id=1, source_target_pairs={{0,4},{4,0},{8,12},{12,8},{16,20},{20,16},{24,28},{28,24},{1,5},{5... | collective-permute-start | bytes 110600 | tf_op jit(solution)/shard_map/ppermute | solution.py:477
  15.8 6.5 %copy-start.4 = (bf16[32,576]{1,0:T(8,128)(2,1)S(1)}, bf16[32,576]{1,0:T(8,128)(2,1)}, u32[]{:S(2)}) copy-start(bf16[32,576]{1,0:T(8,128)(2,1)} %get-tuple-element.30) | copy-start | bytes 110596
  15.8 6.5 %collective-permute-start.1 = (bf16[2,32,576]{2,1,0:T(8,128)(2,1)S(1)}, bf16[2,32,576]{2,1,0:T(8,128)(2,1)S(1)}, u32[]{:S(2)}, u32[]{:S(2)}) collective-permute-start(bf16[2,32,576]{2,1,0:T(8,128)(2,1)S(1)} %pad_maximum_fusion.1), channel_id=1, source_target_pairs={{0,8},{4,12},{8,0},{12,4},{16,24},{20,28},{24,16},{28,20},{1,9},{5... | collective-permute-start | bytes 221192 | tf_op jit(solution)/shard_map/ppermute | solution.py:477
  22.4 4.4 %collective-permute-start.4 = (bf16[64,1792]{1,0:T(8,128)(2,1)S(1)}, bf16[64,1792]{1,0:T(8,128)(2,1)S(1)}, u32[]{:S(2)}, u32[]{:S(2)}) collective-permute-start(bf16[64,1792]{1,0:T(8,128)(2,1)S(1)} %bitcast.10), channel_id=1, source_target_pairs={{0,1},{1,0},{2,3},{3,2},{4,5},{5,4},{6,7},{7,6},{8,9},{9,8},{10,11... | collective-permute-start | bytes 688136 | tf_op jit(solution)/shard_map/ppermute | solution.py:480
  22.4 12.0 %collective-permute-start.3 = (bf16[64,1792]{1,0:T(8,128)(2,1)S(1)}, bf16[64,1792]{1,0:T(8,128)(2,1)S(1)}, u32[]{:S(2)}, u32[]{:S(2)}) collective-permute-start(bf16[64,1792]{1,0:T(8,128)(2,1)S(1)} %bitcast.11), channel_id=1, source_target_pairs={{0,2},{1,3},{2,0},{3,1},{4,6},{5,7},{6,4},{7,5},{8,10},{9,11},{10,... | collective-permute-start | bytes 688136 | tf_op jit(solution)/shard_map/ppermute | solution.py:480
  24.0 10.4 %collective-permute-start.2 = (bf16[4,32,576]{2,1,0:T(8,128)(2,1)S(1)}, bf16[4,32,576]{2,1,0:T(8,128)(2,1)S(1)}, u32[]{:S(2)}, u32[]{:S(2)}) collective-permute-start(bf16[4,32,576]{2,1,0:T(8,128)(2,1)S(1)} %pad_maximum_fusion), channel_id=1, source_target_pairs={{0,16},{4,20},{8,24},{12,28},{16,0},{20,4},{24,8},{28,12},{1,17},{... | collective-permute-start | bytes 442376 | tf_op jit(solution)/shard_map/ppermute | solution.py:477
  34.4 1.5 %collective-permute-start.5 = (bf16[64,1792]{1,0:T(8,128)(2,1)S(1)}, bf16[64,1792]{1,0:T(8,128)(2,1)S(1)}, u32[]{:S(2)}, u32[]{:S(2)}) collective-permute-start(bf16[64,1792]{1,0:T(8,128)(2,1)S(1)} %collective-permute-done.3.far_ref), channel_id=1, source_target_pairs={{0,1},{1,0},{2,3},{3,2},{4,5},{5,4},{6,7},{7,6},{8,9},{9,8},{10,11... | collective-permute-start | bytes 688136 | tf_op jit(solution)/shard_map/ppermute | solution.py:480
  34.5 10.1 %collective-permute-start.7 = (bf16[8,32,576]{2,1,0:T(8,128)(2,1)S(1)}, bf16[8,32,576]{2,1,0:T(8,128)(2,1)S(1)}, u32[]{:S(2)}, u32[]{:S(2)}) collective-permute-start(bf16[8,32,576]{2,1,0:T(8,128)(2,1)S(1)} %constant_dynamic-update-slice_fusion.own_keys), channel_id=1, source_target_pairs={{0,2},{1,3},{2,0},{3,1},{4,6},{5,7},{6,4},{7,5},{8,10},{9,11},{10,... | collective-permute-start | bytes 884744 | tf_op jit(solution)/shard_map/ppermute | solution.py:480
  35.9 10.4 %copy-start.2 = (s32[1024]{0:T(1024)S(1)}, s32[1024]{0:T(1024)}, u32[]{:S(2)}) copy-start(s32[1024]{0:T(1024)} %positions_ref.3) | copy-start | bytes 12292
  40.4 4.2 %collective-permute-start.6 = (bf16[64,1792]{1,0:T(8,128)(2,1)S(1)}, bf16[64,1792]{1,0:T(8,128)(2,1)S(1)}, u32[]{:S(2)}, u32[]{:S(2)}) collective-permute-start(bf16[64,1792]{1,0:T(8,128)(2,1)S(1)} %get-tuple-element.39), channel_id=1, source_target_pairs={{0,1},{1,0},{2,3},{3,2},{4,5},{5,4},{6,7},{7,6},{8,9},{9,8},{10,11... | collective-permute-start | bytes 688136 | tf_op jit(solution)/shard_map/ppermute | solution.py:480
  40.6 5.0 %collective-permute-start.9 = (bf16[8,32,576]{2,1,0:T(8,128)(2,1)S(1)}, bf16[8,32,576]{2,1,0:T(8,128)(2,1)S(1)}, u32[]{:S(2)}, u32[]{:S(2)}) collective-permute-start(bf16[8,32,576]{2,1,0:T(8,128)(2,1)S(1)} %constant_dynamic-update-slice_fusion.own_keys), channel_id=1, source_target_pairs={{0,1},{1,0},{2,3},{3,2},{4,5},{5,4},{6,7},{7,6},{8,9},{9,8},{10,11... | collective-permute-start | bytes 884744 | tf_op jit(solution)/shard_map/ppermute | solution.py:480
  44.6 1.6 %collective-permute-start.10 = (bf16[8,32,576]{2,1,0:T(8,128)(2,1)S(1)}, bf16[8,32,576]{2,1,0:T(8,128)(2,1)S(1)}, u32[]{:S(2)}, u32[]{:S(2)}) collective-permute-start(bf16[8,32,576]{2,1,0:T(8,128)(2,1)S(1)} %collective-permute-done.7.far_keys), channel_id=1, source_target_pairs={{0,1},{1,0},{2,3},{3,2},{4,5},{5,4},{6,7},{7,6},{8,9},{9,8},{10,11... | collective-permute-start | bytes 884744 | tf_op jit(solution)/shard_map/ppermute | solution.py:480
  44.7 8.1 %collective-permute-start.8 = (bf16[64,1792]{1,0:T(8,128)(2,1)S(1)}, bf16[64,1792]{1,0:T(8,128)(2,1)S(1)}, u32[]{:S(2)}, u32[]{:S(2)}) collective-permute-start(bf16[64,1792]{1,0:T(8,128)(2,1)S(1)} %add.4), channel_id=1, source_target_pairs={{0,2},{1,3},{2,0},{3,1},{4,6},{5,7},{6,4},{7,5},{8,10},{9,11},{10,... | collective-permute-start | bytes 688136 | tf_op jit(solution)/shard_map/ppermute | solution.py:480
  45.3 7.5 %collective-permute-start.11 = (bf16[64,1792]{1,0:T(8,128)(2,1)S(1)}, bf16[64,1792]{1,0:T(8,128)(2,1)S(1)}, u32[]{:S(2)}, u32[]{:S(2)}) collective-permute-start(bf16[64,1792]{1,0:T(8,128)(2,1)S(1)} %get-tuple-element.50), channel_id=1, source_target_pairs={{0,1},{1,0},{2,3},{3,2},{4,5},{5,4},{6,7},{7,6},{8,9},{9,8},{10,11... | collective-permute-start | bytes 688136 | tf_op jit(solution)/shard_map/ppermute | solution.py:480
  53.6 14.0 %all-to-all-start.1 = ((bf16[8,8,1792]{2,1,0:T(8,128)(2,1)}), bf16[8,8,1792]{2,1,0:T(8,128)(2,1)S(1)}, u32[]{:S(2)}, u32[]{:S(2)}) async-start(bf16[8,8,1792]{2,1,0:T(8,128)(2,1)} %bitcast.7), calls=%async_computation.1 | async-start | bytes 458752 | tf_op jit(solution)/shard_map/all_to_all | solution.py:483
  58.3 1.3 %copy-start.3 = (bf16[1024,576]{1,0:T(8,128)(2,1)S(1)}, bf16[1024,576]{1,0:T(8,128)(2,1)}, u32[]{:S(2)}) copy-start(bf16[1024,576]{1,0:T(8,128)(2,1)} %get-tuple-element.45.keys_ref) | copy-start | bytes 3538948
  59.6 8.0 %copy-start = (bf16[64,128]{1,0:T(8,128)(2,1)S(1)}, bf16[64,128]{1,0:T(8,128)(2,1)}, u32[]{:S(2)}) copy-start(bf16[64,128]{1,0:T(8,128)(2,1)} %get-tuple-element.47.high_ref) | copy-start | bytes 49156
  59.6 8.0 %copy-start.1 = (bf16[64,128]{1,0:T(8,128)(2,1)S(1)}, bf16[64,128]{1,0:T(8,128)(2,1)}, u32[]{:S(2)}) copy-start(bf16[64,128]{1,0:T(8,128)(2,1)} %get-tuple-element.48.low_ref) | copy-start | bytes 49156
where the time goes:
time: 69.4 us; the launch traced here: 68.8 us
  Pallas kernels  30.7 us (44%)
  starting transfers between devices  22.3 us (32%)
  waiting for transfers between devices  12.8 us (18%)
  local copies, waits for them, and re-layouts  1.37 us (2%)
  other arithmetic  0.9 us (1%)
  between operations  0.76 us (1%)
    all_to_all x2, starting transfers between devices, exchange(): return lax.all_to_all(value, 'ctx', split_axis=0, concat_axis=0, tiled=True)  12 us
    pallas_call x1, Pallas kernels, attend_high(): pl.pallas_call(high_kernel, out_shape=jax.ShapeDtypeStruct((2 * HALF, col...  7.98 us
    ppermute x3, waiting for transfers between devices, over_ctx(): return lax.ppermute(value, 'ctx', [(i, i ^ flip) for i in range(ctx)])  7.42 us
    ppermute x3, starting transfers between devices, over_ctx(): return lax.ppermute(value, 'ctx', [(i, i ^ flip) for i in range(ctx)])  6.68 us
    pallas_call x1, Pallas kernels, attend_low(): pl.pallas_call(low_kernel, out_shape=[jax.ShapeDtypeStruct((key_count, wi...  6.29 us
    ppermute x9, waiting for transfers between devices, over_ep(): return lax.ppermute(value, 'ep', [(i, i ^ flip) for i in range(4)])  5.33 us
    pallas_call x1, Pallas kernels, fold(): pl.pallas_call(fold_kernel, out_shape=jax.ShapeDtypeStruct((2, heads * HA...  4.63 us
    pallas_call x1, Pallas kernels, far_experts(): pl.pallas_call(far_kernel, out_shape=[jax.ShapeDtypeStruct((slots, featur...  4.5 us
  transfers between devices with their start and end apart: 14, of which 6 were waited for; matrix products, arithmetic and copies ran while one was open for 1% of the time, Pallas kernels for 39%

commit v1 on v0

--- a/solution.py
+++ b/solution.py
@@ -26,21 +26,36 @@
 HBM_SPEC = pl.BlockSpec(memory_space=pltpu.HBM)
 
 
-def route_kernel(
-    ep_ref,
-    ids_ref,
-    weights_ref,
-    rope_ref,
-    rows_ref,
-    latent_ref,
-    sent_ref,
-    high_ref,
-    low_ref,
-    packed_ref,
-):
-    quarter = packed_ref.shape[0]
+def gather_order(ctx):
+    bits = ctx.bit_length() - 1
+    return [1 << (bits - 1)] + [1 << bit for bit in range(bits - 1)]
+
+
+def pack_kernel(ep_ref, latent_ref, rope_ref, packed_ref):
     latent_width = latent_ref.shape[1]
-    place = pl.multiple_of(ep_ref[0] * quarter, quarter)
+    rope = rope_ref[...].astype(jnp.float32).T
+    for core in range(2):
+
+        @pl.when(ep_ref[0] % 2 == core)
+        def _():
+            rows = slice(core * HALF, (core + 1) * HALF)
+            packed_ref[:, :latent_width] = latent_ref[rows, :]
+            packed_ref[:, latent_width:] = rope[rows].astype(jnp.bfloat16)
+
+
+def pack(ep, latent, k_rope):
+    return pl.pallas_call(
+        pack_kernel,
+        out_shape=jax.ShapeDtypeStruct((HALF, latent.shape[1] + ROPE), jnp.bfloat16),
+        in_specs=[SMEM_SPEC] + [VMEM_SPEC] * 2,
+        out_specs=VMEM_SPEC,
+        compiler_params=pltpu.CompilerParams(vmem_limit_bytes=FULL),
+        cost_estimate=pl.CostEstimate(flops=0, bytes_accessed=MIB // 4, transcendentals=0),
+        name="pack",
+    )(ep, latent, k_rope.T)
+
+
+def route_kernel(ids_ref, weights_ref, rows_ref, sent_ref, high_ref, low_ref):
     row_count = ids_ref.shape[1]
     slots = sent_ref.shape[0] * CAP
     slot = lax.broadcasted_iota(jnp.int32, (slots, row_count), 0)
@@ -61,25 +76,13 @@
     high = gate.astype(jnp.bfloat16)
     high_ref[...] = high
     low_ref[...] = (gate - high.astype(jnp.float32)).astype(jnp.bfloat16)
-    rope = rope_ref[...].astype(jnp.float32).T
-    packed_ref[:, :latent_width] = latent_ref[pl.ds(place, quarter), :]
-    for part in range(row_count // quarter):
-
-        @pl.when(ep_ref[0] == part)
-        def _():
-            packed_ref[:, latent_width:] = rope[part * quarter : (part + 1) * quarter].astype(
-                jnp.bfloat16
-            )
-
     sent = jnp.dot(select, rows_ref[...], preferred_element_type=jnp.float32)
     for index in range(slots // CAP):
         sent_ref[index] = sent[index * CAP : (index + 1) * CAP].astype(jnp.bfloat16)
 
 
-def route(ep, expert_ids, expert_weights, k_rope, moe_rows, latent, ctx):
+def route(expert_ids, expert_weights, moe_rows, ctx):
     row_count, features = moe_rows.shape
-    quarter = row_count // 4
-    latent_width = latent.shape[1]
     slots = ctx * CAP
     return pl.pallas_call(
         route_kernel,
@@ -87,16 +90,15 @@
             jax.ShapeDtypeStruct((ctx, CAP, features), jnp.bfloat16),
             jax.ShapeDtypeStruct((slots, row_count), jnp.bfloat16),
             jax.ShapeDtypeStruct((slots, row_count), jnp.bfloat16),
-            jax.ShapeDtypeStruct((quarter, latent_width + ROPE), jnp.bfloat16),
         ],
-        in_specs=[SMEM_SPEC] + [VMEM_SPEC] * 5,
-        out_specs=[VMEM_SPEC] * 4,
+        in_specs=[VMEM_SPEC] * 3,
+        out_specs=[VMEM_SPEC] * 3,
         compiler_params=pltpu.CompilerParams(vmem_limit_bytes=FULL),
         cost_estimate=pl.CostEstimate(
             flops=2 * row_count * slots * features, bytes_accessed=1 * MIB, transcendentals=0
         ),
         name="route",
-    )(ep, expert_ids.T, expert_weights.T, k_rope.T, moe_rows, latent)
+    )(expert_ids.T, expert_weights.T, moe_rows)
 
 
 def weight_copies(ep_ref, flips, gate_hbm, up_hbm, gate, up, semaphores):
@@ -358,9 +360,7 @@
     queries_ref,
     w_uv_hbm,
     own_keys,
-    core_own_keys,
-    far_keys,
-    core_far_keys,
+    core_keys,
     keys_ref,
     out_ref,
     w_uv_ref,
@@ -370,9 +370,13 @@
     w_uv_copy.start()
     blocks, block_rows, width = own_keys.shape
     my_ctx, my_ep = own_ref[0], own_ref[1]
-    for flip, source in enumerate((own_keys, core_own_keys, far_keys, core_far_keys)):
+    for flip, source in enumerate((own_keys, core_keys)):
         for index in range(blocks):
-            start = (index ^ my_ctx) * (4 * block_rows) + (my_ep ^ flip) * block_rows
+            source_ctx = my_ctx
+            for bit, step in enumerate(gather_order(blocks)):
+                if index >> bit & 1:
+                    source_ctx = source_ctx ^ step
+            start = source_ctx * (2 * HALF) + ((my_ep % 2) ^ flip) * HALF
             place = pl.multiple_of(positions_ref[start], block_rows)
             keys_ref[pl.ds(place, block_rows), :] = source[index]
     run, base, _ = runs_of(my_ctx, positions_ref)
@@ -420,7 +424,7 @@
             jax.ShapeDtypeStruct((key_count, width), jnp.bfloat16),
             jax.ShapeDtypeStruct((HALF, columns), jnp.bfloat16),
         ],
-        in_specs=[SMEM_SPEC] * 2 + [VMEM_SPEC, HBM_SPEC] + [VMEM_SPEC] * 4,
+        in_specs=[SMEM_SPEC] * 2 + [VMEM_SPEC, HBM_SPEC] + [VMEM_SPEC] * 2,
         out_specs=[VMEM_SPEC] * 2,
         scratch_shapes=[VMEM(w_uv.shape, jnp.bfloat16), pltpu.SemaphoreType.DMA(())],
         compiler_params=pltpu.CompilerParams(vmem_limit_bytes=LIMIT),
@@ -482,42 +486,37 @@
     def exchange(value):
         return lax.all_to_all(value, "ctx", split_axis=0, concat_axis=0, tiled=True)
 
-    outgoing, high, low, packed = route(
-        ep, expert_ids, expert_weights, k_rope, moe_rows, latent, ctx
-    )
+    packed = pack(ep, latent, k_rope)
+    packed, moe_rows = lax.optimization_barrier((packed, moe_rows))
+    outgoing, high, low = route(expert_ids, expert_weights, moe_rows, ctx)
     arrived = exchange(outgoing)
-    packed, q_nope = lax.optimization_barrier((packed, q_nope))
+    high, q_nope = lax.optimization_barrier((high, q_nope))
     queries = fold(q_nope, q_rope, w_uk)
     own_keys = packed[None]
-    step = 1
-    while step < ctx // 2:
-        own_keys = jnp.concatenate([own_keys, over_ctx(own_keys, step)], axis=0)
-        step *= 2
+    flips = gather_order(ctx)
+    for flip in flips[:-1]:
+        own_keys = jnp.concatenate([own_keys, over_ctx(own_keys, flip)], axis=0)
     arrived, queries, own_keys = lax.optimization_barrier((arrived, queries, own_keys))
 
     own = arrived.reshape(ctx * CAP, arrived.shape[2])
     far = over_ep(own, 2)
     core = over_ep(own, 1)
+    received = over_ctx(own_keys, flips[-1])
     gate_part, up_part = near_experts(ep, own, core, w_gate, w_up)
-    received = over_ctx(own_keys, step)
-    received, far, gate_part = lax.optimization_barrier((received, far, gate_part))
+    far, gate_part = lax.optimization_barrier((far, gate_part))
     core_far = over_ep(far, 1)
-    own_keys = jnp.concatenate([own_keys, received], axis=0)
-    far_keys = over_ep(own_keys, 2)
+    core_far, received = lax.optimization_barrier((core_far, received))
     own_out, core_out, far_out, core_far_out = far_experts(
         ep, far, core_far, gate_part, up_part, w_gate, w_up, w_down
     )
     from_core_far = over_ep(core_far_out, 1)
     from_core = over_ep(core_out, 1)
-    core_own_keys = over_ep(own_keys, 1)
-    from_core_far, far_keys = lax.optimization_barrier((from_core_far, far_keys))
+    own_keys = jnp.concatenate([own_keys, received], axis=0)
+    core_keys = over_ep(own_keys, 1)
     to_far = add(far_out, from_core_far)
     from_far = over_ep(to_far, 2)
-    core_far_keys = over_ep(far_keys, 1)
     place = jnp.concatenate([me, ep])
-    keys, low_out = attend_low(
-        place, positions, queries, w_uv, (own_keys, core_own_keys, far_keys, core_far_keys)
-    )
+    keys, low_out = attend_low(place, positions, queries, w_uv, (own_keys, core_keys))
     from_far, keys, low_out = lax.optimization_barrier((from_far, keys, low_out))
     returning = add(own_out, from_core, from_far)
     returned = exchange(returning.reshape(arrived.shape))

time: 69.4 us -> 63.1 us (0.909)
  waiting for transfers between devices: 12.8 us -> 7.79 us
  starting transfers between devices: 22.3 us -> 19.2 us
  Pallas kernels: 30.7 us -> 32.3 us
    all_to_all x2, starting transfers between devices: 12 us -> 8.38 us  [exchange(): return lax.all_to_all(value, 'ctx', split_axis=0, concat_axis=0, tiled=True)]
    ppermute x3, waiting for transfers between devices: 7.42 us -> 4.16 us  [over_ctx(): return lax.ppermute(value, 'ctx', [(i, i ^ flip) for i in range(ctx)])]
    ppermute x9 -> x7, waiting for transfers between devices: 5.33 us -> 3.63 us  [over_ep(): return lax.ppermute(value, 'ep', [(i, i ^ flip) for i in range(4)])]
    pallas_call x0 -> x1, Pallas kernels: none -> 1.64 us  [pack(): pl.pallas_call(pack_kernel, out_shape=jax.ShapeDtypeStruct((HALF, latent....]
    ppermute x3, starting transfers between devices: 6.68 us -> 7.85 us  [over_ctx(): return lax.ppermute(value, 'ctx', [(i, i ^ flip) for i in range(ctx)])]
    ppermute x9 -> x7, starting transfers between devices: 3.69 us -> 2.95 us  [over_ep(): return lax.ppermute(value, 'ep', [(i, i ^ flip) for i in range(4)])]
  transfers between devices with their start and end apart: 14 -> 12, of which waited for: 6 -> 5; matrix products, arithmetic and copies ran while one was open for 1% -> 2% of each run, Pallas kernels for 39% -> 46%
where the time goes in v1:
time: 63.1 us; the launch traced here: 62.4 us
  Pallas kernels  32.3 us (51%)
  starting transfers between devices  19.2 us (30%)
  waiting for transfers between devices  7.79 us (12%)
  local copies, waits for them, and re-layouts  1.4 us (2%)
  other arithmetic  1.05 us (2%)
  between operations  0.76 us (1%)
    all_to_all x2, starting transfers between devices, exchange(): return lax.all_to_all(value, 'ctx', split_axis=0, concat_axis=0, tiled=True)  8.38 us
    pallas_call x1, Pallas kernels, attend_high(): pl.pallas_call(high_kernel, out_shape=jax.ShapeDtypeStruct((2 * HALF, col...  7.98 us
    ppermute x3, starting transfers between devices, over_ctx(): return lax.ppermute(value, 'ctx', [(i, i ^ flip) for i in range(ctx)])  7.85 us
    pallas_call x1, Pallas kernels, attend_low(): pl.pallas_call(low_kernel, out_shape=[jax.ShapeDtypeStruct((key_count, wi...  6.31 us
    pallas_call x1, Pallas kernels, fold(): pl.pallas_call(fold_kernel, out_shape=jax.ShapeDtypeStruct((2, heads * HA...  4.64 us
    pallas_call x1, Pallas kernels, far_experts(): pl.pallas_call(far_kernel, out_shape=[jax.ShapeDtypeStruct((slots, featur...  4.5 us
    ppermute x3, waiting for transfers between devices, over_ctx(): return lax.ppermute(value, 'ctx', [(i, i ^ flip) for i in range(ctx)])  4.16 us
    ppermute x7, waiting for transfers between devices, over_ep(): return lax.ppermute(value, 'ep', [(i, i ^ flip) for i in range(4)])  3.63 us
  transfers between devices with their start and end apart: 12, of which 5 were waited for; matrix products, arithmetic and copies ran while one was open for 2% of the time, Pallas kernels for 46%

profile of v1, /device:TPU:0, one launch (start us, length us, event | category | flops | bytes accessed | tf_op | source)
XLA Modules:
  0.0 62.4 jit_solution(6205931709245437435)
XLA Ops:
  0.6 1.6 %pack.1 = bf16[64,576]{1,0:T(8,128)(2,1)} custom-call(s32[1]{0:T(128)} %bitcast.1.ep_ref, bf16[128,512]{1,0:T(8,128)(2,1)} %latent_ref.1, bf16[64,128]{1,0:T(8,128)(2,1)} %bitcast.16), custom_call_target="tpu_custom_call" | custom-call | bytes 262144 | tf_op jit(solution)/shard_map/pack/pallas_call | solution.py:47
  2.3 4.0 %collective-permute-start = (bf16[1,64,576]{2,1,0:T(8,128)(2,1)}, bf16[1,64,576]{2,1,0:T(8,128)(2,1)S(1)}, u32[]{:S(2)}, u32[]{:S(2)}) collective-permute-start(bf16[1,64,576]{2,1,0:T(8,128)(2,1)} %bitcast.13), channel_id=1, source_target_pairs={{0,16},{4,20},{8,24},{12,28},{16,0},{20,4},{24,8},{28,12},{1,17},{... | collective-permute-start | bytes 221192 | tf_op jit(solution)/shard_map/ppermute | solution.py:481
  6.3 2.1 %route.1 = (bf16[8,8,1792]{2,1,0:T(8,128)(2,1)}, bf16[64,128]{1,0:T(8,128)(2,1)}, bf16[64,128]{1,0:T(8,128)(2,1)}) custom-call(s32[8,128]{1,0:T(8,128)} %bitcast.17, f32[8,128]{1,0:T(8,128)} %bitcast.18, bf16[128,1792]{1,0:T(8,128)(2,1)} %rows_ref), custom_call_target="tpu_custom_call" | custom-call | flops 29360128 | bytes 1048576 | tf_op jit(solution)/shard_map/route/pallas_call | solution.py:87
  8.4 3.8 %all-to-all-start = ((bf16[8,8,1792]{2,1,0:T(8,128)(2,1)}), bf16[8,8,1792]{2,1,0:T(8,128)(2,1)S(1)}, u32[]{:S(2)}, u32[]{:S(2)}) async-start(bf16[8,8,1792]{2,1,0:T(8,128)(2,1)} %get-tuple-element.28), calls=%async_computation | async-start | bytes 458752 | tf_op jit(solution)/shard_map/all_to_all | solution.py:487
  12.2 0.0 collective-permute-done
  12.2 0.9 %pad_maximum_fusion.1 = bf16[2,64,576]{2,1,0:T(8,128)(2,1)S(1)} fusion(bf16[1,64,576]{2,1,0:T(8,128)(2,1)S(1)} %collective-permute-done, bf16[1,64,576]{2,1,0:T(8,128)(2,1)} %bitcast.14), kind=kLoop, calls=%fused_computation.1 | loop fusion | flops 73728 | bytes 294912 | tf_op jit(solution)/shard_map/concatenate | solution.py:498
  13.1 2.1 %collective-permute-start.1 = (bf16[2,64,576]{2,1,0:T(8,128)(2,1)S(1)}, bf16[2,64,576]{2,1,0:T(8,128)(2,1)S(1)}, u32[]{:S(2)}, u32[]{:S(2)}) collective-permute-start(bf16[2,64,576]{2,1,0:T(8,128)(2,1)S(1)} %pad_maximum_fusion.1), channel_id=1, source_target_pairs={{0,4},{4,0},{8,12},{12,8},{16,20},{20,16},{24,28},{28,24},{1,5},{5... | collective-permute-start | bytes 442376 | tf_op jit(solution)/shard_map/ppermute | solution.py:481
  15.2 0.0 copy-start.4
  15.2 4.6 %fold.1.queries_ref = bf16[2,1024,576]{2,1,0:T(8,128)(2,1)} custom-call(bf16[128,2048]{1,0:T(8,128)(2,1)} %q_nope_ref, bf16[128,1024]{1,0:T(8,128)(2,1)} %q_rope_ref.1, bf16[512,2048]{1,0:T(8,128)(2,1)} %w_uk_ref.1), custom_call_target="tpu_custom_call" | custom-call | flops 268435456 | bytes 6291456 | tf_op jit(solution)/shard_map/fold/pallas_call | solution.py:292
  19.9 0.9 %collective-permute-done.1 = bf16[2,64,576]{2,1,0:T(8,128)(2,1)S(1)} collective-permute-done((bf16[2,64,576]{2,1,0:T(8,128)(2,1)S(1)}, bf16[2,64,576]{2,1,0:T(8,128)(2,1)S(1)}, u32[]{:S(2)}, u32[]{:S(2)}) %collective-permute-start.1) | collective-permute-done | bytes 147488 | tf_op jit(solution)/shard_map/ppermute | solution.py:481
  20.7 0.0 copy-done.4
  20.7 0.1 pad_maximum_fusion
  20.8 0.0 all-to-all-done
  20.8 0.1 collective-permute-start.3
  20.9 1.6 %collective-permute-start.2 = (bf16[64,1792]{1,0:T(8,128)(2,1)S(1)}, bf16[64,1792]{1,0:T(8,128)(2,1)S(1)}, u32[]{:S(2)}, u32[]{:S(2)}) collective-permute-start(bf16[64,1792]{1,0:T(8,128)(2,1)S(1)} %bitcast.11), channel_id=1, source_target_pairs={{0,2},{1,3},{2,0},{3,1},{4,6},{5,7},{6,4},{7,5},{8,10},{9,11},{10,... | collective-permute-start | bytes 688136 | tf_op jit(solution)/shard_map/ppermute | solution.py:484
  22.4 1.7 %collective-permute-start.5 = (bf16[4,64,576]{2,1,0:T(8,128)(2,1)S(1)}, bf16[4,64,576]{2,1,0:T(8,128)(2,1)S(1)}, u32[]{:S(2)}, u32[]{:S(2)}) collective-permute-start(bf16[4,64,576]{2,1,0:T(8,128)(2,1)S(1)} %pad_maximum_fusion), channel_id=1, source_target_pairs={{0,8},{4,12},{8,0},{12,4},{16,24},{20,28},{24,16},{28,20},{1,9},{5... | collective-permute-start | bytes 884744 | tf_op jit(solution)/shard_map/ppermute | solution.py:481
  24.2 0.0 collective-permute-done.3.core_ref
  24.2 3.1 %near_experts.1 = (f32[64,256]{1,0:T(8,128)S(1)}, f32[64,256]{1,0:T(8,128)S(1)}) custom-call(s32[1]{0:T(128)} %bitcast.1.ep_ref, bf16[64,1792]{1,0:T(8,128)(2,1)S(1)} %bitcast.12, bf16[64,1792]{1,0:T(8,128)(2,1)S(1)} %collective-permute-done.3.core_ref, bf16[1,7168,256]{2,1,0:T(8,128)(2,1)} %gate_hbm.3, bf16[1,7168,256]{2,1,0:T(8,128)(2,1)} %up_hbm.3), custom_call_target="tpu_custom_call" | custom-call | flops 234881024 | bytes 3670016 | tf_op jit(solution)/shard_map/near_experts/pallas_call | solution.py:138
  27.3 1.7 %collective-permute-done.2.far_ref = bf16[64,1792]{1,0:T(8,128)(2,1)S(1)} collective-permute-done((bf16[64,1792]{1,0:T(8,128)(2,1)S(1)}, bf16[64,1792]{1,0:T(8,128)(2,1)S(1)}, u32[]{:S(2)}, u32[]{:S(2)}) %collective-permute-start.2) | collective-permute-done | bytes 229408 | tf_op jit(solution)/shard_map/ppermute | solution.py:484
  28.9 0.0 collective-permute-start.4
  28.9 3.3 %collective-permute-done.5 = bf16[4,64,576]{2,1,0:T(8,128)(2,1)S(1)} collective-permute-done((bf16[4,64,576]{2,1,0:T(8,128)(2,1)S(1)}, bf16[4,64,576]{2,1,0:T(8,128)(2,1)S(1)}, u32[]{:S(2)}, u32[]{:S(2)}) %collective-permute-start.5) | collective-permute-done | bytes 294944 | tf_op jit(solution)/shard_map/ppermute | solution.py:481
  32.2 0.0 collective-permute-done.4.core_far_ref
  32.3 0.1 collective-permute-start.8
  32.4 0.0 copy-start.2
  32.4 4.5 %far_experts.1 = (bf16[64,1792]{1,0:T(8,128)(2,1)S(1)}, bf16[64,1792]{1,0:T(8,128)(2,1)S(1)}, bf16[64,1792]{1,0:T(8,128)(2,1)S(1)}, bf16[64,1792]{1,0:T(8,128)(2,1)S(1)}) custom-call(s32[1]{0:T(128)} %bitcast.1.ep_ref, bf16[64,1792]{1,0:T(8,128)(2,1)S(1)} %collective-permute-done.2.far_ref, bf16[64,1792]{1,0:T(8,128)(2,1)S(1)} %collective-permute-done.4.core_far_ref, ...), custom_call_target="tpu_custom_call" | custom-call | flops 469762048 | bytes 7340032 | tf_op jit(solution)/shard_map/far_experts/pallas_call | solution.py:206
  36.9 0.6 collective-permute-start.6
  37.4 1.1 %collective-permute-done.6.refs_1_ = bf16[64,1792]{1,0:T(8,128)(2,1)S(1)} collective-permute-done((bf16[64,1792]{1,0:T(8,128)(2,1)S(1)}, bf16[64,1792]{1,0:T(8,128)(2,1)S(1)}, u32[]{:S(2)}, u32[]{:S(2)}) %collective-permute-start.6) | collective-permute-done | bytes 229408 | tf_op jit(solution)/shard_map/ppermute | solution.py:484
  38.5 0.1 add.4
  38.6 0.6 collective-permute-start.7
  39.2 0.1 collective-permute-start.9
  39.3 0.1 pad_add_fusion.own_ref
  39.4 0.0 collective-permute-done.8.core_keys
  39.4 0.0 copy-done.2
  39.4 6.3 %attention_low.1 = (bf16[1024,576]{1,0:T(8,128)(2,1)}, bf16[64,2048]{1,0:T(8,128)(2,1)S(1)}) custom-call(s32[2]{0:T(128)S(1)} %pad_add_fusion.own_ref, s32[1024]{0:T(1024)S(1)} %copy-done.2, bf16[2,1024,576]{2,1,0:T(8,128)(2,1)} %fold.1.queries_ref, bf16[512,2048]{1,0:T(8,128)(2,1)} %w_uv_hbm.3, ...), custom_call_target="tpu_custom_call" | custom-call | flops 1207959552 | bytes 6291456 | tf_op jit(solution)/shard_map/attention_low/pallas_call | solution.py:421
  45.7 0.9 %collective-permute-done.7.refs_2_ = bf16[64,1792]{1,0:T(8,128)(2,1)S(1)} collective-permute-done((bf16[64,1792]{1,0:T(8,128)(2,1)S(1)}, bf16[64,1792]{1,0:T(8,128)(2,1)S(1)}, u32[]{:S(2)}, u32[]{:S(2)}) %collective-permute-start.7) | collective-permute-done | bytes 229408 | tf_op jit(solution)/shard_map/ppermute | solution.py:484
  46.6 0.0 collective-permute-done.9.refs_1_
  46.6 0.8 %add.5 = bf16[64,1792]{1,0:T(8,128)(2,1)} custom-call(bf16[64,1792]{1,0:T(8,128)(2,1)S(1)} %get-tuple-element.49.refs_0_, bf16[64,1792]{1,0:T(8,128)(2,1)S(1)} %collective-permute-done.9.refs_1_, bf16[64,1792]{1,0:T(8,128)(2,1)S(1)} %collective-permute-done.7.refs_2_), custom_call_target="tpu_custom_call" | custom-call | bytes 1048576 | tf_op jit(solution)/shard_map/add/pallas_call | solution.py:236
  47.3 4.6 %all-to-all-start.1 = ((bf16[8,8,1792]{2,1,0:T(8,128)(2,1)}), bf16[8,8,1792]{2,1,0:T(8,128)(2,1)S(1)}, u32[]{:S(2)}, u32[]{:S(2)}) async-start(bf16[8,8,1792]{2,1,0:T(8,128)(2,1)} %bitcast.7), calls=%async_computation.1 | async-start | bytes 458752 | tf_op jit(solution)/shard_map/all_to_all | solution.py:487
  51.9 0.0 copy-start.3
  51.9 1.3 %copy-done.3 = bf16[1024,576]{1,0:T(8,128)(2,1)S(1)} copy-done((bf16[1024,576]{1,0:T(8,128)(2,1)S(1)}, bf16[1024,576]{1,0:T(8,128)(2,1)}, u32[]{:S(2)}) %copy-start.3) | copy-done | bytes 1179672
  53.2 0.0 copy-start
  53.2 0.0 copy-start.1
  53.2 8.0 %attention_high.1 = bf16[128,2048]{1,0:T(8,128)(2,1)} custom-call(s32[2]{0:T(128)S(1)} %pad_add_fusion.own_ref, s32[1024]{0:T(1024)S(1)} %copy-done.2, bf16[2,1024,576]{2,1,0:T(8,128)(2,1)} %fold.1.queries_ref, bf16[512,2048]{1,0:T(8,128)(2,1)} %w_uv_hbm.3, bf16[1024,576]{1,0:T(8,128)(2,1)S(1)} %copy-done.3, bf16[64,2048]{1,0:T(8,128)(2,1)S(1)} %get-tuple-element.46.low_ref), custom_call_target="tpu_custom_call" | custom-call | flops 2415919104 | bytes 6291456 | tf_op jit(solution)/shard_map/attention_high/pallas_call | solution.py:445
  61.2 0.0 all-to-all-done.1
  61.2 0.0 copy-done
  61.2 0.0 copy-done.1
  61.2 1.2 %combine.1 = bf16[128,1792]{1,0:T(8,128)(2,1)} custom-call(bf16[64,128]{1,0:T(8,128)(2,1)S(1)} %copy-done, bf16[64,128]{1,0:T(8,128)(2,1)S(1)} %copy-done.1, bf16[64,1792]{1,0:T(8,128)(2,1)S(1)} %bitcast.9), custom_call_target="tpu_custom_call" | custom-call | flops 58720256 | bytes 1048576 | tf_op jit(solution)/shard_map/combine/pallas_call | solution.py:259
  (2 shorter events, 0.1 us)
Async XLA Ops:
  2.3 9.9 %collective-permute-start = (bf16[1,64,576]{2,1,0:T(8,128)(2,1)}, bf16[1,64,576]{2,1,0:T(8,128)(2,1)S(1)}, u32[]{:S(2)}, u32[]{:S(2)}) collective-permute-start(bf16[1,64,576]{2,1,0:T(8,128)(2,1)} %bitcast.13), channel_id=1, source_target_pairs={{0,16},{4,20},{8,24},{12,28},{16,0},{20,4},{24,8},{28,12},{1,17},{... | collective-permute-start | bytes 221192 | tf_op jit(solution)/shard_map/ppermute | solution.py:481
  8.4 12.4 %all-to-all-start = ((bf16[8,8,1792]{2,1,0:T(8,128)(2,1)}), bf16[8,8,1792]{2,1,0:T(8,128)(2,1)S(1)}, u32[]{:S(2)}, u32[]{:S(2)}) async-start(bf16[8,8,1792]{2,1,0:T(8,128)(2,1)} %get-tuple-element.28), calls=%async_computation | async-start | bytes 458752 | tf_op jit(solution)/shard_map/all_to_all | solution.py:487
  13.1 7.6 %collective-permute-start.1 = (bf16[2,64,576]{2,1,0:T(8,128)(2,1)S(1)}, bf16[2,64,576]{2,1,0:T(8,128)(2,1)S(1)}, u32[]{:S(2)}, u32[]{:S(2)}) collective-permute-start(bf16[2,64,576]{2,1,0:T(8,128)(2,1)S(1)} %pad_maximum_fusion.1), channel_id=1, source_target_pairs={{0,4},{4,0},{8,12},{12,8},{16,20},{20,16},{24,28},{28,24},{1,5},{5... | collective-permute-start | bytes 442376 | tf_op jit(solution)/shard_map/ppermute | solution.py:481
  15.2 5.5 %copy-start.4 = (bf16[64,576]{1,0:T(8,128)(2,1)S(1)}, bf16[64,576]{1,0:T(8,128)(2,1)}, u32[]{:S(2)}) copy-start(bf16[64,576]{1,0:T(8,128)(2,1)} %pack.1) | copy-start | bytes 221188
  20.8 3.4 %collective-permute-start.3 = (bf16[64,1792]{1,0:T(8,128)(2,1)S(1)}, bf16[64,1792]{1,0:T(8,128)(2,1)S(1)}, u32[]{:S(2)}, u32[]{:S(2)}) collective-permute-start(bf16[64,1792]{1,0:T(8,128)(2,1)S(1)} %bitcast.10), channel_id=1, source_target_pairs={{0,1},{1,0},{2,3},{3,2},{4,5},{5,4},{6,7},{7,6},{8,9},{9,8},{10,11... | collective-permute-start | bytes 688136 | tf_op jit(solution)/shard_map/ppermute | solution.py:484
  20.9 8.0 %collective-permute-start.2 = (bf16[64,1792]{1,0:T(8,128)(2,1)S(1)}, bf16[64,1792]{1,0:T(8,128)(2,1)S(1)}, u32[]{:S(2)}, u32[]{:S(2)}) collective-permute-start(bf16[64,1792]{1,0:T(8,128)(2,1)S(1)} %bitcast.11), channel_id=1, source_target_pairs={{0,2},{1,3},{2,0},{3,1},{4,6},{5,7},{6,4},{7,5},{8,10},{9,11},{10,... | collective-permute-start | bytes 688136 | tf_op jit(solution)/shard_map/ppermute | solution.py:484
  22.4 9.8 %collective-permute-start.5 = (bf16[4,64,576]{2,1,0:T(8,128)(2,1)S(1)}, bf16[4,64,576]{2,1,0:T(8,128)(2,1)S(1)}, u32[]{:S(2)}, u32[]{:S(2)}) collective-permute-start(bf16[4,64,576]{2,1,0:T(8,128)(2,1)S(1)} %pad_maximum_fusion), channel_id=1, source_target_pairs={{0,8},{4,12},{8,0},{12,4},{16,24},{20,28},{24,16},{28,20},{1,9},{5... | collective-permute-start | bytes 884744 | tf_op jit(solution)/shard_map/ppermute | solution.py:481
  28.9 3.3 %collective-permute-start.4 = (bf16[64,1792]{1,0:T(8,128)(2,1)S(1)}, bf16[64,1792]{1,0:T(8,128)(2,1)S(1)}, u32[]{:S(2)}, u32[]{:S(2)}) collective-permute-start(bf16[64,1792]{1,0:T(8,128)(2,1)S(1)} %collective-permute-done.2.far_ref), channel_id=1, source_target_pairs={{0,1},{1,0},{2,3},{3,2},{4,5},{5,4},{6,7},{7,6},{8,9},{9,8},{10,11... | collective-permute-start | bytes 688136 | tf_op jit(solution)/shard_map/ppermute | solution.py:484
  32.3 7.1 %collective-permute-start.8 = (bf16[8,64,576]{2,1,0:T(8,128)(2,1)S(1)}, bf16[8,64,576]{2,1,0:T(8,128)(2,1)S(1)}, u32[]{:S(2)}, u32[]{:S(2)}) collective-permute-start(bf16[8,64,576]{2,1,0:T(8,128)(2,1)S(1)} %constant_dynamic-update-slice_fusion.own_keys), channel_id=1, source_target_pairs={{0,1},{1,0},{2,3},{3,2},{4,5},{5,4},{6,7},{7,6},{8,9},{9,8},{10,11... | collective-permute-start | bytes 1769480 | tf_op jit(solution)/shard_map/ppermute | solution.py:484
  32.4 7.0 %copy-start.2 = (s32[1024]{0:T(1024)S(1)}, s32[1024]{0:T(1024)}, u32[]{:S(2)}) copy-start(s32[1024]{0:T(1024)} %positions_ref.3) | copy-start | bytes 12292
  36.9 1.7 %collective-permute-start.6 = (bf16[64,1792]{1,0:T(8,128)(2,1)S(1)}, bf16[64,1792]{1,0:T(8,128)(2,1)S(1)}, u32[]{:S(2)}, u32[]{:S(2)}) collective-permute-start(bf16[64,1792]{1,0:T(8,128)(2,1)S(1)} %get-tuple-element.41), channel_id=1, source_target_pairs={{0,1},{1,0},{2,3},{3,2},{4,5},{5,4},{6,7},{7,6},{8,9},{9,8},{10,11... | collective-permute-start | bytes 688136 | tf_op jit(solution)/shard_map/ppermute | solution.py:484
  38.6 7.9 %collective-permute-start.7 = (bf16[64,1792]{1,0:T(8,128)(2,1)S(1)}, bf16[64,1792]{1,0:T(8,128)(2,1)S(1)}, u32[]{:S(2)}, u32[]{:S(2)}) collective-permute-start(bf16[64,1792]{1,0:T(8,128)(2,1)S(1)} %add.4), channel_id=1, source_target_pairs={{0,2},{1,3},{2,0},{3,1},{4,6},{5,7},{6,4},{7,5},{8,10},{9,11},{10,... | collective-permute-start | bytes 688136 | tf_op jit(solution)/shard_map/ppermute | solution.py:484
  39.2 7.3 %collective-permute-start.9 = (bf16[64,1792]{1,0:T(8,128)(2,1)S(1)}, bf16[64,1792]{1,0:T(8,128)(2,1)S(1)}, u32[]{:S(2)}, u32[]{:S(2)}) collective-permute-start(bf16[64,1792]{1,0:T(8,128)(2,1)S(1)} %get-tuple-element.50), channel_id=1, source_target_pairs={{0,1},{1,0},{2,3},{3,2},{4,5},{5,4},{6,7},{7,6},{8,9},{9,8},{10,11... | collective-permute-start | bytes 688136 | tf_op jit(solution)/shard_map/ppermute | solution.py:484
  47.3 13.9 %all-to-all-start.1 = ((bf16[8,8,1792]{2,1,0:T(8,128)(2,1)}), bf16[8,8,1792]{2,1,0:T(8,128)(2,1)S(1)}, u32[]{:S(2)}, u32[]{:S(2)}) async-start(bf16[8,8,1792]{2,1,0:T(8,128)(2,1)} %bitcast.7), calls=%async_computation.1 | async-start | bytes 458752 | tf_op jit(solution)/shard_map/all_to_all | solution.py:487
  51.9 1.3 %copy-start.3 = (bf16[1024,576]{1,0:T(8,128)(2,1)S(1)}, bf16[1024,576]{1,0:T(8,128)(2,1)}, u32[]{:S(2)}) copy-start(bf16[1024,576]{1,0:T(8,128)(2,1)} %get-tuple-element.45.keys_ref) | copy-start | bytes 3538948
  53.2 8.0 %copy-start = (bf16[64,128]{1,0:T(8,128)(2,1)S(1)}, bf16[64,128]{1,0:T(8,128)(2,1)}, u32[]{:S(2)}) copy-start(bf16[64,128]{1,0:T(8,128)(2,1)} %get-tuple-element.47.high_ref) | copy-start | bytes 49156
  53.2 8.0 %copy-start.1 = (bf16[64,128]{1,0:T(8,128)(2,1)S(1)}, bf16[64,128]{1,0:T(8,128)(2,1)}, u32[]{:S(2)}) copy-start(bf16[64,128]{1,0:T(8,128)(2,1)} %get-tuple-element.48.low_ref) | copy-start | bytes 49156

commit v2 on v1

--- a/solution.py
+++ b/solution.py
@@ -1,3 +1,4 @@
+import functools
 import math
 
 import jax
@@ -17,6 +18,8 @@
 MIB = 1 << 20
 LIMIT = 52 * MIB
 FULL = 60 * MIB
+SMALL = 24 * MIB
+CHUNK = 256
 
 NT = (((1,), (1,)), ((), ()))
 TN = (((0,), (0,)), ((), ()))
@@ -116,9 +119,33 @@
 
 
 def near_kernel(
-    ep_ref, own_ref, core_ref, gate_hbm, up_hbm, gate_out, up_out, gate, up, semaphores
+    ep_ref,
+    own_ref,
+    core_ref,
+    gate_hbm,
+    up_hbm,
+    down_hbm,
+    sums_out,
+    far_gate,
+    far_up,
+    down,
+    gate,
+    up,
+    semaphores,
+    far_semaphores,
+    down_semaphores,
 ):
+    units = gate.shape[2]
+    features = gate.shape[1]
     copies = weight_copies(ep_ref, (0, 1), gate_hbm, up_hbm, gate, up, semaphores)
+    later = weight_copies(ep_ref, (2, 3), gate_hbm, up_hbm, far_gate, far_up, far_semaphores)
+    for flip in (3, 1, 2, 0):
+        place = pl.multiple_of((ep_ref[0] ^ flip) * features, features)
+        copy = pltpu.make_async_copy(
+            down_hbm.at[0, :, pl.ds(place, features)], down.at[flip], down_semaphores.at[flip]
+        )
+        copy.start()
+        later.append(copy)
     gate_sum, up_sum = None, None
     for index, x_ref in enumerate((own_ref, core_ref)):
         rows = x_ref[...]
@@ -128,101 +155,71 @@
         copies[2 * index + 1].wait()
         part = jnp.dot(rows, up[index], preferred_element_type=jnp.float32)
         up_sum = part if up_sum is None else up_sum + part
-    gate_out[...] = gate_sum
-    up_out[...] = up_sum
-
-
-def near_experts(ep, own, core, w_gate, w_up):
+    sums_out[:, :units] = gate_sum
+    sums_out[:, units:] = up_sum
+    for copy in later:
+        copy.wait()
+
+
+def near_experts(ep, own, core, w_gate, w_up, w_down):
     slots, features = own.shape
     units = w_gate.shape[2]
     return pl.pallas_call(
         near_kernel,
-        out_shape=[jax.ShapeDtypeStruct((slots, units), jnp.float32)] * 2,
-        in_specs=[SMEM_SPEC] + [VMEM_SPEC] * 2 + [HBM_SPEC] * 2,
-        out_specs=[VMEM_SPEC] * 2,
+        out_shape=[
+            jax.ShapeDtypeStruct((slots, 2 * units), jnp.float32),
+            jax.ShapeDtypeStruct((2, features, units), jnp.bfloat16),
+            jax.ShapeDtypeStruct((2, features, units), jnp.bfloat16),
+            jax.ShapeDtypeStruct((4, units, features), jnp.bfloat16),
+        ],
+        in_specs=[SMEM_SPEC] + [VMEM_SPEC] * 2 + [HBM_SPEC] * 3,
+        out_specs=[VMEM_SPEC] * 4,
         scratch_shapes=[
             VMEM((2, features, units), jnp.bfloat16),
             VMEM((2, features, units), jnp.bfloat16),
             pltpu.SemaphoreType.DMA((2, 2)),
+            pltpu.SemaphoreType.DMA((2, 2)),
+            pltpu.SemaphoreType.DMA((4,)),
         ],
-        compiler_params=pltpu.CompilerParams(vmem_limit_bytes=LIMIT),
+        compiler_params=pltpu.CompilerParams(vmem_limit_bytes=46 * MIB),
         cost_estimate=pl.CostEstimate(
             flops=8 * slots * features * units,
-            bytes_accessed=8 * features * units,
+            bytes_accessed=24 * features * units,
             transcendentals=0,
         ),
         name="near_experts",
-    )(ep, own, core, w_gate, w_up)
+    )(ep, own, core, w_gate, w_up, w_down)
 
 
 def far_kernel(
-    ep_ref,
-    far_ref,
-    core_far_ref,
-    gate_part,
-    up_part,
-    gate_hbm,
-    up_hbm,
-    down_hbm,
-    own_out,
-    core_out,
-    far_out,
-    core_far_out,
-    gate,
-    up,
-    down,
-    semaphores,
-    down_semaphores,
+    far_ref, core_far_ref, sums_ref, gate, up, down, own_out, core_out, far_out, core_far_out
 ):
-    features = gate.shape[1]
-    copies = weight_copies(ep_ref, (2, 3), gate_hbm, up_hbm, gate, up, semaphores)
-    down_copies = []
-    for flip in (3, 1, 2, 0):
-        place = pl.multiple_of((ep_ref[0] ^ flip) * features, features)
-        copy = pltpu.make_async_copy(
-            down_hbm.at[0, :, pl.ds(place, features)], down.at[flip], down_semaphores.at[flip]
-        )
-        copy.start()
-        down_copies.append(copy)
-    gate_sum, up_sum = gate_part[...], up_part[...]
+    units = gate.shape[2]
+    gate_sum, up_sum = sums_ref[:, :units], sums_ref[:, units:]
     for index, x_ref in enumerate((far_ref, core_far_ref)):
         rows = x_ref[...]
-        copies[2 * index].wait()
         gate_sum = gate_sum + jnp.dot(rows, gate[index], preferred_element_type=jnp.float32)
-        copies[2 * index + 1].wait()
         up_sum = up_sum + jnp.dot(rows, up[index], preferred_element_type=jnp.float32)
     hidden = (gate_sum / (1.0 + jnp.exp(-gate_sum)) * up_sum).astype(jnp.bfloat16)
     outs = (own_out, core_out, far_out, core_far_out)
-    for copy, flip in zip(down_copies, (3, 1, 2, 0)):
-        copy.wait()
+    for flip in (3, 1, 2, 0):
         outs[flip][...] = jnp.dot(
             hidden, down[flip], preferred_element_type=jnp.float32
         ).astype(jnp.bfloat16)
 
 
-def far_experts(ep, far, core_far, gate_part, up_part, w_gate, w_up, w_down):
+def far_experts(far, core_far, sums, gate, up, down):
     slots, features = far.shape
-    units = w_gate.shape[2]
+    units = gate.shape[2]
     return pl.pallas_call(
         far_kernel,
         out_shape=[jax.ShapeDtypeStruct((slots, features), jnp.bfloat16)] * 4,
-        in_specs=[SMEM_SPEC] + [VMEM_SPEC] * 4 + [HBM_SPEC] * 3,
+        in_specs=[VMEM_SPEC] * 6,
         out_specs=[VMEM_SPEC] * 4,
-        scratch_shapes=[
-            VMEM((2, features, units), jnp.bfloat16),
-            VMEM((2, features, units), jnp.bfloat16),
-            VMEM((4, units, features), jnp.bfloat16),
-            pltpu.SemaphoreType.DMA((2, 2)),
-            pltpu.SemaphoreType.DMA((4,)),
-        ],
-        compiler_params=pltpu.CompilerParams(vmem_limit_bytes=LIMIT),
-        cost_estimate=pl.CostEstimate(
-            flops=16 * slots * features * units,
-            bytes_accessed=16 * features * units,
-            transcendentals=slots * units,
-        ),
+        compiler_params=pltpu.CompilerParams(vmem_limit_bytes=SMALL),
+        cost_estimate=pl.CostEstimate(flops=0, bytes_accessed=0, transcendentals=0),
         name="far_experts",
-    )(ep, far, core_far, gate_part, up_part, w_gate, w_up, w_down)
+    )(far, core_far, sums, gate, up, down)
 
 
 def add_kernel(*refs):
@@ -309,67 +306,38 @@
     )(q_nope, q_rope, w_uk)
 
 
-def attend_run(run, base, seen, queries_ref, keys_ref, w_uv_ref, w_uv_copy, store):
-    latent_width = w_uv_ref.shape[0]
-    heads = w_uv_ref.shape[1] // VDIM
-    count = GROUP * HALF
-    factor = math.log2(math.e) / math.sqrt(NOPE + ROPE)
-    query_position = base + lax.rem(lax.broadcasted_iota(jnp.int32, (count, seen), 0), HALF)
-    visible = lax.broadcasted_iota(jnp.int32, (count, seen), 1) <= query_position
-    for group in range(heads // GROUP):
-        scores = lax.dot_general(
-            queries_ref[run, group * count : (group + 1) * count, :],
-            keys_ref[:seen, :],
-            NT,
-            preferred_element_type=jnp.float32,
-        )
-        scores = jnp.where(visible, scores, -jnp.inf)
-        top = jnp.max(scores, axis=1, keepdims=True)
-        part = jnp.exp2((scores - top) * factor)
-        total = jnp.sum(part, axis=1, keepdims=True)
-        summed = jnp.dot(
-            part.astype(jnp.bfloat16),
-            keys_ref[:seen, :latent_width],
-            preferred_element_type=jnp.float32,
-        )
-        mixed = (summed / total).astype(jnp.bfloat16)
-        if not group:
-            w_uv_copy.wait()
-        for index in range(GROUP):
-            head = group * GROUP + index
-            columns = slice(head * VDIM, (head + 1) * VDIM)
-            store(
-                columns,
-                jnp.dot(
-                    mixed[index * HALF : (index + 1) * HALF],
-                    w_uv_ref[:, columns],
-                    preferred_element_type=jnp.float32,
-                ).astype(jnp.bfloat16),
-            )
-
-
-def runs_of(my_ctx, positions_ref):
-    first = my_ctx * (2 * HALF)
-    low = jnp.where(positions_ref[first] < positions_ref[first + HALF], 0, 1)
-    return low, positions_ref[first + low * HALF], positions_ref[first + (1 - low) * HALF]
-
-
-def low_kernel(
+def attention_kernel(
+    first,
+    last,
     own_ref,
     positions_ref,
-    queries_ref,
+    queries_hbm,
     w_uv_hbm,
     own_keys,
     core_keys,
-    keys_ref,
-    out_ref,
-    w_uv_ref,
-    semaphore,
+    *refs,
 ):
-    w_uv_copy = pltpu.make_async_copy(w_uv_hbm, w_uv_ref, semaphore)
-    w_uv_copy.start()
-    blocks, block_rows, width = own_keys.shape
+    done_ref = None
+    if first:
+        done_ref, *refs = refs
+    out_ref, keys, queries, w_uv, scores, tops, mixed, semaphores = refs
+    latent_width = w_uv.shape[0]
+    count = (last - first) * HALF
+    blocks = own_keys.shape[0]
     my_ctx, my_ep = own_ref[0], own_ref[1]
+    mine = my_ctx * (2 * HALF)
+    low = jnp.where(positions_ref[mine] < positions_ref[mine + HALF], 0, 1)
+    high = 1 - low
+    low_base = positions_ref[mine + low * HALF]
+    high_base = positions_ref[mine + high * HALF]
+    copies = []
+
+    def copy(source, target):
+        copies.append(pltpu.make_async_copy(source, target, semaphores.at[len(copies)]))
+        copies[-1].start()
+
+    copy(queries_hbm.at[high, pl.ds(first * HALF, count)], queries.at[pl.ds(0, count)])
+    copy(queries_hbm.at[low, pl.ds(first * HALF, count)], queries.at[pl.ds(count, count)])
     for flip, source in enumerate((own_keys, core_keys)):
         for index in range(blocks):
             source_ctx = my_ctx
@@ -377,85 +345,119 @@
                 if index >> bit & 1:
                     source_ctx = source_ctx ^ step
             start = source_ctx * (2 * HALF) + ((my_ep % 2) ^ flip) * HALF
-            place = pl.multiple_of(positions_ref[start], block_rows)
-            keys_ref[pl.ds(place, block_rows), :] = source[index]
-    run, base, _ = runs_of(my_ctx, positions_ref)
-
-    def store(columns, value):
-        out_ref[:, columns] = value
-
-    seen = keys_ref.shape[0] // 2
-    attend_run(run, base, seen, queries_ref, keys_ref, w_uv_ref, w_uv_copy, store)
-
-
-def high_kernel(
-    own_ref,
-    positions_ref,
-    queries_ref,
-    w_uv_hbm,
-    keys_ref,
-    low_ref,
-    out_ref,
-    w_uv_ref,
-    semaphore,
-):
-    w_uv_copy = pltpu.make_async_copy(w_uv_hbm, w_uv_ref, semaphore)
-    w_uv_copy.start()
-    low, _, base = runs_of(own_ref[0], positions_ref)
-    run = 1 - low
-    out_ref[pl.ds(pl.multiple_of(low * HALF, HALF), HALF), :] = low_ref[...]
-    rows = pl.ds(pl.multiple_of(run * HALF, HALF), HALF)
-
-    def store(columns, value):
-        out_ref[rows, columns] = value
-
-    seen = keys_ref.shape[0]
-    attend_run(run, base, seen, queries_ref, keys_ref, w_uv_ref, w_uv_copy, store)
-
-
-def attend_low(own, positions, queries, w_uv, pieces):
-    columns = w_uv.shape[1]
+            place = pl.multiple_of(positions_ref[start], HALF)
+            copy(source.at[index], keys.at[pl.ds(place, HALF)])
+    copy(w_uv_hbm.at[:, pl.ds(first * VDIM, (last - first) * VDIM)], w_uv)
+    tops[...] = jnp.full(tops.shape, -jnp.inf, jnp.float32)
+    offset = lax.broadcasted_iota(jnp.int32, (HALF, CHUNK), 1) - lax.broadcasted_iota(
+        jnp.int32, (HALF, CHUNK), 0
+    )
+    for pending in copies[:-1]:
+        pending.wait()
+    low_chunks = (low_base + HALF + CHUNK - 1) // CHUNK
+    high_chunks = (high_base + HALF + CHUNK - 1) // CHUNK
+
+    def score(chunk, bases):
+        start = pl.multiple_of(chunk * CHUNK, CHUNK)
+        part = lax.dot_general(
+            queries[: len(bases) * count, :],
+            keys[pl.ds(start, CHUNK), :],
+            NT,
+            preferred_element_type=jnp.float32,
+        )
+        for index, base in enumerate(bases):
+            visible = offset <= base - start
+            for head in range(last - first):
+                rows = slice(index * count + head * HALF, index * count + (head + 1) * HALF)
+                seen = jnp.where(visible, part[rows], -jnp.inf)
+                scores[chunk, rows, :] = seen
+                top = tops[rows, :]
+                for lane in range(0, CHUNK, 128):
+                    top = jnp.maximum(top, seen[:, lane : lane + 128])
+                tops[rows, :] = top
+        return 0
+
+    lax.fori_loop(0, low_chunks, lambda c, _: score(c, (high_base, low_base)), 0)
+    lax.fori_loop(low_chunks, high_chunks, lambda c, _: score(c, (high_base,)), 0)
+    factor = math.log2(math.e) / math.sqrt(NOPE + ROPE)
+
+    def mix(rows, chunks):
+        top = jnp.max(tops[rows, :], axis=1, keepdims=True) * factor
+        total = jnp.zeros((count, 128), jnp.float32)
+        parts = []
+        for chunk in range(chunks):
+            part = jnp.exp2(scores[chunk, rows, :] * factor - top)
+            for lane in range(0, CHUNK, 128):
+                total = total + part[:, lane : lane + 128]
+            parts.append(part.astype(jnp.bfloat16))
+        summed = jnp.dot(
+            jnp.concatenate(parts, axis=1),
+            keys[: chunks * CHUNK, :latent_width],
+            preferred_element_type=jnp.float32,
+        )
+        share = 1.0 / jnp.sum(total, axis=1, keepdims=True)
+        mixed[rows, :] = (summed * share).astype(jnp.bfloat16)
+
+    most = keys.shape[0] // CHUNK
+    for chunks in range(1, most + 1):
+
+        @pl.when(high_chunks == chunks)
+        def _():
+            mix(slice(0, count), chunks)
+
+        @pl.when(low_chunks == chunks)
+        def _():
+            mix(slice(count, 2 * count), chunks)
+
+    copies[-1].wait()
+    high_rows = pl.ds(pl.multiple_of(high * HALF, HALF), HALF)
+    low_rows = pl.ds(pl.multiple_of(low * HALF, HALF), HALF)
+    if first:
+        out_ref[:, : first * VDIM] = done_ref[...]
+    skipped = first * VDIM
+    for head in range(last - first):
+        both = jnp.concatenate(
+            [
+                mixed[head * HALF : (head + 1) * HALF, :],
+                mixed[count + head * HALF : count + (head + 1) * HALF, :],
+            ],
+            axis=0,
+        )
+        value = jnp.dot(
+            both, w_uv[:, head * VDIM : (head + 1) * VDIM], preferred_element_type=jnp.float32
+        ).astype(jnp.bfloat16)
+        columns = slice(skipped + head * VDIM, skipped + (head + 1) * VDIM)
+        out_ref[high_rows, columns] = value[:HALF]
+        out_ref[low_rows, columns] = value[HALF:]
+
+
+def attend(first, last, own, positions, queries, w_uv, own_keys, core_keys, *done):
+    latent_width = w_uv.shape[0]
     key_count = positions.shape[0]
-    width = pieces[0].shape[-1]
-    count = queries.shape[1]
-    return pl.pallas_call(
-        low_kernel,
-        out_shape=[
-            jax.ShapeDtypeStruct((key_count, width), jnp.bfloat16),
-            jax.ShapeDtypeStruct((HALF, columns), jnp.bfloat16),
+    width = own_keys.shape[-1]
+    count = (last - first) * HALF
+    return pl.pallas_call(
+        functools.partial(attention_kernel, first, last),
+        out_shape=jax.ShapeDtypeStruct((2 * HALF, last * VDIM), jnp.bfloat16),
+        in_specs=[SMEM_SPEC] * 2 + [HBM_SPEC] * 4 + [VMEM_SPEC] * len(done),
+        out_specs=VMEM_SPEC,
+        scratch_shapes=[
+            VMEM((key_count, width), jnp.bfloat16),
+            VMEM((2 * count, width), jnp.bfloat16),
+            VMEM((latent_width, (last - first) * VDIM), jnp.bfloat16),
+            VMEM((key_count // CHUNK, 2 * count, CHUNK), jnp.float32),
+            VMEM((2 * count, 128), jnp.float32),
+            VMEM((2 * count, latent_width), jnp.bfloat16),
+            pltpu.SemaphoreType.DMA((2 * own_keys.shape[0] + 3,)),
         ],
-        in_specs=[SMEM_SPEC] * 2 + [VMEM_SPEC, HBM_SPEC] + [VMEM_SPEC] * 2,
-        out_specs=[VMEM_SPEC] * 2,
-        scratch_shapes=[VMEM(w_uv.shape, jnp.bfloat16), pltpu.SemaphoreType.DMA(())],
         compiler_params=pltpu.CompilerParams(vmem_limit_bytes=LIMIT),
         cost_estimate=pl.CostEstimate(
-            flops=2 * count * key_count * width,
-            bytes_accessed=6 * MIB,
-            transcendentals=count * key_count // 2,
-        ),
-        name="attention_low",
-    )(own, positions, queries, w_uv, *pieces)
-
-
-def attend_high(own, positions, queries, w_uv, keys, low):
-    columns = w_uv.shape[1]
-    key_count = positions.shape[0]
-    width = keys.shape[1]
-    count = queries.shape[1]
-    return pl.pallas_call(
-        high_kernel,
-        out_shape=jax.ShapeDtypeStruct((2 * HALF, columns), jnp.bfloat16),
-        in_specs=[SMEM_SPEC] * 2 + [VMEM_SPEC, HBM_SPEC] + [VMEM_SPEC] * 2,
-        out_specs=VMEM_SPEC,
-        scratch_shapes=[VMEM(w_uv.shape, jnp.bfloat16), pltpu.SemaphoreType.DMA(())],
-        compiler_params=pltpu.CompilerParams(vmem_limit_bytes=LIMIT),
-        cost_estimate=pl.CostEstimate(
-            flops=4 * count * key_count * width,
-            bytes_accessed=6 * MIB,
+            flops=3 * count * key_count * width,
+            bytes_accessed=4 * MIB,
             transcendentals=count * key_count,
         ),
-        name="attention_high",
-    )(own, positions, queries, w_uv, keys, low)
+        name="attention",
+    )(own, positions, queries, w_uv, own_keys, core_keys, *done)
 
 
 def shards(
@@ -492,8 +494,8 @@
     arrived = exchange(outgoing)
     high, q_nope = lax.optimization_barrier((high, q_nope))
     queries = fold(q_nope, q_rope, w_uk)
+    flips = gather_order(ctx)
     own_keys = packed[None]
-    flips = gather_order(ctx)
     for flip in flips[:-1]:
         own_keys = jnp.concatenate([own_keys, over_ctx(own_keys, flip)], axis=0)
     arrived, queries, own_keys = lax.optimization_barrier((arrived, queries, own_keys))
@@ -502,25 +504,29 @@
     far = over_ep(own, 2)
     core = over_ep(own, 1)
     received = over_ctx(own_keys, flips[-1])
-    gate_part, up_part = near_experts(ep, own, core, w_gate, w_up)
-    far, gate_part = lax.optimization_barrier((far, gate_part))
+    sums, far_gate, far_up, down = near_experts(ep, own, core, w_gate, w_up, w_down)
+    far, sums = lax.optimization_barrier((far, sums))
     core_far = over_ep(far, 1)
-    core_far, received = lax.optimization_barrier((core_far, received))
     own_out, core_out, far_out, core_far_out = far_experts(
-        ep, far, core_far, gate_part, up_part, w_gate, w_up, w_down
+        far, core_far, sums, far_gate, far_up, down
     )
+    core_far_out, received = lax.optimization_barrier((core_far_out, received))
     from_core_far = over_ep(core_far_out, 1)
     from_core = over_ep(core_out, 1)
+    to_far = add(far_out, from_core_far)
+    from_far = over_ep(to_far, 2)
     own_keys = jnp.concatenate([own_keys, received], axis=0)
     core_keys = over_ep(own_keys, 1)
-    to_far = add(far_out, from_core_far)
-    from_far = over_ep(to_far, 2)
     place = jnp.concatenate([me, ep])
-    keys, low_out = attend_low(place, positions, queries, w_uv, (own_keys, core_keys))
-    from_far, keys, low_out = lax.optimization_barrier((from_far, keys, low_out))
+    heads = q_nope.shape[1] // NOPE
+    split = heads // 2
+    half = attend(0, split, place, positions, queries, w_uv, own_keys, core_keys)
+    from_far, half = lax.optimization_barrier((from_far, half))
     returning = add(own_out, from_core, from_far)
     returned = exchange(returning.reshape(arrived.shape))
-    attention = attend_high(place, positions, queries, w_uv, keys, low_out)
+    attention = attend(
+        split, heads, place, positions, queries, w_uv, own_keys, core_keys, half
+    )
     moe_out = combine(high, low, returned.reshape(own.shape))
     return (attention, moe_out)
 

time: 63.1 us -> 58.4 us (0.926)
  Pallas kernels: 32.3 us -> 29.2 us
  local copies, waits for them, and re-layouts: 1.4 us -> 0.08 us
  waiting for transfers between devices: 7.79 us -> 7.05 us
    pallas_call x1, Pallas kernels: 4.5 us -> 1.47 us  [far_experts(): pl.pallas_call(far_kernel, out_shape=[jax.ShapeDtypeStruct((slots, featur...]
    ppermute x3, waiting for transfers between devices: 4.16 us -> 1.2 us  [over_ctx(): return lax.ppermute(value, 'ctx', [(i, i ^ flip) for i in range(ctx)])]
    all_to_all x2, waiting for transfers between devices: 0.01 us -> 1.75 us  [exchange(): return lax.all_to_all(value, 'ctx', split_axis=0, concat_axis=0, tiled=True)]
    unnamed x11 -> x9, local copies, waits for them, and re-layouts: 1.36 us -> 0.04 us
  transfers between devices with their start and end apart: 12 -> 12, of which waited for: 5 -> 7; matrix products, arithmetic and copies ran while one was open for 2% -> 2% of each run, Pallas kernels for 46% -> 44%
where the time goes in v2:
time: 58.4 us; the launch traced here: 57.8 us
  Pallas kernels  29.2 us (50%)
  starting transfers between devices  19.7 us (34%)
  waiting for transfers between devices  7.05 us (12%)
  other arithmetic  1.05 us (2%)
  between operations  0.74 us (1%)
    pallas_call x2, Pallas kernels, attend(): pl.pallas_call(functools.partial(attention_kernel, first, last), out_shap...  12.9 us
    all_to_all x2, starting transfers between devices, exchange(): return lax.all_to_all(value, 'ctx', split_axis=0, concat_axis=0, tiled=True)  8.38 us
    ppermute x3, starting transfers between devices, over_ctx(): return lax.ppermute(value, 'ctx', [(i, i ^ flip) for i in range(ctx)])  7.85 us
    pallas_call x1, Pallas kernels, fold(): pl.pallas_call(fold_kernel, out_shape=jax.ShapeDtypeStruct((2, heads * HA...  4.66 us
    pallas_call x1, Pallas kernels, near_experts(): pl.pallas_call(near_kernel, out_shape=[jax.ShapeDtypeStruct((slots, 2 * u...  4.4 us
    ppermute x7, waiting for transfers between devices, over_ep(): return lax.ppermute(value, 'ep', [(i, i ^ flip) for i in range(4)])  4.1 us
    ppermute x7, starting transfers between devices, over_ep(): return lax.ppermute(value, 'ep', [(i, i ^ flip) for i in range(4)])  3.43 us
    pallas_call x1, Pallas kernels, route(): pl.pallas_call(route_kernel, out_shape=[jax.ShapeDtypeStruct((ctx, CAP, f...  2.08 us
  transfers between devices with their start and end apart: 12, of which 7 were waited for; matrix products, arithmetic and copies ran while one was open for 2% of the time, Pallas kernels for 44%

profile of v2, /device:TPU:0, one launch (start us, length us, event | category | flops | bytes accessed | tf_op | source)
XLA Modules:
  0.0 57.8 jit_solution(1294808442516795605)
XLA Ops:
  0.6 1.6 %pack.1 = bf16[64,576]{1,0:T(8,128)(2,1)} custom-call(s32[1]{0:T(128)} %bitcast.1.ep_ref, bf16[128,512]{1,0:T(8,128)(2,1)} %latent_ref.1, bf16[64,128]{1,0:T(8,128)(2,1)} %bitcast.16), custom_call_target="tpu_custom_call" | custom-call | bytes 262144 | tf_op jit(solution)/shard_map/pack/pallas_call | solution.py:50
  2.3 4.0 %collective-permute-start = (bf16[1,64,576]{2,1,0:T(8,128)(2,1)}, bf16[1,64,576]{2,1,0:T(8,128)(2,1)S(1)}, u32[]{:S(2)}, u32[]{:S(2)}) collective-permute-start(bf16[1,64,576]{2,1,0:T(8,128)(2,1)} %bitcast.13), channel_id=1, source_target_pairs={{0,16},{4,20},{8,24},{12,28},{16,0},{20,4},{24,8},{28,12},{1,17},{... | collective-permute-start | bytes 221192 | tf_op jit(solution)/shard_map/ppermute | solution.py:483
  6.3 2.1 %route.1 = (bf16[8,8,1792]{2,1,0:T(8,128)(2,1)}, bf16[64,128]{1,0:T(8,128)(2,1)}, bf16[64,128]{1,0:T(8,128)(2,1)}) custom-call(s32[8,128]{1,0:T(8,128)} %bitcast.17, f32[8,128]{1,0:T(8,128)} %bitcast.18, bf16[128,1792]{1,0:T(8,128)(2,1)} %rows_ref), custom_call_target="tpu_custom_call" | custom-call | flops 29360128 | bytes 1048576 | tf_op jit(solution)/shard_map/route/pallas_call | solution.py:90
  8.4 3.8 %all-to-all-start = ((bf16[8,8,1792]{2,1,0:T(8,128)(2,1)}), bf16[8,8,1792]{2,1,0:T(8,128)(2,1)S(1)}, u32[]{:S(2)}, u32[]{:S(2)}) async-start(bf16[8,8,1792]{2,1,0:T(8,128)(2,1)} %get-tuple-element.27), calls=%async_computation | async-start | bytes 458752 | tf_op jit(solution)/shard_map/all_to_all | solution.py:489
  12.2 0.0 collective-permute-done
  12.2 0.9 %pad_maximum_fusion.1 = bf16[2,64,576]{2,1,0:T(8,128)(2,1)S(1)} fusion(bf16[1,64,576]{2,1,0:T(8,128)(2,1)S(1)} %collective-permute-done, bf16[1,64,576]{2,1,0:T(8,128)(2,1)} %bitcast.14), kind=kLoop, calls=%fused_computation.1 | loop fusion | flops 73728 | bytes 294912 | tf_op jit(solution)/shard_map/concatenate | solution.py:500
  13.1 2.1 %collective-permute-start.1 = (bf16[2,64,576]{2,1,0:T(8,128)(2,1)S(1)}, bf16[2,64,576]{2,1,0:T(8,128)(2,1)S(1)}, u32[]{:S(2)}, u32[]{:S(2)}) collective-permute-start(bf16[2,64,576]{2,1,0:T(8,128)(2,1)S(1)} %pad_maximum_fusion.1), channel_id=1, source_target_pairs={{0,4},{4,0},{8,12},{12,8},{16,20},{20,16},{24,28},{28,24},{1,5},{5... | collective-permute-start | bytes 442376 | tf_op jit(solution)/shard_map/ppermute | solution.py:483
  15.2 0.0 copy-start.3
  15.2 4.7 %fold.1.queries_hbm = bf16[2,1024,576]{2,1,0:T(8,128)(2,1)} custom-call(bf16[128,2048]{1,0:T(8,128)(2,1)} %q_nope_ref, bf16[128,1024]{1,0:T(8,128)(2,1)} %q_rope_ref.1, bf16[512,2048]{1,0:T(8,128)(2,1)} %w_uk_ref.1), custom_call_target="tpu_custom_call" | custom-call | flops 268435456 | bytes 6291456 | tf_op jit(solution)/shard_map/fold/pallas_call | solution.py:289
  19.9 0.9 %collective-permute-done.1 = bf16[2,64,576]{2,1,0:T(8,128)(2,1)S(1)} collective-permute-done((bf16[2,64,576]{2,1,0:T(8,128)(2,1)S(1)}, bf16[2,64,576]{2,1,0:T(8,128)(2,1)S(1)}, u32[]{:S(2)}, u32[]{:S(2)}) %collective-permute-start.1) | collective-permute-done | bytes 147488 | tf_op jit(solution)/shard_map/ppermute | solution.py:483
  20.7 0.0 copy-done.3
  20.7 0.1 pad_maximum_fusion
  20.8 0.0 all-to-all-done
  20.8 0.1 collective-permute-start.3
  20.9 1.6 %collective-permute-start.2 = (bf16[64,1792]{1,0:T(8,128)(2,1)S(1)}, bf16[64,1792]{1,0:T(8,128)(2,1)S(1)}, u32[]{:S(2)}, u32[]{:S(2)}) collective-permute-start(bf16[64,1792]{1,0:T(8,128)(2,1)S(1)} %bitcast.11), channel_id=1, source_target_pairs={{0,2},{1,3},{2,0},{3,1},{4,6},{5,7},{6,4},{7,5},{8,10},{9,11},{10,... | collective-permute-start | bytes 688136 | tf_op jit(solution)/shard_map/ppermute | solution.py:486
  22.4 1.7 %collective-permute-start.5 = (bf16[4,64,576]{2,1,0:T(8,128)(2,1)S(1)}, bf16[4,64,576]{2,1,0:T(8,128)(2,1)S(1)}, u32[]{:S(2)}, u32[]{:S(2)}) collective-permute-start(bf16[4,64,576]{2,1,0:T(8,128)(2,1)S(1)} %pad_maximum_fusion), channel_id=1, source_target_pairs={{0,8},{4,12},{8,0},{12,4},{16,24},{20,28},{24,16},{28,20},{1,9},{5... | collective-permute-start | bytes 884744 | tf_op jit(solution)/shard_map/ppermute | solution.py:483
  24.2 0.0 collective-permute-done.3.core_ref
  24.2 4.4 %near_experts.1 = (f32[64,512]{1,0:T(8,128)S(1)}, bf16[2,1792,256]{2,1,0:T(8,128)(2,1)S(1)}, bf16[2,1792,256]{2,1,0:T(8,128)(2,1)S(1)}, bf16[4,256,1792]{2,1,0:T(8,128)(2,1)S(1)}) custom-call(s32[1]{0:T(128)} %bitcast.1.ep_ref, bf16[64,1792]{1,0:T(8,128)(2,1)S(1)} %bitcast.12, bf16[64,1792]{1,0:T(8,128)(2,1)S(1)} %collective-permute-done.3.core_ref, ...), custom_call_target="tpu_custom_call" | custom-call | flops 234881024 | bytes 11010048 | tf_op jit(solution)/shard_map/near_experts/pallas_call | solution.py:167
  28.6 0.3 collective-permute-done.2.far_ref
  28.9 0.0 collective-permute-start.4
  28.9 1.5 %collective-permute-done.4.core_far_ref = bf16[64,1792]{1,0:T(8,128)(2,1)S(1)} collective-permute-done((bf16[64,1792]{1,0:T(8,128)(2,1)S(1)}, bf16[64,1792]{1,0:T(8,128)(2,1)S(1)}, u32[]{:S(2)}, u32[]{:S(2)}) %collective-permute-start.4) | collective-permute-done | bytes 229408 | tf_op jit(solution)/shard_map/ppermute | solution.py:486
  30.4 0.0 copy-start.2
  30.4 1.5 %far_experts.1 = (bf16[64,1792]{1,0:T(8,128)(2,1)S(1)}, bf16[64,1792]{1,0:T(8,128)(2,1)S(1)}, bf16[64,1792]{1,0:T(8,128)(2,1)S(1)}, bf16[64,1792]{1,0:T(8,128)(2,1)S(1)}) custom-call(bf16[64,1792]{1,0:T(8,128)(2,1)S(1)} %collective-permute-done.2.far_ref, bf16[64,1792]{1,0:T(8,128)(2,1)S(1)} %collective-permute-done.4.core_far_ref, ...), custom_call_target="tpu_custom_call" | custom-call | tf_op jit(solution)/shard_map/far_experts/pallas_call | solution.py:214
  31.9 0.3 collective-permute-done.5
  32.3 0.1 collective-permute-start.6
  32.3 0.5 collective-permute-start.7
  32.8 1.9 %collective-permute-done.7.refs_1_ = bf16[64,1792]{1,0:T(8,128)(2,1)S(1)} collective-permute-done((bf16[64,1792]{1,0:T(8,128)(2,1)S(1)}, bf16[64,1792]{1,0:T(8,128)(2,1)S(1)}, u32[]{:S(2)}, u32[]{:S(2)}) %collective-permute-start.7) | collective-permute-done | bytes 229408 | tf_op jit(solution)/shard_map/ppermute | solution.py:486
  34.8 0.1 add.4
  34.8 1.2 %collective-permute-start.8 = (bf16[64,1792]{1,0:T(8,128)(2,1)S(1)}, bf16[64,1792]{1,0:T(8,128)(2,1)S(1)}, u32[]{:S(2)}, u32[]{:S(2)}) collective-permute-start(bf16[64,1792]{1,0:T(8,128)(2,1)S(1)} %add.4), channel_id=1, source_target_pairs={{0,2},{1,3},{2,0},{3,1},{4,6},{5,7},{6,4},{7,5},{8,10},{9,11},{10,... | collective-permute-start | bytes 688136 | tf_op jit(solution)/shard_map/ppermute | solution.py:486
  36.0 0.0 collective-permute-start.9
  36.0 0.1 pad_add_fusion.own_ref
  36.1 0.0 collective-permute-done.6.core_keys
  36.1 0.0 copy-done.2
  36.1 6.0 %attention.2.refs_0_ = bf16[128,1024]{1,0:T(8,128)(2,1)S(1)} custom-call(s32[2]{0:T(128)S(1)} %pad_add_fusion.own_ref, s32[1024]{0:T(1024)S(1)} %copy-done.2, bf16[2,1024,576]{2,1,0:T(8,128)(2,1)} %fold.1.queries_hbm, bf16[512,2048]{1,0:T(8,128)(2,1)} %w_uv_hbm.3, bf16[8,64,576]{2,1,0:T(8,128)(2,1)S(1)} %constant_dynamic-update-slice_fusion.own_keys, ...), custom_call_target="tpu_custom_call" | custom-call | flops 905969664 | bytes 4194304 | tf_op jit(solution)/shard_map/attention/pallas_call | solution.py:439
  42.1 0.4 collective-permute-done.8.refs_2_
  42.5 0.0 collective-permute-done.9.refs_1_
  42.5 0.8 %add.5 = bf16[64,1792]{1,0:T(8,128)(2,1)} custom-call(bf16[64,1792]{1,0:T(8,128)(2,1)S(1)} %get-tuple-element.47.refs_0_, bf16[64,1792]{1,0:T(8,128)(2,1)S(1)} %collective-permute-done.9.refs_1_, bf16[64,1792]{1,0:T(8,128)(2,1)S(1)} %collective-permute-done.8.refs_2_), custom_call_target="tpu_custom_call" | custom-call | bytes 1048576 | tf_op jit(solution)/shard_map/add/pallas_call | solution.py:233
  43.3 4.6 %all-to-all-start.1 = ((bf16[8,8,1792]{2,1,0:T(8,128)(2,1)}), bf16[8,8,1792]{2,1,0:T(8,128)(2,1)S(1)}, u32[]{:S(2)}, u32[]{:S(2)}) async-start(bf16[8,8,1792]{2,1,0:T(8,128)(2,1)} %bitcast.7), calls=%async_computation.1 | async-start | bytes 458752 | tf_op jit(solution)/shard_map/all_to_all | solution.py:489
  47.9 0.0 copy-start
  47.9 0.0 copy-start.1
  47.9 7.0 %attention.3 = bf16[128,2048]{1,0:T(8,128)(2,1)} custom-call(s32[2]{0:T(128)S(1)} %pad_add_fusion.own_ref, s32[1024]{0:T(1024)S(1)} %copy-done.2, bf16[2,1024,576]{2,1,0:T(8,128)(2,1)} %fold.1.queries_hbm, bf16[512,2048]{1,0:T(8,128)(2,1)} %w_uv_hbm.3, bf16[8,64,576]{2,1,0:T(8,128)(2,1)S(1)} %constant_dynamic-update-slice_fusion.own_keys, ...), custom_call_target="tpu_custom_call" | custom-call | flops 905969664 | bytes 4194304 | tf_op jit(solution)/shard_map/attention/pallas_call | solution.py:439
  54.9 1.7 %all-to-all-done.1 = bf16[8,8,1792]{2,1,0:T(8,128)(2,1)S(1)} async-done(((bf16[8,8,1792]{2,1,0:T(8,128)(2,1)}), bf16[8,8,1792]{2,1,0:T(8,128)(2,1)S(1)}, u32[]{:S(2)}, u32[]{:S(2)}) %all-to-all-start.1) | async-done | bytes 229408 | tf_op jit(solution)/shard_map/all_to_all | solution.py:489
  56.6 0.0 copy-done
  56.6 0.0 copy-done.1
  56.6 1.2 %combine.1 = bf16[128,1792]{1,0:T(8,128)(2,1)} custom-call(bf16[64,128]{1,0:T(8,128)(2,1)S(1)} %copy-done, bf16[64,128]{1,0:T(8,128)(2,1)S(1)} %copy-done.1, bf16[64,1792]{1,0:T(8,128)(2,1)S(1)} %bitcast.9), custom_call_target="tpu_custom_call" | custom-call | flops 58720256 | bytes 1048576 | tf_op jit(solution)/shard_map/combine/pallas_call | solution.py:256
  (2 shorter events, 0.1 us)
Async XLA Ops:
  2.3 9.9 %collective-permute-start = (bf16[1,64,576]{2,1,0:T(8,128)(2,1)}, bf16[1,64,576]{2,1,0:T(8,128)(2,1)S(1)}, u32[]{:S(2)}, u32[]{:S(2)}) collective-permute-start(bf16[1,64,576]{2,1,0:T(8,128)(2,1)} %bitcast.13), channel_id=1, source_target_pairs={{0,16},{4,20},{8,24},{12,28},{16,0},{20,4},{24,8},{28,12},{1,17},{... | collective-permute-start | bytes 221192 | tf_op jit(solution)/shard_map/ppermute | solution.py:483
  8.4 12.4 %all-to-all-start = ((bf16[8,8,1792]{2,1,0:T(8,128)(2,1)}), bf16[8,8,1792]{2,1,0:T(8,128)(2,1)S(1)}, u32[]{:S(2)}, u32[]{:S(2)}) async-start(bf16[8,8,1792]{2,1,0:T(8,128)(2,1)} %get-tuple-element.27), calls=%async_computation | async-start | bytes 458752 | tf_op jit(solution)/shard_map/all_to_all | solution.py:489
  13.1 7.6 %collective-permute-start.1 = (bf16[2,64,576]{2,1,0:T(8,128)(2,1)S(1)}, bf16[2,64,576]{2,1,0:T(8,128)(2,1)S(1)}, u32[]{:S(2)}, u32[]{:S(2)}) collective-permute-start(bf16[2,64,576]{2,1,0:T(8,128)(2,1)S(1)} %pad_maximum_fusion.1), channel_id=1, source_target_pairs={{0,4},{4,0},{8,12},{12,8},{16,20},{20,16},{24,28},{28,24},{1,5},{5... | collective-permute-start | bytes 442376 | tf_op jit(solution)/shard_map/ppermute | solution.py:483
  15.2 5.5 %copy-start.3 = (bf16[64,576]{1,0:T(8,128)(2,1)S(1)}, bf16[64,576]{1,0:T(8,128)(2,1)}, u32[]{:S(2)}) copy-start(bf16[64,576]{1,0:T(8,128)(2,1)} %pack.1) | copy-start | bytes 221188
  20.8 3.4 %collective-permute-start.3 = (bf16[64,1792]{1,0:T(8,128)(2,1)S(1)}, bf16[64,1792]{1,0:T(8,128)(2,1)S(1)}, u32[]{:S(2)}, u32[]{:S(2)}) collective-permute-start(bf16[64,1792]{1,0:T(8,128)(2,1)S(1)} %bitcast.10), channel_id=1, source_target_pairs={{0,1},{1,0},{2,3},{3,2},{4,5},{5,4},{6,7},{7,6},{8,9},{9,8},{10,11... | collective-permute-start | bytes 688136 | tf_op jit(solution)/shard_map/ppermute | solution.py:486
  20.9 8.0 %collective-permute-start.2 = (bf16[64,1792]{1,0:T(8,128)(2,1)S(1)}, bf16[64,1792]{1,0:T(8,128)(2,1)S(1)}, u32[]{:S(2)}, u32[]{:S(2)}) collective-permute-start(bf16[64,1792]{1,0:T(8,128)(2,1)S(1)} %bitcast.11), channel_id=1, source_target_pairs={{0,2},{1,3},{2,0},{3,1},{4,6},{5,7},{6,4},{7,5},{8,10},{9,11},{10,... | collective-permute-start | bytes 688136 | tf_op jit(solution)/shard_map/ppermute | solution.py:486
  22.4 9.8 %collective-permute-start.5 = (bf16[4,64,576]{2,1,0:T(8,128)(2,1)S(1)}, bf16[4,64,576]{2,1,0:T(8,128)(2,1)S(1)}, u32[]{:S(2)}, u32[]{:S(2)}) collective-permute-start(bf16[4,64,576]{2,1,0:T(8,128)(2,1)S(1)} %pad_maximum_fusion), channel_id=1, source_target_pairs={{0,8},{4,12},{8,0},{12,4},{16,24},{20,28},{24,16},{28,20},{1,9},{5... | collective-permute-start | bytes 884744 | tf_op jit(solution)/shard_map/ppermute | solution.py:483
  28.9 1.5 %collective-permute-start.4 = (bf16[64,1792]{1,0:T(8,128)(2,1)S(1)}, bf16[64,1792]{1,0:T(8,128)(2,1)S(1)}, u32[]{:S(2)}, u32[]{:S(2)}) collective-permute-start(bf16[64,1792]{1,0:T(8,128)(2,1)S(1)} %collective-permute-done.2.far_ref), channel_id=1, source_target_pairs={{0,1},{1,0},{2,3},{3,2},{4,5},{5,4},{6,7},{7,6},{8,9},{9,8},{10,11... | collective-permute-start | bytes 688136 | tf_op jit(solution)/shard_map/ppermute | solution.py:486
  30.4 5.7 %copy-start.2 = (s32[1024]{0:T(1024)S(1)}, s32[1024]{0:T(1024)}, u32[]{:S(2)}) copy-start(s32[1024]{0:T(1024)} %positions_ref.3) | copy-start | bytes 12292
  32.3 3.9 %collective-permute-start.6 = (bf16[8,64,576]{2,1,0:T(8,128)(2,1)S(1)}, bf16[8,64,576]{2,1,0:T(8,128)(2,1)S(1)}, u32[]{:S(2)}, u32[]{:S(2)}) collective-permute-start(bf16[8,64,576]{2,1,0:T(8,128)(2,1)S(1)} %constant_dynamic-update-slice_fusion.own_keys), channel_id=1, source_target_pairs={{0,1},{1,0},{2,3},{3,2},{4,5},{5,4},{6,7},{7,6},{8,9},{9,8},{10,11... | collective-permute-start | bytes 1769480 | tf_op jit(solution)/shard_map/ppermute | solution.py:486
  32.3 2.4 %collective-permute-start.7 = (bf16[64,1792]{1,0:T(8,128)(2,1)S(1)}, bf16[64,1792]{1,0:T(8,128)(2,1)S(1)}, u32[]{:S(2)}, u32[]{:S(2)}) collective-permute-start(bf16[64,1792]{1,0:T(8,128)(2,1)S(1)} %get-tuple-element.43), channel_id=1, source_target_pairs={{0,1},{1,0},{2,3},{3,2},{4,5},{5,4},{6,7},{7,6},{8,9},{9,8},{10,11... | collective-permute-start | bytes 688136 | tf_op jit(solution)/shard_map/ppermute | solution.py:486
  34.8 7.7 %collective-permute-start.8 = (bf16[64,1792]{1,0:T(8,128)(2,1)S(1)}, bf16[64,1792]{1,0:T(8,128)(2,1)S(1)}, u32[]{:S(2)}, u32[]{:S(2)}) collective-permute-start(bf16[64,1792]{1,0:T(8,128)(2,1)S(1)} %add.4), channel_id=1, source_target_pairs={{0,2},{1,3},{2,0},{3,1},{4,6},{5,7},{6,4},{7,5},{8,10},{9,11},{10,... | collective-permute-start | bytes 688136 | tf_op jit(solution)/shard_map/ppermute | solution.py:486
  36.0 6.5 %collective-permute-start.9 = (bf16[64,1792]{1,0:T(8,128)(2,1)S(1)}, bf16[64,1792]{1,0:T(8,128)(2,1)S(1)}, u32[]{:S(2)}, u32[]{:S(2)}) collective-permute-start(bf16[64,1792]{1,0:T(8,128)(2,1)S(1)} %get-tuple-element.48), channel_id=1, source_target_pairs={{0,1},{1,0},{2,3},{3,2},{4,5},{5,4},{6,7},{7,6},{8,9},{9,8},{10,11... | collective-permute-start | bytes 688136 | tf_op jit(solution)/shard_map/ppermute | solution.py:486
  43.3 13.3 %all-to-all-start.1 = ((bf16[8,8,1792]{2,1,0:T(8,128)(2,1)}), bf16[8,8,1792]{2,1,0:T(8,128)(2,1)S(1)}, u32[]{:S(2)}, u32[]{:S(2)}) async-start(bf16[8,8,1792]{2,1,0:T(8,128)(2,1)} %bitcast.7), calls=%async_computation.1 | async-start | bytes 458752 | tf_op jit(solution)/shard_map/all_to_all | solution.py:489
  47.9 8.7 %copy-start = (bf16[64,128]{1,0:T(8,128)(2,1)S(1)}, bf16[64,128]{1,0:T(8,128)(2,1)}, u32[]{:S(2)}) copy-start(bf16[64,128]{1,0:T(8,128)(2,1)} %get-tuple-element.45.high_ref) | copy-start | bytes 49156
  47.9 8.7 %copy-start.1 = (bf16[64,128]{1,0:T(8,128)(2,1)S(1)}, bf16[64,128]{1,0:T(8,128)(2,1)}, u32[]{:S(2)}) copy-start(bf16[64,128]{1,0:T(8,128)(2,1)} %get-tuple-element.46.low_ref) | copy-start | bytes 49156

commit v3 on v2

--- a/solution.py
+++ b/solution.py
@@ -34,7 +34,18 @@
     return [1 << (bits - 1)] + [1 << bit for bit in range(bits - 1)]
 
 
-def pack_kernel(ep_ref, latent_ref, rope_ref, packed_ref):
+def route_kernel(
+    ep_ref,
+    ids_ref,
+    weights_ref,
+    rope_ref,
+    rows_ref,
+    latent_ref,
+    sent_ref,
+    high_ref,
+    low_ref,
+    packed_ref,
+):
     latent_width = latent_ref.shape[1]
     rope = rope_ref[...].astype(jnp.float32).T
     for core in range(2):
@@ -45,20 +56,6 @@
             packed_ref[:, :latent_width] = latent_ref[rows, :]
             packed_ref[:, latent_width:] = rope[rows].astype(jnp.bfloat16)
 
-
-def pack(ep, latent, k_rope):
-    return pl.pallas_call(
-        pack_kernel,
-        out_shape=jax.ShapeDtypeStruct((HALF, latent.shape[1] + ROPE), jnp.bfloat16),
-        in_specs=[SMEM_SPEC] + [VMEM_SPEC] * 2,
-        out_specs=VMEM_SPEC,
-        compiler_params=pltpu.CompilerParams(vmem_limit_bytes=FULL),
-        cost_estimate=pl.CostEstimate(flops=0, bytes_accessed=MIB // 4, transcendentals=0),
-        name="pack",
-    )(ep, latent, k_rope.T)
-
-
-def route_kernel(ids_ref, weights_ref, rows_ref, sent_ref, high_ref, low_ref):
     row_count = ids_ref.shape[1]
     slots = sent_ref.shape[0] * CAP
     slot = lax.broadcasted_iota(jnp.int32, (slots, row_count), 0)
@@ -84,7 +81,7 @@
         sent_ref[index] = sent[index * CAP : (index + 1) * CAP].astype(jnp.bfloat16)
 
 
-def route(expert_ids, expert_weights, moe_rows, ctx):
+def route(ep, expert_ids, expert_weights, k_rope, moe_rows, latent, ctx):
     row_count, features = moe_rows.shape
     slots = ctx * CAP
     return pl.pallas_call(
@@ -93,15 +90,16 @@
             jax.ShapeDtypeStruct((ctx, CAP, features), jnp.bfloat16),
             jax.ShapeDtypeStruct((slots, row_count), jnp.bfloat16),
             jax.ShapeDtypeStruct((slots, row_count), jnp.bfloat16),
+            jax.ShapeDtypeStruct((HALF, latent.shape[1] + ROPE), jnp.bfloat16),
         ],
-        in_specs=[VMEM_SPEC] * 3,
-        out_specs=[VMEM_SPEC] * 3,
+        in_specs=[SMEM_SPEC] + [VMEM_SPEC] * 5,
+        out_specs=[VMEM_SPEC] * 4,
         compiler_params=pltpu.CompilerParams(vmem_limit_bytes=FULL),
         cost_estimate=pl.CostEstimate(
             flops=2 * row_count * slots * features, bytes_accessed=1 * MIB, transcendentals=0
         ),
         name="route",
-    )(expert_ids.T, expert_weights.T, moe_rows)
+    )(ep, expert_ids.T, expert_weights.T, k_rope.T, moe_rows, latent)
 
 
 def weight_copies(ep_ref, flips, gate_hbm, up_hbm, gate, up, semaphores):
@@ -216,7 +214,7 @@
         out_shape=[jax.ShapeDtypeStruct((slots, features), jnp.bfloat16)] * 4,
         in_specs=[VMEM_SPEC] * 6,
         out_specs=[VMEM_SPEC] * 4,
-        compiler_params=pltpu.CompilerParams(vmem_limit_bytes=SMALL),
+        compiler_params=pltpu.CompilerParams(vmem_limit_bytes=24 * MIB),
         cost_estimate=pl.CostEstimate(flops=0, bytes_accessed=0, transcendentals=0),
         name="far_experts",
     )(far, core_far, sums, gate, up, down)
@@ -266,8 +264,14 @@
     )(high, low, returned)
 
 
-def fold_kernel(q_nope_ref, q_rope_ref, w_uk_ref, out_ref):
+def low_run(my_ctx, positions_ref):
+    mine = my_ctx * (2 * HALF)
+    return jnp.where(positions_ref[mine] < positions_ref[mine + HALF], 0, 1)
+
+
+def fold_kernel(own_ref, positions_ref, q_nope_ref, q_rope_ref, w_uk_ref, out_ref):
     latent_width = w_uk_ref.shape[0]
+    low = low_run(own_ref[0], positions_ref)
     for head in range(GROUP):
         columns = slice(head * NOPE, (head + 1) * NOPE)
         folded = lax.dot_general(
@@ -277,25 +281,31 @@
         for run in range(2):
             rows = slice(run * HALF, (run + 1) * HALF)
             place = slice(head * HALF, (head + 1) * HALF)
-            out_ref[run, place, :latent_width] = folded[rows]
-            out_ref[run, place, latent_width:] = rotated[rows]
-
-
-def fold(q_nope, q_rope, w_uk):
+            slot = 1 - (low ^ run)
+            out_ref[0, slot, place, :latent_width] = folded[rows]
+            out_ref[0, slot, place, latent_width:] = rotated[rows]
+
+
+def fold(own, positions, q_nope, q_rope, w_uk):
     query_count, columns = q_nope.shape
     heads = columns // NOPE
     latent_width = w_uk.shape[0]
     width = latent_width + ROPE
-    return pl.pallas_call(
+    steps = heads // GROUP // 2
+    queries = pl.pallas_call(
         fold_kernel,
-        out_shape=jax.ShapeDtypeStruct((2, heads * HALF, width), jnp.bfloat16),
-        grid=(heads // GROUP,),
+        out_shape=jax.ShapeDtypeStruct((2, 2, heads // 2 * HALF, width), jnp.bfloat16),
+        grid=(2 * steps,),
         in_specs=[
+            SMEM_SPEC,
+            SMEM_SPEC,
             pl.BlockSpec((query_count, GROUP * NOPE), lambda step: (0, step)),
             pl.BlockSpec((query_count, GROUP * ROPE), lambda step: (0, step)),
             pl.BlockSpec((latent_width, GROUP * NOPE), lambda step: (0, step)),
         ],
-        out_specs=pl.BlockSpec((2, GROUP * HALF, width), lambda step: (0, step, 0)),
+        out_specs=pl.BlockSpec(
+            (1, 2, GROUP * HALF, width), lambda step: (step // steps, 0, step % steps, 0)
+        ),
         compiler_params=pltpu.CompilerParams(vmem_limit_bytes=FULL),
         cost_estimate=pl.CostEstimate(
             flops=2 * query_count * columns * latent_width,
@@ -303,41 +313,32 @@
             transcendentals=0,
         ),
         name="fold",
-    )(q_nope, q_rope, w_uk)
-
-
-def attention_kernel(
-    first,
-    last,
+    )(own, positions, q_nope, q_rope, w_uk)
+    return queries.reshape(2, heads * HALF, width)
+
+
+def first_kernel(
     own_ref,
     positions_ref,
-    queries_hbm,
+    queries,
     w_uv_hbm,
     own_keys,
     core_keys,
-    *refs,
+    out_ref,
+    keys,
+    later_w_uv,
+    w_uv,
+    *scratch,
 ):
-    done_ref = None
-    if first:
-        done_ref, *refs = refs
-    out_ref, keys, queries, w_uv, scores, tops, mixed, semaphores = refs
-    latent_width = w_uv.shape[0]
-    count = (last - first) * HALF
+    semaphores = scratch[-1]
+    copies = []
+    for index, target in enumerate((w_uv, later_w_uv)):
+        width = target.shape[1]
+        source = w_uv_hbm.at[:, pl.ds(index * width, width)]
+        copies.append(pltpu.make_async_copy(source, target, semaphores.at[index]))
+        copies[-1].start()
     blocks = own_keys.shape[0]
     my_ctx, my_ep = own_ref[0], own_ref[1]
-    mine = my_ctx * (2 * HALF)
-    low = jnp.where(positions_ref[mine] < positions_ref[mine + HALF], 0, 1)
-    high = 1 - low
-    low_base = positions_ref[mine + low * HALF]
-    high_base = positions_ref[mine + high * HALF]
-    copies = []
-
-    def copy(source, target):
-        copies.append(pltpu.make_async_copy(source, target, semaphores.at[len(copies)]))
-        copies[-1].start()
-
-    copy(queries_hbm.at[high, pl.ds(first * HALF, count)], queries.at[pl.ds(0, count)])
-    copy(queries_hbm.at[low, pl.ds(first * HALF, count)], queries.at[pl.ds(count, count)])
     for flip, source in enumerate((own_keys, core_keys)):
         for index in range(blocks):
             source_ctx = my_ctx
@@ -346,14 +347,36 @@
                     source_ctx = source_ctx ^ step
             start = source_ctx * (2 * HALF) + ((my_ep % 2) ^ flip) * HALF
             place = pl.multiple_of(positions_ref[start], HALF)
-            copy(source.at[index], keys.at[pl.ds(place, HALF)])
-    copy(w_uv_hbm.at[:, pl.ds(first * VDIM, (last - first) * VDIM)], w_uv)
+            keys[pl.ds(place, HALF), :] = source[index]
+    attend_heads(
+        own_ref, positions_ref, queries.at[0], w_uv, keys, out_ref, 0, copies[0].wait, *scratch[:-1]
+    )
+    copies[1].wait()
+
+
+def second_kernel(own_ref, positions_ref, queries, w_uv, keys, done_ref, out_ref, *scratch):
+    skipped = done_ref.shape[1]
+    out_ref[:, :skipped] = done_ref[...]
+    attend_heads(
+        own_ref, positions_ref, queries.at[1], w_uv, keys, out_ref, skipped, lambda: None, *scratch
+    )
+
+
+def attend_heads(
+    own_ref, positions_ref, queries, w_uv, keys, out_ref, skipped, wait, scores, tops, mixed
+):
+    latent_width = w_uv.shape[0]
+    count = queries.shape[0] // 2
+    heads = count // HALF
+    mine = own_ref[0] * (2 * HALF)
+    low = low_run(own_ref[0], positions_ref)
+    high = 1 - low
+    low_base = positions_ref[mine + low * HALF]
+    high_base = positions_ref[mine + high * HALF]
     tops[...] = jnp.full(tops.shape, -jnp.inf, jnp.float32)
     offset = lax.broadcasted_iota(jnp.int32, (HALF, CHUNK), 1) - lax.broadcasted_iota(
         jnp.int32, (HALF, CHUNK), 0
     )
-    for pending in copies[:-1]:
-        pending.wait()
     low_chunks = (low_base + HALF + CHUNK - 1) // CHUNK
     high_chunks = (high_base + HALF + CHUNK - 1) // CHUNK
 
@@ -367,7 +390,7 @@
         )
         for index, base in enumerate(bases):
             visible = offset <= base - start
-            for head in range(last - first):
+            for head in range(heads):
                 rows = slice(index * count + head * HALF, index * count + (head + 1) * HALF)
                 seen = jnp.where(visible, part[rows], -jnp.inf)
                 scores[chunk, rows, :] = seen
@@ -409,13 +432,10 @@
         def _():
             mix(slice(count, 2 * count), chunks)
 
-    copies[-1].wait()
+    wait()
     high_rows = pl.ds(pl.multiple_of(high * HALF, HALF), HALF)
     low_rows = pl.ds(pl.multiple_of(low * HALF, HALF), HALF)
-    if first:
-        out_ref[:, : first * VDIM] = done_ref[...]
-    skipped = first * VDIM
-    for head in range(last - first):
+    for head in range(heads):
         both = jnp.concatenate(
             [
                 mixed[head * HALF : (head + 1) * HALF, :],
@@ -431,33 +451,60 @@
         out_ref[low_rows, columns] = value[HALF:]
 
 
-def attend(first, last, own, positions, queries, w_uv, own_keys, core_keys, *done):
-    latent_width = w_uv.shape[0]
+def attend_scratch(count, key_count, latent_width):
+    return [
+        VMEM((key_count // CHUNK, 2 * count, CHUNK), jnp.float32),
+        VMEM((2 * count, 128), jnp.float32),
+        VMEM((2 * count, latent_width), jnp.bfloat16),
+    ]
+
+
+def attend_cost(count, key_count, width):
+    return pl.CostEstimate(
+        flops=3 * count * key_count * width,
+        bytes_accessed=4 * MIB,
+        transcendentals=count * key_count,
+    )
+
+
+def attend_first(own, positions, queries, w_uv, own_keys, core_keys):
+    latent_width, columns = w_uv.shape
     key_count = positions.shape[0]
     width = own_keys.shape[-1]
-    count = (last - first) * HALF
+    count = queries.shape[1] // 2
+    half = (latent_width, columns // 2)
     return pl.pallas_call(
-        functools.partial(attention_kernel, first, last),
-        out_shape=jax.ShapeDtypeStruct((2 * HALF, last * VDIM), jnp.bfloat16),
-        in_specs=[SMEM_SPEC] * 2 + [HBM_SPEC] * 4 + [VMEM_SPEC] * len(done),
+        first_kernel,
+        out_shape=[
+            jax.ShapeDtypeStruct((2 * HALF, columns // 2), jnp.bfloat16),
+            jax.ShapeDtypeStruct((key_count, width), jnp.bfloat16),
+            jax.ShapeDtypeStruct(half, jnp.bfloat16),
+        ],
+        in_specs=[SMEM_SPEC] * 2 + [VMEM_SPEC, HBM_SPEC] + [VMEM_SPEC] * 2,
+        out_specs=[VMEM_SPEC] * 3,
+        scratch_shapes=[VMEM(half, jnp.bfloat16)]
+        + attend_scratch(count, key_count, latent_width)
+        + [pltpu.SemaphoreType.DMA((2,))],
+        compiler_params=pltpu.CompilerParams(vmem_limit_bytes=48 * MIB),
+        cost_estimate=attend_cost(count, key_count, width),
+        name="attention_first",
+    )(own, positions, queries, w_uv, own_keys, core_keys)
+
+
+def attend_second(own, positions, queries, w_uv, keys, done):
+    latent_width, columns = w_uv.shape
+    key_count, width = keys.shape
+    count = queries.shape[1] // 2
+    return pl.pallas_call(
+        second_kernel,
+        out_shape=jax.ShapeDtypeStruct((2 * HALF, 2 * columns), jnp.bfloat16),
+        in_specs=[SMEM_SPEC] * 2 + [VMEM_SPEC] * 4,
         out_specs=VMEM_SPEC,
-        scratch_shapes=[
-            VMEM((key_count, width), jnp.bfloat16),
-            VMEM((2 * count, width), jnp.bfloat16),
-            VMEM((latent_width, (last - first) * VDIM), jnp.bfloat16),
-            VMEM((key_count // CHUNK, 2 * count, CHUNK), jnp.float32),
-            VMEM((2 * count, 128), jnp.float32),
-            VMEM((2 * count, latent_width), jnp.bfloat16),
-            pltpu.SemaphoreType.DMA((2 * own_keys.shape[0] + 3,)),
-        ],
-        compiler_params=pltpu.CompilerParams(vmem_limit_bytes=LIMIT),
-        cost_estimate=pl.CostEstimate(
-            flops=3 * count * key_count * width,
-            bytes_accessed=4 * MIB,
-            transcendentals=count * key_count,
-        ),
-        name="attention",
-    )(own, positions, queries, w_uv, own_keys, core_keys, *done)
+        scratch_shapes=attend_scratch(count, key_count, latent_width),
+        compiler_params=pltpu.CompilerParams(vmem_limit_bytes=48 * MIB),
+        cost_estimate=attend_cost(count, key_count, width),
+        name="attention_second",
+    )(own, positions, queries, w_uv, keys, done)
 
 
 def shards(
@@ -488,15 +535,17 @@
     def exchange(value):
         return lax.all_to_all(value, "ctx", split_axis=0, concat_axis=0, tiled=True)
 
-    packed = pack(ep, latent, k_rope)
-    packed, moe_rows = lax.optimization_barrier((packed, moe_rows))
-    outgoing, high, low = route(expert_ids, expert_weights, moe_rows, ctx)
+    place = jnp.concatenate([me, ep])
+    outgoing, high, low, packed = route(
+        ep, expert_ids, expert_weights, k_rope, moe_rows, latent, ctx
+    )
     arrived = exchange(outgoing)
-    high, q_nope = lax.optimization_barrier((high, q_nope))
-    queries = fold(q_nope, q_rope, w_uk)
     flips = gather_order(ctx)
-    own_keys = packed[None]
-    for flip in flips[:-1]:
+    received = over_ctx(packed[None], flips[0])
+    high, q_nope, received = lax.optimization_barrier((high, q_nope, received))
+    queries = fold(place, positions, q_nope, q_rope, w_uk)
+    own_keys = jnp.concatenate([packed[None], received], axis=0)
+    for flip in flips[1:-1]:
         own_keys = jnp.concatenate([own_keys, over_ctx(own_keys, flip)], axis=0)
     arrived, queries, own_keys = lax.optimization_barrier((arrived, queries, own_keys))
 
@@ -513,20 +562,18 @@
     core_far_out, received = lax.optimization_barrier((core_far_out, received))
     from_core_far = over_ep(core_far_out, 1)
     from_core = over_ep(core_out, 1)
+    own_keys = jnp.concatenate([own_keys, received], axis=0)
+    own_keys, from_core_far = lax.optimization_barrier((own_keys, from_core_far))
     to_far = add(far_out, from_core_far)
     from_far = over_ep(to_far, 2)
-    own_keys = jnp.concatenate([own_keys, received], axis=0)
     core_keys = over_ep(own_keys, 1)
-    place = jnp.concatenate([me, ep])
-    heads = q_nope.shape[1] // NOPE
-    split = heads // 2
-    half = attend(0, split, place, positions, queries, w_uv, own_keys, core_keys)
+    half, keys, later_w_uv = attend_first(
+        place, positions, queries, w_uv, own_keys, core_keys
+    )
     from_far, half = lax.optimization_barrier((from_far, half))
     returning = add(own_out, from_core, from_far)
     returned = exchange(returning.reshape(arrived.shape))
-    attention = attend(
-        split, heads, place, positions, queries, w_uv, own_keys, core_keys, half
-    )
+    attention = attend_second(place, positions, queries, later_w_uv, keys, half)
     moe_out = combine(high, low, returned.reshape(own.shape))
     return (attention, moe_out)
 

time: 58.4 us -> 58.8 us (level)
  local copies, waits for them, and re-layouts: 0.08 us -> 4.6 us
  Pallas kernels: 29.2 us -> 25.6 us
  waiting for transfers between devices: 7.05 us -> 5.81 us
  other arithmetic: 1.05 us -> 1.73 us
    unnamed x9 -> x22, local copies, waits for them, and re-layouts: 0.04 us -> 4.6 us
    pallas_call x4 -> x3, Pallas kernels: 19.2 us -> 15.5 us  [the longest x1 5.83 us: attend_first(): pl.pallas_call(first_kernel, out_shape=[jax.ShapeDtypeStruct((2 * HALF, c...]
    concatenate x0 -> x2, other arithmetic: none -> 1.01 us  [the longest x1 0.91 us: shards(): own_keys = jnp.concatenate([packed[None], received], axis=0)]
    concatenate x2 -> x1, other arithmetic: 0.97 us -> 0.06 us  [shards(): own_keys = jnp.concatenate([own_keys, over_ctx(own_keys, flip)], axis=0)]
    all_to_all x2, starting transfers between devices: 8.38 us -> 9.02 us  [exchange(): return lax.all_to_all(value, 'ctx', split_axis=0, concat_axis=0, tiled=True)]
    all_to_all x2, waiting for transfers between devices: 1.75 us -> 1.12 us  [exchange(): return lax.all_to_all(value, 'ctx', split_axis=0, concat_axis=0, tiled=True)]
  transfers between devices with their start and end apart: 12 -> 12, of which waited for: 7 -> 7; matrix products, arithmetic and copies ran while one was open for 2% -> 3% of each run, Pallas kernels for 44% -> 37%
where the time goes in v3:
time: 58.8 us; the launch traced here: 58.2 us
  Pallas kernels  25.6 us (44%)
  starting transfers between devices  19.7 us (34%)
  waiting for transfers between devices  5.81 us (10%)
  local copies, waits for them, and re-layouts  4.6 us (8%)
  other arithmetic  1.73 us (3%)
  between operations  0.74 us (1%)
    all_to_all x2, starting transfers between devices, exchange(): return lax.all_to_all(value, 'ctx', split_axis=0, concat_axis=0, tiled=True)  9.02 us
    ppermute x3, starting transfers between devices, over_ctx(): return lax.ppermute(value, 'ctx', [(i, i ^ flip) for i in range(ctx)])  7.58 us
    pallas_call x1, Pallas kernels, attend_first(): pl.pallas_call(first_kernel, out_shape=[jax.ShapeDtypeStruct((2 * HALF, c...  5.83 us
    pallas_call x1, Pallas kernels, attend_second(): pl.pallas_call(second_kernel, out_shape=jax.ShapeDtypeStruct((2 * HALF, 2...  5 us
    pallas_call x1, Pallas kernels, fold(): pl.pallas_call(fold_kernel, out_shape=jax.ShapeDtypeStruct((2, 2, heads /...  4.7 us
    unnamed x22, local copies, waits for them, and re-layouts  4.6 us
    pallas_call x1, Pallas kernels, near_experts(): pl.pallas_call(near_kernel, out_shape=[jax.ShapeDtypeStruct((slots, 2 * u...  4.4 us
    ppermute x7, waiting for transfers between devices, over_ep(): return lax.ppermute(value, 'ep', [(i, i ^ flip) for i in range(4)])  3.71 us
  transfers between devices with their start and end apart: 12, of which 7 were waited for; matrix products, arithmetic and copies ran while one was open for 3% of the time, Pallas kernels for 37%

profile of v3, /device:TPU:0, one launch (start us, length us, event | category | flops | bytes accessed | tf_op | source)
XLA Modules:
  0.0 58.2 jit_solution(16273555679398095065)
XLA Ops:
  0.6 2.2 %route.1 = (bf16[8,8,1792]{2,1,0:T(8,128)(2,1)}, bf16[64,128]{1,0:T(8,128)(2,1)}, bf16[64,128]{1,0:T(8,128)(2,1)}, bf16[64,576]{1,0:T(8,128)(2,1)}) custom-call(s32[1]{0:T(128)} %bitcast.1.ep_ref, s32[8,128]{1,0:T(8,128)} %bitcast.20, f32[8,128]{1,0:T(8,128)} %bitcast.21, bf16[64,128]{1,0:T(8,128)(2,1)} %bitcast.19, bf16[128,1792]{1,0:T(8,128)(2,1)} %rows_ref.1, ...), custom_call_target="tpu_custom_call" | custom-call | flops 29360128 | bytes 1048576 | tf_op jit(solution)/shard_map/route/pallas_call | solution.py:87
  2.9 4.0 %collective-permute-start = (bf16[1,64,576]{2,1,0:T(8,128)(2,1)}, bf16[1,64,576]{2,1,0:T(8,128)(2,1)S(1)}, u32[]{:S(2)}, u32[]{:S(2)}) collective-permute-start(bf16[1,64,576]{2,1,0:T(8,128)(2,1)} %bitcast.16), channel_id=1, source_target_pairs={{0,16},{4,20},{8,24},{12,28},{16,0},{20,4},{24,8},{28,12},{1,17},{... | collective-permute-start | bytes 221192 | tf_op jit(solution)/shard_map/ppermute | solution.py:530
  6.9 3.8 %all-to-all-start = ((bf16[8,8,1792]{2,1,0:T(8,128)(2,1)}), bf16[8,8,1792]{2,1,0:T(8,128)(2,1)S(1)}, u32[]{:S(2)}, u32[]{:S(2)}) async-start(bf16[8,8,1792]{2,1,0:T(8,128)(2,1)} %get-tuple-element.31), calls=%async_computation | async-start | bytes 458752 | tf_op jit(solution)/shard_map/all_to_all | solution.py:536
  10.7 0.6 %collective-permute-done = bf16[1,64,576]{2,1,0:T(8,128)(2,1)S(1)} collective-permute-done((bf16[1,64,576]{2,1,0:T(8,128)(2,1)}, bf16[1,64,576]{2,1,0:T(8,128)(2,1)S(1)}, u32[]{:S(2)}, u32[]{:S(2)}) %collective-permute-start) | collective-permute-done | bytes 73760 | tf_op jit(solution)/shard_map/ppermute | solution.py:530
  11.3 0.9 %pad_maximum_fusion.2 = bf16[2,64,576]{2,1,0:T(8,128)(2,1)S(1)} fusion(bf16[1,64,576]{2,1,0:T(8,128)(2,1)S(1)} %collective-permute-done, bf16[1,64,576]{2,1,0:T(8,128)(2,1)} %bitcast.17), kind=kLoop, calls=%fused_computation.2 | loop fusion | flops 73728 | bytes 294912 | tf_op jit(solution)/shard_map/concatenate | solution.py:547
  12.2 1.8 %collective-permute-start.1 = (bf16[2,64,576]{2,1,0:T(8,128)(2,1)S(1)}, bf16[2,64,576]{2,1,0:T(8,128)(2,1)S(1)}, u32[]{:S(2)}, u32[]{:S(2)}) collective-permute-start(bf16[2,64,576]{2,1,0:T(8,128)(2,1)S(1)} %pad_maximum_fusion.2), channel_id=1, source_target_pairs={{0,4},{4,0},{8,12},{12,8},{16,20},{20,16},{24,28},{28,24},{1,5},{5... | collective-permute-start | bytes 442376 | tf_op jit(solution)/shard_map/ppermute | solution.py:530
  14.0 0.7 %pad_add_fusion.own_ref = s32[2]{0:T(128)} fusion(s32[1]{0:T(128)} %bitcast.1.ep_ref, s32[1]{0:T(128)} %bitcast), kind=kLoop, calls=%fused_computation.3 | loop fusion | flops 2 | bytes 16 | tf_op jit(solution)/shard_map/concatenate | solution.py:538
  14.7 0.0 copy-start.10
  14.7 4.7 %fold.1 = bf16[2,2,512,576]{3,2,1,0:T(8,128)(2,1)} custom-call(s32[2]{0:T(128)} %pad_add_fusion.own_ref, s32[1024]{0:T(1024)} %positions_ref.5, bf16[128,2048]{1,0:T(8,128)(2,1)} %q_nope_ref, bf16[128,1024]{1,0:T(8,128)(2,1)} %q_rope_ref.1, bf16[512,2048]{1,0:T(8,128)(2,1)} %w_uk_ref.1), custom_call_target="tpu_custom_call" | custom-call | flops 268435456 | bytes 6291456 | tf_op jit(solution)/shard_map/fold/pallas_call | solution.py:295
  19.4 0.0 collective-permute-done.1
  19.4 0.0 copy-done.10
  19.4 0.1 pad_maximum_fusion.1
  19.4 0.0 all-to-all-done
  19.4 0.1 collective-permute-start.3
  19.5 1.6 %collective-permute-start.2 = (bf16[64,1792]{1,0:T(8,128)(2,1)S(1)}, bf16[64,1792]{1,0:T(8,128)(2,1)S(1)}, u32[]{:S(2)}, u32[]{:S(2)}) collective-permute-start(bf16[64,1792]{1,0:T(8,128)(2,1)S(1)} %bitcast.14), channel_id=1, source_target_pairs={{0,2},{1,3},{2,0},{3,1},{4,6},{5,7},{6,4},{7,5},{8,10},{9,11},{10,... | collective-permute-start | bytes 688136 | tf_op jit(solution)/shard_map/ppermute | solution.py:533
  21.1 1.8 %collective-permute-start.5 = (bf16[4,64,576]{2,1,0:T(8,128)(2,1)S(1)}, bf16[4,64,576]{2,1,0:T(8,128)(2,1)S(1)}, u32[]{:S(2)}, u32[]{:S(2)}) collective-permute-start(bf16[4,64,576]{2,1,0:T(8,128)(2,1)S(1)} %pad_maximum_fusion.1), channel_id=1, source_target_pairs={{0,8},{4,12},{8,0},{12,4},{16,24},{20,28},{24,16},{28,20},{1,9},{5... | collective-permute-start | bytes 884744 | tf_op jit(solution)/shard_map/ppermute | solution.py:530
  22.9 0.0 collective-permute-done.3.core_ref
  22.9 4.4 %near_experts.1 = (f32[64,512]{1,0:T(8,128)S(1)}, bf16[2,1792,256]{2,1,0:T(8,128)(2,1)S(1)}, bf16[2,1792,256]{2,1,0:T(8,128)(2,1)S(1)}, bf16[4,256,1792]{2,1,0:T(8,128)(2,1)S(1)}) custom-call(s32[1]{0:T(128)} %bitcast.1.ep_ref, bf16[64,1792]{1,0:T(8,128)(2,1)S(1)} %bitcast.15, bf16[64,1792]{1,0:T(8,128)(2,1)S(1)} %collective-permute-done.3.core_ref, ...), custom_call_target="tpu_custom_call" | custom-call | flops 234881024 | bytes 11010048 | tf_op jit(solution)/shard_map/near_experts/pallas_call | solution.py:165
  27.3 0.3 collective-permute-done.2.far_ref
  27.5 0.0 collective-permute-start.4
  27.6 1.5 %collective-permute-done.4.core_far_ref = bf16[64,1792]{1,0:T(8,128)(2,1)S(1)} collective-permute-done((bf16[64,1792]{1,0:T(8,128)(2,1)S(1)}, bf16[64,1792]{1,0:T(8,128)(2,1)S(1)}, u32[]{:S(2)}, u32[]{:S(2)}) %collective-permute-start.4) | collective-permute-done | bytes 229408 | tf_op jit(solution)/shard_map/ppermute | solution.py:533
  29.0 0.0 copy-start.1
  29.0 0.0 copy-start.6
  29.0 0.0 copy-start.9
  29.0 1.5 %far_experts.1 = (bf16[64,1792]{1,0:T(8,128)(2,1)S(1)}, bf16[64,1792]{1,0:T(8,128)(2,1)S(1)}, bf16[64,1792]{1,0:T(8,128)(2,1)S(1)}, bf16[64,1792]{1,0:T(8,128)(2,1)S(1)}) custom-call(bf16[64,1792]{1,0:T(8,128)(2,1)S(1)} %collective-permute-done.2.far_ref, bf16[64,1792]{1,0:T(8,128)(2,1)S(1)} %collective-permute-done.4.core_far_ref, ...), custom_call_target="tpu_custom_call" | custom-call | tf_op jit(solution)/shard_map/far_experts/pallas_call | solution.py:212
  30.5 0.4 collective-permute-done.5
  30.9 0.0 collective-permute-start.6
  30.9 0.1 pad_maximum_fusion.own_keys
  31.0 1.4 %collective-permute-done.6.refs_1_ = bf16[64,1792]{1,0:T(8,128)(2,1)S(1)} collective-permute-done((bf16[64,1792]{1,0:T(8,128)(2,1)S(1)}, bf16[64,1792]{1,0:T(8,128)(2,1)S(1)}, u32[]{:S(2)}, u32[]{:S(2)}) %collective-permute-start.6) | collective-permute-done | bytes 229408 | tf_op jit(solution)/shard_map/ppermute | solution.py:533
  32.4 0.1 collective-permute-start.7
  32.5 0.1 add.4
  32.6 1.3 %collective-permute-start.8 = (bf16[64,1792]{1,0:T(8,128)(2,1)S(1)}, bf16[64,1792]{1,0:T(8,128)(2,1)S(1)}, u32[]{:S(2)}, u32[]{:S(2)}) collective-permute-start(bf16[64,1792]{1,0:T(8,128)(2,1)S(1)} %add.4), channel_id=1, source_target_pairs={{0,2},{1,3},{2,0},{3,1},{4,6},{5,7},{6,4},{7,5},{8,10},{9,11},{10,... | collective-permute-start | bytes 688136 | tf_op jit(solution)/shard_map/ppermute | solution.py:533
  33.9 0.0 copy-start
  33.9 0.1 collective-permute-start.9
  33.9 0.5 collective-permute-done.7.core_keys
  34.5 0.0 copy-done.1
  34.5 0.0 copy-done.6
  34.5 0.0 copy-done.9
  34.5 5.8 %attention_first.1 = (bf16[128,1024]{1,0:T(8,128)(2,1)S(1)}, bf16[1024,576]{1,0:T(8,128)(2,1)S(1)}, bf16[512,1024]{1,0:T(8,128)(2,1)S(1)}) custom-call(s32[2]{0:T(128)S(1)} %copy-done.9, s32[1024]{0:T(1024)S(1)} %copy-done.6, bf16[2,1024,576]{2,1,0:T(8,128)(2,1)} %bitcast.10, bf16[512,2048]{1,0:T(8,128)(2,1)S(1)} %copy-done.1, ...), custom_call_target="tpu_custom_call" | custom-call | flops 905969664 | bytes 4194304 | tf_op jit(solution)/shard_map/attention_first/pallas_call | solution.py:476
  40.3 0.0 copy-start.2
  40.3 1.1 %copy-done.2 = bf16[1024,576]{1,0:T(8,128)(2,1)} copy-done((bf16[1024,576]{1,0:T(8,128)(2,1)}, bf16[1024,576]{1,0:T(8,128)(2,1)S(1)}, u32[]{:S(2)}) %copy-start.2) | copy-done | bytes 1179672
  41.4 0.0 copy-start.4
  41.4 1.0 %copy-done.4 = bf16[512,1024]{1,0:T(8,128)(2,1)} copy-done((bf16[512,1024]{1,0:T(8,128)(2,1)}, bf16[512,1024]{1,0:T(8,128)(2,1)S(1)}, u32[]{:S(2)}) %copy-start.4) | copy-done | bytes 1048600
  42.4 0.0 collective-permute-done.8.refs_2_
  42.4 0.0 collective-permute-done.9.refs_1_
  42.4 0.8 %add.5 = bf16[64,1792]{1,0:T(8,128)(2,1)} custom-call(bf16[64,1792]{1,0:T(8,128)(2,1)S(1)} %get-tuple-element.57.refs_0_, bf16[64,1792]{1,0:T(8,128)(2,1)S(1)} %collective-permute-done.9.refs_1_, bf16[64,1792]{1,0:T(8,128)(2,1)S(1)} %collective-permute-done.8.refs_2_), custom_call_target="tpu_custom_call" | custom-call | bytes 1048576 | tf_op jit(solution)/shard_map/add/pallas_call | solution.py:231
  43.2 5.2 %all-to-all-start.1 = ((bf16[8,8,1792]{2,1,0:T(8,128)(2,1)}), bf16[8,8,1792]{2,1,0:T(8,128)(2,1)S(1)}, u32[]{:S(2)}, u32[]{:S(2)}) async-start(bf16[8,8,1792]{2,1,0:T(8,128)(2,1)} %bitcast.8), calls=%async_computation.1 | async-start | bytes 458752 | tf_op jit(solution)/shard_map/all_to_all | solution.py:536
  48.4 0.0 copy-done
  48.4 0.0 copy-start.3
  48.4 1.3 %copy-done.3 = bf16[1024,576]{1,0:T(8,128)(2,1)S(1)} copy-done((bf16[1024,576]{1,0:T(8,128)(2,1)S(1)}, bf16[1024,576]{1,0:T(8,128)(2,1)}, u32[]{:S(2)}) %copy-start.3) | copy-done | bytes 1179672
  49.7 0.0 copy-start.5
  49.7 1.2 %copy-done.5 = bf16[512,1024]{1,0:T(8,128)(2,1)S(1)} copy-done((bf16[512,1024]{1,0:T(8,128)(2,1)S(1)}, bf16[512,1024]{1,0:T(8,128)(2,1)}, u32[]{:S(2)}) %copy-start.5) | copy-done | bytes 1048600
  50.9 0.0 copy-start.7
  50.9 0.0 copy-start.8
  50.9 5.0 %attention_second.1 = bf16[128,2048]{1,0:T(8,128)(2,1)} custom-call(s32[2]{0:T(128)S(1)} %copy-done.9, s32[1024]{0:T(1024)S(1)} %copy-done.6, bf16[2,1024,576]{2,1,0:T(8,128)(2,1)S(1)} %bitcast.11, bf16[512,1024]{1,0:T(8,128)(2,1)S(1)} %copy-done.5, bf16[1024,576]{1,0:T(8,128)(2,1)S(1)} %copy-done.3, bf16[128,1024]{1,0:T(8,128)(2,1)S(1)} %get-tuple-element.54.done_ref), custom_call_target="tpu_custom_call" | custom-call | flops 905969664 | bytes 4194304 | tf_op jit(solution)/shard_map/attention_second/pallas_call | solution.py:498
  55.9 1.1 %all-to-all-done.1 = bf16[8,8,1792]{2,1,0:T(8,128)(2,1)S(1)} async-done(((bf16[8,8,1792]{2,1,0:T(8,128)(2,1)}), bf16[8,8,1792]{2,1,0:T(8,128)(2,1)S(1)}, u32[]{:S(2)}, u32[]{:S(2)}) %all-to-all-start.1) | async-done | bytes 229408 | tf_op jit(solution)/shard_map/all_to_all | solution.py:536
  57.0 0.0 copy-done.7
  57.0 0.0 copy-done.8
  57.1 1.2 %combine.1 = bf16[128,1792]{1,0:T(8,128)(2,1)} custom-call(bf16[64,128]{1,0:T(8,128)(2,1)S(1)} %copy-done.7, bf16[64,128]{1,0:T(8,128)(2,1)S(1)} %copy-done.8, bf16[64,1792]{1,0:T(8,128)(2,1)S(1)} %bitcast.12), custom_call_target="tpu_custom_call" | custom-call | flops 58720256 | bytes 1048576 | tf_op jit(solution)/shard_map/combine/pallas_call | solution.py:254
Async XLA Ops:
  2.9 8.5 %collective-permute-start = (bf16[1,64,576]{2,1,0:T(8,128)(2,1)}, bf16[1,64,576]{2,1,0:T(8,128)(2,1)S(1)}, u32[]{:S(2)}, u32[]{:S(2)}) collective-permute-start(bf16[1,64,576]{2,1,0:T(8,128)(2,1)} %bitcast.16), channel_id=1, source_target_pairs={{0,16},{4,20},{8,24},{12,28},{16,0},{20,4},{24,8},{28,12},{1,17},{... | collective-permute-start | bytes 221192 | tf_op jit(solution)/shard_map/ppermute | solution.py:530
  6.9 12.5 %all-to-all-start = ((bf16[8,8,1792]{2,1,0:T(8,128)(2,1)}), bf16[8,8,1792]{2,1,0:T(8,128)(2,1)S(1)}, u32[]{:S(2)}, u32[]{:S(2)}) async-start(bf16[8,8,1792]{2,1,0:T(8,128)(2,1)} %get-tuple-element.31), calls=%async_computation | async-start | bytes 458752 | tf_op jit(solution)/shard_map/all_to_all | solution.py:536
  12.2 7.1 %collective-permute-start.1 = (bf16[2,64,576]{2,1,0:T(8,128)(2,1)S(1)}, bf16[2,64,576]{2,1,0:T(8,128)(2,1)S(1)}, u32[]{:S(2)}, u32[]{:S(2)}) collective-permute-start(bf16[2,64,576]{2,1,0:T(8,128)(2,1)S(1)} %pad_maximum_fusion.2), channel_id=1, source_target_pairs={{0,4},{4,0},{8,12},{12,8},{16,20},{20,16},{24,28},{28,24},{1,5},{5... | collective-permute-start | bytes 442376 | tf_op jit(solution)/shard_map/ppermute | solution.py:530
  14.7 4.7 %copy-start.10 = (bf16[64,576]{1,0:T(8,128)(2,1)S(1)}, bf16[64,576]{1,0:T(8,128)(2,1)}, u32[]{:S(2)}) copy-start(bf16[64,576]{1,0:T(8,128)(2,1)} %get-tuple-element.33) | copy-start | bytes 221188
  19.4 3.4 %collective-permute-start.3 = (bf16[64,1792]{1,0:T(8,128)(2,1)S(1)}, bf16[64,1792]{1,0:T(8,128)(2,1)S(1)}, u32[]{:S(2)}, u32[]{:S(2)}) collective-permute-start(bf16[64,1792]{1,0:T(8,128)(2,1)S(1)} %bitcast.13), channel_id=1, source_target_pairs={{0,1},{1,0},{2,3},{3,2},{4,5},{5,4},{6,7},{7,6},{8,9},{9,8},{10,11... | collective-permute-start | bytes 688136 | tf_op jit(solution)/shard_map/ppermute | solution.py:533
  19.5 8.0 %collective-permute-start.2 = (bf16[64,1792]{1,0:T(8,128)(2,1)S(1)}, bf16[64,1792]{1,0:T(8,128)(2,1)S(1)}, u32[]{:S(2)}, u32[]{:S(2)}) collective-permute-start(bf16[64,1792]{1,0:T(8,128)(2,1)S(1)} %bitcast.14), channel_id=1, source_target_pairs={{0,2},{1,3},{2,0},{3,1},{4,6},{5,7},{6,4},{7,5},{8,10},{9,11},{10,... | collective-permute-start | bytes 688136 | tf_op jit(solution)/shard_map/ppermute | solution.py:533
  21.1 9.8 %collective-permute-start.5 = (bf16[4,64,576]{2,1,0:T(8,128)(2,1)S(1)}, bf16[4,64,576]{2,1,0:T(8,128)(2,1)S(1)}, u32[]{:S(2)}, u32[]{:S(2)}) collective-permute-start(bf16[4,64,576]{2,1,0:T(8,128)(2,1)S(1)} %pad_maximum_fusion.1), channel_id=1, source_target_pairs={{0,8},{4,12},{8,0},{12,4},{16,24},{20,28},{24,16},{28,20},{1,9},{5... | collective-permute-start | bytes 884744 | tf_op jit(solution)/shard_map/ppermute | solution.py:530
  27.5 1.5 %collective-permute-start.4 = (bf16[64,1792]{1,0:T(8,128)(2,1)S(1)}, bf16[64,1792]{1,0:T(8,128)(2,1)S(1)}, u32[]{:S(2)}, u32[]{:S(2)}) collective-permute-start(bf16[64,1792]{1,0:T(8,128)(2,1)S(1)} %collective-permute-done.2.far_ref), channel_id=1, source_target_pairs={{0,1},{1,0},{2,3},{3,2},{4,5},{5,4},{6,7},{7,6},{8,9},{9,8},{10,11... | collective-permute-start | bytes 688136 | tf_op jit(solution)/shard_map/ppermute | solution.py:533
  29.0 5.4 %copy-start.1 = (bf16[512,2048]{1,0:T(8,128)(2,1)S(1)}, bf16[512,2048]{1,0:T(8,128)(2,1)}, u32[]{:S(2)}) copy-start(bf16[512,2048]{1,0:T(8,128)(2,1)} %w_uv_hbm.1) | copy-start | bytes 6291460
  29.0 5.4 %copy-start.6 = (s32[1024]{0:T(1024)S(1)}, s32[1024]{0:T(1024)}, u32[]{:S(2)}) copy-start(s32[1024]{0:T(1024)} %positions_ref.5) | copy-start | bytes 12292
  29.0 5.4 %copy-start.9 = (s32[2]{0:T(128)S(1)}, s32[2]{0:T(128)}, u32[]{:S(2)}) copy-start(s32[2]{0:T(128)} %pad_add_fusion.own_ref) | copy-start | bytes 28
  30.9 1.5 %collective-permute-start.6 = (bf16[64,1792]{1,0:T(8,128)(2,1)S(1)}, bf16[64,1792]{1,0:T(8,128)(2,1)S(1)}, u32[]{:S(2)}, u32[]{:S(2)}) collective-permute-start(bf16[64,1792]{1,0:T(8,128)(2,1)S(1)} %get-tuple-element.47), channel_id=1, source_target_pairs={{0,1},{1,0},{2,3},{3,2},{4,5},{5,4},{6,7},{7,6},{8,9},{9,8},{10,11... | collective-permute-start | bytes 688136 | tf_op jit(solution)/shard_map/ppermute | solution.py:533
  32.4 2.1 %collective-permute-start.7 = (bf16[8,64,576]{2,1,0:T(8,128)(2,1)S(1)}, bf16[8,64,576]{2,1,0:T(8,128)(2,1)S(1)}, u32[]{:S(2)}, u32[]{:S(2)}) collective-permute-start(bf16[8,64,576]{2,1,0:T(8,128)(2,1)S(1)} %pad_maximum_fusion.own_keys), channel_id=1, source_target_pairs={{0,1},{1,0},{2,3},{3,2},{4,5},{5,4},{6,7},{7,6},{8,9},{9,8},{10,11... | collective-permute-start | bytes 1769480 | tf_op jit(solution)/shard_map/ppermute | solution.py:533
  32.6 9.8 %collective-permute-start.8 = (bf16[64,1792]{1,0:T(8,128)(2,1)S(1)}, bf16[64,1792]{1,0:T(8,128)(2,1)S(1)}, u32[]{:S(2)}, u32[]{:S(2)}) collective-permute-start(bf16[64,1792]{1,0:T(8,128)(2,1)S(1)} %add.4), channel_id=1, source_target_pairs={{0,2},{1,3},{2,0},{3,1},{4,6},{5,7},{6,4},{7,5},{8,10},{9,11},{10,... | collective-permute-start | bytes 688136 | tf_op jit(solution)/shard_map/ppermute | solution.py:533
  33.9 14.5 %copy-start = (bf16[2,2,512,576]{3,2,1,0:T(8,128)(2,1)S(1)}, bf16[2,2,512,576]{3,2,1,0:T(8,128)(2,1)}, u32[]{:S(2)}) copy-start(bf16[2,2,512,576]{3,2,1,0:T(8,128)(2,1)} %fold.1) | copy-start | bytes 7077892
  33.9 8.5 %collective-permute-start.9 = (bf16[64,1792]{1,0:T(8,128)(2,1)S(1)}, bf16[64,1792]{1,0:T(8,128)(2,1)S(1)}, u32[]{:S(2)}, u32[]{:S(2)}) collective-permute-start(bf16[64,1792]{1,0:T(8,128)(2,1)S(1)} %get-tuple-element.58), channel_id=1, source_target_pairs={{0,1},{1,0},{2,3},{3,2},{4,5},{5,4},{6,7},{7,6},{8,9},{9,8},{10,11... | collective-permute-start | bytes 688136 | tf_op jit(solution)/shard_map/ppermute | solution.py:533
  40.3 1.1 %copy-start.2 = (bf16[1024,576]{1,0:T(8,128)(2,1)}, bf16[1024,576]{1,0:T(8,128)(2,1)S(1)}, u32[]{:S(2)}) copy-start(bf16[1024,576]{1,0:T(8,128)(2,1)S(1)} %get-tuple-element.50.keys) | copy-start | bytes 3538948
  41.4 1.0 %copy-start.4 = (bf16[512,1024]{1,0:T(8,128)(2,1)}, bf16[512,1024]{1,0:T(8,128)(2,1)S(1)}, u32[]{:S(2)}) copy-start(bf16[512,1024]{1,0:T(8,128)(2,1)S(1)} %get-tuple-element.49.w_uv) | copy-start | bytes 3145732
  43.2 13.9 %all-to-all-start.1 = ((bf16[8,8,1792]{2,1,0:T(8,128)(2,1)}), bf16[8,8,1792]{2,1,0:T(8,128)(2,1)S(1)}, u32[]{:S(2)}, u32[]{:S(2)}) async-start(bf16[8,8,1792]{2,1,0:T(8,128)(2,1)} %bitcast.8), calls=%async_computation.1 | async-start | bytes 458752 | tf_op jit(solution)/shard_map/all_to_all | solution.py:536
  48.4 1.3 %copy-start.3 = (bf16[1024,576]{1,0:T(8,128)(2,1)S(1)}, bf16[1024,576]{1,0:T(8,128)(2,1)}, u32[]{:S(2)}) copy-start(bf16[1024,576]{1,0:T(8,128)(2,1)} %copy-done.2) | copy-start | bytes 3538948
  49.7 1.2 %copy-start.5 = (bf16[512,1024]{1,0:T(8,128)(2,1)S(1)}, bf16[512,1024]{1,0:T(8,128)(2,1)}, u32[]{:S(2)}) copy-start(bf16[512,1024]{1,0:T(8,128)(2,1)} %copy-done.4) | copy-start | bytes 3145732
  50.9 6.1 %copy-start.7 = (bf16[64,128]{1,0:T(8,128)(2,1)S(1)}, bf16[64,128]{1,0:T(8,128)(2,1)}, u32[]{:S(2)}) copy-start(bf16[64,128]{1,0:T(8,128)(2,1)} %get-tuple-element.55.high_ref) | copy-start | bytes 49156
  50.9 6.1 %copy-start.8 = (bf16[64,128]{1,0:T(8,128)(2,1)S(1)}, bf16[64,128]{1,0:T(8,128)(2,1)}, u32[]{:S(2)}) copy-start(bf16[64,128]{1,0:T(8,128)(2,1)} %get-tuple-element.56.low_ref) | copy-start | bytes 49156

commit v4 on v3

--- a/solution.py
+++ b/solution.py
@@ -319,8 +319,9 @@
 
 def first_kernel(
     own_ref,
+    ep_ref,
     positions_ref,
-    queries,
+    queries_hbm,
     w_uv_hbm,
     own_keys,
     core_keys,
@@ -328,17 +329,19 @@
     keys,
     later_w_uv,
     w_uv,
+    queries,
     *scratch,
 ):
     semaphores = scratch[-1]
-    copies = []
+    copies = [pltpu.make_async_copy(queries_hbm.at[0], queries, semaphores.at[2])]
+    copies[0].start()
     for index, target in enumerate((w_uv, later_w_uv)):
         width = target.shape[1]
         source = w_uv_hbm.at[:, pl.ds(index * width, width)]
         copies.append(pltpu.make_async_copy(source, target, semaphores.at[index]))
         copies[-1].start()
     blocks = own_keys.shape[0]
-    my_ctx, my_ep = own_ref[0], own_ref[1]
+    my_ctx, my_ep = own_ref[0], ep_ref[0]
     for flip, source in enumerate((own_keys, core_keys)):
         for index in range(blocks):
             source_ctx = my_ctx
@@ -348,10 +351,11 @@
             start = source_ctx * (2 * HALF) + ((my_ep % 2) ^ flip) * HALF
             place = pl.multiple_of(positions_ref[start], HALF)
             keys[pl.ds(place, HALF), :] = source[index]
+    copies[0].wait()
     attend_heads(
-        own_ref, positions_ref, queries.at[0], w_uv, keys, out_ref, 0, copies[0].wait, *scratch[:-1]
-    )
-    copies[1].wait()
+        own_ref, positions_ref, queries, w_uv, keys, out_ref, 0, copies[1].wait, *scratch[:-1]
+    )
+    copies[2].wait()
 
 
 def second_kernel(own_ref, positions_ref, queries, w_uv, keys, done_ref, out_ref, *scratch):
@@ -459,6 +463,10 @@
     ]
 
 
+def attend_limit(key_count):
+    return (12 + -(-9 * key_count // 1024)) * MIB
+
+
 def attend_cost(count, key_count, width):
     return pl.CostEstimate(
         flops=3 * count * key_count * width,
@@ -467,7 +475,7 @@
     )
 
 
-def attend_first(own, positions, queries, w_uv, own_keys, core_keys):
+def attend_first(own, ep, positions, queries, w_uv, own_keys, core_keys):
     latent_width, columns = w_uv.shape
     key_count = positions.shape[0]
     width = own_keys.shape[-1]
@@ -480,15 +488,15 @@
             jax.ShapeDtypeStruct((key_count, width), jnp.bfloat16),
             jax.ShapeDtypeStruct(half, jnp.bfloat16),
         ],
-        in_specs=[SMEM_SPEC] * 2 + [VMEM_SPEC, HBM_SPEC] + [VMEM_SPEC] * 2,
+        in_specs=[SMEM_SPEC] * 3 + [HBM_SPEC] * 2 + [VMEM_SPEC] * 2,
         out_specs=[VMEM_SPEC] * 3,
-        scratch_shapes=[VMEM(half, jnp.bfloat16)]
+        scratch_shapes=[VMEM(half, jnp.bfloat16), VMEM(queries.shape[1:], jnp.bfloat16)]
         + attend_scratch(count, key_count, latent_width)
-        + [pltpu.SemaphoreType.DMA((2,))],
-        compiler_params=pltpu.CompilerParams(vmem_limit_bytes=48 * MIB),
+        + [pltpu.SemaphoreType.DMA((3,))],
+        compiler_params=pltpu.CompilerParams(vmem_limit_bytes=attend_limit(key_count)),
         cost_estimate=attend_cost(count, key_count, width),
         name="attention_first",
-    )(own, positions, queries, w_uv, own_keys, core_keys)
+    )(own, ep, positions, queries, w_uv, own_keys, core_keys)
 
 
 def attend_second(own, positions, queries, w_uv, keys, done):
@@ -501,7 +509,7 @@
         in_specs=[SMEM_SPEC] * 2 + [VMEM_SPEC] * 4,
         out_specs=VMEM_SPEC,
         scratch_shapes=attend_scratch(count, key_count, latent_width),
-        compiler_params=pltpu.CompilerParams(vmem_limit_bytes=48 * MIB),
+        compiler_params=pltpu.CompilerParams(vmem_limit_bytes=attend_limit(key_count)),
         cost_estimate=attend_cost(count, key_count, width),
         name="attention_second",
     )(own, positions, queries, w_uv, keys, done)
@@ -535,7 +543,6 @@
     def exchange(value):
         return lax.all_to_all(value, "ctx", split_axis=0, concat_axis=0, tiled=True)
 
-    place = jnp.concatenate([me, ep])
     outgoing, high, low, packed = route(
         ep, expert_ids, expert_weights, k_rope, moe_rows, latent, ctx
     )
@@ -543,7 +550,7 @@
     flips = gather_order(ctx)
     received = over_ctx(packed[None], flips[0])
     high, q_nope, received = lax.optimization_barrier((high, q_nope, received))
-    queries = fold(place, positions, q_nope, q_rope, w_uk)
+    queries = fold(me, positions, q_nope, q_rope, w_uk)
     own_keys = jnp.concatenate([packed[None], received], axis=0)
     for flip in flips[1:-1]:
         own_keys = jnp.concatenate([own_keys, over_ctx(own_keys, flip)], axis=0)
@@ -568,12 +575,12 @@
     from_far = over_ep(to_far, 2)
     core_keys = over_ep(own_keys, 1)
     half, keys, later_w_uv = attend_first(
-        place, positions, queries, w_uv, own_keys, core_keys
+        me, ep, positions, queries, w_uv, own_keys, core_keys
     )
     from_far, half = lax.optimization_barrier((from_far, half))
     returning = add(own_out, from_core, from_far)
     returned = exchange(returning.reshape(arrived.shape))
-    attention = attend_second(place, positions, queries, later_w_uv, keys, half)
+    attention = attend_second(me, positions, queries, later_w_uv, keys, half)
     moe_out = combine(high, low, returned.reshape(own.shape))
     return (attention, moe_out)
 

time: 58.8 us -> 57.5 us (0.978)
  other arithmetic: 1.73 us -> 1.06 us
  Pallas kernels: 25.6 us -> 25 us
    pallas_call x1, Pallas kernels: 5.83 us -> 4.93 us  [attend_first(): pl.pallas_call(first_kernel, out_shape=[jax.ShapeDtypeStruct((2 * HALF, c...]
    ppermute x3, waiting for transfers between devices: 0.97 us -> 1.64 us  [over_ctx(): return lax.ppermute(value, 'ctx', [(i, i ^ flip) for i in range(ctx)])]
    concatenate x1 -> x0, other arithmetic: 0.66 us -> none  [shards(): place = jnp.concatenate([me, ep])]
    unnamed x22 -> x20, local copies, waits for them, and re-layouts: 4.6 us -> 4.59 us
  transfers between devices with their start and end apart: 12 -> 12, of which waited for: 7 -> 8; matrix products, arithmetic and copies ran while one was open for 3% -> 2% of each run, Pallas kernels for 37% -> 37%
where the time goes in v4:
time: 57.5 us; the launch traced here: 57.1 us
  Pallas kernels  25 us (43%)
  starting transfers between devices  19.5 us (34%)
  waiting for transfers between devices  6.26 us (11%)
  local copies, waits for them, and re-layouts  4.59 us (8%)
  other arithmetic  1.06 us (2%)
  between operations  0.73 us (1%)
    all_to_all x2, starting transfers between devices, exchange(): return lax.all_to_all(value, 'ctx', split_axis=0, concat_axis=0, tiled=True)  8.75 us
    ppermute x3, starting transfers between devices, over_ctx(): return lax.ppermute(value, 'ctx', [(i, i ^ flip) for i in range(ctx)])  7.71 us
    pallas_call x1, Pallas kernels, attend_second(): pl.pallas_call(second_kernel, out_shape=jax.ShapeDtypeStruct((2 * HALF, 2...  5.29 us
    pallas_call x1, Pallas kernels, attend_first(): pl.pallas_call(first_kernel, out_shape=[jax.ShapeDtypeStruct((2 * HALF, c...  4.93 us
    pallas_call x1, Pallas kernels, fold(): pl.pallas_call(fold_kernel, out_shape=jax.ShapeDtypeStruct((2, 2, heads /...  4.69 us
    unnamed x20, local copies, waits for them, and re-layouts  4.59 us
    pallas_call x1, Pallas kernels, near_experts(): pl.pallas_call(near_kernel, out_shape=[jax.ShapeDtypeStruct((slots, 2 * u...  4.4 us
    ppermute x7, waiting for transfers between devices, over_ep(): return lax.ppermute(value, 'ep', [(i, i ^ flip) for i in range(4)])  3.71 us
  transfers between devices with their start and end apart: 12, of which 8 were waited for; matrix products, arithmetic and copies ran while one was open for 2% of the time, Pallas kernels for 37%

profile of v4, /device:TPU:0, one launch (start us, length us, event | category | flops | bytes accessed | tf_op | source)
XLA Modules:
  0.0 57.1 jit_solution(9202551651000344566)
XLA Ops:
  0.6 2.2 %route.1 = (bf16[8,8,1792]{2,1,0:T(8,128)(2,1)}, bf16[64,128]{1,0:T(8,128)(2,1)}, bf16[64,128]{1,0:T(8,128)(2,1)}, bf16[64,576]{1,0:T(8,128)(2,1)}) custom-call(s32[1]{0:T(128)} %bitcast.1.ep_ref, s32[8,128]{1,0:T(8,128)} %bitcast.20, f32[8,128]{1,0:T(8,128)} %bitcast.21, bf16[64,128]{1,0:T(8,128)(2,1)} %bitcast.19, bf16[128,1792]{1,0:T(8,128)(2,1)} %rows_ref.1, ...), custom_call_target="tpu_custom_call" | custom-call | flops 29360128 | bytes 1048576 | tf_op jit(solution)/shard_map/route/pallas_call | solution.py:87
  2.9 4.0 %collective-permute-start = (bf16[1,64,576]{2,1,0:T(8,128)(2,1)}, bf16[1,64,576]{2,1,0:T(8,128)(2,1)S(1)}, u32[]{:S(2)}, u32[]{:S(2)}) collective-permute-start(bf16[1,64,576]{2,1,0:T(8,128)(2,1)} %bitcast.16), channel_id=1, source_target_pairs={{0,16},{4,20},{8,24},{12,28},{16,0},{20,4},{24,8},{28,12},{1,17},{... | collective-permute-start | bytes 221192 | tf_op jit(solution)/shard_map/ppermute | solution.py:538
  6.9 3.8 %all-to-all-start = ((bf16[8,8,1792]{2,1,0:T(8,128)(2,1)}), bf16[8,8,1792]{2,1,0:T(8,128)(2,1)S(1)}, u32[]{:S(2)}, u32[]{:S(2)}) async-start(bf16[8,8,1792]{2,1,0:T(8,128)(2,1)} %get-tuple-element.31), calls=%async_computation | async-start | bytes 458752 | tf_op jit(solution)/shard_map/all_to_all | solution.py:544
  10.7 0.6 %collective-permute-done = bf16[1,64,576]{2,1,0:T(8,128)(2,1)S(1)} collective-permute-done((bf16[1,64,576]{2,1,0:T(8,128)(2,1)}, bf16[1,64,576]{2,1,0:T(8,128)(2,1)S(1)}, u32[]{:S(2)}, u32[]{:S(2)}) %collective-permute-start) | collective-permute-done | bytes 73760 | tf_op jit(solution)/shard_map/ppermute | solution.py:538
  11.3 0.9 %pad_maximum_fusion.2 = bf16[2,64,576]{2,1,0:T(8,128)(2,1)S(1)} fusion(bf16[1,64,576]{2,1,0:T(8,128)(2,1)S(1)} %collective-permute-done, bf16[1,64,576]{2,1,0:T(8,128)(2,1)} %bitcast.17), kind=kLoop, calls=%fused_computation.2 | loop fusion | flops 73728 | bytes 294912 | tf_op jit(solution)/shard_map/concatenate | solution.py:554
  12.2 1.8 %collective-permute-start.1 = (bf16[2,64,576]{2,1,0:T(8,128)(2,1)S(1)}, bf16[2,64,576]{2,1,0:T(8,128)(2,1)S(1)}, u32[]{:S(2)}, u32[]{:S(2)}) collective-permute-start(bf16[2,64,576]{2,1,0:T(8,128)(2,1)S(1)} %pad_maximum_fusion.2), channel_id=1, source_target_pairs={{0,4},{4,0},{8,12},{12,8},{16,20},{20,16},{24,28},{28,24},{1,5},{5... | collective-permute-start | bytes 442376 | tf_op jit(solution)/shard_map/ppermute | solution.py:538
  14.0 0.0 copy-start.9
  14.0 4.7 %fold.1 = bf16[2,2,512,576]{3,2,1,0:T(8,128)(2,1)} custom-call(s32[1]{0:T(128)} %bitcast.own_ref, s32[1024]{0:T(1024)} %positions_ref.5, bf16[128,2048]{1,0:T(8,128)(2,1)} %q_nope_ref, bf16[128,1024]{1,0:T(8,128)(2,1)} %q_rope_ref.1, bf16[512,2048]{1,0:T(8,128)(2,1)} %w_uk_ref.1), custom_call_target="tpu_custom_call" | custom-call | flops 268435456 | bytes 6291456 | tf_op jit(solution)/shard_map/fold/pallas_call | solution.py:295
  18.7 0.5 collective-permute-done.1
  19.2 0.0 copy-done.9
  19.2 0.1 pad_maximum_fusion.1
  19.3 0.0 all-to-all-done
  19.3 0.1 collective-permute-start.3
  19.4 1.6 %collective-permute-start.2 = (bf16[64,1792]{1,0:T(8,128)(2,1)S(1)}, bf16[64,1792]{1,0:T(8,128)(2,1)S(1)}, u32[]{:S(2)}, u32[]{:S(2)}) collective-permute-start(bf16[64,1792]{1,0:T(8,128)(2,1)S(1)} %bitcast.14), channel_id=1, source_target_pairs={{0,2},{1,3},{2,0},{3,1},{4,6},{5,7},{6,4},{7,5},{8,10},{9,11},{10,... | collective-permute-start | bytes 688136 | tf_op jit(solution)/shard_map/ppermute | solution.py:541
  20.9 1.9 %collective-permute-start.5 = (bf16[4,64,576]{2,1,0:T(8,128)(2,1)S(1)}, bf16[4,64,576]{2,1,0:T(8,128)(2,1)S(1)}, u32[]{:S(2)}, u32[]{:S(2)}) collective-permute-start(bf16[4,64,576]{2,1,0:T(8,128)(2,1)S(1)} %pad_maximum_fusion.1), channel_id=1, source_target_pairs={{0,8},{4,12},{8,0},{12,4},{16,24},{20,28},{24,16},{28,20},{1,9},{5... | collective-permute-start | bytes 884744 | tf_op jit(solution)/shard_map/ppermute | solution.py:538
  22.9 0.0 collective-permute-done.3.core_ref
  22.9 4.4 %near_experts.1 = (f32[64,512]{1,0:T(8,128)S(1)}, bf16[2,1792,256]{2,1,0:T(8,128)(2,1)S(1)}, bf16[2,1792,256]{2,1,0:T(8,128)(2,1)S(1)}, bf16[4,256,1792]{2,1,0:T(8,128)(2,1)S(1)}) custom-call(s32[1]{0:T(128)} %bitcast.1.ep_ref, bf16[64,1792]{1,0:T(8,128)(2,1)S(1)} %bitcast.15, bf16[64,1792]{1,0:T(8,128)(2,1)S(1)} %collective-permute-done.3.core_ref, ...), custom_call_target="tpu_custom_call" | custom-call | flops 234881024 | bytes 11010048 | tf_op jit(solution)/shard_map/near_experts/pallas_call | solution.py:165
  27.3 0.2 collective-permute-done.2.far_ref
  27.4 0.0 collective-permute-start.4
  27.4 1.5 %collective-permute-done.4.core_far_ref = bf16[64,1792]{1,0:T(8,128)(2,1)S(1)} collective-permute-done((bf16[64,1792]{1,0:T(8,128)(2,1)S(1)}, bf16[64,1792]{1,0:T(8,128)(2,1)S(1)}, u32[]{:S(2)}, u32[]{:S(2)}) %collective-permute-start.4) | collective-permute-done | bytes 229408 | tf_op jit(solution)/shard_map/ppermute | solution.py:541
  28.9 0.0 copy-start
  28.9 0.0 copy-start.1
  28.9 0.0 copy-start.6
  28.9 1.5 %far_experts.1 = (bf16[64,1792]{1,0:T(8,128)(2,1)S(1)}, bf16[64,1792]{1,0:T(8,128)(2,1)S(1)}, bf16[64,1792]{1,0:T(8,128)(2,1)S(1)}, bf16[64,1792]{1,0:T(8,128)(2,1)S(1)}) custom-call(bf16[64,1792]{1,0:T(8,128)(2,1)S(1)} %collective-permute-done.2.far_ref, bf16[64,1792]{1,0:T(8,128)(2,1)S(1)} %collective-permute-done.4.core_far_ref, ...), custom_call_target="tpu_custom_call" | custom-call | tf_op jit(solution)/shard_map/far_experts/pallas_call | solution.py:212
  30.4 0.5 collective-permute-done.5
  30.9 0.0 collective-permute-start.6
  30.9 0.1 pad_maximum_fusion.own_keys
  31.0 1.4 %collective-permute-done.6.refs_1_ = bf16[64,1792]{1,0:T(8,128)(2,1)S(1)} collective-permute-done((bf16[64,1792]{1,0:T(8,128)(2,1)S(1)}, bf16[64,1792]{1,0:T(8,128)(2,1)S(1)}, u32[]{:S(2)}, u32[]{:S(2)}) %collective-permute-start.6) | collective-permute-done | bytes 229408 | tf_op jit(solution)/shard_map/ppermute | solution.py:541
  32.4 0.1 collective-permute-start.7
  32.5 0.1 add.2
  32.6 1.1 %collective-permute-start.8 = (bf16[64,1792]{1,0:T(8,128)(2,1)S(1)}, bf16[64,1792]{1,0:T(8,128)(2,1)S(1)}, u32[]{:S(2)}, u32[]{:S(2)}) collective-permute-start(bf16[64,1792]{1,0:T(8,128)(2,1)S(1)} %add.2), channel_id=1, source_target_pairs={{0,2},{1,3},{2,0},{3,1},{4,6},{5,7},{6,4},{7,5},{8,10},{9,11},{10,... | collective-permute-start | bytes 688136 | tf_op jit(solution)/shard_map/ppermute | solution.py:541
  33.7 0.1 collective-permute-start.9
  33.8 0.7 %collective-permute-done.7.core_keys = bf16[8,64,576]{2,1,0:T(8,128)(2,1)S(1)} collective-permute-done((bf16[8,64,576]{2,1,0:T(8,128)(2,1)S(1)}, bf16[8,64,576]{2,1,0:T(8,128)(2,1)S(1)}, u32[]{:S(2)}, u32[]{:S(2)}) %collective-permute-start.7) | collective-permute-done | bytes 589856 | tf_op jit(solution)/shard_map/ppermute | solution.py:541
  34.5 0.0 copy-done
  34.5 0.0 copy-done.1
  34.5 0.0 copy-done.6
  34.5 4.9 %attention_first.1 = (bf16[128,1024]{1,0:T(8,128)(2,1)S(1)}, bf16[1024,576]{1,0:T(8,128)(2,1)S(1)}, bf16[512,1024]{1,0:T(8,128)(2,1)S(1)}) custom-call(s32[1]{0:T(128)} %bitcast.own_ref, s32[1]{0:T(128)} %bitcast.1.ep_ref, s32[1024]{0:T(1024)S(1)} %copy-done.6, bf16[2,1024,576]{2,1,0:T(8,128)(2,1)S(1)} %bitcast.10, bf16[512,2048]{1,0:T(8,128)(2,1)S(1)} %copy-done.1, ...), custom_call_target="tpu_custom_call" | custom-call | flops 905969664 | bytes 4194304 | tf_op jit(solution)/shard_map/attention_first/pallas_call | solution.py:484
  39.4 0.0 copy-start.2
  39.4 1.1 %copy-done.2 = bf16[1024,576]{1,0:T(8,128)(2,1)} copy-done((bf16[1024,576]{1,0:T(8,128)(2,1)}, bf16[1024,576]{1,0:T(8,128)(2,1)S(1)}, u32[]{:S(2)}) %copy-start.2) | copy-done | bytes 1179672
  40.5 0.0 copy-start.4
  40.5 1.0 %copy-done.4 = bf16[512,1024]{1,0:T(8,128)(2,1)} copy-done((bf16[512,1024]{1,0:T(8,128)(2,1)}, bf16[512,1024]{1,0:T(8,128)(2,1)S(1)}, u32[]{:S(2)}) %copy-start.4) | copy-done | bytes 1048600
  41.5 0.0 collective-permute-done.8.refs_2_
  41.5 0.0 collective-permute-done.9.refs_1_
  41.5 0.8 %add.3 = bf16[64,1792]{1,0:T(8,128)(2,1)} custom-call(bf16[64,1792]{1,0:T(8,128)(2,1)S(1)} %get-tuple-element.57.refs_0_, bf16[64,1792]{1,0:T(8,128)(2,1)S(1)} %collective-permute-done.9.refs_1_, bf16[64,1792]{1,0:T(8,128)(2,1)S(1)} %collective-permute-done.8.refs_2_), custom_call_target="tpu_custom_call" | custom-call | bytes 1048576 | tf_op jit(solution)/shard_map/add/pallas_call | solution.py:231
  42.3 4.9 %all-to-all-start.1 = ((bf16[8,8,1792]{2,1,0:T(8,128)(2,1)}), bf16[8,8,1792]{2,1,0:T(8,128)(2,1)S(1)}, u32[]{:S(2)}, u32[]{:S(2)}) async-start(bf16[8,8,1792]{2,1,0:T(8,128)(2,1)} %bitcast.8), calls=%async_computation.1 | async-start | bytes 458752 | tf_op jit(solution)/shard_map/all_to_all | solution.py:544
  47.2 0.0 copy-start.3
  47.2 1.3 %copy-done.3 = bf16[1024,576]{1,0:T(8,128)(2,1)S(1)} copy-done((bf16[1024,576]{1,0:T(8,128)(2,1)S(1)}, bf16[1024,576]{1,0:T(8,128)(2,1)}, u32[]{:S(2)}) %copy-start.3) | copy-done | bytes 1179672
  48.5 0.0 copy-start.5
  48.5 1.2 %copy-done.5 = bf16[512,1024]{1,0:T(8,128)(2,1)S(1)} copy-done((bf16[512,1024]{1,0:T(8,128)(2,1)S(1)}, bf16[512,1024]{1,0:T(8,128)(2,1)}, u32[]{:S(2)}) %copy-start.5) | copy-done | bytes 1048600
  49.7 0.0 copy-start.7
  49.7 0.0 copy-start.8
  49.7 5.3 %attention_second.1 = bf16[128,2048]{1,0:T(8,128)(2,1)} custom-call(s32[1]{0:T(128)} %bitcast.own_ref, s32[1024]{0:T(1024)S(1)} %copy-done.6, bf16[2,1024,576]{2,1,0:T(8,128)(2,1)S(1)} %bitcast.11, bf16[512,1024]{1,0:T(8,128)(2,1)S(1)} %copy-done.5, bf16[1024,576]{1,0:T(8,128)(2,1)S(1)} %copy-done.3, bf16[128,1024]{1,0:T(8,128)(2,1)S(1)} %get-tuple-element.54.done_ref), custom_call_target="tpu_custom_call" | custom-call | flops 905969664 | bytes 4194304 | tf_op jit(solution)/shard_map/attention_second/pallas_call | solution.py:506
  55.0 0.9 %all-to-all-done.1 = bf16[8,8,1792]{2,1,0:T(8,128)(2,1)S(1)} async-done(((bf16[8,8,1792]{2,1,0:T(8,128)(2,1)}), bf16[8,8,1792]{2,1,0:T(8,128)(2,1)S(1)}, u32[]{:S(2)}, u32[]{:S(2)}) %all-to-all-start.1) | async-done | bytes 229408 | tf_op jit(solution)/shard_map/all_to_all | solution.py:544
  55.9 0.0 copy-done.7
  55.9 0.0 copy-done.8
  55.9 1.2 %combine.1 = bf16[128,1792]{1,0:T(8,128)(2,1)} custom-call(bf16[64,128]{1,0:T(8,128)(2,1)S(1)} %copy-done.7, bf16[64,128]{1,0:T(8,128)(2,1)S(1)} %copy-done.8, bf16[64,1792]{1,0:T(8,128)(2,1)S(1)} %bitcast.12), custom_call_target="tpu_custom_call" | custom-call | flops 58720256 | bytes 1048576 | tf_op jit(solution)/shard_map/combine/pallas_call | solution.py:254
Async XLA Ops:
  2.9 8.5 %collective-permute-start = (bf16[1,64,576]{2,1,0:T(8,128)(2,1)}, bf16[1,64,576]{2,1,0:T(8,128)(2,1)S(1)}, u32[]{:S(2)}, u32[]{:S(2)}) collective-permute-start(bf16[1,64,576]{2,1,0:T(8,128)(2,1)} %bitcast.16), channel_id=1, source_target_pairs={{0,16},{4,20},{8,24},{12,28},{16,0},{20,4},{24,8},{28,12},{1,17},{... | collective-permute-start | bytes 221192 | tf_op jit(solution)/shard_map/ppermute | solution.py:538
  6.9 12.4 %all-to-all-start = ((bf16[8,8,1792]{2,1,0:T(8,128)(2,1)}), bf16[8,8,1792]{2,1,0:T(8,128)(2,1)S(1)}, u32[]{:S(2)}, u32[]{:S(2)}) async-start(bf16[8,8,1792]{2,1,0:T(8,128)(2,1)} %get-tuple-element.31), calls=%async_computation | async-start | bytes 458752 | tf_op jit(solution)/shard_map/all_to_all | solution.py:544
  12.2 7.0 %collective-permute-start.1 = (bf16[2,64,576]{2,1,0:T(8,128)(2,1)S(1)}, bf16[2,64,576]{2,1,0:T(8,128)(2,1)S(1)}, u32[]{:S(2)}, u32[]{:S(2)}) collective-permute-start(bf16[2,64,576]{2,1,0:T(8,128)(2,1)S(1)} %pad_maximum_fusion.2), channel_id=1, source_target_pairs={{0,4},{4,0},{8,12},{12,8},{16,20},{20,16},{24,28},{28,24},{1,5},{5... | collective-permute-start | bytes 442376 | tf_op jit(solution)/shard_map/ppermute | solution.py:538
  14.0 5.2 %copy-start.9 = (bf16[64,576]{1,0:T(8,128)(2,1)S(1)}, bf16[64,576]{1,0:T(8,128)(2,1)}, u32[]{:S(2)}) copy-start(bf16[64,576]{1,0:T(8,128)(2,1)} %get-tuple-element.33) | copy-start | bytes 221188
  19.3 3.5 %collective-permute-start.3 = (bf16[64,1792]{1,0:T(8,128)(2,1)S(1)}, bf16[64,1792]{1,0:T(8,128)(2,1)S(1)}, u32[]{:S(2)}, u32[]{:S(2)}) collective-permute-start(bf16[64,1792]{1,0:T(8,128)(2,1)S(1)} %bitcast.13), channel_id=1, source_target_pairs={{0,1},{1,0},{2,3},{3,2},{4,5},{5,4},{6,7},{7,6},{8,9},{9,8},{10,11... | collective-permute-start | bytes 688136 | tf_op jit(solution)/shard_map/ppermute | solution.py:541
  19.4 8.0 %collective-permute-start.2 = (bf16[64,1792]{1,0:T(8,128)(2,1)S(1)}, bf16[64,1792]{1,0:T(8,128)(2,1)S(1)}, u32[]{:S(2)}, u32[]{:S(2)}) collective-permute-start(bf16[64,1792]{1,0:T(8,128)(2,1)S(1)} %bitcast.14), channel_id=1, source_target_pairs={{0,2},{1,3},{2,0},{3,1},{4,6},{5,7},{6,4},{7,5},{8,10},{9,11},{10,... | collective-permute-start | bytes 688136 | tf_op jit(solution)/shard_map/ppermute | solution.py:541
  20.9 9.9 %collective-permute-start.5 = (bf16[4,64,576]{2,1,0:T(8,128)(2,1)S(1)}, bf16[4,64,576]{2,1,0:T(8,128)(2,1)S(1)}, u32[]{:S(2)}, u32[]{:S(2)}) collective-permute-start(bf16[4,64,576]{2,1,0:T(8,128)(2,1)S(1)} %pad_maximum_fusion.1), channel_id=1, source_target_pairs={{0,8},{4,12},{8,0},{12,4},{16,24},{20,28},{24,16},{28,20},{1,9},{5... | collective-permute-start | bytes 884744 | tf_op jit(solution)/shard_map/ppermute | solution.py:538
  27.4 1.5 %collective-permute-start.4 = (bf16[64,1792]{1,0:T(8,128)(2,1)S(1)}, bf16[64,1792]{1,0:T(8,128)(2,1)S(1)}, u32[]{:S(2)}, u32[]{:S(2)}) collective-permute-start(bf16[64,1792]{1,0:T(8,128)(2,1)S(1)} %collective-permute-done.2.far_ref), channel_id=1, source_target_pairs={{0,1},{1,0},{2,3},{3,2},{4,5},{5,4},{6,7},{7,6},{8,9},{9,8},{10,11... | collective-permute-start | bytes 688136 | tf_op jit(solution)/shard_map/ppermute | solution.py:541
  28.9 5.6 %copy-start = (bf16[2,2,512,576]{3,2,1,0:T(8,128)(2,1)S(1)}, bf16[2,2,512,576]{3,2,1,0:T(8,128)(2,1)}, u32[]{:S(2)}) copy-start(bf16[2,2,512,576]{3,2,1,0:T(8,128)(2,1)} %fold.1) | copy-start | bytes 7077892
  28.9 5.6 %copy-start.1 = (bf16[512,2048]{1,0:T(8,128)(2,1)S(1)}, bf16[512,2048]{1,0:T(8,128)(2,1)}, u32[]{:S(2)}) copy-start(bf16[512,2048]{1,0:T(8,128)(2,1)} %w_uv_hbm.1) | copy-start | bytes 6291460
  28.9 5.6 %copy-start.6 = (s32[1024]{0:T(1024)S(1)}, s32[1024]{0:T(1024)}, u32[]{:S(2)}) copy-start(s32[1024]{0:T(1024)} %positions_ref.5) | copy-start | bytes 12292
  30.9 1.5 %collective-permute-start.6 = (bf16[64,1792]{1,0:T(8,128)(2,1)S(1)}, bf16[64,1792]{1,0:T(8,128)(2,1)S(1)}, u32[]{:S(2)}, u32[]{:S(2)}) collective-permute-start(bf16[64,1792]{1,0:T(8,128)(2,1)S(1)} %get-tuple-element.47), channel_id=1, source_target_pairs={{0,1},{1,0},{2,3},{3,2},{4,5},{5,4},{6,7},{7,6},{8,9},{9,8},{10,11... | collective-permute-start | bytes 688136 | tf_op jit(solution)/shard_map/ppermute | solution.py:541
  32.4 2.1 %collective-permute-start.7 = (bf16[8,64,576]{2,1,0:T(8,128)(2,1)S(1)}, bf16[8,64,576]{2,1,0:T(8,128)(2,1)S(1)}, u32[]{:S(2)}, u32[]{:S(2)}) collective-permute-start(bf16[8,64,576]{2,1,0:T(8,128)(2,1)S(1)} %pad_maximum_fusion.own_keys), channel_id=1, source_target_pairs={{0,1},{1,0},{2,3},{3,2},{4,5},{5,4},{6,7},{7,6},{8,9},{9,8},{10,11... | collective-permute-start | bytes 1769480 | tf_op jit(solution)/shard_map/ppermute | solution.py:541
  32.6 8.9 %collective-permute-start.8 = (bf16[64,1792]{1,0:T(8,128)(2,1)S(1)}, bf16[64,1792]{1,0:T(8,128)(2,1)S(1)}, u32[]{:S(2)}, u32[]{:S(2)}) collective-permute-start(bf16[64,1792]{1,0:T(8,128)(2,1)S(1)} %add.2), channel_id=1, source_target_pairs={{0,2},{1,3},{2,0},{3,1},{4,6},{5,7},{6,4},{7,5},{8,10},{9,11},{10,... | collective-permute-start | bytes 688136 | tf_op jit(solution)/shard_map/ppermute | solution.py:541
  33.7 7.8 %collective-permute-start.9 = (bf16[64,1792]{1,0:T(8,128)(2,1)S(1)}, bf16[64,1792]{1,0:T(8,128)(2,1)S(1)}, u32[]{:S(2)}, u32[]{:S(2)}) collective-permute-start(bf16[64,1792]{1,0:T(8,128)(2,1)S(1)} %get-tuple-element.58), channel_id=1, source_target_pairs={{0,1},{1,0},{2,3},{3,2},{4,5},{5,4},{6,7},{7,6},{8,9},{9,8},{10,11... | collective-permute-start | bytes 688136 | tf_op jit(solution)/shard_map/ppermute | solution.py:541
  39.4 1.1 %copy-start.2 = (bf16[1024,576]{1,0:T(8,128)(2,1)}, bf16[1024,576]{1,0:T(8,128)(2,1)S(1)}, u32[]{:S(2)}) copy-start(bf16[1024,576]{1,0:T(8,128)(2,1)S(1)} %get-tuple-element.50.keys) | copy-start | bytes 3538948
  40.5 1.0 %copy-start.4 = (bf16[512,1024]{1,0:T(8,128)(2,1)}, bf16[512,1024]{1,0:T(8,128)(2,1)S(1)}, u32[]{:S(2)}) copy-start(bf16[512,1024]{1,0:T(8,128)(2,1)S(1)} %get-tuple-element.49.w_uv) | copy-start | bytes 3145732
  42.3 13.7 %all-to-all-start.1 = ((bf16[8,8,1792]{2,1,0:T(8,128)(2,1)}), bf16[8,8,1792]{2,1,0:T(8,128)(2,1)S(1)}, u32[]{:S(2)}, u32[]{:S(2)}) async-start(bf16[8,8,1792]{2,1,0:T(8,128)(2,1)} %bitcast.8), calls=%async_computation.1 | async-start | bytes 458752 | tf_op jit(solution)/shard_map/all_to_all | solution.py:544
  47.2 1.3 %copy-start.3 = (bf16[1024,576]{1,0:T(8,128)(2,1)S(1)}, bf16[1024,576]{1,0:T(8,128)(2,1)}, u32[]{:S(2)}) copy-start(bf16[1024,576]{1,0:T(8,128)(2,1)} %copy-done.2) | copy-start | bytes 3538948
  48.5 1.2 %copy-start.5 = (bf16[512,1024]{1,0:T(8,128)(2,1)S(1)}, bf16[512,1024]{1,0:T(8,128)(2,1)}, u32[]{:S(2)}) copy-start(bf16[512,1024]{1,0:T(8,128)(2,1)} %copy-done.4) | copy-start | bytes 3145732
  49.7 6.2 %copy-start.7 = (bf16[64,128]{1,0:T(8,128)(2,1)S(1)}, bf16[64,128]{1,0:T(8,128)(2,1)}, u32[]{:S(2)}) copy-start(bf16[64,128]{1,0:T(8,128)(2,1)} %get-tuple-element.55.high_ref) | copy-start | bytes 49156
  49.7 6.2 %copy-start.8 = (bf16[64,128]{1,0:T(8,128)(2,1)S(1)}, bf16[64,128]{1,0:T(8,128)(2,1)}, u32[]{:S(2)}) copy-start(bf16[64,128]{1,0:T(8,128)(2,1)} %get-tuple-element.56.low_ref) | copy-start | bytes 49156

commit v5 on v4

--- a/solution.py
+++ b/solution.py
@@ -317,57 +317,51 @@
     return queries.reshape(2, heads * HALF, width)
 
 
-def first_kernel(
+def attention_kernel(
+    index,
     own_ref,
     ep_ref,
     positions_ref,
-    queries_hbm,
-    w_uv_hbm,
+    queries_ref,
+    w_uv_ref,
     own_keys,
     core_keys,
-    out_ref,
-    keys,
-    later_w_uv,
-    w_uv,
-    queries,
-    *scratch,
+    *refs,
 ):
-    semaphores = scratch[-1]
-    copies = [pltpu.make_async_copy(queries_hbm.at[0], queries, semaphores.at[2])]
-    copies[0].start()
-    for index, target in enumerate((w_uv, later_w_uv)):
-        width = target.shape[1]
-        source = w_uv_hbm.at[:, pl.ds(index * width, width)]
-        copies.append(pltpu.make_async_copy(source, target, semaphores.at[index]))
-        copies[-1].start()
+    done_ref = None
+    if index:
+        done_ref, *refs = refs
+    out_ref, keys, *scratch = refs
+    columns = w_uv_ref.shape[1] // 2
     blocks = own_keys.shape[0]
     my_ctx, my_ep = own_ref[0], ep_ref[0]
     for flip, source in enumerate((own_keys, core_keys)):
-        for index in range(blocks):
+        for block in range(blocks):
             source_ctx = my_ctx
             for bit, step in enumerate(gather_order(blocks)):
-                if index >> bit & 1:
+                if block >> bit & 1:
                     source_ctx = source_ctx ^ step
             start = source_ctx * (2 * HALF) + ((my_ep % 2) ^ flip) * HALF
             place = pl.multiple_of(positions_ref[start], HALF)
-            keys[pl.ds(place, HALF), :] = source[index]
-    copies[0].wait()
+            keys[pl.ds(place, HALF), :] = source[block]
+    skipped = 0
+    if index:
+        skipped = columns
+        out_ref[:, :columns] = done_ref[...]
     attend_heads(
-        own_ref, positions_ref, queries, w_uv, keys, out_ref, 0, copies[1].wait, *scratch[:-1]
-    )
-    copies[2].wait()
-
-
-def second_kernel(own_ref, positions_ref, queries, w_uv, keys, done_ref, out_ref, *scratch):
-    skipped = done_ref.shape[1]
-    out_ref[:, :skipped] = done_ref[...]
-    attend_heads(
-        own_ref, positions_ref, queries.at[1], w_uv, keys, out_ref, skipped, lambda: None, *scratch
+        own_ref,
+        positions_ref,
+        queries_ref.at[index],
+        w_uv_ref.at[:, pl.ds(index * columns, columns)],
+        keys,
+        out_ref,
+        skipped,
+        *scratch,
     )
 
 
 def attend_heads(
-    own_ref, positions_ref, queries, w_uv, keys, out_ref, skipped, wait, scores, tops, mixed
+    own_ref, positions_ref, queries, w_uv, keys, out_ref, skipped, scores, tops, mixed
 ):
     latent_width = w_uv.shape[0]
     count = queries.shape[0] // 2
@@ -436,7 +430,6 @@
         def _():
             mix(slice(count, 2 * count), chunks)
 
-    wait()
     high_rows = pl.ds(pl.multiple_of(high * HALF, HALF), HALF)
     low_rows = pl.ds(pl.multiple_of(low * HALF, HALF), HALF)
     for head in range(heads):
@@ -475,44 +468,22 @@
     )
 
 
-def attend_first(own, ep, positions, queries, w_uv, own_keys, core_keys):
+def attend(index, own, ep, positions, queries, w_uv, own_keys, core_keys, *done):
     latent_width, columns = w_uv.shape
     key_count = positions.shape[0]
     width = own_keys.shape[-1]
     count = queries.shape[1] // 2
-    half = (latent_width, columns // 2)
     return pl.pallas_call(
-        first_kernel,
-        out_shape=[
-            jax.ShapeDtypeStruct((2 * HALF, columns // 2), jnp.bfloat16),
-            jax.ShapeDtypeStruct((key_count, width), jnp.bfloat16),
-            jax.ShapeDtypeStruct(half, jnp.bfloat16),
-        ],
-        in_specs=[SMEM_SPEC] * 3 + [HBM_SPEC] * 2 + [VMEM_SPEC] * 2,
-        out_specs=[VMEM_SPEC] * 3,
-        scratch_shapes=[VMEM(half, jnp.bfloat16), VMEM(queries.shape[1:], jnp.bfloat16)]
-        + attend_scratch(count, key_count, latent_width)
-        + [pltpu.SemaphoreType.DMA((3,))],
+        functools.partial(attention_kernel, index),
+        out_shape=jax.ShapeDtypeStruct((2 * HALF, (1 + index) * columns // 2), jnp.bfloat16),
+        in_specs=[SMEM_SPEC] * 3 + [VMEM_SPEC] * (4 + len(done)),
+        out_specs=VMEM_SPEC,
+        scratch_shapes=[VMEM((key_count, width), jnp.bfloat16)]
+        + attend_scratch(count, key_count, latent_width),
         compiler_params=pltpu.CompilerParams(vmem_limit_bytes=attend_limit(key_count)),
         cost_estimate=attend_cost(count, key_count, width),
-        name="attention_first",
-    )(own, ep, positions, queries, w_uv, own_keys, core_keys)
-
-
-def attend_second(own, positions, queries, w_uv, keys, done):
-    latent_width, columns = w_uv.shape
-    key_count, width = keys.shape
-    count = queries.shape[1] // 2
-    return pl.pallas_call(
-        second_kernel,
-        out_shape=jax.ShapeDtypeStruct((2 * HALF, 2 * columns), jnp.bfloat16),
-        in_specs=[SMEM_SPEC] * 2 + [VMEM_SPEC] * 4,
-        out_specs=VMEM_SPEC,
-        scratch_shapes=attend_scratch(count, key_count, latent_width),
-        compiler_params=pltpu.CompilerParams(vmem_limit_bytes=attend_limit(key_count)),
-        cost_estimate=attend_cost(count, key_count, width),
-        name="attention_second",
-    )(own, positions, queries, w_uv, keys, done)
+        name="attention",
+    )(own, ep, positions, queries, w_uv, own_keys, core_keys, *done)
 
 
 def shards(
@@ -574,13 +545,11 @@
     to_far = add(far_out, from_core_far)
     from_far = over_ep(to_far, 2)
     core_keys = over_ep(own_keys, 1)
-    half, keys, later_w_uv = attend_first(
-        me, ep, positions, queries, w_uv, own_keys, core_keys
-    )
+    half = attend(0, me, ep, positions, queries, w_uv, own_keys, core_keys)
     from_far, half = lax.optimization_barrier((from_far, half))
     returning = add(own_out, from_core, from_far)
     returned = exchange(returning.reshape(arrived.shape))
-    attention = attend_second(me, positions, queries, later_w_uv, keys, half)
+    attention = attend(1, me, ep, positions, queries, w_uv, own_keys, core_keys, half)
     moe_out = combine(high, low, returned.reshape(own.shape))
     return (attention, moe_out)
 

time: 57.5 us -> 58.8 us (1.023)
  waiting for transfers between devices: 6.26 us -> 7.68 us
  Pallas kernels: 25 us -> 24.3 us
    ppermute x7, waiting for transfers between devices: 3.71 us -> 5.57 us  [over_ep(): return lax.ppermute(value, 'ep', [(i, i ^ flip) for i in range(4)])]
    pallas_call x2, Pallas kernels: 10.2 us -> 9.23 us  [attend(): pl.pallas_call(functools.partial(attention_kernel, index), out_shape=jax....]
    pallas_call x1, Pallas kernels: 1.2 us -> 2.12 us  [combine(): pl.pallas_call(combine_kernel, out_shape=jax.ShapeDtypeStruct((row_count,...]
    pallas_call x2, Pallas kernels: 0.83 us -> 0.14 us  [add(): pl.pallas_call(add_kernel, out_shape=jax.ShapeDtypeStruct(parts[0].shape,...]
    unnamed x20 -> x24, local copies, waits for them, and re-layouts: 4.59 us -> 4.82 us
  transfers between devices with their start and end apart: 12 -> 12, of which waited for: 8 -> 9; matrix products, arithmetic and copies ran while one was open for 2% -> 2% of each run, Pallas kernels for 37% -> 34%
where the time goes in v5:
time: 58.8 us; the launch traced here: 58.1 us
  Pallas kernels  24.3 us (41%)
  starting transfers between devices  19.5 us (33%)
  waiting for transfers between devices  7.68 us (13%)
  local copies, waits for them, and re-layouts  4.82 us (8%)
  other arithmetic  1.06 us (2%)
  between operations  0.76 us (1%)
    pallas_call x2, Pallas kernels, attend(): pl.pallas_call(functools.partial(attention_kernel, index), out_shape=jax....  9.23 us
    all_to_all x2, starting transfers between devices, exchange(): return lax.all_to_all(value, 'ctx', split_axis=0, concat_axis=0, tiled=True)  8.75 us
    ppermute x3, starting transfers between devices, over_ctx(): return lax.ppermute(value, 'ctx', [(i, i ^ flip) for i in range(ctx)])  7.71 us
    ppermute x7, waiting for transfers between devices, over_ep(): return lax.ppermute(value, 'ep', [(i, i ^ flip) for i in range(4)])  5.57 us
    unnamed x24, local copies, waits for them, and re-layouts  4.82 us
    pallas_call x1, Pallas kernels, fold(): pl.pallas_call(fold_kernel, out_shape=jax.ShapeDtypeStruct((2, 2, heads /...  4.69 us
    pallas_call x1, Pallas kernels, near_experts(): pl.pallas_call(near_kernel, out_shape=[jax.ShapeDtypeStruct((slots, 2 * u...  4.4 us
    ppermute x7, starting transfers between devices, over_ep(): return lax.ppermute(value, 'ep', [(i, i ^ flip) for i in range(4)])  3 us
  transfers between devices with their start and end apart: 12, of which 9 were waited for; matrix products, arithmetic and copies ran while one was open for 2% of the time, Pallas kernels for 34%

profile of v5, /device:TPU:0, one launch (start us, length us, event | category | flops | bytes accessed | tf_op | source)
XLA Modules:
  0.0 58.1 jit_solution(3837829541092575135)
XLA Ops:
  0.6 2.2 %route.1 = (bf16[8,8,1792]{2,1,0:T(8,128)(2,1)}, bf16[64,128]{1,0:T(8,128)(2,1)}, bf16[64,128]{1,0:T(8,128)(2,1)}, bf16[64,576]{1,0:T(8,128)(2,1)}) custom-call(s32[1]{0:T(128)} %bitcast.1.ep_ref, s32[8,128]{1,0:T(8,128)} %bitcast.20, f32[8,128]{1,0:T(8,128)} %bitcast.21, bf16[64,128]{1,0:T(8,128)(2,1)} %bitcast.19, bf16[128,1792]{1,0:T(8,128)(2,1)} %rows_ref.1, ...), custom_call_target="tpu_custom_call" | custom-call | flops 29360128 | bytes 1048576 | tf_op jit(solution)/shard_map/route/pallas_call | solution.py:87
  2.9 4.0 %collective-permute-start = (bf16[1,64,576]{2,1,0:T(8,128)(2,1)}, bf16[1,64,576]{2,1,0:T(8,128)(2,1)S(1)}, u32[]{:S(2)}, u32[]{:S(2)}) collective-permute-start(bf16[1,64,576]{2,1,0:T(8,128)(2,1)} %bitcast.16), channel_id=1, source_target_pairs={{0,16},{4,20},{8,24},{12,28},{16,0},{20,4},{24,8},{28,12},{1,17},{... | collective-permute-start | bytes 221192 | tf_op jit(solution)/shard_map/ppermute | solution.py:509
  6.9 3.8 %all-to-all-start = ((bf16[8,8,1792]{2,1,0:T(8,128)(2,1)}), bf16[8,8,1792]{2,1,0:T(8,128)(2,1)S(1)}, u32[]{:S(2)}, u32[]{:S(2)}) async-start(bf16[8,8,1792]{2,1,0:T(8,128)(2,1)} %get-tuple-element.28), calls=%async_computation | async-start | bytes 458752 | tf_op jit(solution)/shard_map/all_to_all | solution.py:515
  10.7 0.6 %collective-permute-done = bf16[1,64,576]{2,1,0:T(8,128)(2,1)S(1)} collective-permute-done((bf16[1,64,576]{2,1,0:T(8,128)(2,1)}, bf16[1,64,576]{2,1,0:T(8,128)(2,1)S(1)}, u32[]{:S(2)}, u32[]{:S(2)}) %collective-permute-start) | collective-permute-done | bytes 73760 | tf_op jit(solution)/shard_map/ppermute | solution.py:509
  11.3 0.9 %pad_maximum_fusion.2 = bf16[2,64,576]{2,1,0:T(8,128)(2,1)S(1)} fusion(bf16[1,64,576]{2,1,0:T(8,128)(2,1)S(1)} %collective-permute-done, bf16[1,64,576]{2,1,0:T(8,128)(2,1)} %bitcast.17), kind=kLoop, calls=%fused_computation.2 | loop fusion | flops 73728 | bytes 294912 | tf_op jit(solution)/shard_map/concatenate | solution.py:525
  12.2 1.8 %collective-permute-start.1 = (bf16[2,64,576]{2,1,0:T(8,128)(2,1)S(1)}, bf16[2,64,576]{2,1,0:T(8,128)(2,1)S(1)}, u32[]{:S(2)}, u32[]{:S(2)}) collective-permute-start(bf16[2,64,576]{2,1,0:T(8,128)(2,1)S(1)} %pad_maximum_fusion.2), channel_id=1, source_target_pairs={{0,4},{4,0},{8,12},{12,8},{16,20},{20,16},{24,28},{28,24},{1,5},{5... | collective-permute-start | bytes 442376 | tf_op jit(solution)/shard_map/ppermute | solution.py:509
  14.0 0.0 copy-start.11
  14.0 4.7 %fold.1 = bf16[2,2,512,576]{3,2,1,0:T(8,128)(2,1)} custom-call(s32[1]{0:T(128)} %bitcast.own_ref, s32[1024]{0:T(1024)} %positions_ref.5, bf16[128,2048]{1,0:T(8,128)(2,1)} %q_nope_ref, bf16[128,1024]{1,0:T(8,128)(2,1)} %q_rope_ref.1, bf16[512,2048]{1,0:T(8,128)(2,1)} %w_uk_ref.1), custom_call_target="tpu_custom_call" | custom-call | flops 268435456 | bytes 6291456 | tf_op jit(solution)/shard_map/fold/pallas_call | solution.py:295
  18.7 0.5 collective-permute-done.1
  19.2 0.0 copy-done.11
  19.2 0.1 pad_maximum_fusion.1
  19.3 0.0 copy-start.9
  19.3 0.0 all-to-all-done
  19.3 0.1 collective-permute-start.3
  19.4 1.6 %collective-permute-start.2 = (bf16[64,1792]{1,0:T(8,128)(2,1)S(1)}, bf16[64,1792]{1,0:T(8,128)(2,1)S(1)}, u32[]{:S(2)}, u32[]{:S(2)}) collective-permute-start(bf16[64,1792]{1,0:T(8,128)(2,1)S(1)} %bitcast.14), channel_id=1, source_target_pairs={{0,2},{1,3},{2,0},{3,1},{4,6},{5,7},{6,4},{7,5},{8,10},{9,11},{10,... | collective-permute-start | bytes 688136 | tf_op jit(solution)/shard_map/ppermute | solution.py:512
  21.0 1.9 %collective-permute-start.5 = (bf16[4,64,576]{2,1,0:T(8,128)(2,1)S(1)}, bf16[4,64,576]{2,1,0:T(8,128)(2,1)S(1)}, u32[]{:S(2)}, u32[]{:S(2)}) collective-permute-start(bf16[4,64,576]{2,1,0:T(8,128)(2,1)S(1)} %pad_maximum_fusion.1), channel_id=1, source_target_pairs={{0,8},{4,12},{8,0},{12,4},{16,24},{20,28},{24,16},{28,20},{1,9},{5... | collective-permute-start | bytes 884744 | tf_op jit(solution)/shard_map/ppermute | solution.py:509
  22.9 0.0 collective-permute-done.3.core_ref
  22.9 4.4 %near_experts.1 = (f32[64,512]{1,0:T(8,128)S(1)}, bf16[2,1792,256]{2,1,0:T(8,128)(2,1)S(1)}, bf16[2,1792,256]{2,1,0:T(8,128)(2,1)S(1)}, bf16[4,256,1792]{2,1,0:T(8,128)(2,1)S(1)}) custom-call(s32[1]{0:T(128)} %bitcast.1.ep_ref, bf16[64,1792]{1,0:T(8,128)(2,1)S(1)} %bitcast.15, bf16[64,1792]{1,0:T(8,128)(2,1)S(1)} %collective-permute-done.3.core_ref, ...), custom_call_target="tpu_custom_call" | custom-call | flops 234881024 | bytes 11010048 | tf_op jit(solution)/shard_map/near_experts/pallas_call | solution.py:165
  27.3 0.0 copy-done.9
  27.3 0.1 collective-permute-done.2.far_ref
  27.4 0.0 collective-permute-start.4
  27.4 1.5 %collective-permute-done.4.core_far_ref = bf16[64,1792]{1,0:T(8,128)(2,1)S(1)} collective-permute-done((bf16[64,1792]{1,0:T(8,128)(2,1)S(1)}, bf16[64,1792]{1,0:T(8,128)(2,1)S(1)}, u32[]{:S(2)}, u32[]{:S(2)}) %collective-permute-start.4) | collective-permute-done | bytes 229408 | tf_op jit(solution)/shard_map/ppermute | solution.py:512
  28.9 0.0 copy-start.10
  28.9 0.0 copy-start
  28.9 0.0 copy-start.1
  28.9 0.0 copy-start.6
  28.9 1.5 %far_experts.1 = (bf16[64,1792]{1,0:T(8,128)(2,1)S(1)}, bf16[64,1792]{1,0:T(8,128)(2,1)S(1)}, bf16[64,1792]{1,0:T(8,128)(2,1)S(1)}, bf16[64,1792]{1,0:T(8,128)(2,1)S(1)}) custom-call(bf16[64,1792]{1,0:T(8,128)(2,1)S(1)} %collective-permute-done.2.far_ref, bf16[64,1792]{1,0:T(8,128)(2,1)S(1)} %collective-permute-done.4.core_far_ref, ...), custom_call_target="tpu_custom_call" | custom-call | tf_op jit(solution)/shard_map/far_experts/pallas_call | solution.py:212
  30.4 0.5 collective-permute-done.5
  30.9 0.0 collective-permute-start.6
  30.9 0.0 copy-done.10
  30.9 0.1 pad_maximum_fusion.own_keys
  31.0 1.4 %collective-permute-done.6.refs_1_ = bf16[64,1792]{1,0:T(8,128)(2,1)S(1)} collective-permute-done((bf16[64,1792]{1,0:T(8,128)(2,1)S(1)}, bf16[64,1792]{1,0:T(8,128)(2,1)S(1)}, u32[]{:S(2)}, u32[]{:S(2)}) %collective-permute-start.6) | collective-permute-done | bytes 229408 | tf_op jit(solution)/shard_map/ppermute | solution.py:512
  32.4 0.1 collective-permute-start.7
  32.5 0.1 add.2
  32.6 1.2 %collective-permute-start.8 = (bf16[64,1792]{1,0:T(8,128)(2,1)S(1)}, bf16[64,1792]{1,0:T(8,128)(2,1)S(1)}, u32[]{:S(2)}, u32[]{:S(2)}) collective-permute-start(bf16[64,1792]{1,0:T(8,128)(2,1)S(1)} %add.2), channel_id=1, source_target_pairs={{0,2},{1,3},{2,0},{3,1},{4,6},{5,7},{6,4},{7,5},{8,10},{9,11},{10,... | collective-permute-start | bytes 688136 | tf_op jit(solution)/shard_map/ppermute | solution.py:512
  33.7 0.1 collective-permute-start.9
  33.8 0.7 %collective-permute-done.7.core_keys = bf16[8,64,576]{2,1,0:T(8,128)(2,1)S(1)} collective-permute-done((bf16[8,64,576]{2,1,0:T(8,128)(2,1)S(1)}, bf16[8,64,576]{2,1,0:T(8,128)(2,1)S(1)}, u32[]{:S(2)}, u32[]{:S(2)}) %collective-permute-start.7) | collective-permute-done | bytes 589856 | tf_op jit(solution)/shard_map/ppermute | solution.py:512
  34.5 0.0 copy-done
  34.5 0.0 copy-done.1
  34.5 0.0 copy-done.6
  34.5 0.0 copy-start.3
  34.5 4.1 %attention.2.refs_0_ = bf16[128,1024]{1,0:T(8,128)(2,1)S(1)} custom-call(s32[1]{0:T(128)} %bitcast.own_ref, s32[1]{0:T(128)} %bitcast.1.ep_ref, s32[1024]{0:T(1024)S(1)} %copy-done.6, bf16[2,1024,576]{2,1,0:T(8,128)(2,1)S(1)} %bitcast.10, bf16[512,2048]{1,0:T(8,128)(2,1)S(1)} %copy-done.1, bf16[8,64,576]{2,1,0:T(8,128)(2,1)S(1)} %pad_maximum_fusion.own_keys, ...), custom_call_target="tpu_custom_call" | custom-call | flops 905969664 | bytes 4194304 | tf_op jit(solution)/shard_map/attention/pallas_call | solution.py:476
  38.6 0.0 copy-done.3
  38.7 1.9 %collective-permute-done.8.refs_2_ = bf16[64,1792]{1,0:T(8,128)(2,1)S(1)} collective-permute-done((bf16[64,1792]{1,0:T(8,128)(2,1)S(1)}, bf16[64,1792]{1,0:T(8,128)(2,1)S(1)}, u32[]{:S(2)}, u32[]{:S(2)}) %collective-permute-start.8) | collective-permute-done | bytes 229408 | tf_op jit(solution)/shard_map/ppermute | solution.py:512
  40.5 0.0 collective-permute-done.9.refs_1_
  40.5 0.1 add.3
  40.6 0.0 copy-start.5
  40.6 0.7 %copy-done.5 = bf16[64,1792]{1,0:T(8,128)(2,1)} copy-done((bf16[64,1792]{1,0:T(8,128)(2,1)}, bf16[64,1792]{1,0:T(8,128)(2,1)S(1)}, u32[]{:S(2)}) %copy-start.5) | copy-done | bytes 229400
  41.3 4.9 %all-to-all-start.1 = ((bf16[8,8,1792]{2,1,0:T(8,128)(2,1)}), bf16[8,8,1792]{2,1,0:T(8,128)(2,1)}, u32[]{:S(2)}, u32[]{:S(2)}) async-start(bf16[8,8,1792]{2,1,0:T(8,128)(2,1)} %bitcast.12), calls=%async_computation.1 | async-start | bytes 458752 | tf_op jit(solution)/shard_map/all_to_all | solution.py:515
  46.3 0.0 copy-start.2
  46.3 1.6 %copy-done.2 = bf16[512,2048]{1,0:T(8,128)(2,1)S(1)} copy-done((bf16[512,2048]{1,0:T(8,128)(2,1)S(1)}, bf16[512,2048]{1,0:T(8,128)(2,1)}, u32[]{:S(2)}) %copy-start.2) | copy-done | bytes 2097176
  47.9 0.0 copy-start.4
  47.9 1.1 %copy-done.4 = bf16[8,64,576]{2,1,0:T(8,128)(2,1)S(1)} copy-done((bf16[8,64,576]{2,1,0:T(8,128)(2,1)S(1)}, bf16[8,64,576]{2,1,0:T(8,128)(2,1)}, u32[]{:S(2)}) %copy-start.4) | copy-done | bytes 589848
  48.9 5.1 %attention.3 = bf16[128,2048]{1,0:T(8,128)(2,1)} custom-call(s32[1]{0:T(128)} %bitcast.own_ref, s32[1]{0:T(128)} %bitcast.1.ep_ref, s32[1024]{0:T(1024)S(1)} %copy-done.6, bf16[2,1024,576]{2,1,0:T(8,128)(2,1)S(1)} %bitcast.11, bf16[512,2048]{1,0:T(8,128)(2,1)S(1)} %copy-done.2, bf16[8,64,576]{2,1,0:T(8,128)(2,1)S(1)} %pad_maximum_fusion.own_keys, ...), custom_call_target="tpu_custom_call" | custom-call | flops 905969664 | bytes 4194304 | tf_op jit(solution)/shard_map/attention/pallas_call | solution.py:476
  54.0 0.5 all-to-all-done.1
  54.5 0.0 copy-start.7
  54.5 0.7 %copy-done.7 = bf16[64,128]{1,0:T(8,128)(2,1)S(1)} copy-done((bf16[64,128]{1,0:T(8,128)(2,1)S(1)}, bf16[64,128]{1,0:T(8,128)(2,1)}, u32[]{:S(2)}) %copy-start.7) | copy-done | bytes 16408
  55.2 0.0 copy-start.8
  55.2 0.7 %copy-done.8 = bf16[64,128]{1,0:T(8,128)(2,1)S(1)} copy-done((bf16[64,128]{1,0:T(8,128)(2,1)S(1)}, bf16[64,128]{1,0:T(8,128)(2,1)}, u32[]{:S(2)}) %copy-start.8) | copy-done | bytes 16408
  56.0 2.1 %combine.1 = bf16[128,1792]{1,0:T(8,128)(2,1)} custom-call(bf16[64,128]{1,0:T(8,128)(2,1)S(1)} %copy-done.7, bf16[64,128]{1,0:T(8,128)(2,1)S(1)} %copy-done.8, bf16[64,1792]{1,0:T(8,128)(2,1)} %bitcast.9.returned_ref), custom_call_target="tpu_custom_call" | custom-call | flops 58720256 | bytes 1048576 | tf_op jit(solution)/shard_map/combine/pallas_call | solution.py:254
Async XLA Ops:
  2.9 8.5 %collective-permute-start = (bf16[1,64,576]{2,1,0:T(8,128)(2,1)}, bf16[1,64,576]{2,1,0:T(8,128)(2,1)S(1)}, u32[]{:S(2)}, u32[]{:S(2)}) collective-permute-start(bf16[1,64,576]{2,1,0:T(8,128)(2,1)} %bitcast.16), channel_id=1, source_target_pairs={{0,16},{4,20},{8,24},{12,28},{16,0},{20,4},{24,8},{28,12},{1,17},{... | collective-permute-start | bytes 221192 | tf_op jit(solution)/shard_map/ppermute | solution.py:509
  6.9 12.4 %all-to-all-start = ((bf16[8,8,1792]{2,1,0:T(8,128)(2,1)}), bf16[8,8,1792]{2,1,0:T(8,128)(2,1)S(1)}, u32[]{:S(2)}, u32[]{:S(2)}) async-start(bf16[8,8,1792]{2,1,0:T(8,128)(2,1)} %get-tuple-element.28), calls=%async_computation | async-start | bytes 458752 | tf_op jit(solution)/shard_map/all_to_all | solution.py:515
  12.2 7.0 %collective-permute-start.1 = (bf16[2,64,576]{2,1,0:T(8,128)(2,1)S(1)}, bf16[2,64,576]{2,1,0:T(8,128)(2,1)S(1)}, u32[]{:S(2)}, u32[]{:S(2)}) collective-permute-start(bf16[2,64,576]{2,1,0:T(8,128)(2,1)S(1)} %pad_maximum_fusion.2), channel_id=1, source_target_pairs={{0,4},{4,0},{8,12},{12,8},{16,20},{20,16},{24,28},{28,24},{1,5},{5... | collective-permute-start | bytes 442376 | tf_op jit(solution)/shard_map/ppermute | solution.py:509
  14.0 5.2 %copy-start.11 = (bf16[64,576]{1,0:T(8,128)(2,1)S(1)}, bf16[64,576]{1,0:T(8,128)(2,1)}, u32[]{:S(2)}) copy-start(bf16[64,576]{1,0:T(8,128)(2,1)} %get-tuple-element.30) | copy-start | bytes 221188
  19.3 8.0 %copy-start.9 = (bf16[4,64,576]{2,1,0:T(8,128)(2,1)}, bf16[4,64,576]{2,1,0:T(8,128)(2,1)S(1)}, u32[]{:S(2)}) copy-start(bf16[4,64,576]{2,1,0:T(8,128)(2,1)S(1)} %pad_maximum_fusion.1) | copy-start | bytes 884740
  19.3 3.5 %collective-permute-start.3 = (bf16[64,1792]{1,0:T(8,128)(2,1)S(1)}, bf16[64,1792]{1,0:T(8,128)(2,1)S(1)}, u32[]{:S(2)}, u32[]{:S(2)}) collective-permute-start(bf16[64,1792]{1,0:T(8,128)(2,1)S(1)} %bitcast.13), channel_id=1, source_target_pairs={{0,1},{1,0},{2,3},{3,2},{4,5},{5,4},{6,7},{7,6},{8,9},{9,8},{10,11... | collective-permute-start | bytes 688136 | tf_op jit(solution)/shard_map/ppermute | solution.py:512
  19.4 8.0 %collective-permute-start.2 = (bf16[64,1792]{1,0:T(8,128)(2,1)S(1)}, bf16[64,1792]{1,0:T(8,128)(2,1)S(1)}, u32[]{:S(2)}, u32[]{:S(2)}) collective-permute-start(bf16[64,1792]{1,0:T(8,128)(2,1)S(1)} %bitcast.14), channel_id=1, source_target_pairs={{0,2},{1,3},{2,0},{3,1},{4,6},{5,7},{6,4},{7,5},{8,10},{9,11},{10,... | collective-permute-start | bytes 688136 | tf_op jit(solution)/shard_map/ppermute | solution.py:512
  21.0 9.9 %collective-permute-start.5 = (bf16[4,64,576]{2,1,0:T(8,128)(2,1)S(1)}, bf16[4,64,576]{2,1,0:T(8,128)(2,1)S(1)}, u32[]{:S(2)}, u32[]{:S(2)}) collective-permute-start(bf16[4,64,576]{2,1,0:T(8,128)(2,1)S(1)} %pad_maximum_fusion.1), channel_id=1, source_target_pairs={{0,8},{4,12},{8,0},{12,4},{16,24},{20,28},{24,16},{28,20},{1,9},{5... | collective-permute-start | bytes 884744 | tf_op jit(solution)/shard_map/ppermute | solution.py:509
  27.4 1.5 %collective-permute-start.4 = (bf16[64,1792]{1,0:T(8,128)(2,1)S(1)}, bf16[64,1792]{1,0:T(8,128)(2,1)S(1)}, u32[]{:S(2)}, u32[]{:S(2)}) collective-permute-start(bf16[64,1792]{1,0:T(8,128)(2,1)S(1)} %collective-permute-done.2.far_ref), channel_id=1, source_target_pairs={{0,1},{1,0},{2,3},{3,2},{4,5},{5,4},{6,7},{7,6},{8,9},{9,8},{10,11... | collective-permute-start | bytes 688136 | tf_op jit(solution)/shard_map/ppermute | solution.py:512
  28.9 2.0 %copy-start.10 = (bf16[4,64,576]{2,1,0:T(8,128)(2,1)S(1)}, bf16[4,64,576]{2,1,0:T(8,128)(2,1)}, u32[]{:S(2)}) copy-start(bf16[4,64,576]{2,1,0:T(8,128)(2,1)} %copy-done.9) | copy-start | bytes 884740
  28.9 5.6 %copy-start = (bf16[2,2,512,576]{3,2,1,0:T(8,128)(2,1)S(1)}, bf16[2,2,512,576]{3,2,1,0:T(8,128)(2,1)}, u32[]{:S(2)}) copy-start(bf16[2,2,512,576]{3,2,1,0:T(8,128)(2,1)} %fold.1) | copy-start | bytes 7077892
  28.9 5.6 %copy-start.1 = (bf16[512,2048]{1,0:T(8,128)(2,1)S(1)}, bf16[512,2048]{1,0:T(8,128)(2,1)}, u32[]{:S(2)}) copy-start(bf16[512,2048]{1,0:T(8,128)(2,1)} %w_uv_ref.3) | copy-start | bytes 6291460
  28.9 5.6 %copy-start.6 = (s32[1024]{0:T(1024)S(1)}, s32[1024]{0:T(1024)}, u32[]{:S(2)}) copy-start(s32[1024]{0:T(1024)} %positions_ref.5) | copy-start | bytes 12292
  30.9 1.5 %collective-permute-start.6 = (bf16[64,1792]{1,0:T(8,128)(2,1)S(1)}, bf16[64,1792]{1,0:T(8,128)(2,1)S(1)}, u32[]{:S(2)}, u32[]{:S(2)}) collective-permute-start(bf16[64,1792]{1,0:T(8,128)(2,1)S(1)} %get-tuple-element.44), channel_id=1, source_target_pairs={{0,1},{1,0},{2,3},{3,2},{4,5},{5,4},{6,7},{7,6},{8,9},{9,8},{10,11... | collective-permute-start | bytes 688136 | tf_op jit(solution)/shard_map/ppermute | solution.py:512
  32.4 2.1 %collective-permute-start.7 = (bf16[8,64,576]{2,1,0:T(8,128)(2,1)S(1)}, bf16[8,64,576]{2,1,0:T(8,128)(2,1)S(1)}, u32[]{:S(2)}, u32[]{:S(2)}) collective-permute-start(bf16[8,64,576]{2,1,0:T(8,128)(2,1)S(1)} %pad_maximum_fusion.own_keys), channel_id=1, source_target_pairs={{0,1},{1,0},{2,3},{3,2},{4,5},{5,4},{6,7},{7,6},{8,9},{9,8},{10,11... | collective-permute-start | bytes 1769480 | tf_op jit(solution)/shard_map/ppermute | solution.py:512
  32.6 7.9 %collective-permute-start.8 = (bf16[64,1792]{1,0:T(8,128)(2,1)S(1)}, bf16[64,1792]{1,0:T(8,128)(2,1)S(1)}, u32[]{:S(2)}, u32[]{:S(2)}) collective-permute-start(bf16[64,1792]{1,0:T(8,128)(2,1)S(1)} %add.2), channel_id=1, source_target_pairs={{0,2},{1,3},{2,0},{3,1},{4,6},{5,7},{6,4},{7,5},{8,10},{9,11},{10,... | collective-permute-start | bytes 688136 | tf_op jit(solution)/shard_map/ppermute | solution.py:512
  33.7 6.8 %collective-permute-start.9 = (bf16[64,1792]{1,0:T(8,128)(2,1)S(1)}, bf16[64,1792]{1,0:T(8,128)(2,1)S(1)}, u32[]{:S(2)}, u32[]{:S(2)}) collective-permute-start(bf16[64,1792]{1,0:T(8,128)(2,1)S(1)} %get-tuple-element.52), channel_id=1, source_target_pairs={{0,1},{1,0},{2,3},{3,2},{4,5},{5,4},{6,7},{7,6},{8,9},{9,8},{10,11... | collective-permute-start | bytes 688136 | tf_op jit(solution)/shard_map/ppermute | solution.py:512
  34.5 4.1 %copy-start.3 = (bf16[8,64,576]{2,1,0:T(8,128)(2,1)}, bf16[8,64,576]{2,1,0:T(8,128)(2,1)S(1)}, u32[]{:S(2)}) copy-start(bf16[8,64,576]{2,1,0:T(8,128)(2,1)S(1)} %collective-permute-done.7.core_keys) | copy-start | bytes 1769476
  40.6 0.7 %copy-start.5 = (bf16[64,1792]{1,0:T(8,128)(2,1)}, bf16[64,1792]{1,0:T(8,128)(2,1)S(1)}, u32[]{:S(2)}) copy-start(bf16[64,1792]{1,0:T(8,128)(2,1)S(1)} %add.3) | copy-start | bytes 688132
  41.3 13.2 %all-to-all-start.1 = ((bf16[8,8,1792]{2,1,0:T(8,128)(2,1)}), bf16[8,8,1792]{2,1,0:T(8,128)(2,1)}, u32[]{:S(2)}, u32[]{:S(2)}) async-start(bf16[8,8,1792]{2,1,0:T(8,128)(2,1)} %bitcast.12), calls=%async_computation.1 | async-start | bytes 458752 | tf_op jit(solution)/shard_map/all_to_all | solution.py:515
  46.3 1.6 %copy-start.2 = (bf16[512,2048]{1,0:T(8,128)(2,1)S(1)}, bf16[512,2048]{1,0:T(8,128)(2,1)}, u32[]{:S(2)}) copy-start(bf16[512,2048]{1,0:T(8,128)(2,1)} %w_uv_ref.3) | copy-start | bytes 6291460
  47.9 1.1 %copy-start.4 = (bf16[8,64,576]{2,1,0:T(8,128)(2,1)S(1)}, bf16[8,64,576]{2,1,0:T(8,128)(2,1)}, u32[]{:S(2)}) copy-start(bf16[8,64,576]{2,1,0:T(8,128)(2,1)} %copy-done.3) | copy-start | bytes 1769476
  54.5 0.7 %copy-start.7 = (bf16[64,128]{1,0:T(8,128)(2,1)S(1)}, bf16[64,128]{1,0:T(8,128)(2,1)}, u32[]{:S(2)}) copy-start(bf16[64,128]{1,0:T(8,128)(2,1)} %get-tuple-element.49.high_ref) | copy-start | bytes 49156
  55.2 0.7 %copy-start.8 = (bf16[64,128]{1,0:T(8,128)(2,1)S(1)}, bf16[64,128]{1,0:T(8,128)(2,1)}, u32[]{:S(2)}) copy-start(bf16[64,128]{1,0:T(8,128)(2,1)} %get-tuple-element.50.low_ref) | copy-start | bytes 49156

commit v6 on v5

--- a/solution.py
+++ b/solution.py
@@ -1,4 +1,3 @@
-import functools
 import math
 
 import jax
@@ -73,6 +72,8 @@
     taken = (named > 0.0) & (rank == (slot % CAP).astype(jnp.float32))
     select = jnp.where(taken, 1.0, 0.0).astype(jnp.bfloat16)
     gate = jnp.where(taken, gate, 0.0)
+    blocks = [gate[index * CAP : (index + 1) * CAP] for index in range(slots // CAP)]
+    gate = jnp.concatenate([block for block in blocks for _ in range(2)], axis=0)
     high = gate.astype(jnp.bfloat16)
     high_ref[...] = high
     low_ref[...] = (gate - high.astype(jnp.float32)).astype(jnp.bfloat16)
@@ -88,8 +89,8 @@
         route_kernel,
         out_shape=[
             jax.ShapeDtypeStruct((ctx, CAP, features), jnp.bfloat16),
-            jax.ShapeDtypeStruct((slots, row_count), jnp.bfloat16),
-            jax.ShapeDtypeStruct((slots, row_count), jnp.bfloat16),
+            jax.ShapeDtypeStruct((2 * slots, row_count), jnp.bfloat16),
+            jax.ShapeDtypeStruct((2 * slots, row_count), jnp.bfloat16),
             jax.ShapeDtypeStruct((HALF, latent.shape[1] + ROPE), jnp.bfloat16),
         ],
         in_specs=[SMEM_SPEC] + [VMEM_SPEC] * 5,
@@ -220,23 +221,28 @@
     )(far, core_far, sums, gate, up, down)
 
 
-def add_kernel(*refs):
-    total = refs[0][...].astype(jnp.float32)
-    for ref in refs[1:-1]:
-        total = total + ref[...].astype(jnp.float32)
-    refs[-1][...] = total.astype(jnp.bfloat16)
-
-
-def add(*parts):
+def sum_kernel(ep_ref, own_ref, from_core_ref, far_ref, from_core_far_ref, out_ref):
+    my_x = ep_ref[0] // 2
+    for flip, (mine, other) in enumerate(
+        ((own_ref, from_core_ref), (far_ref, from_core_far_ref))
+    ):
+        total = mine[...].astype(jnp.float32) + other[...].astype(jnp.float32)
+        for index in range(out_ref.shape[0]):
+            block = total[index * CAP : (index + 1) * CAP].astype(jnp.bfloat16)
+            out_ref[index, my_x ^ flip] = block
+
+
+def sum_cores(ep, own, from_core, far, from_core_far, ctx):
+    features = own.shape[1]
     return pl.pallas_call(
-        add_kernel,
-        out_shape=jax.ShapeDtypeStruct(parts[0].shape, jnp.bfloat16),
-        in_specs=[VMEM_SPEC] * len(parts),
+        sum_kernel,
+        out_shape=jax.ShapeDtypeStruct((ctx, 2, CAP, features), jnp.bfloat16),
+        in_specs=[SMEM_SPEC] + [VMEM_SPEC] * 4,
         out_specs=VMEM_SPEC,
-        compiler_params=pltpu.CompilerParams(vmem_limit_bytes=8 * MIB),
+        compiler_params=pltpu.CompilerParams(vmem_limit_bytes=16 * MIB),
         cost_estimate=pl.CostEstimate(flops=0, bytes_accessed=MIB, transcendentals=0),
-        name="add",
-    )(*parts)
+        name="sum_cores",
+    )(ep, own, from_core, far, from_core_far)
 
 
 def combine_kernel(high_ref, low_ref, returned_ref, out_ref):
@@ -318,21 +324,29 @@
 
 
 def attention_kernel(
-    index,
     own_ref,
     ep_ref,
     positions_ref,
-    queries_ref,
-    w_uv_ref,
+    queries_hbm,
+    w_uv_hbm,
     own_keys,
     core_keys,
-    *refs,
+    out_ref,
+    keys,
+    queries,
+    w_uv,
+    scores,
+    tops,
+    mixed,
+    semaphores,
 ):
-    done_ref = None
-    if index:
-        done_ref, *refs = refs
-    out_ref, keys, *scratch = refs
-    columns = w_uv_ref.shape[1] // 2
+    query_copies = [
+        pltpu.make_async_copy(queries_hbm.at[part], queries.at[part], semaphores.at[part])
+        for part in range(2)
+    ]
+    w_uv_copy = pltpu.make_async_copy(w_uv_hbm, w_uv, semaphores.at[2])
+    for copy in (query_copies[0], w_uv_copy, query_copies[1]):
+        copy.start()
     blocks = own_keys.shape[0]
     my_ctx, my_ep = own_ref[0], ep_ref[0]
     for flip, source in enumerate((own_keys, core_keys)):
@@ -344,24 +358,25 @@
             start = source_ctx * (2 * HALF) + ((my_ep % 2) ^ flip) * HALF
             place = pl.multiple_of(positions_ref[start], HALF)
             keys[pl.ds(place, HALF), :] = source[block]
-    skipped = 0
-    if index:
-        skipped = columns
-        out_ref[:, :columns] = done_ref[...]
-    attend_heads(
-        own_ref,
-        positions_ref,
-        queries_ref.at[index],
-        w_uv_ref.at[:, pl.ds(index * columns, columns)],
-        keys,
-        out_ref,
-        skipped,
-        *scratch,
-    )
+    for part in range(2):
+        query_copies[part].wait()
+        attend_heads(
+            own_ref,
+            positions_ref,
+            queries.at[part],
+            w_uv,
+            keys,
+            out_ref,
+            part * (w_uv.shape[1] // 2),
+            scores,
+            tops,
+            mixed,
+            w_uv_copy.wait if not part else lambda: None,
+        )
 
 
 def attend_heads(
-    own_ref, positions_ref, queries, w_uv, keys, out_ref, skipped, scores, tops, mixed
+    own_ref, positions_ref, queries, w_uv, keys, out_ref, skipped, scores, tops, mixed, wait
 ):
     latent_width = w_uv.shape[0]
     count = queries.shape[0] // 2
@@ -430,6 +445,7 @@
         def _():
             mix(slice(count, 2 * count), chunks)
 
+    wait()
     high_rows = pl.ds(pl.multiple_of(high * HALF, HALF), HALF)
     low_rows = pl.ds(pl.multiple_of(low * HALF, HALF), HALF)
     for head in range(heads):
@@ -440,50 +456,37 @@
             ],
             axis=0,
         )
+        columns = slice(skipped + head * VDIM, skipped + (head + 1) * VDIM)
         value = jnp.dot(
-            both, w_uv[:, head * VDIM : (head + 1) * VDIM], preferred_element_type=jnp.float32
+            both, w_uv[:, columns], preferred_element_type=jnp.float32
         ).astype(jnp.bfloat16)
-        columns = slice(skipped + head * VDIM, skipped + (head + 1) * VDIM)
         out_ref[high_rows, columns] = value[:HALF]
         out_ref[low_rows, columns] = value[HALF:]
 
 
-def attend_scratch(count, key_count, latent_width):
-    return [
-        VMEM((key_count // CHUNK, 2 * count, CHUNK), jnp.float32),
-        VMEM((2 * count, 128), jnp.float32),
-        VMEM((2 * count, latent_width), jnp.bfloat16),
-    ]
-
-
-def attend_limit(key_count):
-    return (12 + -(-9 * key_count // 1024)) * MIB
-
-
-def attend_cost(count, key_count, width):
-    return pl.CostEstimate(
-        flops=3 * count * key_count * width,
-        bytes_accessed=4 * MIB,
-        transcendentals=count * key_count,
-    )
-
-
-def attend(index, own, ep, positions, queries, w_uv, own_keys, core_keys, *done):
+def attend(own, ep, positions, queries, w_uv, own_keys, core_keys):
     latent_width, columns = w_uv.shape
     key_count = positions.shape[0]
     width = own_keys.shape[-1]
-    count = queries.shape[1] // 2
+    rows = queries.shape[1]
     return pl.pallas_call(
-        functools.partial(attention_kernel, index),
-        out_shape=jax.ShapeDtypeStruct((2 * HALF, (1 + index) * columns // 2), jnp.bfloat16),
-        in_specs=[SMEM_SPEC] * 3 + [VMEM_SPEC] * (4 + len(done)),
+        attention_kernel,
+        out_shape=jax.ShapeDtypeStruct((2 * HALF, columns), jnp.bfloat16),
+        in_specs=[SMEM_SPEC] * 3 + [HBM_SPEC] * 2 + [VMEM_SPEC] * 2,
         out_specs=VMEM_SPEC,
-        scratch_shapes=[VMEM((key_count, width), jnp.bfloat16)]
-        + attend_scratch(count, key_count, latent_width),
-        compiler_params=pltpu.CompilerParams(vmem_limit_bytes=attend_limit(key_count)),
-        cost_estimate=attend_cost(count, key_count, width),
+        scratch_shapes=[
+            VMEM((key_count, width), jnp.bfloat16),
+            VMEM(queries.shape, jnp.bfloat16),
+            VMEM(w_uv.shape, jnp.bfloat16),
+            VMEM((key_count // CHUNK, rows, CHUNK), jnp.float32),
+            VMEM((rows, 128), jnp.float32),
+            VMEM((rows, latent_width), jnp.bfloat16),
+            pltpu.SemaphoreType.DMA((3,)),
+        ],
+        compiler_params=pltpu.CompilerParams(vmem_limit_bytes=61 * MIB),
+        cost_estimate=pl.CostEstimate(flops=0, bytes_accessed=0, transcendentals=0),
         name="attention",
-    )(own, ep, positions, queries, w_uv, own_keys, core_keys, *done)
+    )(own, ep, positions, queries, w_uv, own_keys, core_keys)
 
 
 def shards(
@@ -503,76 +506,78 @@
 ):
     ctx = lax.axis_size("ctx")
     me = lax.axis_index("ctx").astype(jnp.int32).reshape(1)
-    ep = lax.axis_index("ep").astype(jnp.int32).reshape(1)
+    ep = lax.axis_index(("x", "core")).astype(jnp.int32).reshape(1)
 
     def over_ctx(value, flip):
         return lax.ppermute(value, "ctx", [(i, i ^ flip) for i in range(ctx)])
 
-    def over_ep(value, flip):
-        return lax.ppermute(value, "ep", [(i, i ^ flip) for i in range(4)])
-
-    def exchange(value):
-        return lax.all_to_all(value, "ctx", split_axis=0, concat_axis=0, tiled=True)
+    def over(value, axis):
+        return lax.ppermute(value, axis, [(0, 1), (1, 0)])
 
     outgoing, high, low, packed = route(
         ep, expert_ids, expert_weights, k_rope, moe_rows, latent, ctx
     )
-    arrived = exchange(outgoing)
+    arrived = lax.all_to_all(outgoing, "ctx", split_axis=0, concat_axis=0, tiled=True)
+    high, q_nope = lax.optimization_barrier((high, q_nope))
+    queries = fold(me, positions, q_nope, q_rope, w_uk)
     flips = gather_order(ctx)
-    received = over_ctx(packed[None], flips[0])
-    high, q_nope, received = lax.optimization_barrier((high, q_nope, received))
-    queries = fold(me, positions, q_nope, q_rope, w_uk)
-    own_keys = jnp.concatenate([packed[None], received], axis=0)
-    for flip in flips[1:-1]:
+    own_keys = packed[None]
+    for flip in flips[:-2]:
         own_keys = jnp.concatenate([own_keys, over_ctx(own_keys, flip)], axis=0)
-    arrived, queries, own_keys = lax.optimization_barrier((arrived, queries, own_keys))
+    arrived, queries = lax.optimization_barrier((arrived, queries))
 
     own = arrived.reshape(ctx * CAP, arrived.shape[2])
-    far = over_ep(own, 2)
-    core = over_ep(own, 1)
+    far = over(own, "x")
+    core = over(own, "core")
+    received = over_ctx(own_keys, flips[-2])
+    sums, far_gate, far_up, down = near_experts(ep, own, core, w_gate, w_up, w_down)
+    far, sums, received = lax.optimization_barrier((far, sums, received))
+    core_far = over(far, "core")
+    own_keys = jnp.concatenate([own_keys, received], axis=0)
     received = over_ctx(own_keys, flips[-1])
-    sums, far_gate, far_up, down = near_experts(ep, own, core, w_gate, w_up, w_down)
-    far, sums = lax.optimization_barrier((far, sums))
-    core_far = over_ep(far, 1)
     own_out, core_out, far_out, core_far_out = far_experts(
         far, core_far, sums, far_gate, far_up, down
     )
-    core_far_out, received = lax.optimization_barrier((core_far_out, received))
-    from_core_far = over_ep(core_far_out, 1)
-    from_core = over_ep(core_out, 1)
+    from_core_far = over(core_far_out, "core")
+    from_core = over(core_out, "core")
+    returning = sum_cores(ep, own_out, from_core, far_out, from_core_far, ctx)
+    returning, received = lax.optimization_barrier((returning, received))
+    returned = lax.all_to_all(
+        returning.reshape(2 * ctx, CAP, returning.shape[3]),
+        ("ctx", "x"),
+        split_axis=0,
+        concat_axis=0,
+        tiled=True,
+    )
     own_keys = jnp.concatenate([own_keys, received], axis=0)
-    own_keys, from_core_far = lax.optimization_barrier((own_keys, from_core_far))
-    to_far = add(far_out, from_core_far)
-    from_far = over_ep(to_far, 2)
-    core_keys = over_ep(own_keys, 1)
-    half = attend(0, me, ep, positions, queries, w_uv, own_keys, core_keys)
-    from_far, half = lax.optimization_barrier((from_far, half))
-    returning = add(own_out, from_core, from_far)
-    returned = exchange(returning.reshape(arrived.shape))
-    attention = attend(1, me, ep, positions, queries, w_uv, own_keys, core_keys, half)
-    moe_out = combine(high, low, returned.reshape(own.shape))
+    core_keys = over(own_keys, "core")
+    attention = attend(me, ep, positions, queries, w_uv, own_keys, core_keys)
+    moe_out = combine(high, low, returned.reshape(2 * ctx * CAP, returned.shape[2]))
     return (attention, moe_out)
 
 
 def solution(mesh):
+    split = (mesh.shape["ctx"], mesh.shape["ep"] // 2, 2)
+    mesh = jax.sharding.Mesh(mesh.devices.reshape(split), ("ctx", "x", "core"))
+    ep = ("x", "core")
     return jax.shard_map(
         shards,
         mesh=mesh,
         in_specs=(
-            P("ctx", "ep"),
-            P("ctx", "ep"),
+            P("ctx", ep),
+            P("ctx", ep),
             P("ctx", None),
             P("ctx", None),
-            P(None, "ep"),
-            P(None, "ep"),
+            P(None, ep),
+            P(None, ep),
             P(),
-            P("ctx", "ep"),
+            P("ctx", ep),
             P("ctx", None),
             P("ctx", None),
-            P("ctx", None, "ep"),
-            P("ctx", None, "ep"),
-            P("ctx", "ep", None),
+            P("ctx", None, ep),
+            P("ctx", None, ep),
+            P("ctx", ep, None),
         ),
-        out_specs=(P("ctx", "ep"), P("ctx", "ep")),
+        out_specs=(P("ctx", ep), P("ctx", ep)),
         check_vma=False,
     )

time: 58.8 us -> 59.2 us (level)
  waiting for transfers between devices: 7.68 us -> 12.1 us
  local copies, waits for them, and re-layouts: 4.82 us -> 0.85 us
  Pallas kernels: 24.3 us -> 25.8 us
  other arithmetic: 1.06 us -> 0.2 us
    unnamed x24 -> x10, local copies, waits for them, and re-layouts: 4.82 us -> 0.85 us
    ppermute x3, waiting for transfers between devices: 1.64 us -> 5.03 us  [over_ctx(): return lax.ppermute(value, 'ctx', [(i, i ^ flip) for i in range(ctx)])]
    all_to_all x2, starting transfers between devices: 8.75 us -> 11.6 us  [the longest x1 7.28 us: shards(): lax.all_to_all(outgoing, 'ctx', split_axis=0, concat_axis=0, tiled=True)]
    all_to_all x2, waiting for transfers between devices: 0.48 us -> 3.27 us  [the longest x1 3.27 us: shards(): lax.all_to_all(outgoing, 'ctx', split_axis=0, concat_axis=0, tiled=True)]
    pallas_call x4 -> x2, Pallas kernels: 9.37 us -> 11.8 us  [the longest x1 10.9 us: attend(): pl.pallas_call(attention_kernel, out_shape=jax.ShapeDtypeStruct((2 * HALF...]
    ppermute x3, starting transfers between devices: 7.71 us -> 5.55 us  [over_ctx(): return lax.ppermute(value, 'ctx', [(i, i ^ flip) for i in range(ctx)])]
    ppermute x7 -> x6, waiting for transfers between devices: 5.57 us -> 3.76 us  [over(): return lax.ppermute(value, axis, [(0, 1), (1, 0)])]
    pallas_call x1, Pallas kernels: 2.12 us -> 1.19 us  [combine(): pl.pallas_call(combine_kernel, out_shape=jax.ShapeDtypeStruct((row_count,...]
  transfers between devices with their start and end apart: 12 -> 11, of which waited for: 9 -> 8; matrix products, arithmetic and copies ran while one was open for 2% -> 0% of each run, Pallas kernels for 34% -> 38%
where the time goes in v6:
time: 59.2 us; the launch traced here: 58.9 us
  Pallas kernels  25.8 us (44%)
  starting transfers between devices  19.3 us (33%)
  waiting for transfers between devices  12.1 us (20%)
  local copies, waits for them, and re-layouts  0.85 us (1%)
  between operations  0.76 us (1%)
    pallas_call x1, Pallas kernels, attend(): pl.pallas_call(attention_kernel, out_shape=jax.ShapeDtypeStruct((2 * HALF...  10.9 us
    all_to_all x1, starting transfers between devices, shards(): lax.all_to_all(outgoing, 'ctx', split_axis=0, concat_axis=0, tiled=True)  7.28 us
    ppermute x3, starting transfers between devices, over_ctx(): return lax.ppermute(value, 'ctx', [(i, i ^ flip) for i in range(ctx)])  5.55 us
    ppermute x3, waiting for transfers between devices, over_ctx(): return lax.ppermute(value, 'ctx', [(i, i ^ flip) for i in range(ctx)])  5.03 us
    pallas_call x1, Pallas kernels, fold(): pl.pallas_call(fold_kernel, out_shape=jax.ShapeDtypeStruct((2, 2, heads /...  4.66 us
    pallas_call x1, Pallas kernels, near_experts(): pl.pallas_call(near_kernel, out_shape=[jax.ShapeDtypeStruct((slots, 2 * u...  4.4 us
    all_to_all x1, starting transfers between devices, shards(): lax.all_to_all(returning.reshape(2 * ctx, CAP, returning.shape[3]), ('ctx...  4.29 us
    ppermute x6, waiting for transfers between devices, over(): return lax.ppermute(value, axis, [(0, 1), (1, 0)])  3.76 us
  transfers between devices with their start and end apart: 11, of which 8 were waited for; matrix products, arithmetic and copies ran while one was open for 0% of the time, Pallas kernels for 38%

profile of v6, /device:TPU:0, one launch (start us, length us, event | category | flops | bytes accessed | tf_op | source)
XLA Modules:
  0.0 58.9 jit_solution(15646382672401847721)
XLA Ops:
  0.6 2.2 %route.1 = (bf16[8,8,1792]{2,1,0:T(8,128)(2,1)}, bf16[128,128]{1,0:T(8,128)(2,1)}, bf16[128,128]{1,0:T(8,128)(2,1)}, bf16[64,576]{1,0:T(8,128)(2,1)}) custom-call(s32[1]{0:T(128)} %bitcast.1.ep_ref, s32[8,128]{1,0:T(8,128)} %bitcast.20, f32[8,128]{1,0:T(8,128)} %bitcast.21, bf16[64,128]{1,0:T(8,128)(2,1)} %bitcast.19, bf16[128,1792]{1,0:T(8,128)(2,1)} %rows_ref.1, ...), custom_call_target="tpu_custom_call" | custom-call | flops 29360128 | bytes 1048576 | tf_op jit(solution)/shard_map/route/pallas_call | solution.py:88
  2.9 7.3 %all-to-all-start = ((bf16[8,8,1792]{2,1,0:T(8,128)(2,1)}), bf16[8,8,1792]{2,1,0:T(8,128)(2,1)S(1)}, u32[]{:S(2)}, u32[]{:S(2)}) async-start(bf16[8,8,1792]{2,1,0:T(8,128)(2,1)} %get-tuple-element.23), calls=%async_computation | async-start | bytes 458752 | tf_op jit(solution)/shard_map/all_to_all | solution.py:520
  10.1 2.9 %collective-permute-start = (bf16[1,64,576]{2,1,0:T(8,128)(2,1)}, bf16[1,64,576]{2,1,0:T(8,128)(2,1)S(1)}, u32[]{:S(2)}, u32[]{:S(2)}) collective-permute-start(bf16[1,64,576]{2,1,0:T(8,128)(2,1)} %bitcast.15), channel_id=1, source_target_pairs={{0,16},{4,20},{8,24},{12,28},{16,0},{20,4},{24,8},{28,12},{1,17},{... | collective-permute-start | bytes 221192 | tf_op jit(solution)/shard_map/ppermute | solution.py:512
  13.1 0.0 copy-start.3
  13.1 4.7 %fold.1 = bf16[2,2,512,576]{3,2,1,0:T(8,128)(2,1)} custom-call(s32[1]{0:T(128)} %bitcast.own_ref, s32[1024]{0:T(1024)} %positions_ref.3, bf16[128,2048]{1,0:T(8,128)(2,1)} %q_nope_ref, bf16[128,1024]{1,0:T(8,128)(2,1)} %q_rope_ref.1, bf16[512,2048]{1,0:T(8,128)(2,1)} %w_uk_ref.1), custom_call_target="tpu_custom_call" | custom-call | flops 268435456 | bytes 6291456 | tf_op jit(solution)/shard_map/fold/pallas_call | solution.py:301
  17.7 3.3 %all-to-all-done = bf16[8,8,1792]{2,1,0:T(8,128)(2,1)S(1)} async-done(((bf16[8,8,1792]{2,1,0:T(8,128)(2,1)}), bf16[8,8,1792]{2,1,0:T(8,128)(2,1)S(1)}, u32[]{:S(2)}, u32[]{:S(2)}) %all-to-all-start) | async-done | bytes 229408 | tf_op jit(solution)/shard_map/all_to_all | solution.py:520
  21.0 0.0 collective-permute-start.2
  21.0 1.5 %collective-permute-start.1 = (bf16[64,1792]{1,0:T(8,128)(2,1)S(1)}, bf16[64,1792]{1,0:T(8,128)(2,1)S(1)}, u32[]{:S(2)}, u32[]{:S(2)}) collective-permute-start(bf16[64,1792]{1,0:T(8,128)(2,1)S(1)} %bitcast.12), channel_id=1, source_target_pairs={{0,2},{2,0},{1,3},{3,1},{4,6},{6,4},{5,7},{7,5},{8,10},{10,8},{9,1... | collective-permute-start | bytes 688136 | tf_op jit(solution)/shard_map/ppermute | solution.py:515
  22.5 0.0 collective-permute-done
  22.5 0.0 copy-done.3
  22.5 1.5 %collective-permute-start.3 = (bf16[2,64,576]{2,1,0:T(8,128)(2,1)S(1)}, bf16[2,64,576]{2,1,0:T(8,128)(2,1)S(1)}, u32[]{:S(2)}, u32[]{:S(2)}) collective-permute-start(bf16[2,64,576]{2,1,0:T(8,128)(2,1)S(1)} %pad_maximum_fusion.2), channel_id=1, source_target_pairs={{0,4},{4,0},{8,12},{12,8},{16,20},{20,16},{24,28},{28,24},{1,5},{5... | collective-permute-start | bytes 442376 | tf_op jit(solution)/shard_map/ppermute | solution.py:512
  24.0 0.0 collective-permute-done.2.core_ref
  24.0 4.4 %near_experts.1 = (f32[64,512]{1,0:T(8,128)S(1)}, bf16[2,1792,256]{2,1,0:T(8,128)(2,1)S(1)}, bf16[2,1792,256]{2,1,0:T(8,128)(2,1)S(1)}, bf16[4,256,1792]{2,1,0:T(8,128)(2,1)S(1)}) custom-call(s32[1]{0:T(128)} %bitcast.1.ep_ref, bf16[64,1792]{1,0:T(8,128)(2,1)S(1)} %bitcast.13, bf16[64,1792]{1,0:T(8,128)(2,1)S(1)} %collective-permute-done.2.core_ref, ...), custom_call_target="tpu_custom_call" | custom-call | flops 234881024 | bytes 11010048 | tf_op jit(solution)/shard_map/near_experts/pallas_call | solution.py:166
  28.4 0.5 collective-permute-done.3
  28.9 0.1 collective-permute-done.1.far_ref
  29.0 0.0 collective-permute-start.4
  29.0 0.1 pad_maximum_fusion.1
  29.1 1.1 %collective-permute-start.7 = (bf16[4,64,576]{2,1,0:T(8,128)(2,1)S(1)}, bf16[4,64,576]{2,1,0:T(8,128)(2,1)S(1)}, u32[]{:S(2)}, u32[]{:S(2)}) collective-permute-start(bf16[4,64,576]{2,1,0:T(8,128)(2,1)S(1)} %pad_maximum_fusion.1), channel_id=1, source_target_pairs={{0,8},{4,12},{8,0},{12,4},{16,24},{20,28},{24,16},{28,20},{1,9},{5... | collective-permute-start | bytes 884744 | tf_op jit(solution)/shard_map/ppermute | solution.py:512
  30.2 0.3 collective-permute-done.4.core_far_ref
  30.5 1.5 %far_experts.1 = (bf16[64,1792]{1,0:T(8,128)(2,1)S(1)}, bf16[64,1792]{1,0:T(8,128)(2,1)S(1)}, bf16[64,1792]{1,0:T(8,128)(2,1)S(1)}, bf16[64,1792]{1,0:T(8,128)(2,1)S(1)}) custom-call(bf16[64,1792]{1,0:T(8,128)(2,1)S(1)} %collective-permute-done.1.far_ref, bf16[64,1792]{1,0:T(8,128)(2,1)S(1)} %collective-permute-done.4.core_far_ref, ...), custom_call_target="tpu_custom_call" | custom-call | tf_op jit(solution)/shard_map/far_experts/pallas_call | solution.py:213
  32.0 0.2 collective-permute-start.5
  32.2 0.4 collective-permute-start.6
  32.6 1.0 %collective-permute-done.5.from_core_ref = bf16[64,1792]{1,0:T(8,128)(2,1)S(1)} collective-permute-done((bf16[64,1792]{1,0:T(8,128)(2,1)S(1)}, bf16[64,1792]{1,0:T(8,128)(2,1)S(1)}, u32[]{:S(2)}, u32[]{:S(2)}) %collective-permute-start.5) | collective-permute-done | bytes 229408 | tf_op jit(solution)/shard_map/ppermute | solution.py:515
  33.6 0.3 collective-permute-done.6.from_core_far_ref
  33.9 0.9 %sum_cores.1 = bf16[8,2,8,1792]{3,2,1,0:T(8,128)(2,1)} custom-call(s32[1]{0:T(128)} %bitcast.1.ep_ref, bf16[64,1792]{1,0:T(8,128)(2,1)S(1)} %get-tuple-element.36.own_ref, bf16[64,1792]{1,0:T(8,128)(2,1)S(1)} %collective-permute-done.5.from_core_ref, bf16[64,1792]{1,0:T(8,128)(2,1)S(1)} %get-tuple-element.38.far_ref, ...), custom_call_target="tpu_custom_call" | custom-call | bytes 1048576 | tf_op jit(solution)/shard_map/sum_cores/pallas_call | solution.py:237
  34.8 4.5 %collective-permute-done.7 = bf16[4,64,576]{2,1,0:T(8,128)(2,1)S(1)} collective-permute-done((bf16[4,64,576]{2,1,0:T(8,128)(2,1)S(1)}, bf16[4,64,576]{2,1,0:T(8,128)(2,1)S(1)}, u32[]{:S(2)}, u32[]{:S(2)}) %collective-permute-start.7) | collective-permute-done | bytes 294944 | tf_op jit(solution)/shard_map/ppermute | solution.py:512
  39.3 4.3 %all-to-all-start.1 = ((bf16[16,8,1792]{2,1,0:T(8,128)(2,1)}), bf16[16,8,1792]{2,1,0:T(8,128)(2,1)S(1)}, u32[]{:S(2)}, u32[]{:S(2)}) async-start(bf16[16,8,1792]{2,1,0:T(8,128)(2,1)} %bitcast.8), calls=%async_computation.1 | async-start | bytes 917504 | tf_op jit(solution)/shard_map/all_to_all | solution.py:545
  43.6 0.1 pad_maximum_fusion.own_keys
  43.7 0.0 copy-start.2
  43.7 0.0 copy-start
  43.7 0.0 copy-start.1
  43.7 0.1 collective-permute-start.8
  43.8 2.1 %collective-permute-done.8.core_keys = bf16[8,64,576]{2,1,0:T(8,128)(2,1)S(1)} collective-permute-done((bf16[8,64,576]{2,1,0:T(8,128)(2,1)S(1)}, bf16[8,64,576]{2,1,0:T(8,128)(2,1)S(1)}, u32[]{:S(2)}, u32[]{:S(2)}) %collective-permute-start.8) | collective-permute-done | bytes 589856 | tf_op jit(solution)/shard_map/ppermute | solution.py:515
  45.9 0.0 copy-done.2
  45.9 0.0 copy-start.4
  45.9 0.8 %copy-done.4 = bf16[8,64,576]{2,1,0:T(8,128)(2,1)} copy-done((bf16[8,64,576]{2,1,0:T(8,128)(2,1)}, bf16[8,64,576]{2,1,0:T(8,128)(2,1)S(1)}, u32[]{:S(2)}) %copy-start.4) | copy-done | bytes 589848
  46.7 10.9 %attention.1 = bf16[128,2048]{1,0:T(8,128)(2,1)} custom-call(s32[1]{0:T(128)} %bitcast.own_ref, s32[1]{0:T(128)} %bitcast.1.ep_ref, s32[1024]{0:T(1024)} %positions_ref.3, bf16[2,1024,576]{2,1,0:T(8,128)(2,1)} %bitcast.14, bf16[512,2048]{1,0:T(8,128)(2,1)} %w_uv_hbm.1, bf16[8,64,576]{2,1,0:T(8,128)(2,1)} %copy-done.2, bf16[8,64,576]{2,1,0:T(8,128)(2,1)} %copy-done.4), custom_call_target="tpu_custom_call" | custom-call | tf_op jit(solution)/shard_map/attention/pallas_call | solution.py:472
  57.7 0.0 all-to-all-done.1
  57.7 0.0 copy-done
  57.7 0.0 copy-done.1
  57.7 1.2 %combine.1 = bf16[128,1792]{1,0:T(8,128)(2,1)} custom-call(bf16[128,128]{1,0:T(8,128)(2,1)S(1)} %copy-done, bf16[128,128]{1,0:T(8,128)(2,1)S(1)} %copy-done.1, bf16[128,1792]{1,0:T(8,128)(2,1)S(1)} %bitcast.10), custom_call_target="tpu_custom_call" | custom-call | flops 117440512 | bytes 1048576 | tf_op jit(solution)/shard_map/combine/pallas_call | solution.py:260
  (1 shorter events, 0.0 us)
Async XLA Ops:
  2.9 18.1 %all-to-all-start = ((bf16[8,8,1792]{2,1,0:T(8,128)(2,1)}), bf16[8,8,1792]{2,1,0:T(8,128)(2,1)S(1)}, u32[]{:S(2)}, u32[]{:S(2)}) async-start(bf16[8,8,1792]{2,1,0:T(8,128)(2,1)} %get-tuple-element.23), calls=%async_computation | async-start | bytes 458752 | tf_op jit(solution)/shard_map/all_to_all | solution.py:520
  10.1 12.4 %collective-permute-start = (bf16[1,64,576]{2,1,0:T(8,128)(2,1)}, bf16[1,64,576]{2,1,0:T(8,128)(2,1)S(1)}, u32[]{:S(2)}, u32[]{:S(2)}) collective-permute-start(bf16[1,64,576]{2,1,0:T(8,128)(2,1)} %bitcast.15), channel_id=1, source_target_pairs={{0,16},{4,20},{8,24},{12,28},{16,0},{20,4},{24,8},{28,12},{1,17},{... | collective-permute-start | bytes 221192 | tf_op jit(solution)/shard_map/ppermute | solution.py:512
  13.1 9.4 %copy-start.3 = (bf16[64,576]{1,0:T(8,128)(2,1)S(1)}, bf16[64,576]{1,0:T(8,128)(2,1)}, u32[]{:S(2)}) copy-start(bf16[64,576]{1,0:T(8,128)(2,1)} %get-tuple-element.27) | copy-start | bytes 221188
  21.0 3.0 %collective-permute-start.2 = (bf16[64,1792]{1,0:T(8,128)(2,1)S(1)}, bf16[64,1792]{1,0:T(8,128)(2,1)S(1)}, u32[]{:S(2)}, u32[]{:S(2)}) collective-permute-start(bf16[64,1792]{1,0:T(8,128)(2,1)S(1)} %bitcast.11), channel_id=1, source_target_pairs={{0,1},{1,0},{2,3},{3,2},{4,5},{5,4},{6,7},{7,6},{8,9},{9,8},{10,11... | collective-permute-start | bytes 688136 | tf_op jit(solution)/shard_map/ppermute | solution.py:515
  21.0 8.0 %collective-permute-start.1 = (bf16[64,1792]{1,0:T(8,128)(2,1)S(1)}, bf16[64,1792]{1,0:T(8,128)(2,1)S(1)}, u32[]{:S(2)}, u32[]{:S(2)}) collective-permute-start(bf16[64,1792]{1,0:T(8,128)(2,1)S(1)} %bitcast.12), channel_id=1, source_target_pairs={{0,2},{2,0},{1,3},{3,1},{4,6},{6,4},{5,7},{7,5},{8,10},{10,8},{9,1... | collective-permute-start | bytes 688136 | tf_op jit(solution)/shard_map/ppermute | solution.py:515
  22.5 6.4 %collective-permute-start.3 = (bf16[2,64,576]{2,1,0:T(8,128)(2,1)S(1)}, bf16[2,64,576]{2,1,0:T(8,128)(2,1)S(1)}, u32[]{:S(2)}, u32[]{:S(2)}) collective-permute-start(bf16[2,64,576]{2,1,0:T(8,128)(2,1)S(1)} %pad_maximum_fusion.2), channel_id=1, source_target_pairs={{0,4},{4,0},{8,12},{12,8},{16,20},{20,16},{24,28},{28,24},{1,5},{5... | collective-permute-start | bytes 442376 | tf_op jit(solution)/shard_map/ppermute | solution.py:512
  29.0 1.5 %collective-permute-start.4 = (bf16[64,1792]{1,0:T(8,128)(2,1)S(1)}, bf16[64,1792]{1,0:T(8,128)(2,1)S(1)}, u32[]{:S(2)}, u32[]{:S(2)}) collective-permute-start(bf16[64,1792]{1,0:T(8,128)(2,1)S(1)} %collective-permute-done.1.far_ref), channel_id=1, source_target_pairs={{0,1},{1,0},{2,3},{3,2},{4,5},{5,4},{6,7},{7,6},{8,9},{9,8},{10,11... | collective-permute-start | bytes 688136 | tf_op jit(solution)/shard_map/ppermute | solution.py:515
  29.1 10.2 %collective-permute-start.7 = (bf16[4,64,576]{2,1,0:T(8,128)(2,1)S(1)}, bf16[4,64,576]{2,1,0:T(8,128)(2,1)S(1)}, u32[]{:S(2)}, u32[]{:S(2)}) collective-permute-start(bf16[4,64,576]{2,1,0:T(8,128)(2,1)S(1)} %pad_maximum_fusion.1), channel_id=1, source_target_pairs={{0,8},{4,12},{8,0},{12,4},{16,24},{20,28},{24,16},{28,20},{1,9},{5... | collective-permute-start | bytes 884744 | tf_op jit(solution)/shard_map/ppermute | solution.py:512
  32.0 1.6 %collective-permute-start.5 = (bf16[64,1792]{1,0:T(8,128)(2,1)S(1)}, bf16[64,1792]{1,0:T(8,128)(2,1)S(1)}, u32[]{:S(2)}, u32[]{:S(2)}) collective-permute-start(bf16[64,1792]{1,0:T(8,128)(2,1)S(1)} %get-tuple-element.37), channel_id=1, source_target_pairs={{0,1},{1,0},{2,3},{3,2},{4,5},{5,4},{6,7},{7,6},{8,9},{9,8},{10,11... | collective-permute-start | bytes 688136 | tf_op jit(solution)/shard_map/ppermute | solution.py:515
  32.2 1.7 %collective-permute-start.6 = (bf16[64,1792]{1,0:T(8,128)(2,1)S(1)}, bf16[64,1792]{1,0:T(8,128)(2,1)S(1)}, u32[]{:S(2)}, u32[]{:S(2)}) collective-permute-start(bf16[64,1792]{1,0:T(8,128)(2,1)S(1)} %get-tuple-element.39), channel_id=1, source_target_pairs={{0,1},{1,0},{2,3},{3,2},{4,5},{5,4},{6,7},{7,6},{8,9},{9,8},{10,11... | collective-permute-start | bytes 688136 | tf_op jit(solution)/shard_map/ppermute | solution.py:515
  39.3 18.4 %all-to-all-start.1 = ((bf16[16,8,1792]{2,1,0:T(8,128)(2,1)}), bf16[16,8,1792]{2,1,0:T(8,128)(2,1)S(1)}, u32[]{:S(2)}, u32[]{:S(2)}) async-start(bf16[16,8,1792]{2,1,0:T(8,128)(2,1)} %bitcast.8), calls=%async_computation.1 | async-start | bytes 917504 | tf_op jit(solution)/shard_map/all_to_all | solution.py:545
  43.7 2.2 %copy-start.2 = (bf16[8,64,576]{2,1,0:T(8,128)(2,1)}, bf16[8,64,576]{2,1,0:T(8,128)(2,1)S(1)}, u32[]{:S(2)}) copy-start(bf16[8,64,576]{2,1,0:T(8,128)(2,1)S(1)} %pad_maximum_fusion.own_keys) | copy-start | bytes 1769476
  43.7 14.0 %copy-start = (bf16[128,128]{1,0:T(8,128)(2,1)S(1)}, bf16[128,128]{1,0:T(8,128)(2,1)}, u32[]{:S(2)}) copy-start(bf16[128,128]{1,0:T(8,128)(2,1)} %get-tuple-element.41.high_ref) | copy-start | bytes 98308
  43.7 14.0 %copy-start.1 = (bf16[128,128]{1,0:T(8,128)(2,1)S(1)}, bf16[128,128]{1,0:T(8,128)(2,1)}, u32[]{:S(2)}) copy-start(bf16[128,128]{1,0:T(8,128)(2,1)} %get-tuple-element.42.low_ref) | copy-start | bytes 98308
  43.7 2.2 %collective-permute-start.8 = (bf16[8,64,576]{2,1,0:T(8,128)(2,1)S(1)}, bf16[8,64,576]{2,1,0:T(8,128)(2,1)S(1)}, u32[]{:S(2)}, u32[]{:S(2)}) collective-permute-start(bf16[8,64,576]{2,1,0:T(8,128)(2,1)S(1)} %pad_maximum_fusion.own_keys), channel_id=1, source_target_pairs={{0,1},{1,0},{2,3},{3,2},{4,5},{5,4},{6,7},{7,6},{8,9},{9,8},{10,11... | collective-permute-start | bytes 1769480 | tf_op jit(solution)/shard_map/ppermute | solution.py:515
  45.9 0.8 %copy-start.4 = (bf16[8,64,576]{2,1,0:T(8,128)(2,1)}, bf16[8,64,576]{2,1,0:T(8,128)(2,1)S(1)}, u32[]{:S(2)}) copy-start(bf16[8,64,576]{2,1,0:T(8,128)(2,1)S(1)} %collective-permute-done.8.core_keys) | copy-start | bytes 1769476

commit v7 on v6

--- a/solution.py
+++ b/solution.py
@@ -483,7 +483,7 @@
             VMEM((rows, latent_width), jnp.bfloat16),
             pltpu.SemaphoreType.DMA((3,)),
         ],
-        compiler_params=pltpu.CompilerParams(vmem_limit_bytes=61 * MIB),
+        compiler_params=pltpu.CompilerParams(vmem_limit_bytes=52 * MIB),
         cost_estimate=pl.CostEstimate(flops=0, bytes_accessed=0, transcendentals=0),
         name="attention",
     )(own, ep, positions, queries, w_uv, own_keys, core_keys)
@@ -518,30 +518,32 @@
         ep, expert_ids, expert_weights, k_rope, moe_rows, latent, ctx
     )
     arrived = lax.all_to_all(outgoing, "ctx", split_axis=0, concat_axis=0, tiled=True)
-    high, q_nope = lax.optimization_barrier((high, q_nope))
+    flips = gather_order(ctx)
+    received = over_ctx(packed[None], flips[0])
+    high, q_nope, received = lax.optimization_barrier((high, q_nope, received))
     queries = fold(me, positions, q_nope, q_rope, w_uk)
-    flips = gather_order(ctx)
-    own_keys = packed[None]
-    for flip in flips[:-2]:
+    own_keys = jnp.concatenate([packed[None], received], axis=0)
+    for flip in flips[1:-1]:
         own_keys = jnp.concatenate([own_keys, over_ctx(own_keys, flip)], axis=0)
-    arrived, queries = lax.optimization_barrier((arrived, queries))
+    arrived, queries, own_keys = lax.optimization_barrier((arrived, queries, own_keys))
 
     own = arrived.reshape(ctx * CAP, arrived.shape[2])
     far = over(own, "x")
     core = over(own, "core")
-    received = over_ctx(own_keys, flips[-2])
+    received = over_ctx(own_keys, flips[-1])
     sums, far_gate, far_up, down = near_experts(ep, own, core, w_gate, w_up, w_down)
-    far, sums, received = lax.optimization_barrier((far, sums, received))
+    far, sums = lax.optimization_barrier((far, sums))
     core_far = over(far, "core")
-    own_keys = jnp.concatenate([own_keys, received], axis=0)
-    received = over_ctx(own_keys, flips[-1])
     own_out, core_out, far_out, core_far_out = far_experts(
         far, core_far, sums, far_gate, far_up, down
     )
+    core_far_out, received = lax.optimization_barrier((core_far_out, received))
     from_core_far = over(core_far_out, "core")
     from_core = over(core_out, "core")
+    own_keys = jnp.concatenate([own_keys, received], axis=0)
+    own_keys, from_core_far = lax.optimization_barrier((own_keys, from_core_far))
+    core_keys = over(own_keys, "core")
     returning = sum_cores(ep, own_out, from_core, far_out, from_core_far, ctx)
-    returning, received = lax.optimization_barrier((returning, received))
     returned = lax.all_to_all(
         returning.reshape(2 * ctx, CAP, returning.shape[3]),
         ("ctx", "x"),
@@ -549,8 +551,6 @@
         concat_axis=0,
         tiled=True,
     )
-    own_keys = jnp.concatenate([own_keys, received], axis=0)
-    core_keys = over(own_keys, "core")
     attention = attend(me, ep, positions, queries, w_uv, own_keys, core_keys)
     moe_out = combine(high, low, returned.reshape(2 * ctx * CAP, returned.shape[2]))
     return (attention, moe_out)

time: 59.2 us -> 55.2 us (0.932)
  waiting for transfers between devices: 12.1 us -> 8.38 us
  other arithmetic: 0.2 us -> 1.06 us
  local copies, waits for them, and re-layouts: 0.85 us -> 0.02 us
  Pallas kernels: 25.8 us -> 25.1 us
    all_to_all x1, starting transfers between devices: 7.28 us -> 3.81 us  [shards(): lax.all_to_all(outgoing, 'ctx', split_axis=0, concat_axis=0, tiled=True)]
    ppermute x3, waiting for transfers between devices: 5.03 us -> 1.66 us  [over_ctx(): return lax.ppermute(value, 'ctx', [(i, i ^ flip) for i in range(ctx)])]
    all_to_all x1, waiting for transfers between devices: 3.27 us -> 0.01 us  [shards(): lax.all_to_all(outgoing, 'ctx', split_axis=0, concat_axis=0, tiled=True)]
    ppermute x3, starting transfers between devices: 5.55 us -> 7.71 us  [over_ctx(): return lax.ppermute(value, 'ctx', [(i, i ^ flip) for i in range(ctx)])]
    all_to_all x1, waiting for transfers between devices: 0.01 us -> 1.77 us  [shards(): lax.all_to_all(returning.reshape(2 * ctx, CAP, returning.shape[3]), ('ctx...]
    all_to_all x1, starting transfers between devices: 4.29 us -> 5.72 us  [shards(): lax.all_to_all(returning.reshape(2 * ctx, CAP, returning.shape[3]), ('ctx...]
    ppermute x6, waiting for transfers between devices: 3.76 us -> 4.94 us  [over(): return lax.ppermute(value, axis, [(0, 1), (1, 0)])]
    concatenate x0 -> x1, other arithmetic: none -> 0.91 us  [shards(): own_keys = jnp.concatenate([packed[None], received], axis=0)]
  transfers between devices with their start and end apart: 11 -> 11, of which waited for: 8 -> 9; matrix products, arithmetic and copies ran while one was open for 0% -> 2% of each run, Pallas kernels for 38% -> 38%
where the time goes in v7:
time: 55.2 us; the launch traced here: 54.7 us
  Pallas kernels  25.1 us (45%)
  starting transfers between devices  19.4 us (35%)
  waiting for transfers between devices  8.38 us (15%)
  other arithmetic  1.06 us (2%)
  between operations  0.74 us (1%)
    pallas_call x1, Pallas kernels, attend(): pl.pallas_call(attention_kernel, out_shape=jax.ShapeDtypeStruct((2 * HALF...  10.2 us
    ppermute x3, starting transfers between devices, over_ctx(): return lax.ppermute(value, 'ctx', [(i, i ^ flip) for i in range(ctx)])  7.71 us
    all_to_all x1, starting transfers between devices, shards(): lax.all_to_all(returning.reshape(2 * ctx, CAP, returning.shape[3]), ('ctx...  5.72 us
    ppermute x6, waiting for transfers between devices, over(): return lax.ppermute(value, axis, [(0, 1), (1, 0)])  4.94 us
    pallas_call x1, Pallas kernels, fold(): pl.pallas_call(fold_kernel, out_shape=jax.ShapeDtypeStruct((2, 2, heads /...  4.66 us
    pallas_call x1, Pallas kernels, near_experts(): pl.pallas_call(near_kernel, out_shape=[jax.ShapeDtypeStruct((slots, 2 * u...  4.39 us
    all_to_all x1, starting transfers between devices, shards(): lax.all_to_all(outgoing, 'ctx', split_axis=0, concat_axis=0, tiled=True)  3.81 us
    pallas_call x1, Pallas kernels, route(): pl.pallas_call(route_kernel, out_shape=[jax.ShapeDtypeStruct((ctx, CAP, f...  2.23 us
  transfers between devices with their start and end apart: 11, of which 9 were waited for; matrix products, arithmetic and copies ran while one was open for 2% of the time, Pallas kernels for 38%

profile of v7, /device:TPU:0, one launch (start us, length us, event | category | flops | bytes accessed | tf_op | source)
XLA Modules:
  0.0 54.7 jit_solution(12474921598238625041)
XLA Ops:
  0.6 2.2 %route.1 = (bf16[8,8,1792]{2,1,0:T(8,128)(2,1)}, bf16[128,128]{1,0:T(8,128)(2,1)}, bf16[128,128]{1,0:T(8,128)(2,1)}, bf16[64,576]{1,0:T(8,128)(2,1)}) custom-call(s32[1]{0:T(128)} %bitcast.1.ep_ref, s32[8,128]{1,0:T(8,128)} %bitcast.19, f32[8,128]{1,0:T(8,128)} %bitcast.20, bf16[64,128]{1,0:T(8,128)(2,1)} %bitcast.18, bf16[128,1792]{1,0:T(8,128)(2,1)} %rows_ref.1, ...), custom_call_target="tpu_custom_call" | custom-call | flops 29360128 | bytes 1048576 | tf_op jit(solution)/shard_map/route/pallas_call | solution.py:88
  2.9 4.0 %collective-permute-start = (bf16[1,64,576]{2,1,0:T(8,128)(2,1)}, bf16[1,64,576]{2,1,0:T(8,128)(2,1)S(1)}, u32[]{:S(2)}, u32[]{:S(2)}) collective-permute-start(bf16[1,64,576]{2,1,0:T(8,128)(2,1)} %bitcast.15), channel_id=1, source_target_pairs={{0,16},{4,20},{8,24},{12,28},{16,0},{20,4},{24,8},{28,12},{1,17},{... | collective-permute-start | bytes 221192 | tf_op jit(solution)/shard_map/ppermute | solution.py:512
  6.9 3.8 %all-to-all-start = ((bf16[8,8,1792]{2,1,0:T(8,128)(2,1)}), bf16[8,8,1792]{2,1,0:T(8,128)(2,1)S(1)}, u32[]{:S(2)}, u32[]{:S(2)}) async-start(bf16[8,8,1792]{2,1,0:T(8,128)(2,1)} %get-tuple-element.26), calls=%async_computation | async-start | bytes 458752 | tf_op jit(solution)/shard_map/all_to_all | solution.py:520
  10.7 0.6 %collective-permute-done = bf16[1,64,576]{2,1,0:T(8,128)(2,1)S(1)} collective-permute-done((bf16[1,64,576]{2,1,0:T(8,128)(2,1)}, bf16[1,64,576]{2,1,0:T(8,128)(2,1)S(1)}, u32[]{:S(2)}, u32[]{:S(2)}) %collective-permute-start) | collective-permute-done | bytes 73760 | tf_op jit(solution)/shard_map/ppermute | solution.py:512
  11.3 0.9 %pad_maximum_fusion.2 = bf16[2,64,576]{2,1,0:T(8,128)(2,1)S(1)} fusion(bf16[1,64,576]{2,1,0:T(8,128)(2,1)S(1)} %collective-permute-done, bf16[1,64,576]{2,1,0:T(8,128)(2,1)} %bitcast.16), kind=kLoop, calls=%fused_computation.2 | loop fusion | flops 73728 | bytes 294912 | tf_op jit(solution)/shard_map/concatenate | solution.py:525
  12.2 1.8 %collective-permute-start.1 = (bf16[2,64,576]{2,1,0:T(8,128)(2,1)S(1)}, bf16[2,64,576]{2,1,0:T(8,128)(2,1)S(1)}, u32[]{:S(2)}, u32[]{:S(2)}) collective-permute-start(bf16[2,64,576]{2,1,0:T(8,128)(2,1)S(1)} %pad_maximum_fusion.2), channel_id=1, source_target_pairs={{0,4},{4,0},{8,12},{12,8},{16,20},{20,16},{24,28},{28,24},{1,5},{5... | collective-permute-start | bytes 442376 | tf_op jit(solution)/shard_map/ppermute | solution.py:512
  14.0 0.0 copy-start.3
  14.0 4.7 %fold.1 = bf16[2,2,512,576]{3,2,1,0:T(8,128)(2,1)} custom-call(s32[1]{0:T(128)} %bitcast.own_ref, s32[1024]{0:T(1024)} %positions_ref.3, bf16[128,2048]{1,0:T(8,128)(2,1)} %q_nope_ref, bf16[128,1024]{1,0:T(8,128)(2,1)} %q_rope_ref.1, bf16[512,2048]{1,0:T(8,128)(2,1)} %w_uk_ref.1), custom_call_target="tpu_custom_call" | custom-call | flops 268435456 | bytes 6291456 | tf_op jit(solution)/shard_map/fold/pallas_call | solution.py:301
  18.7 0.6 %collective-permute-done.1 = bf16[2,64,576]{2,1,0:T(8,128)(2,1)S(1)} collective-permute-done((bf16[2,64,576]{2,1,0:T(8,128)(2,1)S(1)}, bf16[2,64,576]{2,1,0:T(8,128)(2,1)S(1)}, u32[]{:S(2)}, u32[]{:S(2)}) %collective-permute-start.1) | collective-permute-done | bytes 147488 | tf_op jit(solution)/shard_map/ppermute | solution.py:512
  19.2 0.0 copy-done.3
  19.2 0.1 pad_maximum_fusion.1
  19.3 0.0 all-to-all-done
  19.3 0.1 collective-permute-start.3
  19.4 1.6 %collective-permute-start.2 = (bf16[64,1792]{1,0:T(8,128)(2,1)S(1)}, bf16[64,1792]{1,0:T(8,128)(2,1)S(1)}, u32[]{:S(2)}, u32[]{:S(2)}) collective-permute-start(bf16[64,1792]{1,0:T(8,128)(2,1)S(1)} %bitcast.12), channel_id=1, source_target_pairs={{0,2},{2,0},{1,3},{3,1},{4,6},{6,4},{5,7},{7,5},{8,10},{10,8},{9,1... | collective-permute-start | bytes 688136 | tf_op jit(solution)/shard_map/ppermute | solution.py:515
  20.9 1.9 %collective-permute-start.5 = (bf16[4,64,576]{2,1,0:T(8,128)(2,1)S(1)}, bf16[4,64,576]{2,1,0:T(8,128)(2,1)S(1)}, u32[]{:S(2)}, u32[]{:S(2)}) collective-permute-start(bf16[4,64,576]{2,1,0:T(8,128)(2,1)S(1)} %pad_maximum_fusion.1), channel_id=1, source_target_pairs={{0,8},{4,12},{8,0},{12,4},{16,24},{20,28},{24,16},{28,20},{1,9},{5... | collective-permute-start | bytes 884744 | tf_op jit(solution)/shard_map/ppermute | solution.py:512
  22.9 0.0 collective-permute-done.3.core_ref
  22.9 4.4 %near_experts.1 = (f32[64,512]{1,0:T(8,128)S(1)}, bf16[2,1792,256]{2,1,0:T(8,128)(2,1)S(1)}, bf16[2,1792,256]{2,1,0:T(8,128)(2,1)S(1)}, bf16[4,256,1792]{2,1,0:T(8,128)(2,1)S(1)}) custom-call(s32[1]{0:T(128)} %bitcast.1.ep_ref, bf16[64,1792]{1,0:T(8,128)(2,1)S(1)} %bitcast.13, bf16[64,1792]{1,0:T(8,128)(2,1)S(1)} %collective-permute-done.3.core_ref, ...), custom_call_target="tpu_custom_call" | custom-call | flops 234881024 | bytes 11010048 | tf_op jit(solution)/shard_map/near_experts/pallas_call | solution.py:166
  27.3 0.2 collective-permute-done.2.far_ref
  27.4 0.0 collective-permute-start.4
  27.4 1.5 %collective-permute-done.4.core_far_ref = bf16[64,1792]{1,0:T(8,128)(2,1)S(1)} collective-permute-done((bf16[64,1792]{1,0:T(8,128)(2,1)S(1)}, bf16[64,1792]{1,0:T(8,128)(2,1)S(1)}, u32[]{:S(2)}, u32[]{:S(2)}) %collective-permute-start.4) | collective-permute-done | bytes 229408 | tf_op jit(solution)/shard_map/ppermute | solution.py:515
  28.9 1.5 %far_experts.1 = (bf16[64,1792]{1,0:T(8,128)(2,1)S(1)}, bf16[64,1792]{1,0:T(8,128)(2,1)S(1)}, bf16[64,1792]{1,0:T(8,128)(2,1)S(1)}, bf16[64,1792]{1,0:T(8,128)(2,1)S(1)}) custom-call(bf16[64,1792]{1,0:T(8,128)(2,1)S(1)} %collective-permute-done.2.far_ref, bf16[64,1792]{1,0:T(8,128)(2,1)S(1)} %collective-permute-done.4.core_far_ref, ...), custom_call_target="tpu_custom_call" | custom-call | tf_op jit(solution)/shard_map/far_experts/pallas_call | solution.py:213
  30.4 0.0 copy-start.2
  30.4 0.5 collective-permute-done.5
  30.9 0.0 collective-permute-start.6
  30.9 0.5 collective-permute-start.8
  31.4 0.1 pad_maximum_fusion.own_keys
  31.5 0.9 %collective-permute-done.6.from_core_far_ref = bf16[64,1792]{1,0:T(8,128)(2,1)S(1)} collective-permute-done((bf16[64,1792]{1,0:T(8,128)(2,1)S(1)}, bf16[64,1792]{1,0:T(8,128)(2,1)S(1)}, u32[]{:S(2)}, u32[]{:S(2)}) %collective-permute-start.6) | collective-permute-done | bytes 229408 | tf_op jit(solution)/shard_map/ppermute | solution.py:515
  32.4 0.3 collective-permute-done.8.from_core_ref
  32.7 0.9 %sum_cores.1 = bf16[8,2,8,1792]{3,2,1,0:T(8,128)(2,1)} custom-call(s32[1]{0:T(128)} %bitcast.1.ep_ref, bf16[64,1792]{1,0:T(8,128)(2,1)S(1)} %get-tuple-element.46.own_ref, bf16[64,1792]{1,0:T(8,128)(2,1)S(1)} %collective-permute-done.8.from_core_ref, bf16[64,1792]{1,0:T(8,128)(2,1)S(1)} %get-tuple-element.48.far_ref, ...), custom_call_target="tpu_custom_call" | custom-call | bytes 1048576 | tf_op jit(solution)/shard_map/sum_cores/pallas_call | solution.py:237
  33.6 5.7 %all-to-all-start.1 = ((bf16[16,8,1792]{2,1,0:T(8,128)(2,1)}), bf16[16,8,1792]{2,1,0:T(8,128)(2,1)S(1)}, u32[]{:S(2)}, u32[]{:S(2)}) async-start(bf16[16,8,1792]{2,1,0:T(8,128)(2,1)} %bitcast.8), calls=%async_computation.1 | async-start | bytes 917504 | tf_op jit(solution)/shard_map/all_to_all | solution.py:547
  39.3 0.0 copy-start
  39.3 0.0 copy-start.1
  39.3 0.1 collective-permute-start.7
  39.4 2.1 %collective-permute-done.7.core_keys = bf16[8,64,576]{2,1,0:T(8,128)(2,1)S(1)} collective-permute-done((bf16[8,64,576]{2,1,0:T(8,128)(2,1)S(1)}, bf16[8,64,576]{2,1,0:T(8,128)(2,1)S(1)}, u32[]{:S(2)}, u32[]{:S(2)}) %collective-permute-start.7) | collective-permute-done | bytes 589856 | tf_op jit(solution)/shard_map/ppermute | solution.py:515
  41.5 0.0 copy-done.2
  41.5 10.2 %attention.1 = bf16[128,2048]{1,0:T(8,128)(2,1)} custom-call(s32[1]{0:T(128)} %bitcast.own_ref, s32[1]{0:T(128)} %bitcast.1.ep_ref, s32[1024]{0:T(1024)S(1)} %copy-done.2, bf16[2,1024,576]{2,1,0:T(8,128)(2,1)} %bitcast.14, bf16[512,2048]{1,0:T(8,128)(2,1)} %w_uv_hbm.1, bf16[8,64,576]{2,1,0:T(8,128)(2,1)S(1)} %pad_maximum_fusion.own_keys, ...), custom_call_target="tpu_custom_call" | custom-call | tf_op jit(solution)/shard_map/attention/pallas_call | solution.py:472
  51.7 1.8 %all-to-all-done.1 = bf16[16,8,1792]{2,1,0:T(8,128)(2,1)S(1)} async-done(((bf16[16,8,1792]{2,1,0:T(8,128)(2,1)}), bf16[16,8,1792]{2,1,0:T(8,128)(2,1)S(1)}, u32[]{:S(2)}, u32[]{:S(2)}) %all-to-all-start.1) | async-done | bytes 458784 | tf_op jit(solution)/shard_map/all_to_all | solution.py:547
  53.5 0.0 copy-done
  53.5 0.0 copy-done.1
  53.5 1.2 %combine.1 = bf16[128,1792]{1,0:T(8,128)(2,1)} custom-call(bf16[128,128]{1,0:T(8,128)(2,1)S(1)} %copy-done, bf16[128,128]{1,0:T(8,128)(2,1)S(1)} %copy-done.1, bf16[128,1792]{1,0:T(8,128)(2,1)S(1)} %bitcast.10), custom_call_target="tpu_custom_call" | custom-call | flops 117440512 | bytes 1048576 | tf_op jit(solution)/shard_map/combine/pallas_call | solution.py:260
Async XLA Ops:
  2.9 8.4 %collective-permute-start = (bf16[1,64,576]{2,1,0:T(8,128)(2,1)}, bf16[1,64,576]{2,1,0:T(8,128)(2,1)S(1)}, u32[]{:S(2)}, u32[]{:S(2)}) collective-permute-start(bf16[1,64,576]{2,1,0:T(8,128)(2,1)} %bitcast.15), channel_id=1, source_target_pairs={{0,16},{4,20},{8,24},{12,28},{16,0},{20,4},{24,8},{28,12},{1,17},{... | collective-permute-start | bytes 221192 | tf_op jit(solution)/shard_map/ppermute | solution.py:512
  6.9 12.4 %all-to-all-start = ((bf16[8,8,1792]{2,1,0:T(8,128)(2,1)}), bf16[8,8,1792]{2,1,0:T(8,128)(2,1)S(1)}, u32[]{:S(2)}, u32[]{:S(2)}) async-start(bf16[8,8,1792]{2,1,0:T(8,128)(2,1)} %get-tuple-element.26), calls=%async_computation | async-start | bytes 458752 | tf_op jit(solution)/shard_map/all_to_all | solution.py:520
  12.2 7.0 %collective-permute-start.1 = (bf16[2,64,576]{2,1,0:T(8,128)(2,1)S(1)}, bf16[2,64,576]{2,1,0:T(8,128)(2,1)S(1)}, u32[]{:S(2)}, u32[]{:S(2)}) collective-permute-start(bf16[2,64,576]{2,1,0:T(8,128)(2,1)S(1)} %pad_maximum_fusion.2), channel_id=1, source_target_pairs={{0,4},{4,0},{8,12},{12,8},{16,20},{20,16},{24,28},{28,24},{1,5},{5... | collective-permute-start | bytes 442376 | tf_op jit(solution)/shard_map/ppermute | solution.py:512
  14.0 5.2 %copy-start.3 = (bf16[64,576]{1,0:T(8,128)(2,1)S(1)}, bf16[64,576]{1,0:T(8,128)(2,1)}, u32[]{:S(2)}) copy-start(bf16[64,576]{1,0:T(8,128)(2,1)} %get-tuple-element.28) | copy-start | bytes 221188
  19.3 3.5 %collective-permute-start.3 = (bf16[64,1792]{1,0:T(8,128)(2,1)S(1)}, bf16[64,1792]{1,0:T(8,128)(2,1)S(1)}, u32[]{:S(2)}, u32[]{:S(2)}) collective-permute-start(bf16[64,1792]{1,0:T(8,128)(2,1)S(1)} %bitcast.11), channel_id=1, source_target_pairs={{0,1},{1,0},{2,3},{3,2},{4,5},{5,4},{6,7},{7,6},{8,9},{9,8},{10,11... | collective-permute-start | bytes 688136 | tf_op jit(solution)/shard_map/ppermute | solution.py:515
  19.4 8.0 %collective-permute-start.2 = (bf16[64,1792]{1,0:T(8,128)(2,1)S(1)}, bf16[64,1792]{1,0:T(8,128)(2,1)S(1)}, u32[]{:S(2)}, u32[]{:S(2)}) collective-permute-start(bf16[64,1792]{1,0:T(8,128)(2,1)S(1)} %bitcast.12), channel_id=1, source_target_pairs={{0,2},{2,0},{1,3},{3,1},{4,6},{6,4},{5,7},{7,5},{8,10},{10,8},{9,1... | collective-permute-start | bytes 688136 | tf_op jit(solution)/shard_map/ppermute | solution.py:515
  20.9 9.9 %collective-permute-start.5 = (bf16[4,64,576]{2,1,0:T(8,128)(2,1)S(1)}, bf16[4,64,576]{2,1,0:T(8,128)(2,1)S(1)}, u32[]{:S(2)}, u32[]{:S(2)}) collective-permute-start(bf16[4,64,576]{2,1,0:T(8,128)(2,1)S(1)} %pad_maximum_fusion.1), channel_id=1, source_target_pairs={{0,8},{4,12},{8,0},{12,4},{16,24},{20,28},{24,16},{28,20},{1,9},{5... | collective-permute-start | bytes 884744 | tf_op jit(solution)/shard_map/ppermute | solution.py:512
  27.4 1.5 %collective-permute-start.4 = (bf16[64,1792]{1,0:T(8,128)(2,1)S(1)}, bf16[64,1792]{1,0:T(8,128)(2,1)S(1)}, u32[]{:S(2)}, u32[]{:S(2)}) collective-permute-start(bf16[64,1792]{1,0:T(8,128)(2,1)S(1)} %collective-permute-done.2.far_ref), channel_id=1, source_target_pairs={{0,1},{1,0},{2,3},{3,2},{4,5},{5,4},{6,7},{7,6},{8,9},{9,8},{10,11... | collective-permute-start | bytes 688136 | tf_op jit(solution)/shard_map/ppermute | solution.py:515
  30.4 11.1 %copy-start.2 = (s32[1024]{0:T(1024)S(1)}, s32[1024]{0:T(1024)}, u32[]{:S(2)}) copy-start(s32[1024]{0:T(1024)} %positions_ref.3) | copy-start | bytes 12292
  30.9 1.5 %collective-permute-start.6 = (bf16[64,1792]{1,0:T(8,128)(2,1)S(1)}, bf16[64,1792]{1,0:T(8,128)(2,1)S(1)}, u32[]{:S(2)}, u32[]{:S(2)}) collective-permute-start(bf16[64,1792]{1,0:T(8,128)(2,1)S(1)} %get-tuple-element.42), channel_id=1, source_target_pairs={{0,1},{1,0},{2,3},{3,2},{4,5},{5,4},{6,7},{7,6},{8,9},{9,8},{10,11... | collective-permute-start | bytes 688136 | tf_op jit(solution)/shard_map/ppermute | solution.py:515
  30.9 1.8 %collective-permute-start.8 = (bf16[64,1792]{1,0:T(8,128)(2,1)S(1)}, bf16[64,1792]{1,0:T(8,128)(2,1)S(1)}, u32[]{:S(2)}, u32[]{:S(2)}) collective-permute-start(bf16[64,1792]{1,0:T(8,128)(2,1)S(1)} %get-tuple-element.47), channel_id=1, source_target_pairs={{0,1},{1,0},{2,3},{3,2},{4,5},{5,4},{6,7},{7,6},{8,9},{9,8},{10,11... | collective-permute-start | bytes 688136 | tf_op jit(solution)/shard_map/ppermute | solution.py:515
  33.6 19.9 %all-to-all-start.1 = ((bf16[16,8,1792]{2,1,0:T(8,128)(2,1)}), bf16[16,8,1792]{2,1,0:T(8,128)(2,1)S(1)}, u32[]{:S(2)}, u32[]{:S(2)}) async-start(bf16[16,8,1792]{2,1,0:T(8,128)(2,1)} %bitcast.8), calls=%async_computation.1 | async-start | bytes 917504 | tf_op jit(solution)/shard_map/all_to_all | solution.py:547
  39.3 14.2 %copy-start = (bf16[128,128]{1,0:T(8,128)(2,1)S(1)}, bf16[128,128]{1,0:T(8,128)(2,1)}, u32[]{:S(2)}) copy-start(bf16[128,128]{1,0:T(8,128)(2,1)} %get-tuple-element.44.high_ref) | copy-start | bytes 98308
  39.3 14.2 %copy-start.1 = (bf16[128,128]{1,0:T(8,128)(2,1)S(1)}, bf16[128,128]{1,0:T(8,128)(2,1)}, u32[]{:S(2)}) copy-start(bf16[128,128]{1,0:T(8,128)(2,1)} %get-tuple-element.45.low_ref) | copy-start | bytes 98308
  39.3 2.2 %collective-permute-start.7 = (bf16[8,64,576]{2,1,0:T(8,128)(2,1)S(1)}, bf16[8,64,576]{2,1,0:T(8,128)(2,1)S(1)}, u32[]{:S(2)}, u32[]{:S(2)}) collective-permute-start(bf16[8,64,576]{2,1,0:T(8,128)(2,1)S(1)} %pad_maximum_fusion.own_keys), channel_id=1, source_target_pairs={{0,1},{1,0},{2,3},{3,2},{4,5},{5,4},{6,7},{7,6},{8,9},{9,8},{10,11... | collective-permute-start | bytes 1769480 | tf_op jit(solution)/shard_map/ppermute | solution.py:515

commit v8 on v7

--- a/solution.py
+++ b/solution.py
@@ -544,6 +544,7 @@
     own_keys, from_core_far = lax.optimization_barrier((own_keys, from_core_far))
     core_keys = over(own_keys, "core")
     returning = sum_cores(ep, own_out, from_core, far_out, from_core_far, ctx)
+    returning, core_keys = lax.optimization_barrier((returning, core_keys))
     returned = lax.all_to_all(
         returning.reshape(2 * ctx, CAP, returning.shape[3]),
         ("ctx", "x"),

time: 55.2 us -> 57.2 us (1.036)
  waiting for transfers between devices: 8.38 us -> 11 us
  Pallas kernels: 25.1 us -> 24.5 us
    all_to_all x1, waiting for transfers between devices: 1.77 us -> 4.41 us  [shards(): lax.all_to_all(returning.reshape(2 * ctx, CAP, returning.shape[3]), ('ctx...]
  transfers between devices with their start and end apart: 11 -> 11, of which waited for: 9 -> 8; matrix products, arithmetic and copies ran while one was open for 2% -> 2% of each run, Pallas kernels for 38% -> 37%
where the time goes in v8:
time: 57.2 us; the launch traced here: 56.8 us
  Pallas kernels  24.5 us (43%)
  starting transfers between devices  19.4 us (34%)
  waiting for transfers between devices  11 us (19%)
  other arithmetic  1.06 us (2%)
  between operations  0.74 us (1%)
    pallas_call x1, Pallas kernels, attend(): pl.pallas_call(attention_kernel, out_shape=jax.ShapeDtypeStruct((2 * HALF...  9.72 us
    ppermute x3, starting transfers between devices, over_ctx(): return lax.ppermute(value, 'ctx', [(i, i ^ flip) for i in range(ctx)])  7.71 us
    all_to_all x1, starting transfers between devices, shards(): lax.all_to_all(returning.reshape(2 * ctx, CAP, returning.shape[3]), ('ctx...  5.72 us
    ppermute x6, waiting for transfers between devices, over(): return lax.ppermute(value, axis, [(0, 1), (1, 0)])  4.95 us
    pallas_call x1, Pallas kernels, fold(): pl.pallas_call(fold_kernel, out_shape=jax.ShapeDtypeStruct((2, 2, heads /...  4.66 us
    all_to_all x1, waiting for transfers between devices, shards(): lax.all_to_all(returning.reshape(2 * ctx, CAP, returning.shape[3]), ('ctx...  4.41 us
    pallas_call x1, Pallas kernels, near_experts(): pl.pallas_call(near_kernel, out_shape=[jax.ShapeDtypeStruct((slots, 2 * u...  4.39 us
    all_to_all x1, starting transfers between devices, shards(): lax.all_to_all(outgoing, 'ctx', split_axis=0, concat_axis=0, tiled=True)  3.81 us
  transfers between devices with their start and end apart: 11, of which 8 were waited for; matrix products, arithmetic and copies ran while one was open for 2% of the time, Pallas kernels for 37%

profile of v8, /device:TPU:0, one launch (start us, length us, event | category | flops | bytes accessed | tf_op | source)
XLA Modules:
  0.0 56.8 jit_solution(14596187684442440974)
XLA Ops:
  0.6 2.2 %route.1 = (bf16[8,8,1792]{2,1,0:T(8,128)(2,1)}, bf16[128,128]{1,0:T(8,128)(2,1)}, bf16[128,128]{1,0:T(8,128)(2,1)}, bf16[64,576]{1,0:T(8,128)(2,1)}) custom-call(s32[1]{0:T(128)} %bitcast.1.ep_ref, s32[8,128]{1,0:T(8,128)} %bitcast.19, f32[8,128]{1,0:T(8,128)} %bitcast.20, bf16[64,128]{1,0:T(8,128)(2,1)} %bitcast.18, bf16[128,1792]{1,0:T(8,128)(2,1)} %rows_ref.1, ...), custom_call_target="tpu_custom_call" | custom-call | flops 29360128 | bytes 1048576 | tf_op jit(solution)/shard_map/route/pallas_call | solution.py:88
  2.9 4.0 %collective-permute-start = (bf16[1,64,576]{2,1,0:T(8,128)(2,1)}, bf16[1,64,576]{2,1,0:T(8,128)(2,1)S(1)}, u32[]{:S(2)}, u32[]{:S(2)}) collective-permute-start(bf16[1,64,576]{2,1,0:T(8,128)(2,1)} %bitcast.15), channel_id=1, source_target_pairs={{0,16},{4,20},{8,24},{12,28},{16,0},{20,4},{24,8},{28,12},{1,17},{... | collective-permute-start | bytes 221192 | tf_op jit(solution)/shard_map/ppermute | solution.py:512
  6.9 3.8 %all-to-all-start = ((bf16[8,8,1792]{2,1,0:T(8,128)(2,1)}), bf16[8,8,1792]{2,1,0:T(8,128)(2,1)S(1)}, u32[]{:S(2)}, u32[]{:S(2)}) async-start(bf16[8,8,1792]{2,1,0:T(8,128)(2,1)} %get-tuple-element.28), calls=%async_computation | async-start | bytes 458752 | tf_op jit(solution)/shard_map/all_to_all | solution.py:520
  10.7 0.6 %collective-permute-done = bf16[1,64,576]{2,1,0:T(8,128)(2,1)S(1)} collective-permute-done((bf16[1,64,576]{2,1,0:T(8,128)(2,1)}, bf16[1,64,576]{2,1,0:T(8,128)(2,1)S(1)}, u32[]{:S(2)}, u32[]{:S(2)}) %collective-permute-start) | collective-permute-done | bytes 73760 | tf_op jit(solution)/shard_map/ppermute | solution.py:512
  11.3 0.9 %pad_maximum_fusion.2 = bf16[2,64,576]{2,1,0:T(8,128)(2,1)S(1)} fusion(bf16[1,64,576]{2,1,0:T(8,128)(2,1)S(1)} %collective-permute-done, bf16[1,64,576]{2,1,0:T(8,128)(2,1)} %bitcast.16), kind=kLoop, calls=%fused_computation.2 | loop fusion | flops 73728 | bytes 294912 | tf_op jit(solution)/shard_map/concatenate | solution.py:525
  12.2 1.8 %collective-permute-start.1 = (bf16[2,64,576]{2,1,0:T(8,128)(2,1)S(1)}, bf16[2,64,576]{2,1,0:T(8,128)(2,1)S(1)}, u32[]{:S(2)}, u32[]{:S(2)}) collective-permute-start(bf16[2,64,576]{2,1,0:T(8,128)(2,1)S(1)} %pad_maximum_fusion.2), channel_id=1, source_target_pairs={{0,4},{4,0},{8,12},{12,8},{16,20},{20,16},{24,28},{28,24},{1,5},{5... | collective-permute-start | bytes 442376 | tf_op jit(solution)/shard_map/ppermute | solution.py:512
  14.0 0.0 copy-start.3
  14.0 4.7 %fold.1 = bf16[2,2,512,576]{3,2,1,0:T(8,128)(2,1)} custom-call(s32[1]{0:T(128)} %bitcast.own_ref, s32[1024]{0:T(1024)} %positions_ref.3, bf16[128,2048]{1,0:T(8,128)(2,1)} %q_nope_ref, bf16[128,1024]{1,0:T(8,128)(2,1)} %q_rope_ref.1, bf16[512,2048]{1,0:T(8,128)(2,1)} %w_uk_ref.1), custom_call_target="tpu_custom_call" | custom-call | flops 268435456 | bytes 6291456 | tf_op jit(solution)/shard_map/fold/pallas_call | solution.py:301
  18.7 0.6 collective-permute-done.1
  19.2 0.0 copy-done.3
  19.2 0.1 pad_maximum_fusion.1
  19.3 0.0 all-to-all-done
  19.3 0.1 collective-permute-start.3
  19.4 1.6 %collective-permute-start.2 = (bf16[64,1792]{1,0:T(8,128)(2,1)S(1)}, bf16[64,1792]{1,0:T(8,128)(2,1)S(1)}, u32[]{:S(2)}, u32[]{:S(2)}) collective-permute-start(bf16[64,1792]{1,0:T(8,128)(2,1)S(1)} %bitcast.12), channel_id=1, source_target_pairs={{0,2},{2,0},{1,3},{3,1},{4,6},{6,4},{5,7},{7,5},{8,10},{10,8},{9,1... | collective-permute-start | bytes 688136 | tf_op jit(solution)/shard_map/ppermute | solution.py:515
  20.9 1.9 %collective-permute-start.5 = (bf16[4,64,576]{2,1,0:T(8,128)(2,1)S(1)}, bf16[4,64,576]{2,1,0:T(8,128)(2,1)S(1)}, u32[]{:S(2)}, u32[]{:S(2)}) collective-permute-start(bf16[4,64,576]{2,1,0:T(8,128)(2,1)S(1)} %pad_maximum_fusion.1), channel_id=1, source_target_pairs={{0,8},{4,12},{8,0},{12,4},{16,24},{20,28},{24,16},{28,20},{1,9},{5... | collective-permute-start | bytes 884744 | tf_op jit(solution)/shard_map/ppermute | solution.py:512
  22.9 0.0 collective-permute-done.3.core_ref
  22.9 4.4 %near_experts.1 = (f32[64,512]{1,0:T(8,128)S(1)}, bf16[2,1792,256]{2,1,0:T(8,128)(2,1)S(1)}, bf16[2,1792,256]{2,1,0:T(8,128)(2,1)S(1)}, bf16[4,256,1792]{2,1,0:T(8,128)(2,1)S(1)}) custom-call(s32[1]{0:T(128)} %bitcast.1.ep_ref, bf16[64,1792]{1,0:T(8,128)(2,1)S(1)} %bitcast.13, bf16[64,1792]{1,0:T(8,128)(2,1)S(1)} %collective-permute-done.3.core_ref, ...), custom_call_target="tpu_custom_call" | custom-call | flops 234881024 | bytes 11010048 | tf_op jit(solution)/shard_map/near_experts/pallas_call | solution.py:166
  27.3 0.2 collective-permute-done.2.far_ref
  27.4 0.0 collective-permute-start.4
  27.4 1.5 %collective-permute-done.4.core_far_ref = bf16[64,1792]{1,0:T(8,128)(2,1)S(1)} collective-permute-done((bf16[64,1792]{1,0:T(8,128)(2,1)S(1)}, bf16[64,1792]{1,0:T(8,128)(2,1)S(1)}, u32[]{:S(2)}, u32[]{:S(2)}) %collective-permute-start.4) | collective-permute-done | bytes 229408 | tf_op jit(solution)/shard_map/ppermute | solution.py:515
  28.9 1.5 %far_experts.1 = (bf16[64,1792]{1,0:T(8,128)(2,1)S(1)}, bf16[64,1792]{1,0:T(8,128)(2,1)S(1)}, bf16[64,1792]{1,0:T(8,128)(2,1)S(1)}, bf16[64,1792]{1,0:T(8,128)(2,1)S(1)}) custom-call(bf16[64,1792]{1,0:T(8,128)(2,1)S(1)} %collective-permute-done.2.far_ref, bf16[64,1792]{1,0:T(8,128)(2,1)S(1)} %collective-permute-done.4.core_far_ref, ...), custom_call_target="tpu_custom_call" | custom-call | tf_op jit(solution)/shard_map/far_experts/pallas_call | solution.py:213
  30.4 0.0 copy-start.2
  30.4 0.5 collective-permute-done.5
  30.9 0.0 collective-permute-start.6
  30.9 0.1 pad_maximum_fusion.own_keys
  31.0 1.4 %collective-permute-done.6.from_core_far_ref = bf16[64,1792]{1,0:T(8,128)(2,1)S(1)} collective-permute-done((bf16[64,1792]{1,0:T(8,128)(2,1)S(1)}, bf16[64,1792]{1,0:T(8,128)(2,1)S(1)}, u32[]{:S(2)}, u32[]{:S(2)}) %collective-permute-start.6) | collective-permute-done | bytes 229408 | tf_op jit(solution)/shard_map/ppermute | solution.py:515
  32.4 0.1 collective-permute-start.8
  32.5 0.4 collective-permute-start.7
  32.9 1.9 %collective-permute-done.7.from_core_ref = bf16[64,1792]{1,0:T(8,128)(2,1)S(1)} collective-permute-done((bf16[64,1792]{1,0:T(8,128)(2,1)S(1)}, bf16[64,1792]{1,0:T(8,128)(2,1)S(1)}, u32[]{:S(2)}, u32[]{:S(2)}) %collective-permute-start.7) | collective-permute-done | bytes 229408 | tf_op jit(solution)/shard_map/ppermute | solution.py:515
  34.8 0.9 %sum_cores.1 = bf16[8,2,8,1792]{3,2,1,0:T(8,128)(2,1)} custom-call(s32[1]{0:T(128)} %bitcast.1.ep_ref, bf16[64,1792]{1,0:T(8,128)(2,1)S(1)} %get-tuple-element.46.own_ref, bf16[64,1792]{1,0:T(8,128)(2,1)S(1)} %collective-permute-done.7.from_core_ref, bf16[64,1792]{1,0:T(8,128)(2,1)S(1)} %get-tuple-element.48.far_ref, ...), custom_call_target="tpu_custom_call" | custom-call | bytes 1048576 | tf_op jit(solution)/shard_map/sum_cores/pallas_call | solution.py:237
  35.7 0.0 collective-permute-done.8.core_keys
  35.7 5.7 %all-to-all-start.1 = ((bf16[16,8,1792]{2,1,0:T(8,128)(2,1)}), bf16[16,8,1792]{2,1,0:T(8,128)(2,1)S(1)}, u32[]{:S(2)}, u32[]{:S(2)}) async-start(bf16[16,8,1792]{2,1,0:T(8,128)(2,1)} %bitcast.8), calls=%async_computation.1 | async-start | bytes 917504 | tf_op jit(solution)/shard_map/all_to_all | solution.py:548
  41.4 0.0 copy-done.2
  41.4 0.0 copy-start
  41.4 0.0 copy-start.1
  41.4 9.7 %attention.1 = bf16[128,2048]{1,0:T(8,128)(2,1)} custom-call(s32[1]{0:T(128)} %bitcast.own_ref, s32[1]{0:T(128)} %bitcast.1.ep_ref, s32[1024]{0:T(1024)S(1)} %copy-done.2, bf16[2,1024,576]{2,1,0:T(8,128)(2,1)} %bitcast.14, bf16[512,2048]{1,0:T(8,128)(2,1)} %w_uv_hbm.1, bf16[8,64,576]{2,1,0:T(8,128)(2,1)S(1)} %pad_maximum_fusion.own_keys, ...), custom_call_target="tpu_custom_call" | custom-call | tf_op jit(solution)/shard_map/attention/pallas_call | solution.py:472
  51.2 4.4 %all-to-all-done.1 = bf16[16,8,1792]{2,1,0:T(8,128)(2,1)S(1)} async-done(((bf16[16,8,1792]{2,1,0:T(8,128)(2,1)}), bf16[16,8,1792]{2,1,0:T(8,128)(2,1)S(1)}, u32[]{:S(2)}, u32[]{:S(2)}) %all-to-all-start.1) | async-done | bytes 458784 | tf_op jit(solution)/shard_map/all_to_all | solution.py:548
  55.6 0.0 copy-done
  55.6 0.0 copy-done.1
  55.6 1.2 %combine.1 = bf16[128,1792]{1,0:T(8,128)(2,1)} custom-call(bf16[128,128]{1,0:T(8,128)(2,1)S(1)} %copy-done, bf16[128,128]{1,0:T(8,128)(2,1)S(1)} %copy-done.1, bf16[128,1792]{1,0:T(8,128)(2,1)S(1)} %bitcast.10), custom_call_target="tpu_custom_call" | custom-call | flops 117440512 | bytes 1048576 | tf_op jit(solution)/shard_map/combine/pallas_call | solution.py:260
Async XLA Ops:
  2.9 8.4 %collective-permute-start = (bf16[1,64,576]{2,1,0:T(8,128)(2,1)}, bf16[1,64,576]{2,1,0:T(8,128)(2,1)S(1)}, u32[]{:S(2)}, u32[]{:S(2)}) collective-permute-start(bf16[1,64,576]{2,1,0:T(8,128)(2,1)} %bitcast.15), channel_id=1, source_target_pairs={{0,16},{4,20},{8,24},{12,28},{16,0},{20,4},{24,8},{28,12},{1,17},{... | collective-permute-start | bytes 221192 | tf_op jit(solution)/shard_map/ppermute | solution.py:512
  6.9 12.4 %all-to-all-start = ((bf16[8,8,1792]{2,1,0:T(8,128)(2,1)}), bf16[8,8,1792]{2,1,0:T(8,128)(2,1)S(1)}, u32[]{:S(2)}, u32[]{:S(2)}) async-start(bf16[8,8,1792]{2,1,0:T(8,128)(2,1)} %get-tuple-element.28), calls=%async_computation | async-start | bytes 458752 | tf_op jit(solution)/shard_map/all_to_all | solution.py:520
  12.2 7.0 %collective-permute-start.1 = (bf16[2,64,576]{2,1,0:T(8,128)(2,1)S(1)}, bf16[2,64,576]{2,1,0:T(8,128)(2,1)S(1)}, u32[]{:S(2)}, u32[]{:S(2)}) collective-permute-start(bf16[2,64,576]{2,1,0:T(8,128)(2,1)S(1)} %pad_maximum_fusion.2), channel_id=1, source_target_pairs={{0,4},{4,0},{8,12},{12,8},{16,20},{20,16},{24,28},{28,24},{1,5},{5... | collective-permute-start | bytes 442376 | tf_op jit(solution)/shard_map/ppermute | solution.py:512
  14.0 5.2 %copy-start.3 = (bf16[64,576]{1,0:T(8,128)(2,1)S(1)}, bf16[64,576]{1,0:T(8,128)(2,1)}, u32[]{:S(2)}) copy-start(bf16[64,576]{1,0:T(8,128)(2,1)} %get-tuple-element.30) | copy-start | bytes 221188
  19.3 3.5 %collective-permute-start.3 = (bf16[64,1792]{1,0:T(8,128)(2,1)S(1)}, bf16[64,1792]{1,0:T(8,128)(2,1)S(1)}, u32[]{:S(2)}, u32[]{:S(2)}) collective-permute-start(bf16[64,1792]{1,0:T(8,128)(2,1)S(1)} %bitcast.11), channel_id=1, source_target_pairs={{0,1},{1,0},{2,3},{3,2},{4,5},{5,4},{6,7},{7,6},{8,9},{9,8},{10,11... | collective-permute-start | bytes 688136 | tf_op jit(solution)/shard_map/ppermute | solution.py:515
  19.4 8.0 %collective-permute-start.2 = (bf16[64,1792]{1,0:T(8,128)(2,1)S(1)}, bf16[64,1792]{1,0:T(8,128)(2,1)S(1)}, u32[]{:S(2)}, u32[]{:S(2)}) collective-permute-start(bf16[64,1792]{1,0:T(8,128)(2,1)S(1)} %bitcast.12), channel_id=1, source_target_pairs={{0,2},{2,0},{1,3},{3,1},{4,6},{6,4},{5,7},{7,5},{8,10},{10,8},{9,1... | collective-permute-start | bytes 688136 | tf_op jit(solution)/shard_map/ppermute | solution.py:515
  20.9 9.9 %collective-permute-start.5 = (bf16[4,64,576]{2,1,0:T(8,128)(2,1)S(1)}, bf16[4,64,576]{2,1,0:T(8,128)(2,1)S(1)}, u32[]{:S(2)}, u32[]{:S(2)}) collective-permute-start(bf16[4,64,576]{2,1,0:T(8,128)(2,1)S(1)} %pad_maximum_fusion.1), channel_id=1, source_target_pairs={{0,8},{4,12},{8,0},{12,4},{16,24},{20,28},{24,16},{28,20},{1,9},{5... | collective-permute-start | bytes 884744 | tf_op jit(solution)/shard_map/ppermute | solution.py:512
  27.4 1.5 %collective-permute-start.4 = (bf16[64,1792]{1,0:T(8,128)(2,1)S(1)}, bf16[64,1792]{1,0:T(8,128)(2,1)S(1)}, u32[]{:S(2)}, u32[]{:S(2)}) collective-permute-start(bf16[64,1792]{1,0:T(8,128)(2,1)S(1)} %collective-permute-done.2.far_ref), channel_id=1, source_target_pairs={{0,1},{1,0},{2,3},{3,2},{4,5},{5,4},{6,7},{7,6},{8,9},{9,8},{10,11... | collective-permute-start | bytes 688136 | tf_op jit(solution)/shard_map/ppermute | solution.py:515
  30.4 11.0 %copy-start.2 = (s32[1024]{0:T(1024)S(1)}, s32[1024]{0:T(1024)}, u32[]{:S(2)}) copy-start(s32[1024]{0:T(1024)} %positions_ref.3) | copy-start | bytes 12292
  30.9 1.5 %collective-permute-start.6 = (bf16[64,1792]{1,0:T(8,128)(2,1)S(1)}, bf16[64,1792]{1,0:T(8,128)(2,1)S(1)}, u32[]{:S(2)}, u32[]{:S(2)}) collective-permute-start(bf16[64,1792]{1,0:T(8,128)(2,1)S(1)} %get-tuple-element.44), channel_id=1, source_target_pairs={{0,1},{1,0},{2,3},{3,2},{4,5},{5,4},{6,7},{7,6},{8,9},{9,8},{10,11... | collective-permute-start | bytes 688136 | tf_op jit(solution)/shard_map/ppermute | solution.py:515
  32.4 3.3 %collective-permute-start.8 = (bf16[8,64,576]{2,1,0:T(8,128)(2,1)S(1)}, bf16[8,64,576]{2,1,0:T(8,128)(2,1)S(1)}, u32[]{:S(2)}, u32[]{:S(2)}) collective-permute-start(bf16[8,64,576]{2,1,0:T(8,128)(2,1)S(1)} %pad_maximum_fusion.own_keys), channel_id=1, source_target_pairs={{0,1},{1,0},{2,3},{3,2},{4,5},{5,4},{6,7},{7,6},{8,9},{9,8},{10,11... | collective-permute-start | bytes 1769480 | tf_op jit(solution)/shard_map/ppermute | solution.py:515
  32.5 2.3 %collective-permute-start.7 = (bf16[64,1792]{1,0:T(8,128)(2,1)S(1)}, bf16[64,1792]{1,0:T(8,128)(2,1)S(1)}, u32[]{:S(2)}, u32[]{:S(2)}) collective-permute-start(bf16[64,1792]{1,0:T(8,128)(2,1)S(1)} %get-tuple-element.47), channel_id=1, source_target_pairs={{0,1},{1,0},{2,3},{3,2},{4,5},{5,4},{6,7},{7,6},{8,9},{9,8},{10,11... | collective-permute-start | bytes 688136 | tf_op jit(solution)/shard_map/ppermute | solution.py:515
  35.7 19.9 %all-to-all-start.1 = ((bf16[16,8,1792]{2,1,0:T(8,128)(2,1)}), bf16[16,8,1792]{2,1,0:T(8,128)(2,1)S(1)}, u32[]{:S(2)}, u32[]{:S(2)}) async-start(bf16[16,8,1792]{2,1,0:T(8,128)(2,1)} %bitcast.8), calls=%async_computation.1 | async-start | bytes 917504 | tf_op jit(solution)/shard_map/all_to_all | solution.py:548
  41.4 14.2 %copy-start = (bf16[128,128]{1,0:T(8,128)(2,1)S(1)}, bf16[128,128]{1,0:T(8,128)(2,1)}, u32[]{:S(2)}) copy-start(bf16[128,128]{1,0:T(8,128)(2,1)} %get-tuple-element.51.high_ref) | copy-start | bytes 98308
  41.4 14.2 %copy-start.1 = (bf16[128,128]{1,0:T(8,128)(2,1)S(1)}, bf16[128,128]{1,0:T(8,128)(2,1)}, u32[]{:S(2)}) copy-start(bf16[128,128]{1,0:T(8,128)(2,1)} %get-tuple-element.52.low_ref) | copy-start | bytes 98308

commit v9 on v7

--- a/solution.py
+++ b/solution.py
@@ -484,7 +484,11 @@
             pltpu.SemaphoreType.DMA((3,)),
         ],
         compiler_params=pltpu.CompilerParams(vmem_limit_bytes=52 * MIB),
-        cost_estimate=pl.CostEstimate(flops=0, bytes_accessed=0, transcendentals=0),
+        cost_estimate=pl.CostEstimate(
+            flops=24 * rows * key_count * width,
+            bytes_accessed=8 * MIB,
+            transcendentals=rows * key_count,
+        ),
         name="attention",
     )(own, ep, positions, queries, w_uv, own_keys, core_keys)
 

time: 55.2 us -> 57.2 us (1.036)
  waiting for transfers between devices: 8.38 us -> 11 us
    all_to_all x1, waiting for transfers between devices: 1.77 us -> 4.38 us  [shards(): lax.all_to_all(returning.reshape(2 * ctx, CAP, returning.shape[3]), ('ctx...]
  transfers between devices with their start and end apart: 11 -> 11, of which waited for: 9 -> 8; matrix products, arithmetic and copies ran while one was open for 2% -> 2% of each run, Pallas kernels for 38% -> 37%
where the time goes in v9:
time: 57.2 us; the launch traced here: 56.8 us
  Pallas kernels  24.6 us (43%)
  starting transfers between devices  19.4 us (34%)
  waiting for transfers between devices  11 us (19%)
  other arithmetic  1.06 us (2%)
  between operations  0.75 us (1%)
    pallas_call x1, Pallas kernels, attend(): pl.pallas_call(attention_kernel, out_shape=jax.ShapeDtypeStruct((2 * HALF...  9.74 us
    ppermute x3, starting transfers between devices, over_ctx(): return lax.ppermute(value, 'ctx', [(i, i ^ flip) for i in range(ctx)])  7.71 us
    all_to_all x1, starting transfers between devices, shards(): lax.all_to_all(returning.reshape(2 * ctx, CAP, returning.shape[3]), ('ctx...  5.72 us
    ppermute x6, waiting for transfers between devices, over(): return lax.ppermute(value, axis, [(0, 1), (1, 0)])  4.95 us
    pallas_call x1, Pallas kernels, fold(): pl.pallas_call(fold_kernel, out_shape=jax.ShapeDtypeStruct((2, 2, heads /...  4.66 us
    pallas_call x1, Pallas kernels, near_experts(): pl.pallas_call(near_kernel, out_shape=[jax.ShapeDtypeStruct((slots, 2 * u...  4.39 us
    all_to_all x1, waiting for transfers between devices, shards(): lax.all_to_all(returning.reshape(2 * ctx, CAP, returning.shape[3]), ('ctx...  4.38 us
    all_to_all x1, starting transfers between devices, shards(): lax.all_to_all(outgoing, 'ctx', split_axis=0, concat_axis=0, tiled=True)  3.81 us
  transfers between devices with their start and end apart: 11, of which 8 were waited for; matrix products, arithmetic and copies ran while one was open for 2% of the time, Pallas kernels for 37%

profile of v9, /device:TPU:0, one launch (start us, length us, event | category | flops | bytes accessed | tf_op | source)
XLA Modules:
  0.0 56.8 jit_solution(3959065186294575301)
XLA Ops:
  0.6 2.2 %route.1 = (bf16[8,8,1792]{2,1,0:T(8,128)(2,1)}, bf16[128,128]{1,0:T(8,128)(2,1)}, bf16[128,128]{1,0:T(8,128)(2,1)}, bf16[64,576]{1,0:T(8,128)(2,1)}) custom-call(s32[1]{0:T(128)} %bitcast.1.ep_ref, s32[8,128]{1,0:T(8,128)} %bitcast.19, f32[8,128]{1,0:T(8,128)} %bitcast.20, bf16[64,128]{1,0:T(8,128)(2,1)} %bitcast.18, bf16[128,1792]{1,0:T(8,128)(2,1)} %rows_ref.1, ...), custom_call_target="tpu_custom_call" | custom-call | flops 29360128 | bytes 1048576 | tf_op jit(solution)/shard_map/route/pallas_call | solution.py:88
  2.9 4.0 %collective-permute-start = (bf16[1,64,576]{2,1,0:T(8,128)(2,1)}, bf16[1,64,576]{2,1,0:T(8,128)(2,1)S(1)}, u32[]{:S(2)}, u32[]{:S(2)}) collective-permute-start(bf16[1,64,576]{2,1,0:T(8,128)(2,1)} %bitcast.15), channel_id=1, source_target_pairs={{0,16},{4,20},{8,24},{12,28},{16,0},{20,4},{24,8},{28,12},{1,17},{... | collective-permute-start | bytes 221192 | tf_op jit(solution)/shard_map/ppermute | solution.py:516
  6.9 3.8 %all-to-all-start = ((bf16[8,8,1792]{2,1,0:T(8,128)(2,1)}), bf16[8,8,1792]{2,1,0:T(8,128)(2,1)S(1)}, u32[]{:S(2)}, u32[]{:S(2)}) async-start(bf16[8,8,1792]{2,1,0:T(8,128)(2,1)} %get-tuple-element.26), calls=%async_computation | async-start | bytes 458752 | tf_op jit(solution)/shard_map/all_to_all | solution.py:524
  10.7 0.6 %collective-permute-done = bf16[1,64,576]{2,1,0:T(8,128)(2,1)S(1)} collective-permute-done((bf16[1,64,576]{2,1,0:T(8,128)(2,1)}, bf16[1,64,576]{2,1,0:T(8,128)(2,1)S(1)}, u32[]{:S(2)}, u32[]{:S(2)}) %collective-permute-start) | collective-permute-done | bytes 73760 | tf_op jit(solution)/shard_map/ppermute | solution.py:516
  11.3 0.9 %pad_maximum_fusion.2 = bf16[2,64,576]{2,1,0:T(8,128)(2,1)S(1)} fusion(bf16[1,64,576]{2,1,0:T(8,128)(2,1)S(1)} %collective-permute-done, bf16[1,64,576]{2,1,0:T(8,128)(2,1)} %bitcast.16), kind=kLoop, calls=%fused_computation.2 | loop fusion | flops 73728 | bytes 294912 | tf_op jit(solution)/shard_map/concatenate | solution.py:529
  12.2 1.8 %collective-permute-start.1 = (bf16[2,64,576]{2,1,0:T(8,128)(2,1)S(1)}, bf16[2,64,576]{2,1,0:T(8,128)(2,1)S(1)}, u32[]{:S(2)}, u32[]{:S(2)}) collective-permute-start(bf16[2,64,576]{2,1,0:T(8,128)(2,1)S(1)} %pad_maximum_fusion.2), channel_id=1, source_target_pairs={{0,4},{4,0},{8,12},{12,8},{16,20},{20,16},{24,28},{28,24},{1,5},{5... | collective-permute-start | bytes 442376 | tf_op jit(solution)/shard_map/ppermute | solution.py:516
  14.0 0.0 copy-start.3
  14.0 4.7 %fold.1 = bf16[2,2,512,576]{3,2,1,0:T(8,128)(2,1)} custom-call(s32[1]{0:T(128)} %bitcast.own_ref, s32[1024]{0:T(1024)} %positions_ref.3, bf16[128,2048]{1,0:T(8,128)(2,1)} %q_nope_ref, bf16[128,1024]{1,0:T(8,128)(2,1)} %q_rope_ref.1, bf16[512,2048]{1,0:T(8,128)(2,1)} %w_uk_ref.1), custom_call_target="tpu_custom_call" | custom-call | flops 268435456 | bytes 6291456 | tf_op jit(solution)/shard_map/fold/pallas_call | solution.py:301
  18.7 0.6 collective-permute-done.1
  19.2 0.0 copy-done.3
  19.2 0.1 pad_maximum_fusion.1
  19.3 0.0 all-to-all-done
  19.3 0.1 collective-permute-start.3
  19.4 1.6 %collective-permute-start.2 = (bf16[64,1792]{1,0:T(8,128)(2,1)S(1)}, bf16[64,1792]{1,0:T(8,128)(2,1)S(1)}, u32[]{:S(2)}, u32[]{:S(2)}) collective-permute-start(bf16[64,1792]{1,0:T(8,128)(2,1)S(1)} %bitcast.12), channel_id=1, source_target_pairs={{0,2},{2,0},{1,3},{3,1},{4,6},{6,4},{5,7},{7,5},{8,10},{10,8},{9,1... | collective-permute-start | bytes 688136 | tf_op jit(solution)/shard_map/ppermute | solution.py:519
  20.9 1.9 %collective-permute-start.5 = (bf16[4,64,576]{2,1,0:T(8,128)(2,1)S(1)}, bf16[4,64,576]{2,1,0:T(8,128)(2,1)S(1)}, u32[]{:S(2)}, u32[]{:S(2)}) collective-permute-start(bf16[4,64,576]{2,1,0:T(8,128)(2,1)S(1)} %pad_maximum_fusion.1), channel_id=1, source_target_pairs={{0,8},{4,12},{8,0},{12,4},{16,24},{20,28},{24,16},{28,20},{1,9},{5... | collective-permute-start | bytes 884744 | tf_op jit(solution)/shard_map/ppermute | solution.py:516
  22.9 0.0 collective-permute-done.3.core_ref
  22.9 4.4 %near_experts.1 = (f32[64,512]{1,0:T(8,128)S(1)}, bf16[2,1792,256]{2,1,0:T(8,128)(2,1)S(1)}, bf16[2,1792,256]{2,1,0:T(8,128)(2,1)S(1)}, bf16[4,256,1792]{2,1,0:T(8,128)(2,1)S(1)}) custom-call(s32[1]{0:T(128)} %bitcast.1.ep_ref, bf16[64,1792]{1,0:T(8,128)(2,1)S(1)} %bitcast.13, bf16[64,1792]{1,0:T(8,128)(2,1)S(1)} %collective-permute-done.3.core_ref, ...), custom_call_target="tpu_custom_call" | custom-call | flops 234881024 | bytes 11010048 | tf_op jit(solution)/shard_map/near_experts/pallas_call | solution.py:166
  27.3 0.2 collective-permute-done.2.far_ref
  27.4 0.0 collective-permute-start.4
  27.4 1.5 %collective-permute-done.4.core_far_ref = bf16[64,1792]{1,0:T(8,128)(2,1)S(1)} collective-permute-done((bf16[64,1792]{1,0:T(8,128)(2,1)S(1)}, bf16[64,1792]{1,0:T(8,128)(2,1)S(1)}, u32[]{:S(2)}, u32[]{:S(2)}) %collective-permute-start.4) | collective-permute-done | bytes 229408 | tf_op jit(solution)/shard_map/ppermute | solution.py:519
  28.9 1.5 %far_experts.1 = (bf16[64,1792]{1,0:T(8,128)(2,1)S(1)}, bf16[64,1792]{1,0:T(8,128)(2,1)S(1)}, bf16[64,1792]{1,0:T(8,128)(2,1)S(1)}, bf16[64,1792]{1,0:T(8,128)(2,1)S(1)}) custom-call(bf16[64,1792]{1,0:T(8,128)(2,1)S(1)} %collective-permute-done.2.far_ref, bf16[64,1792]{1,0:T(8,128)(2,1)S(1)} %collective-permute-done.4.core_far_ref, ...), custom_call_target="tpu_custom_call" | custom-call | tf_op jit(solution)/shard_map/far_experts/pallas_call | solution.py:213
  30.4 0.0 copy-start.2
  30.4 0.5 collective-permute-done.5
  30.9 0.0 collective-permute-start.6
  30.9 0.1 pad_maximum_fusion.own_keys
  31.0 1.4 %collective-permute-done.6.from_core_far_ref = bf16[64,1792]{1,0:T(8,128)(2,1)S(1)} collective-permute-done((bf16[64,1792]{1,0:T(8,128)(2,1)S(1)}, bf16[64,1792]{1,0:T(8,128)(2,1)S(1)}, u32[]{:S(2)}, u32[]{:S(2)}) %collective-permute-start.6) | collective-permute-done | bytes 229408 | tf_op jit(solution)/shard_map/ppermute | solution.py:519
  32.4 0.1 collective-permute-start.7
  32.5 0.4 collective-permute-start.8
  32.9 1.9 %collective-permute-done.8.from_core_ref = bf16[64,1792]{1,0:T(8,128)(2,1)S(1)} collective-permute-done((bf16[64,1792]{1,0:T(8,128)(2,1)S(1)}, bf16[64,1792]{1,0:T(8,128)(2,1)S(1)}, u32[]{:S(2)}, u32[]{:S(2)}) %collective-permute-start.8) | collective-permute-done | bytes 229408 | tf_op jit(solution)/shard_map/ppermute | solution.py:519
  34.8 0.9 %sum_cores.1 = bf16[8,2,8,1792]{3,2,1,0:T(8,128)(2,1)} custom-call(s32[1]{0:T(128)} %bitcast.1.ep_ref, bf16[64,1792]{1,0:T(8,128)(2,1)S(1)} %get-tuple-element.46.own_ref, bf16[64,1792]{1,0:T(8,128)(2,1)S(1)} %collective-permute-done.8.from_core_ref, bf16[64,1792]{1,0:T(8,128)(2,1)S(1)} %get-tuple-element.48.far_ref, ...), custom_call_target="tpu_custom_call" | custom-call | bytes 1048576 | tf_op jit(solution)/shard_map/sum_cores/pallas_call | solution.py:237
  35.7 5.7 %all-to-all-start.1 = ((bf16[16,8,1792]{2,1,0:T(8,128)(2,1)}), bf16[16,8,1792]{2,1,0:T(8,128)(2,1)S(1)}, u32[]{:S(2)}, u32[]{:S(2)}) async-start(bf16[16,8,1792]{2,1,0:T(8,128)(2,1)} %bitcast.8), calls=%async_computation.1 | async-start | bytes 917504 | tf_op jit(solution)/shard_map/all_to_all | solution.py:551
  41.4 0.0 copy-start
  41.4 0.0 copy-start.1
  41.4 0.0 collective-permute-done.7.core_keys
  41.4 0.0 copy-done.2
  41.4 9.7 %attention.1 = bf16[128,2048]{1,0:T(8,128)(2,1)} custom-call(s32[1]{0:T(128)} %bitcast.own_ref, s32[1]{0:T(128)} %bitcast.1.ep_ref, s32[1024]{0:T(1024)S(1)} %copy-done.2, bf16[2,1024,576]{2,1,0:T(8,128)(2,1)} %bitcast.14, bf16[512,2048]{1,0:T(8,128)(2,1)} %w_uv_hbm.1, bf16[8,64,576]{2,1,0:T(8,128)(2,1)S(1)} %pad_maximum_fusion.own_keys, ...), custom_call_target="tpu_custom_call" | custom-call | flops 14495514624 | bytes 8388608 | tf_op jit(solution)/shard_map/attention/pallas_call | solution.py:472
  51.2 4.4 %all-to-all-done.1 = bf16[16,8,1792]{2,1,0:T(8,128)(2,1)S(1)} async-done(((bf16[16,8,1792]{2,1,0:T(8,128)(2,1)}), bf16[16,8,1792]{2,1,0:T(8,128)(2,1)S(1)}, u32[]{:S(2)}, u32[]{:S(2)}) %all-to-all-start.1) | async-done | bytes 458784 | tf_op jit(solution)/shard_map/all_to_all | solution.py:551
  55.6 0.0 copy-done
  55.6 0.0 copy-done.1
  55.6 1.2 %combine.1 = bf16[128,1792]{1,0:T(8,128)(2,1)} custom-call(bf16[128,128]{1,0:T(8,128)(2,1)S(1)} %copy-done, bf16[128,128]{1,0:T(8,128)(2,1)S(1)} %copy-done.1, bf16[128,1792]{1,0:T(8,128)(2,1)S(1)} %bitcast.10), custom_call_target="tpu_custom_call" | custom-call | flops 117440512 | bytes 1048576 | tf_op jit(solution)/shard_map/combine/pallas_call | solution.py:260
Async XLA Ops:
  2.9 8.4 %collective-permute-start = (bf16[1,64,576]{2,1,0:T(8,128)(2,1)}, bf16[1,64,576]{2,1,0:T(8,128)(2,1)S(1)}, u32[]{:S(2)}, u32[]{:S(2)}) collective-permute-start(bf16[1,64,576]{2,1,0:T(8,128)(2,1)} %bitcast.15), channel_id=1, source_target_pairs={{0,16},{4,20},{8,24},{12,28},{16,0},{20,4},{24,8},{28,12},{1,17},{... | collective-permute-start | bytes 221192 | tf_op jit(solution)/shard_map/ppermute | solution.py:516
  6.9 12.4 %all-to-all-start = ((bf16[8,8,1792]{2,1,0:T(8,128)(2,1)}), bf16[8,8,1792]{2,1,0:T(8,128)(2,1)S(1)}, u32[]{:S(2)}, u32[]{:S(2)}) async-start(bf16[8,8,1792]{2,1,0:T(8,128)(2,1)} %get-tuple-element.26), calls=%async_computation | async-start | bytes 458752 | tf_op jit(solution)/shard_map/all_to_all | solution.py:524
  12.2 7.0 %collective-permute-start.1 = (bf16[2,64,576]{2,1,0:T(8,128)(2,1)S(1)}, bf16[2,64,576]{2,1,0:T(8,128)(2,1)S(1)}, u32[]{:S(2)}, u32[]{:S(2)}) collective-permute-start(bf16[2,64,576]{2,1,0:T(8,128)(2,1)S(1)} %pad_maximum_fusion.2), channel_id=1, source_target_pairs={{0,4},{4,0},{8,12},{12,8},{16,20},{20,16},{24,28},{28,24},{1,5},{5... | collective-permute-start | bytes 442376 | tf_op jit(solution)/shard_map/ppermute | solution.py:516
  14.0 5.2 %copy-start.3 = (bf16[64,576]{1,0:T(8,128)(2,1)S(1)}, bf16[64,576]{1,0:T(8,128)(2,1)}, u32[]{:S(2)}) copy-start(bf16[64,576]{1,0:T(8,128)(2,1)} %get-tuple-element.28) | copy-start | bytes 221188
  19.3 3.5 %collective-permute-start.3 = (bf16[64,1792]{1,0:T(8,128)(2,1)S(1)}, bf16[64,1792]{1,0:T(8,128)(2,1)S(1)}, u32[]{:S(2)}, u32[]{:S(2)}) collective-permute-start(bf16[64,1792]{1,0:T(8,128)(2,1)S(1)} %bitcast.11), channel_id=1, source_target_pairs={{0,1},{1,0},{2,3},{3,2},{4,5},{5,4},{6,7},{7,6},{8,9},{9,8},{10,11... | collective-permute-start | bytes 688136 | tf_op jit(solution)/shard_map/ppermute | solution.py:519
  19.4 8.0 %collective-permute-start.2 = (bf16[64,1792]{1,0:T(8,128)(2,1)S(1)}, bf16[64,1792]{1,0:T(8,128)(2,1)S(1)}, u32[]{:S(2)}, u32[]{:S(2)}) collective-permute-start(bf16[64,1792]{1,0:T(8,128)(2,1)S(1)} %bitcast.12), channel_id=1, source_target_pairs={{0,2},{2,0},{1,3},{3,1},{4,6},{6,4},{5,7},{7,5},{8,10},{10,8},{9,1... | collective-permute-start | bytes 688136 | tf_op jit(solution)/shard_map/ppermute | solution.py:519
  20.9 9.9 %collective-permute-start.5 = (bf16[4,64,576]{2,1,0:T(8,128)(2,1)S(1)}, bf16[4,64,576]{2,1,0:T(8,128)(2,1)S(1)}, u32[]{:S(2)}, u32[]{:S(2)}) collective-permute-start(bf16[4,64,576]{2,1,0:T(8,128)(2,1)S(1)} %pad_maximum_fusion.1), channel_id=1, source_target_pairs={{0,8},{4,12},{8,0},{12,4},{16,24},{20,28},{24,16},{28,20},{1,9},{5... | collective-permute-start | bytes 884744 | tf_op jit(solution)/shard_map/ppermute | solution.py:516
  27.4 1.5 %collective-permute-start.4 = (bf16[64,1792]{1,0:T(8,128)(2,1)S(1)}, bf16[64,1792]{1,0:T(8,128)(2,1)S(1)}, u32[]{:S(2)}, u32[]{:S(2)}) collective-permute-start(bf16[64,1792]{1,0:T(8,128)(2,1)S(1)} %collective-permute-done.2.far_ref), channel_id=1, source_target_pairs={{0,1},{1,0},{2,3},{3,2},{4,5},{5,4},{6,7},{7,6},{8,9},{9,8},{10,11... | collective-permute-start | bytes 688136 | tf_op jit(solution)/shard_map/ppermute | solution.py:519
  30.4 11.1 %copy-start.2 = (s32[1024]{0:T(1024)S(1)}, s32[1024]{0:T(1024)}, u32[]{:S(2)}) copy-start(s32[1024]{0:T(1024)} %positions_ref.3) | copy-start | bytes 12292
  30.9 1.5 %collective-permute-start.6 = (bf16[64,1792]{1,0:T(8,128)(2,1)S(1)}, bf16[64,1792]{1,0:T(8,128)(2,1)S(1)}, u32[]{:S(2)}, u32[]{:S(2)}) collective-permute-start(bf16[64,1792]{1,0:T(8,128)(2,1)S(1)} %get-tuple-element.42), channel_id=1, source_target_pairs={{0,1},{1,0},{2,3},{3,2},{4,5},{5,4},{6,7},{7,6},{8,9},{9,8},{10,11... | collective-permute-start | bytes 688136 | tf_op jit(solution)/shard_map/ppermute | solution.py:519
  32.4 9.0 %collective-permute-start.7 = (bf16[8,64,576]{2,1,0:T(8,128)(2,1)S(1)}, bf16[8,64,576]{2,1,0:T(8,128)(2,1)S(1)}, u32[]{:S(2)}, u32[]{:S(2)}) collective-permute-start(bf16[8,64,576]{2,1,0:T(8,128)(2,1)S(1)} %pad_maximum_fusion.own_keys), channel_id=1, source_target_pairs={{0,1},{1,0},{2,3},{3,2},{4,5},{5,4},{6,7},{7,6},{8,9},{9,8},{10,11... | collective-permute-start | bytes 1769480 | tf_op jit(solution)/shard_map/ppermute | solution.py:519
  32.5 2.3 %collective-permute-start.8 = (bf16[64,1792]{1,0:T(8,128)(2,1)S(1)}, bf16[64,1792]{1,0:T(8,128)(2,1)S(1)}, u32[]{:S(2)}, u32[]{:S(2)}) collective-permute-start(bf16[64,1792]{1,0:T(8,128)(2,1)S(1)} %get-tuple-element.47), channel_id=1, source_target_pairs={{0,1},{1,0},{2,3},{3,2},{4,5},{5,4},{6,7},{7,6},{8,9},{9,8},{10,11... | collective-permute-start | bytes 688136 | tf_op jit(solution)/shard_map/ppermute | solution.py:519
  35.7 19.9 %all-to-all-start.1 = ((bf16[16,8,1792]{2,1,0:T(8,128)(2,1)}), bf16[16,8,1792]{2,1,0:T(8,128)(2,1)S(1)}, u32[]{:S(2)}, u32[]{:S(2)}) async-start(bf16[16,8,1792]{2,1,0:T(8,128)(2,1)} %bitcast.8), calls=%async_computation.1 | async-start | bytes 917504 | tf_op jit(solution)/shard_map/all_to_all | solution.py:551
  41.4 14.2 %copy-start = (bf16[128,128]{1,0:T(8,128)(2,1)S(1)}, bf16[128,128]{1,0:T(8,128)(2,1)}, u32[]{:S(2)}) copy-start(bf16[128,128]{1,0:T(8,128)(2,1)} %get-tuple-element.44.high_ref) | copy-start | bytes 98308
  41.4 14.2 %copy-start.1 = (bf16[128,128]{1,0:T(8,128)(2,1)S(1)}, bf16[128,128]{1,0:T(8,128)(2,1)}, u32[]{:S(2)}) copy-start(bf16[128,128]{1,0:T(8,128)(2,1)} %get-tuple-element.45.low_ref) | copy-start | bytes 98308

commit v10 on v9

--- a/solution.py
+++ b/solution.py
@@ -191,7 +191,7 @@
 
 
 def far_kernel(
-    far_ref, core_far_ref, sums_ref, gate, up, down, own_out, core_out, far_out, core_far_out
+    far_ref, core_far_ref, sums_ref, gate, up, down, kept_out, sent_out
 ):
     units = gate.shape[2]
     gate_sum, up_sum = sums_ref[:, :units], sums_ref[:, units:]
@@ -200,9 +200,9 @@
         gate_sum = gate_sum + jnp.dot(rows, gate[index], preferred_element_type=jnp.float32)
         up_sum = up_sum + jnp.dot(rows, up[index], preferred_element_type=jnp.float32)
     hidden = (gate_sum / (1.0 + jnp.exp(-gate_sum)) * up_sum).astype(jnp.bfloat16)
-    outs = (own_out, core_out, far_out, core_far_out)
-    for flip in (3, 1, 2, 0):
-        outs[flip][...] = jnp.dot(
+    for flip in range(4):
+        out = sent_out if flip % 2 else kept_out
+        out[flip // 2] = jnp.dot(
             hidden, down[flip], preferred_element_type=jnp.float32
         ).astype(jnp.bfloat16)
 
@@ -212,37 +212,35 @@
     units = gate.shape[2]
     return pl.pallas_call(
         far_kernel,
-        out_shape=[jax.ShapeDtypeStruct((slots, features), jnp.bfloat16)] * 4,
+        out_shape=[jax.ShapeDtypeStruct((2, slots, features), jnp.bfloat16)] * 2,
         in_specs=[VMEM_SPEC] * 6,
-        out_specs=[VMEM_SPEC] * 4,
+        out_specs=[VMEM_SPEC] * 2,
         compiler_params=pltpu.CompilerParams(vmem_limit_bytes=24 * MIB),
         cost_estimate=pl.CostEstimate(flops=0, bytes_accessed=0, transcendentals=0),
         name="far_experts",
     )(far, core_far, sums, gate, up, down)
 
 
-def sum_kernel(ep_ref, own_ref, from_core_ref, far_ref, from_core_far_ref, out_ref):
+def sum_kernel(ep_ref, kept_ref, received_ref, out_ref):
     my_x = ep_ref[0] // 2
-    for flip, (mine, other) in enumerate(
-        ((own_ref, from_core_ref), (far_ref, from_core_far_ref))
-    ):
-        total = mine[...].astype(jnp.float32) + other[...].astype(jnp.float32)
+    for flip in range(2):
+        total = kept_ref[flip].astype(jnp.float32) + received_ref[flip].astype(jnp.float32)
         for index in range(out_ref.shape[0]):
             block = total[index * CAP : (index + 1) * CAP].astype(jnp.bfloat16)
             out_ref[index, my_x ^ flip] = block
 
 
-def sum_cores(ep, own, from_core, far, from_core_far, ctx):
-    features = own.shape[1]
+def sum_cores(ep, kept, received, ctx):
+    features = kept.shape[2]
     return pl.pallas_call(
         sum_kernel,
         out_shape=jax.ShapeDtypeStruct((ctx, 2, CAP, features), jnp.bfloat16),
-        in_specs=[SMEM_SPEC] + [VMEM_SPEC] * 4,
+        in_specs=[SMEM_SPEC] + [VMEM_SPEC] * 2,
         out_specs=VMEM_SPEC,
         compiler_params=pltpu.CompilerParams(vmem_limit_bytes=16 * MIB),
         cost_estimate=pl.CostEstimate(flops=0, bytes_accessed=MIB, transcendentals=0),
         name="sum_cores",
-    )(ep, own, from_core, far, from_core_far)
+    )(ep, kept, received)
 
 
 def combine_kernel(high_ref, low_ref, returned_ref, out_ref):
@@ -329,8 +327,10 @@
     positions_ref,
     queries_hbm,
     w_uv_hbm,
-    own_keys,
-    core_keys,
+    own_near,
+    own_far,
+    core_near,
+    core_far,
     out_ref,
     keys,
     queries,
@@ -347,12 +347,14 @@
     w_uv_copy = pltpu.make_async_copy(w_uv_hbm, w_uv, semaphores.at[2])
     for copy in (query_copies[0], w_uv_copy, query_copies[1]):
         copy.start()
-    blocks = own_keys.shape[0]
+    blocks = own_near.shape[0]
     my_ctx, my_ep = own_ref[0], ep_ref[0]
-    for flip, source in enumerate((own_keys, core_keys)):
+    flips = gather_order(2 * blocks)
+    sources = ((own_near, 0, 0), (own_far, 0, 1), (core_near, 1, 0), (core_far, 1, 1))
+    for source, flip, last in sources:
         for block in range(blocks):
-            source_ctx = my_ctx
-            for bit, step in enumerate(gather_order(blocks)):
+            source_ctx = my_ctx ^ flips[-1] if last else my_ctx
+            for bit, step in enumerate(flips[:-1]):
                 if block >> bit & 1:
                     source_ctx = source_ctx ^ step
             start = source_ctx * (2 * HALF) + ((my_ep % 2) ^ flip) * HALF
@@ -464,15 +466,15 @@
         out_ref[low_rows, columns] = value[HALF:]
 
 
-def attend(own, ep, positions, queries, w_uv, own_keys, core_keys):
+def attend(own, ep, positions, queries, w_uv, *pieces):
     latent_width, columns = w_uv.shape
     key_count = positions.shape[0]
-    width = own_keys.shape[-1]
+    width = pieces[0].shape[-1]
     rows = queries.shape[1]
     return pl.pallas_call(
         attention_kernel,
         out_shape=jax.ShapeDtypeStruct((2 * HALF, columns), jnp.bfloat16),
-        in_specs=[SMEM_SPEC] * 3 + [HBM_SPEC] * 2 + [VMEM_SPEC] * 2,
+        in_specs=[SMEM_SPEC] * 3 + [HBM_SPEC] * 2 + [VMEM_SPEC] * 4,
         out_specs=VMEM_SPEC,
         scratch_shapes=[
             VMEM((key_count, width), jnp.bfloat16),
@@ -490,7 +492,7 @@
             transcendentals=rows * key_count,
         ),
         name="attention",
-    )(own, ep, positions, queries, w_uv, own_keys, core_keys)
+    )(own, ep, positions, queries, w_uv, *pieces)
 
 
 def shards(
@@ -534,20 +536,17 @@
     own = arrived.reshape(ctx * CAP, arrived.shape[2])
     far = over(own, "x")
     core = over(own, "core")
-    received = over_ctx(own_keys, flips[-1])
+    far_keys = over_ctx(own_keys, flips[-1])
     sums, far_gate, far_up, down = near_experts(ep, own, core, w_gate, w_up, w_down)
-    far, sums = lax.optimization_barrier((far, sums))
+    core_keys = over(own_keys, "core")
+    far, sums, core_keys = lax.optimization_barrier((far, sums, core_keys))
     core_far = over(far, "core")
-    own_out, core_out, far_out, core_far_out = far_experts(
-        far, core_far, sums, far_gate, far_up, down
-    )
-    core_far_out, received = lax.optimization_barrier((core_far_out, received))
-    from_core_far = over(core_far_out, "core")
-    from_core = over(core_out, "core")
-    own_keys = jnp.concatenate([own_keys, received], axis=0)
-    own_keys, from_core_far = lax.optimization_barrier((own_keys, from_core_far))
-    core_keys = over(own_keys, "core")
-    returning = sum_cores(ep, own_out, from_core, far_out, from_core_far, ctx)
+    kept, sent = far_experts(far, core_far, sums, far_gate, far_up, down)
+    sent, far_keys = lax.optimization_barrier((sent, far_keys))
+    received = over(sent, "core")
+    far_keys, received = lax.optimization_barrier((far_keys, received))
+    core_far_keys = over(far_keys, "core")
+    returning = sum_cores(ep, kept, received, ctx)
     returned = lax.all_to_all(
         returning.reshape(2 * ctx, CAP, returning.shape[3]),
         ("ctx", "x"),
@@ -555,7 +554,9 @@
         concat_axis=0,
         tiled=True,
     )
-    attention = attend(me, ep, positions, queries, w_uv, own_keys, core_keys)
+    attention = attend(
+        me, ep, positions, queries, w_uv, own_keys, far_keys, core_keys, core_far_keys
+    )
     moe_out = combine(high, low, returned.reshape(2 * ctx * CAP, returned.shape[2]))
     return (attention, moe_out)
 

time: 57.2 us -> 55.5 us (0.970)
  waiting for transfers between devices: 11 us -> 8.69 us
    ppermute x6, waiting for transfers between devices: 4.95 us -> 3.29 us  [over(): return lax.ppermute(value, axis, [(0, 1), (1, 0)])]
  transfers between devices with their start and end apart: 11 -> 11, of which waited for: 8 -> 6; matrix products, arithmetic and copies ran while one was open for 2% -> 2% of each run, Pallas kernels for 37% -> 39%
where the time goes in v10:
time: 55.5 us; the launch traced here: 55.1 us
  Pallas kernels  25.1 us (45%)
  starting transfers between devices  19.5 us (35%)
  waiting for transfers between devices  8.69 us (16%)
  other arithmetic  0.97 us (2%)
  between operations  0.76 us (1%)
    pallas_call x1, Pallas kernels, attend(): pl.pallas_call(attention_kernel, out_shape=jax.ShapeDtypeStruct((2 * HALF...  10.3 us
    ppermute x3, starting transfers between devices, over_ctx(): return lax.ppermute(value, 'ctx', [(i, i ^ flip) for i in range(ctx)])  7.71 us
    all_to_all x1, starting transfers between devices, shards(): lax.all_to_all(returning.reshape(2 * ctx, CAP, returning.shape[3]), ('ctx...  5.72 us
    pallas_call x1, Pallas kernels, fold(): pl.pallas_call(fold_kernel, out_shape=jax.ShapeDtypeStruct((2, 2, heads /...  4.66 us
    pallas_call x1, Pallas kernels, near_experts(): pl.pallas_call(near_kernel, out_shape=[jax.ShapeDtypeStruct((slots, 2 * u...  4.4 us
    all_to_all x1, waiting for transfers between devices, shards(): lax.all_to_all(returning.reshape(2 * ctx, CAP, returning.shape[3]), ('ctx...  4.02 us
    all_to_all x1, starting transfers between devices, shards(): lax.all_to_all(outgoing, 'ctx', split_axis=0, concat_axis=0, tiled=True)  3.81 us
    ppermute x6, waiting for transfers between devices, over(): return lax.ppermute(value, axis, [(0, 1), (1, 0)])  3.29 us
  transfers between devices with their start and end apart: 11, of which 6 were waited for; matrix products, arithmetic and copies ran while one was open for 2% of the time, Pallas kernels for 39%

profile of v10, /device:TPU:0, one launch (start us, length us, event | category | flops | bytes accessed | tf_op | source)
XLA Modules:
  0.0 55.1 jit_solution(3327060763850490367)
XLA Ops:
  0.6 2.2 %route.1 = (bf16[8,8,1792]{2,1,0:T(8,128)(2,1)}, bf16[128,128]{1,0:T(8,128)(2,1)}, bf16[128,128]{1,0:T(8,128)(2,1)}, bf16[64,576]{1,0:T(8,128)(2,1)}) custom-call(s32[1]{0:T(128)} %bitcast.1.ep_ref, s32[8,128]{1,0:T(8,128)} %bitcast.19, f32[8,128]{1,0:T(8,128)} %bitcast.20, bf16[64,128]{1,0:T(8,128)(2,1)} %bitcast.18, bf16[128,1792]{1,0:T(8,128)(2,1)} %rows_ref.1, ...), custom_call_target="tpu_custom_call" | custom-call | flops 29360128 | bytes 1048576 | tf_op jit(solution)/shard_map/route/pallas_call | solution.py:88
  2.9 4.0 %collective-permute-start = (bf16[1,64,576]{2,1,0:T(8,128)(2,1)}, bf16[1,64,576]{2,1,0:T(8,128)(2,1)S(1)}, u32[]{:S(2)}, u32[]{:S(2)}) collective-permute-start(bf16[1,64,576]{2,1,0:T(8,128)(2,1)} %bitcast.15), channel_id=1, source_target_pairs={{0,16},{4,20},{8,24},{12,28},{16,0},{20,4},{24,8},{28,12},{1,17},{... | collective-permute-start | bytes 221192 | tf_op jit(solution)/shard_map/ppermute | solution.py:518
  6.9 3.8 %all-to-all-start = ((bf16[8,8,1792]{2,1,0:T(8,128)(2,1)}), bf16[8,8,1792]{2,1,0:T(8,128)(2,1)S(1)}, u32[]{:S(2)}, u32[]{:S(2)}) async-start(bf16[8,8,1792]{2,1,0:T(8,128)(2,1)} %get-tuple-element.25), calls=%async_computation | async-start | bytes 458752 | tf_op jit(solution)/shard_map/all_to_all | solution.py:526
  10.7 0.6 %collective-permute-done = bf16[1,64,576]{2,1,0:T(8,128)(2,1)S(1)} collective-permute-done((bf16[1,64,576]{2,1,0:T(8,128)(2,1)}, bf16[1,64,576]{2,1,0:T(8,128)(2,1)S(1)}, u32[]{:S(2)}, u32[]{:S(2)}) %collective-permute-start) | collective-permute-done | bytes 73760 | tf_op jit(solution)/shard_map/ppermute | solution.py:518
  11.3 0.9 %pad_maximum_fusion.1 = bf16[2,64,576]{2,1,0:T(8,128)(2,1)S(1)} fusion(bf16[1,64,576]{2,1,0:T(8,128)(2,1)S(1)} %collective-permute-done, bf16[1,64,576]{2,1,0:T(8,128)(2,1)} %bitcast.16), kind=kLoop, calls=%fused_computation.1 | loop fusion | flops 73728 | bytes 294912 | tf_op jit(solution)/shard_map/concatenate | solution.py:531
  12.2 1.8 %collective-permute-start.1 = (bf16[2,64,576]{2,1,0:T(8,128)(2,1)S(1)}, bf16[2,64,576]{2,1,0:T(8,128)(2,1)S(1)}, u32[]{:S(2)}, u32[]{:S(2)}) collective-permute-start(bf16[2,64,576]{2,1,0:T(8,128)(2,1)S(1)} %pad_maximum_fusion.1), channel_id=1, source_target_pairs={{0,4},{4,0},{8,12},{12,8},{16,20},{20,16},{24,28},{28,24},{1,5},{5... | collective-permute-start | bytes 442376 | tf_op jit(solution)/shard_map/ppermute | solution.py:518
  14.0 0.0 copy-start.3
  14.0 4.7 %fold.1 = bf16[2,2,512,576]{3,2,1,0:T(8,128)(2,1)} custom-call(s32[1]{0:T(128)} %bitcast.own_ref, s32[1024]{0:T(1024)} %positions_ref.3, bf16[128,2048]{1,0:T(8,128)(2,1)} %q_nope_ref, bf16[128,1024]{1,0:T(8,128)(2,1)} %q_rope_ref.1, bf16[512,2048]{1,0:T(8,128)(2,1)} %w_uk_ref.1), custom_call_target="tpu_custom_call" | custom-call | flops 268435456 | bytes 6291456 | tf_op jit(solution)/shard_map/fold/pallas_call | solution.py:299
  18.7 0.6 %collective-permute-done.1 = bf16[2,64,576]{2,1,0:T(8,128)(2,1)S(1)} collective-permute-done((bf16[2,64,576]{2,1,0:T(8,128)(2,1)S(1)}, bf16[2,64,576]{2,1,0:T(8,128)(2,1)S(1)}, u32[]{:S(2)}, u32[]{:S(2)}) %collective-permute-start.1) | collective-permute-done | bytes 147488 | tf_op jit(solution)/shard_map/ppermute | solution.py:518
  19.2 0.0 copy-done.3
  19.2 0.1 pad_maximum_fusion.own_near
  19.3 0.0 all-to-all-done
  19.3 0.1 collective-permute-start.4
  19.4 0.5 collective-permute-start.3
  19.9 1.5 %collective-permute-start.2 = (bf16[64,1792]{1,0:T(8,128)(2,1)S(1)}, bf16[64,1792]{1,0:T(8,128)(2,1)S(1)}, u32[]{:S(2)}, u32[]{:S(2)}) collective-permute-start(bf16[64,1792]{1,0:T(8,128)(2,1)S(1)} %bitcast.12), channel_id=1, source_target_pairs={{0,2},{2,0},{1,3},{3,1},{4,6},{6,4},{5,7},{7,5},{8,10},{10,8},{9,1... | collective-permute-start | bytes 688136 | tf_op jit(solution)/shard_map/ppermute | solution.py:521
  21.4 1.9 %collective-permute-start.6 = (bf16[4,64,576]{2,1,0:T(8,128)(2,1)S(1)}, bf16[4,64,576]{2,1,0:T(8,128)(2,1)S(1)}, u32[]{:S(2)}, u32[]{:S(2)}) collective-permute-start(bf16[4,64,576]{2,1,0:T(8,128)(2,1)S(1)} %pad_maximum_fusion.own_near), channel_id=1, source_target_pairs={{0,8},{4,12},{8,0},{12,4},{16,24},{20,28},{24,16},{28,20},{1,9},{5... | collective-permute-start | bytes 884744 | tf_op jit(solution)/shard_map/ppermute | solution.py:518
  23.3 0.0 collective-permute-done.3.core_ref
  23.3 4.4 %near_experts.1 = (f32[64,512]{1,0:T(8,128)S(1)}, bf16[2,1792,256]{2,1,0:T(8,128)(2,1)S(1)}, bf16[2,1792,256]{2,1,0:T(8,128)(2,1)S(1)}, bf16[4,256,1792]{2,1,0:T(8,128)(2,1)S(1)}) custom-call(s32[1]{0:T(128)} %bitcast.1.ep_ref, bf16[64,1792]{1,0:T(8,128)(2,1)S(1)} %bitcast.13, bf16[64,1792]{1,0:T(8,128)(2,1)S(1)} %collective-permute-done.3.core_ref, ...), custom_call_target="tpu_custom_call" | custom-call | flops 234881024 | bytes 11010048 | tf_op jit(solution)/shard_map/near_experts/pallas_call | solution.py:166
  27.7 0.0 collective-permute-done.2.far_ref
  27.7 0.0 collective-permute-done.4.core_near
  27.7 0.1 collective-permute-start.5
  27.8 1.5 %collective-permute-done.5.core_far_ref = bf16[64,1792]{1,0:T(8,128)(2,1)S(1)} collective-permute-done((bf16[64,1792]{1,0:T(8,128)(2,1)S(1)}, bf16[64,1792]{1,0:T(8,128)(2,1)S(1)}, u32[]{:S(2)}, u32[]{:S(2)}) %collective-permute-start.5) | collective-permute-done | bytes 229408 | tf_op jit(solution)/shard_map/ppermute | solution.py:521
  29.3 0.0 copy-start.2
  29.3 1.5 %far_experts.1 = (bf16[2,64,1792]{2,1,0:T(8,128)(2,1)S(1)}, bf16[2,64,1792]{2,1,0:T(8,128)(2,1)S(1)}) custom-call(bf16[64,1792]{1,0:T(8,128)(2,1)S(1)} %collective-permute-done.2.far_ref, bf16[64,1792]{1,0:T(8,128)(2,1)S(1)} %collective-permute-done.5.core_far_ref, f32[64,512]{1,0:T(8,128)S(1)} %get-tuple-element.35.sums_ref, ...), custom_call_target="tpu_custom_call" | custom-call | tf_op jit(solution)/shard_map/far_experts/pallas_call | solution.py:213
  30.8 0.2 collective-permute-done.6.own_far
  31.0 0.0 collective-permute-start.7
  31.0 1.8 %collective-permute-done.7.received_ref = bf16[2,64,1792]{2,1,0:T(8,128)(2,1)S(1)} collective-permute-done((bf16[2,64,1792]{2,1,0:T(8,128)(2,1)S(1)}, bf16[2,64,1792]{2,1,0:T(8,128)(2,1)S(1)}, u32[]{:S(2)}, u32[]{:S(2)}) %collective-permute-start.7) | collective-permute-done | bytes 458784 | tf_op jit(solution)/shard_map/ppermute | solution.py:521
  32.8 0.1 collective-permute-start.8
  32.9 0.9 %sum_cores.1 = bf16[8,2,8,1792]{3,2,1,0:T(8,128)(2,1)} custom-call(s32[1]{0:T(128)} %bitcast.1.ep_ref, bf16[2,64,1792]{2,1,0:T(8,128)(2,1)S(1)} %get-tuple-element.46.kept_ref, bf16[2,64,1792]{2,1,0:T(8,128)(2,1)S(1)} %collective-permute-done.7.received_ref), custom_call_target="tpu_custom_call" | custom-call | bytes 1048576 | tf_op jit(solution)/shard_map/sum_cores/pallas_call | solution.py:235
  33.8 5.7 %all-to-all-start.1 = ((bf16[16,8,1792]{2,1,0:T(8,128)(2,1)}), bf16[16,8,1792]{2,1,0:T(8,128)(2,1)S(1)}, u32[]{:S(2)}, u32[]{:S(2)}) async-start(bf16[16,8,1792]{2,1,0:T(8,128)(2,1)} %bitcast.8), calls=%async_computation.1 | async-start | bytes 917504 | tf_op jit(solution)/shard_map/all_to_all | solution.py:550
  39.5 0.0 copy-start
  39.5 0.0 copy-start.1
  39.5 0.0 collective-permute-done.8.core_far
  39.5 0.0 copy-done.2
  39.6 10.3 %attention.1 = bf16[128,2048]{1,0:T(8,128)(2,1)} custom-call(s32[1]{0:T(128)} %bitcast.own_ref, s32[1]{0:T(128)} %bitcast.1.ep_ref, s32[1024]{0:T(1024)S(1)} %copy-done.2, bf16[2,1024,576]{2,1,0:T(8,128)(2,1)} %bitcast.14, bf16[512,2048]{1,0:T(8,128)(2,1)} %w_uv_hbm.1, bf16[4,64,576]{2,1,0:T(8,128)(2,1)S(1)} %pad_maximum_fusion.own_near, ...), custom_call_target="tpu_custom_call" | custom-call | flops 14495514624 | bytes 8388608 | tf_op jit(solution)/shard_map/attention/pallas_call | solution.py:474
  49.8 4.0 %all-to-all-done.1 = bf16[16,8,1792]{2,1,0:T(8,128)(2,1)S(1)} async-done(((bf16[16,8,1792]{2,1,0:T(8,128)(2,1)}), bf16[16,8,1792]{2,1,0:T(8,128)(2,1)S(1)}, u32[]{:S(2)}, u32[]{:S(2)}) %all-to-all-start.1) | async-done | bytes 458784 | tf_op jit(solution)/shard_map/all_to_all | solution.py:550
  53.9 0.0 copy-done
  53.9 0.0 copy-done.1
  53.9 1.2 %combine.1 = bf16[128,1792]{1,0:T(8,128)(2,1)} custom-call(bf16[128,128]{1,0:T(8,128)(2,1)S(1)} %copy-done, bf16[128,128]{1,0:T(8,128)(2,1)S(1)} %copy-done.1, bf16[128,1792]{1,0:T(8,128)(2,1)S(1)} %bitcast.10), custom_call_target="tpu_custom_call" | custom-call | flops 117440512 | bytes 1048576 | tf_op jit(solution)/shard_map/combine/pallas_call | solution.py:258
Async XLA Ops:
  2.9 8.4 %collective-permute-start = (bf16[1,64,576]{2,1,0:T(8,128)(2,1)}, bf16[1,64,576]{2,1,0:T(8,128)(2,1)S(1)}, u32[]{:S(2)}, u32[]{:S(2)}) collective-permute-start(bf16[1,64,576]{2,1,0:T(8,128)(2,1)} %bitcast.15), channel_id=1, source_target_pairs={{0,16},{4,20},{8,24},{12,28},{16,0},{20,4},{24,8},{28,12},{1,17},{... | collective-permute-start | bytes 221192 | tf_op jit(solution)/shard_map/ppermute | solution.py:518
  6.9 12.4 %all-to-all-start = ((bf16[8,8,1792]{2,1,0:T(8,128)(2,1)}), bf16[8,8,1792]{2,1,0:T(8,128)(2,1)S(1)}, u32[]{:S(2)}, u32[]{:S(2)}) async-start(bf16[8,8,1792]{2,1,0:T(8,128)(2,1)} %get-tuple-element.25), calls=%async_computation | async-start | bytes 458752 | tf_op jit(solution)/shard_map/all_to_all | solution.py:526
  12.2 7.0 %collective-permute-start.1 = (bf16[2,64,576]{2,1,0:T(8,128)(2,1)S(1)}, bf16[2,64,576]{2,1,0:T(8,128)(2,1)S(1)}, u32[]{:S(2)}, u32[]{:S(2)}) collective-permute-start(bf16[2,64,576]{2,1,0:T(8,128)(2,1)S(1)} %pad_maximum_fusion.1), channel_id=1, source_target_pairs={{0,4},{4,0},{8,12},{12,8},{16,20},{20,16},{24,28},{28,24},{1,5},{5... | collective-permute-start | bytes 442376 | tf_op jit(solution)/shard_map/ppermute | solution.py:518
  14.0 5.2 %copy-start.3 = (bf16[64,576]{1,0:T(8,128)(2,1)S(1)}, bf16[64,576]{1,0:T(8,128)(2,1)}, u32[]{:S(2)}) copy-start(bf16[64,576]{1,0:T(8,128)(2,1)} %get-tuple-element.27) | copy-start | bytes 221188
  19.3 8.4 %collective-permute-start.4 = (bf16[4,64,576]{2,1,0:T(8,128)(2,1)S(1)}, bf16[4,64,576]{2,1,0:T(8,128)(2,1)S(1)}, u32[]{:S(2)}, u32[]{:S(2)}) collective-permute-start(bf16[4,64,576]{2,1,0:T(8,128)(2,1)S(1)} %pad_maximum_fusion.own_near), channel_id=1, source_target_pairs={{0,1},{1,0},{2,3},{3,2},{4,5},{5,4},{6,7},{7,6},{8,9},{9,8},{10,11... | collective-permute-start | bytes 884744 | tf_op jit(solution)/shard_map/ppermute | solution.py:521
  19.4 3.9 %collective-permute-start.3 = (bf16[64,1792]{1,0:T(8,128)(2,1)S(1)}, bf16[64,1792]{1,0:T(8,128)(2,1)S(1)}, u32[]{:S(2)}, u32[]{:S(2)}) collective-permute-start(bf16[64,1792]{1,0:T(8,128)(2,1)S(1)} %bitcast.11), channel_id=1, source_target_pairs={{0,1},{1,0},{2,3},{3,2},{4,5},{5,4},{6,7},{7,6},{8,9},{9,8},{10,11... | collective-permute-start | bytes 688136 | tf_op jit(solution)/shard_map/ppermute | solution.py:521
  19.9 7.8 %collective-permute-start.2 = (bf16[64,1792]{1,0:T(8,128)(2,1)S(1)}, bf16[64,1792]{1,0:T(8,128)(2,1)S(1)}, u32[]{:S(2)}, u32[]{:S(2)}) collective-permute-start(bf16[64,1792]{1,0:T(8,128)(2,1)S(1)} %bitcast.12), channel_id=1, source_target_pairs={{0,2},{2,0},{1,3},{3,1},{4,6},{6,4},{5,7},{7,5},{8,10},{10,8},{9,1... | collective-permute-start | bytes 688136 | tf_op jit(solution)/shard_map/ppermute | solution.py:521
  21.4 9.6 %collective-permute-start.6 = (bf16[4,64,576]{2,1,0:T(8,128)(2,1)S(1)}, bf16[4,64,576]{2,1,0:T(8,128)(2,1)S(1)}, u32[]{:S(2)}, u32[]{:S(2)}) collective-permute-start(bf16[4,64,576]{2,1,0:T(8,128)(2,1)S(1)} %pad_maximum_fusion.own_near), channel_id=1, source_target_pairs={{0,8},{4,12},{8,0},{12,4},{16,24},{20,28},{24,16},{28,20},{1,9},{5... | collective-permute-start | bytes 884744 | tf_op jit(solution)/shard_map/ppermute | solution.py:518
  27.7 1.6 %collective-permute-start.5 = (bf16[64,1792]{1,0:T(8,128)(2,1)S(1)}, bf16[64,1792]{1,0:T(8,128)(2,1)S(1)}, u32[]{:S(2)}, u32[]{:S(2)}) collective-permute-start(bf16[64,1792]{1,0:T(8,128)(2,1)S(1)} %collective-permute-done.2.far_ref), channel_id=1, source_target_pairs={{0,1},{1,0},{2,3},{3,2},{4,5},{5,4},{6,7},{7,6},{8,9},{9,8},{10,11... | collective-permute-start | bytes 688136 | tf_op jit(solution)/shard_map/ppermute | solution.py:521
  29.3 10.3 %copy-start.2 = (s32[1024]{0:T(1024)S(1)}, s32[1024]{0:T(1024)}, u32[]{:S(2)}) copy-start(s32[1024]{0:T(1024)} %positions_ref.3) | copy-start | bytes 12292
  31.0 1.8 %collective-permute-start.7 = (bf16[2,64,1792]{2,1,0:T(8,128)(2,1)S(1)}, bf16[2,64,1792]{2,1,0:T(8,128)(2,1)S(1)}, u32[]{:S(2)}, u32[]{:S(2)}) collective-permute-start(bf16[2,64,1792]{2,1,0:T(8,128)(2,1)S(1)} %get-tuple-element.41), channel_id=1, source_target_pairs={{0,1},{1,0},{2,3},{3,2},{4,5},{5,4},{6,7},{7,6},{8,9},{9,8},{10,11... | collective-permute-start | bytes 1376264 | tf_op jit(solution)/shard_map/ppermute | solution.py:521
  32.8 6.8 %collective-permute-start.8 = (bf16[4,64,576]{2,1,0:T(8,128)(2,1)S(1)}, bf16[4,64,576]{2,1,0:T(8,128)(2,1)S(1)}, u32[]{:S(2)}, u32[]{:S(2)}) collective-permute-start(bf16[4,64,576]{2,1,0:T(8,128)(2,1)S(1)} %collective-permute-done.6.own_far), channel_id=1, source_target_pairs={{0,1},{1,0},{2,3},{3,2},{4,5},{5,4},{6,7},{7,6},{8,9},{9,8},{10,11... | collective-permute-start | bytes 884744 | tf_op jit(solution)/shard_map/ppermute | solution.py:521
  33.8 20.1 %all-to-all-start.1 = ((bf16[16,8,1792]{2,1,0:T(8,128)(2,1)}), bf16[16,8,1792]{2,1,0:T(8,128)(2,1)S(1)}, u32[]{:S(2)}, u32[]{:S(2)}) async-start(bf16[16,8,1792]{2,1,0:T(8,128)(2,1)} %bitcast.8), calls=%async_computation.1 | async-start | bytes 917504 | tf_op jit(solution)/shard_map/all_to_all | solution.py:550
  39.5 14.3 %copy-start = (bf16[128,128]{1,0:T(8,128)(2,1)S(1)}, bf16[128,128]{1,0:T(8,128)(2,1)}, u32[]{:S(2)}) copy-start(bf16[128,128]{1,0:T(8,128)(2,1)} %get-tuple-element.44.high_ref) | copy-start | bytes 98308
  39.5 14.3 %copy-start.1 = (bf16[128,128]{1,0:T(8,128)(2,1)S(1)}, bf16[128,128]{1,0:T(8,128)(2,1)}, u32[]{:S(2)}) copy-start(bf16[128,128]{1,0:T(8,128)(2,1)} %get-tuple-element.45.low_ref) | copy-start | bytes 98308

commit v11 on v10

--- a/solution.py
+++ b/solution.py
@@ -190,35 +190,49 @@
     )(ep, own, core, w_gate, w_up, w_down)
 
 
-def far_kernel(
-    far_ref, core_far_ref, sums_ref, gate, up, down, kept_out, sent_out
-):
+def far_kernel(far_ref, sums_ref, gate, up, sums_out):
     units = gate.shape[2]
-    gate_sum, up_sum = sums_ref[:, :units], sums_ref[:, units:]
-    for index, x_ref in enumerate((far_ref, core_far_ref)):
-        rows = x_ref[...]
-        gate_sum = gate_sum + jnp.dot(rows, gate[index], preferred_element_type=jnp.float32)
-        up_sum = up_sum + jnp.dot(rows, up[index], preferred_element_type=jnp.float32)
+    rows = far_ref[...]
+    for place, weights in ((slice(0, units), gate), (slice(units, 2 * units), up)):
+        sums_out[:, place] = sums_ref[:, place] + jnp.dot(
+            rows, weights[0], preferred_element_type=jnp.float32
+        )
+
+
+def sent_kernel(core_far_ref, sums_ref, gate, up, down, hidden_out, sent_out):
+    units = gate.shape[2]
+    rows = core_far_ref[...]
+    gate_sum = sums_ref[:, :units] + jnp.dot(
+        rows, gate[1], preferred_element_type=jnp.float32
+    )
+    up_sum = sums_ref[:, units:] + jnp.dot(rows, up[1], preferred_element_type=jnp.float32)
     hidden = (gate_sum / (1.0 + jnp.exp(-gate_sum)) * up_sum).astype(jnp.bfloat16)
-    for flip in range(4):
-        out = sent_out if flip % 2 else kept_out
-        out[flip // 2] = jnp.dot(
-            hidden, down[flip], preferred_element_type=jnp.float32
+    hidden_out[...] = hidden
+    for index in range(2):
+        sent_out[index] = jnp.dot(
+            hidden, down[2 * index + 1], preferred_element_type=jnp.float32
         ).astype(jnp.bfloat16)
 
 
-def far_experts(far, core_far, sums, gate, up, down):
-    slots, features = far.shape
-    units = gate.shape[2]
+def kept_kernel(hidden_ref, down, kept_out):
+    for index in range(2):
+        kept_out[index] = jnp.dot(
+            hidden_ref[...], down[2 * index], preferred_element_type=jnp.float32
+        ).astype(jnp.bfloat16)
+
+
+def expert_step(kernel, name, out_shape, *operands):
     return pl.pallas_call(
-        far_kernel,
-        out_shape=[jax.ShapeDtypeStruct((2, slots, features), jnp.bfloat16)] * 2,
-        in_specs=[VMEM_SPEC] * 6,
-        out_specs=[VMEM_SPEC] * 2,
-        compiler_params=pltpu.CompilerParams(vmem_limit_bytes=24 * MIB),
-        cost_estimate=pl.CostEstimate(flops=0, bytes_accessed=0, transcendentals=0),
-        name="far_experts",
-    )(far, core_far, sums, gate, up, down)
+        kernel,
+        out_shape=out_shape,
+        in_specs=[VMEM_SPEC] * len(operands),
+        out_specs=jax.tree.map(lambda _: VMEM_SPEC, out_shape),
+        compiler_params=pltpu.CompilerParams(vmem_limit_bytes=SMALL),
+        cost_estimate=pl.CostEstimate(
+            flops=1 << 28, bytes_accessed=2 * MIB, transcendentals=1 << 14
+        ),
+        name=name,
+    )(*operands)
 
 
 def sum_kernel(ep_ref, kept_ref, received_ref, out_ref):
@@ -538,13 +552,34 @@
     core = over(own, "core")
     far_keys = over_ctx(own_keys, flips[-1])
     sums, far_gate, far_up, down = near_experts(ep, own, core, w_gate, w_up, w_down)
-    core_keys = over(own_keys, "core")
-    far, sums, core_keys = lax.optimization_barrier((far, sums, core_keys))
+    far, sums = lax.optimization_barrier((far, sums))
     core_far = over(far, "core")
-    kept, sent = far_experts(far, core_far, sums, far_gate, far_up, down)
+    slots, features = own.shape
+    pieces = jax.ShapeDtypeStruct((2, slots, features), jnp.bfloat16)
+    sums = expert_step(
+        far_kernel,
+        "far_rows",
+        jax.ShapeDtypeStruct(sums.shape, jnp.float32),
+        far,
+        sums,
+        far_gate,
+        far_up,
+    )
+    hidden, sent = expert_step(
+        sent_kernel,
+        "sent_pieces",
+        (jax.ShapeDtypeStruct((slots, down.shape[1]), jnp.bfloat16), pieces),
+        core_far,
+        sums,
+        far_gate,
+        far_up,
+        down,
+    )
     sent, far_keys = lax.optimization_barrier((sent, far_keys))
     received = over(sent, "core")
-    far_keys, received = lax.optimization_barrier((far_keys, received))
+    kept = expert_step(kept_kernel, "kept_pieces", pieces, hidden, down)
+    own_keys, far_keys, received = lax.optimization_barrier((own_keys, far_keys, received))
+    core_keys = over(own_keys, "core")
     core_far_keys = over(far_keys, "core")
     returning = sum_cores(ep, kept, received, ctx)
     returned = lax.all_to_all(

time: 55.5 us -> 55.4 us (level)
  waiting for transfers between devices: 8.69 us -> 9.71 us
  starting transfers between devices: 19.5 us -> 18.7 us
    ppermute x3, waiting for transfers between devices: 1.38 us -> 2.31 us  [over_ctx(): return lax.ppermute(value, 'ctx', [(i, i ^ flip) for i in range(ctx)])]
    all_to_all x1, starting transfers between devices: 5.72 us -> 5.07 us  [shards(): lax.all_to_all(returning.reshape(2 * ctx, CAP, returning.shape[3]), ('ctx...]
    pallas_call x1 -> x3, Pallas kernels: 1.47 us -> 1.74 us  [expert_step(): pl.pallas_call(kernel, out_shape=out_shape, in_specs=[VMEM_SPEC] * len(op...]
  transfers between devices with their start and end apart: 11 -> 11, of which waited for: 6 -> 7; matrix products, arithmetic and copies ran while one was open for 2% -> 2% of each run, Pallas kernels for 39% -> 39%
where the time goes in v11:
time: 55.4 us; the launch traced here: 55 us
  Pallas kernels  24.8 us (45%)
  starting transfers between devices  18.7 us (34%)
  waiting for transfers between devices  9.71 us (18%)
  other arithmetic  0.97 us (2%)
  between operations  0.74 us (1%)
    pallas_call x1, Pallas kernels, attend(): pl.pallas_call(attention_kernel, out_shape=jax.ShapeDtypeStruct((2 * HALF...  9.72 us
    ppermute x3, starting transfers between devices, over_ctx(): return lax.ppermute(value, 'ctx', [(i, i ^ flip) for i in range(ctx)])  7.71 us
    all_to_all x1, starting transfers between devices, shards(): lax.all_to_all(returning.reshape(2 * ctx, CAP, returning.shape[3]), ('ctx...  5.07 us
    pallas_call x1, Pallas kernels, fold(): pl.pallas_call(fold_kernel, out_shape=jax.ShapeDtypeStruct((2, 2, heads /...  4.66 us
    pallas_call x1, Pallas kernels, near_experts(): pl.pallas_call(near_kernel, out_shape=[jax.ShapeDtypeStruct((slots, 2 * u...  4.39 us
    all_to_all x1, waiting for transfers between devices, shards(): lax.all_to_all(returning.reshape(2 * ctx, CAP, returning.shape[3]), ('ctx...  4.39 us
    all_to_all x1, starting transfers between devices, shards(): lax.all_to_all(outgoing, 'ctx', split_axis=0, concat_axis=0, tiled=True)  3.81 us
    ppermute x6, waiting for transfers between devices, over(): return lax.ppermute(value, axis, [(0, 1), (1, 0)])  3.02 us
  transfers between devices with their start and end apart: 11, of which 7 were waited for; matrix products, arithmetic and copies ran while one was open for 2% of the time, Pallas kernels for 39%

profile of v11, /device:TPU:0, one launch (start us, length us, event | category | flops | bytes accessed | tf_op | source)
XLA Modules:
  0.0 55.0 jit_solution(17611601677724986447)
XLA Ops:
  0.6 2.2 %route.1 = (bf16[8,8,1792]{2,1,0:T(8,128)(2,1)}, bf16[128,128]{1,0:T(8,128)(2,1)}, bf16[128,128]{1,0:T(8,128)(2,1)}, bf16[64,576]{1,0:T(8,128)(2,1)}) custom-call(s32[1]{0:T(128)} %bitcast.1.ep_ref, s32[8,128]{1,0:T(8,128)} %bitcast.19, f32[8,128]{1,0:T(8,128)} %bitcast.20, bf16[64,128]{1,0:T(8,128)(2,1)} %bitcast.18, bf16[128,1792]{1,0:T(8,128)(2,1)} %rows_ref.1, ...), custom_call_target="tpu_custom_call" | custom-call | flops 29360128 | bytes 1048576 | tf_op jit(solution)/shard_map/route/pallas_call | solution.py:88
  2.9 4.0 %collective-permute-start = (bf16[1,64,576]{2,1,0:T(8,128)(2,1)}, bf16[1,64,576]{2,1,0:T(8,128)(2,1)S(1)}, u32[]{:S(2)}, u32[]{:S(2)}) collective-permute-start(bf16[1,64,576]{2,1,0:T(8,128)(2,1)} %bitcast.15), channel_id=1, source_target_pairs={{0,16},{4,20},{8,24},{12,28},{16,0},{20,4},{24,8},{28,12},{1,17},{... | collective-permute-start | bytes 221192 | tf_op jit(solution)/shard_map/ppermute | solution.py:532
  6.9 3.8 %all-to-all-start = ((bf16[8,8,1792]{2,1,0:T(8,128)(2,1)}), bf16[8,8,1792]{2,1,0:T(8,128)(2,1)S(1)}, u32[]{:S(2)}, u32[]{:S(2)}) async-start(bf16[8,8,1792]{2,1,0:T(8,128)(2,1)} %get-tuple-element.25), calls=%async_computation | async-start | bytes 458752 | tf_op jit(solution)/shard_map/all_to_all | solution.py:540
  10.7 0.6 %collective-permute-done = bf16[1,64,576]{2,1,0:T(8,128)(2,1)S(1)} collective-permute-done((bf16[1,64,576]{2,1,0:T(8,128)(2,1)}, bf16[1,64,576]{2,1,0:T(8,128)(2,1)S(1)}, u32[]{:S(2)}, u32[]{:S(2)}) %collective-permute-start) | collective-permute-done | bytes 73760 | tf_op jit(solution)/shard_map/ppermute | solution.py:532
  11.3 0.9 %pad_maximum_fusion.1 = bf16[2,64,576]{2,1,0:T(8,128)(2,1)S(1)} fusion(bf16[1,64,576]{2,1,0:T(8,128)(2,1)S(1)} %collective-permute-done, bf16[1,64,576]{2,1,0:T(8,128)(2,1)} %bitcast.16), kind=kLoop, calls=%fused_computation.1 | loop fusion | flops 73728 | bytes 294912 | tf_op jit(solution)/shard_map/concatenate | solution.py:545
  12.2 1.8 %collective-permute-start.1 = (bf16[2,64,576]{2,1,0:T(8,128)(2,1)S(1)}, bf16[2,64,576]{2,1,0:T(8,128)(2,1)S(1)}, u32[]{:S(2)}, u32[]{:S(2)}) collective-permute-start(bf16[2,64,576]{2,1,0:T(8,128)(2,1)S(1)} %pad_maximum_fusion.1), channel_id=1, source_target_pairs={{0,4},{4,0},{8,12},{12,8},{16,20},{20,16},{24,28},{28,24},{1,5},{5... | collective-permute-start | bytes 442376 | tf_op jit(solution)/shard_map/ppermute | solution.py:532
  14.0 0.0 copy-start.3
  14.0 4.7 %fold.1 = bf16[2,2,512,576]{3,2,1,0:T(8,128)(2,1)} custom-call(s32[1]{0:T(128)} %bitcast.own_ref, s32[1024]{0:T(1024)} %positions_ref.3, bf16[128,2048]{1,0:T(8,128)(2,1)} %q_nope_ref, bf16[128,1024]{1,0:T(8,128)(2,1)} %q_rope_ref.1, bf16[512,2048]{1,0:T(8,128)(2,1)} %w_uk_ref.1), custom_call_target="tpu_custom_call" | custom-call | flops 268435456 | bytes 6291456 | tf_op jit(solution)/shard_map/fold/pallas_call | solution.py:313
  18.7 0.6 %collective-permute-done.1 = bf16[2,64,576]{2,1,0:T(8,128)(2,1)S(1)} collective-permute-done((bf16[2,64,576]{2,1,0:T(8,128)(2,1)S(1)}, bf16[2,64,576]{2,1,0:T(8,128)(2,1)S(1)}, u32[]{:S(2)}, u32[]{:S(2)}) %collective-permute-start.1) | collective-permute-done | bytes 147488 | tf_op jit(solution)/shard_map/ppermute | solution.py:532
  19.2 0.0 copy-done.3
  19.2 0.1 pad_maximum_fusion.own_near
  19.3 0.0 all-to-all-done
  19.3 0.1 collective-permute-start.3
  19.4 1.6 %collective-permute-start.2 = (bf16[64,1792]{1,0:T(8,128)(2,1)S(1)}, bf16[64,1792]{1,0:T(8,128)(2,1)S(1)}, u32[]{:S(2)}, u32[]{:S(2)}) collective-permute-start(bf16[64,1792]{1,0:T(8,128)(2,1)S(1)} %bitcast.12), channel_id=1, source_target_pairs={{0,2},{2,0},{1,3},{3,1},{4,6},{6,4},{5,7},{7,5},{8,10},{10,8},{9,1... | collective-permute-start | bytes 688136 | tf_op jit(solution)/shard_map/ppermute | solution.py:535
  20.9 1.9 %collective-permute-start.5 = (bf16[4,64,576]{2,1,0:T(8,128)(2,1)S(1)}, bf16[4,64,576]{2,1,0:T(8,128)(2,1)S(1)}, u32[]{:S(2)}, u32[]{:S(2)}) collective-permute-start(bf16[4,64,576]{2,1,0:T(8,128)(2,1)S(1)} %pad_maximum_fusion.own_near), channel_id=1, source_target_pairs={{0,8},{4,12},{8,0},{12,4},{16,24},{20,28},{24,16},{28,20},{1,9},{5... | collective-permute-start | bytes 884744 | tf_op jit(solution)/shard_map/ppermute | solution.py:532
  22.9 0.0 collective-permute-done.3.core_ref
  22.9 4.4 %near_experts.1 = (f32[64,512]{1,0:T(8,128)S(1)}, bf16[2,1792,256]{2,1,0:T(8,128)(2,1)S(1)}, bf16[2,1792,256]{2,1,0:T(8,128)(2,1)S(1)}, bf16[4,256,1792]{2,1,0:T(8,128)(2,1)S(1)}) custom-call(s32[1]{0:T(128)} %bitcast.1.ep_ref, bf16[64,1792]{1,0:T(8,128)(2,1)S(1)} %bitcast.13, bf16[64,1792]{1,0:T(8,128)(2,1)S(1)} %collective-permute-done.3.core_ref, ...), custom_call_target="tpu_custom_call" | custom-call | flops 234881024 | bytes 11010048 | tf_op jit(solution)/shard_map/near_experts/pallas_call | solution.py:166
  27.3 0.2 collective-permute-done.2.far_ref
  27.4 0.0 collective-permute-start.4
  27.4 0.4 far_rows.1.sums_ref
  27.9 1.0 %collective-permute-done.4.core_far_ref = bf16[64,1792]{1,0:T(8,128)(2,1)S(1)} collective-permute-done((bf16[64,1792]{1,0:T(8,128)(2,1)S(1)}, bf16[64,1792]{1,0:T(8,128)(2,1)S(1)}, u32[]{:S(2)}, u32[]{:S(2)}) %collective-permute-start.4) | collective-permute-done | bytes 229408 | tf_op jit(solution)/shard_map/ppermute | solution.py:535
  28.9 0.9 %sent_pieces.1 = (bf16[64,256]{1,0:T(8,128)(2,1)S(1)}, bf16[2,64,1792]{2,1,0:T(8,128)(2,1)S(1)}) custom-call(bf16[64,1792]{1,0:T(8,128)(2,1)S(1)} %collective-permute-done.4.core_far_ref, f32[64,512]{1,0:T(8,128)S(1)} %far_rows.1.sums_ref, bf16[2,1792,256]{2,1,0:T(8,128)(2,1)S(1)} %get-tuple-element.36.gate, bf16[2,1792,256]{2,1,0:T(8,128)(2,1)S(1)} %get-tuple-element.37.up, ...), custom_call_target="tpu_custom_call" | custom-call | flops 268435456 | bytes 2097152 | tf_op jit(solution)/shard_map/sent_pieces/pallas_call | solution.py:225
  29.8 1.1 %collective-permute-done.5.own_far = bf16[4,64,576]{2,1,0:T(8,128)(2,1)S(1)} collective-permute-done((bf16[4,64,576]{2,1,0:T(8,128)(2,1)S(1)}, bf16[4,64,576]{2,1,0:T(8,128)(2,1)S(1)}, u32[]{:S(2)}, u32[]{:S(2)}) %collective-permute-start.5) | collective-permute-done | bytes 294944 | tf_op jit(solution)/shard_map/ppermute | solution.py:532
  30.9 0.0 collective-permute-start.6
  30.9 1.8 %collective-permute-done.6.received_ref = bf16[2,64,1792]{2,1,0:T(8,128)(2,1)S(1)} collective-permute-done((bf16[2,64,1792]{2,1,0:T(8,128)(2,1)S(1)}, bf16[2,64,1792]{2,1,0:T(8,128)(2,1)S(1)}, u32[]{:S(2)}, u32[]{:S(2)}) %collective-permute-start.6) | collective-permute-done | bytes 458784 | tf_op jit(solution)/shard_map/ppermute | solution.py:535
  32.7 0.1 collective-permute-start.7
  32.8 0.4 collective-permute-start.8
  33.2 0.0 copy-start.2
  33.2 0.4 kept_pieces.1.kept_ref
  33.7 0.9 %sum_cores.1 = bf16[8,2,8,1792]{3,2,1,0:T(8,128)(2,1)} custom-call(s32[1]{0:T(128)} %bitcast.1.ep_ref, bf16[2,64,1792]{2,1,0:T(8,128)(2,1)S(1)} %kept_pieces.1.kept_ref, bf16[2,64,1792]{2,1,0:T(8,128)(2,1)S(1)} %collective-permute-done.6.received_ref), custom_call_target="tpu_custom_call" | custom-call | bytes 1048576 | tf_op jit(solution)/shard_map/sum_cores/pallas_call | solution.py:249
  34.5 5.1 %all-to-all-start.1 = ((bf16[16,8,1792]{2,1,0:T(8,128)(2,1)}), bf16[16,8,1792]{2,1,0:T(8,128)(2,1)S(1)}, u32[]{:S(2)}, u32[]{:S(2)}) async-start(bf16[16,8,1792]{2,1,0:T(8,128)(2,1)} %bitcast.8), calls=%async_computation.1 | async-start | bytes 917504 | tf_op jit(solution)/shard_map/all_to_all | solution.py:585
  39.6 0.0 copy-start
  39.6 0.0 copy-start.1
  39.6 0.0 collective-permute-done.7.core_near
  39.7 0.0 collective-permute-done.8.core_far
  39.7 0.0 copy-done.2
  39.7 9.7 %attention.1 = bf16[128,2048]{1,0:T(8,128)(2,1)} custom-call(s32[1]{0:T(128)} %bitcast.own_ref, s32[1]{0:T(128)} %bitcast.1.ep_ref, s32[1024]{0:T(1024)S(1)} %copy-done.2, bf16[2,1024,576]{2,1,0:T(8,128)(2,1)} %bitcast.14, bf16[512,2048]{1,0:T(8,128)(2,1)} %w_uv_hbm.1, bf16[4,64,576]{2,1,0:T(8,128)(2,1)S(1)} %pad_maximum_fusion.own_near, ...), custom_call_target="tpu_custom_call" | custom-call | flops 14495514624 | bytes 8388608 | tf_op jit(solution)/shard_map/attention/pallas_call | solution.py:488
  49.4 4.4 %all-to-all-done.1 = bf16[16,8,1792]{2,1,0:T(8,128)(2,1)S(1)} async-done(((bf16[16,8,1792]{2,1,0:T(8,128)(2,1)}), bf16[16,8,1792]{2,1,0:T(8,128)(2,1)S(1)}, u32[]{:S(2)}, u32[]{:S(2)}) %all-to-all-start.1) | async-done | bytes 458784 | tf_op jit(solution)/shard_map/all_to_all | solution.py:585
  53.8 0.0 copy-done
  53.8 0.0 copy-done.1
  53.8 1.2 %combine.1 = bf16[128,1792]{1,0:T(8,128)(2,1)} custom-call(bf16[128,128]{1,0:T(8,128)(2,1)S(1)} %copy-done, bf16[128,128]{1,0:T(8,128)(2,1)S(1)} %copy-done.1, bf16[128,1792]{1,0:T(8,128)(2,1)S(1)} %bitcast.10), custom_call_target="tpu_custom_call" | custom-call | flops 117440512 | bytes 1048576 | tf_op jit(solution)/shard_map/combine/pallas_call | solution.py:272
Async XLA Ops:
  2.9 8.4 %collective-permute-start = (bf16[1,64,576]{2,1,0:T(8,128)(2,1)}, bf16[1,64,576]{2,1,0:T(8,128)(2,1)S(1)}, u32[]{:S(2)}, u32[]{:S(2)}) collective-permute-start(bf16[1,64,576]{2,1,0:T(8,128)(2,1)} %bitcast.15), channel_id=1, source_target_pairs={{0,16},{4,20},{8,24},{12,28},{16,0},{20,4},{24,8},{28,12},{1,17},{... | collective-permute-start | bytes 221192 | tf_op jit(solution)/shard_map/ppermute | solution.py:532
  6.9 12.4 %all-to-all-start = ((bf16[8,8,1792]{2,1,0:T(8,128)(2,1)}), bf16[8,8,1792]{2,1,0:T(8,128)(2,1)S(1)}, u32[]{:S(2)}, u32[]{:S(2)}) async-start(bf16[8,8,1792]{2,1,0:T(8,128)(2,1)} %get-tuple-element.25), calls=%async_computation | async-start | bytes 458752 | tf_op jit(solution)/shard_map/all_to_all | solution.py:540
  12.2 7.0 %collective-permute-start.1 = (bf16[2,64,576]{2,1,0:T(8,128)(2,1)S(1)}, bf16[2,64,576]{2,1,0:T(8,128)(2,1)S(1)}, u32[]{:S(2)}, u32[]{:S(2)}) collective-permute-start(bf16[2,64,576]{2,1,0:T(8,128)(2,1)S(1)} %pad_maximum_fusion.1), channel_id=1, source_target_pairs={{0,4},{4,0},{8,12},{12,8},{16,20},{20,16},{24,28},{28,24},{1,5},{5... | collective-permute-start | bytes 442376 | tf_op jit(solution)/shard_map/ppermute | solution.py:532
  14.0 5.2 %copy-start.3 = (bf16[64,576]{1,0:T(8,128)(2,1)S(1)}, bf16[64,576]{1,0:T(8,128)(2,1)}, u32[]{:S(2)}) copy-start(bf16[64,576]{1,0:T(8,128)(2,1)} %get-tuple-element.27) | copy-start | bytes 221188
  19.3 3.5 %collective-permute-start.3 = (bf16[64,1792]{1,0:T(8,128)(2,1)S(1)}, bf16[64,1792]{1,0:T(8,128)(2,1)S(1)}, u32[]{:S(2)}, u32[]{:S(2)}) collective-permute-start(bf16[64,1792]{1,0:T(8,128)(2,1)S(1)} %bitcast.11), channel_id=1, source_target_pairs={{0,1},{1,0},{2,3},{3,2},{4,5},{5,4},{6,7},{7,6},{8,9},{9,8},{10,11... | collective-permute-start | bytes 688136 | tf_op jit(solution)/shard_map/ppermute | solution.py:535
  19.4 8.0 %collective-permute-start.2 = (bf16[64,1792]{1,0:T(8,128)(2,1)S(1)}, bf16[64,1792]{1,0:T(8,128)(2,1)S(1)}, u32[]{:S(2)}, u32[]{:S(2)}) collective-permute-start(bf16[64,1792]{1,0:T(8,128)(2,1)S(1)} %bitcast.12), channel_id=1, source_target_pairs={{0,2},{2,0},{1,3},{3,1},{4,6},{6,4},{5,7},{7,5},{8,10},{10,8},{9,1... | collective-permute-start | bytes 688136 | tf_op jit(solution)/shard_map/ppermute | solution.py:535
  20.9 9.9 %collective-permute-start.5 = (bf16[4,64,576]{2,1,0:T(8,128)(2,1)S(1)}, bf16[4,64,576]{2,1,0:T(8,128)(2,1)S(1)}, u32[]{:S(2)}, u32[]{:S(2)}) collective-permute-start(bf16[4,64,576]{2,1,0:T(8,128)(2,1)S(1)} %pad_maximum_fusion.own_near), channel_id=1, source_target_pairs={{0,8},{4,12},{8,0},{12,4},{16,24},{20,28},{24,16},{28,20},{1,9},{5... | collective-permute-start | bytes 884744 | tf_op jit(solution)/shard_map/ppermute | solution.py:532
  27.4 1.5 %collective-permute-start.4 = (bf16[64,1792]{1,0:T(8,128)(2,1)S(1)}, bf16[64,1792]{1,0:T(8,128)(2,1)S(1)}, u32[]{:S(2)}, u32[]{:S(2)}) collective-permute-start(bf16[64,1792]{1,0:T(8,128)(2,1)S(1)} %collective-permute-done.2.far_ref), channel_id=1, source_target_pairs={{0,1},{1,0},{2,3},{3,2},{4,5},{5,4},{6,7},{7,6},{8,9},{9,8},{10,11... | collective-permute-start | bytes 688136 | tf_op jit(solution)/shard_map/ppermute | solution.py:535
  30.9 1.8 %collective-permute-start.6 = (bf16[2,64,1792]{2,1,0:T(8,128)(2,1)S(1)}, bf16[2,64,1792]{2,1,0:T(8,128)(2,1)S(1)}, u32[]{:S(2)}, u32[]{:S(2)}) collective-permute-start(bf16[2,64,1792]{2,1,0:T(8,128)(2,1)S(1)} %get-tuple-element.41), channel_id=1, source_target_pairs={{0,1},{1,0},{2,3},{3,2},{4,5},{5,4},{6,7},{7,6},{8,9},{9,8},{10,11... | collective-permute-start | bytes 1376264 | tf_op jit(solution)/shard_map/ppermute | solution.py:535
  32.7 6.9 %collective-permute-start.7 = (bf16[4,64,576]{2,1,0:T(8,128)(2,1)S(1)}, bf16[4,64,576]{2,1,0:T(8,128)(2,1)S(1)}, u32[]{:S(2)}, u32[]{:S(2)}) collective-permute-start(bf16[4,64,576]{2,1,0:T(8,128)(2,1)S(1)} %pad_maximum_fusion.own_near), channel_id=1, source_target_pairs={{0,1},{1,0},{2,3},{3,2},{4,5},{5,4},{6,7},{7,6},{8,9},{9,8},{10,11... | collective-permute-start | bytes 884744 | tf_op jit(solution)/shard_map/ppermute | solution.py:535
  32.8 6.8 %collective-permute-start.8 = (bf16[4,64,576]{2,1,0:T(8,128)(2,1)S(1)}, bf16[4,64,576]{2,1,0:T(8,128)(2,1)S(1)}, u32[]{:S(2)}, u32[]{:S(2)}) collective-permute-start(bf16[4,64,576]{2,1,0:T(8,128)(2,1)S(1)} %collective-permute-done.5.own_far), channel_id=1, source_target_pairs={{0,1},{1,0},{2,3},{3,2},{4,5},{5,4},{6,7},{7,6},{8,9},{9,8},{10,11... | collective-permute-start | bytes 884744 | tf_op jit(solution)/shard_map/ppermute | solution.py:535
  33.2 6.4 %copy-start.2 = (s32[1024]{0:T(1024)S(1)}, s32[1024]{0:T(1024)}, u32[]{:S(2)}) copy-start(s32[1024]{0:T(1024)} %positions_ref.3) | copy-start | bytes 12292
  34.5 19.2 %all-to-all-start.1 = ((bf16[16,8,1792]{2,1,0:T(8,128)(2,1)}), bf16[16,8,1792]{2,1,0:T(8,128)(2,1)S(1)}, u32[]{:S(2)}, u32[]{:S(2)}) async-start(bf16[16,8,1792]{2,1,0:T(8,128)(2,1)} %bitcast.8), calls=%async_computation.1 | async-start | bytes 917504 | tf_op jit(solution)/shard_map/all_to_all | solution.py:585
  39.6 14.2 %copy-start = (bf16[128,128]{1,0:T(8,128)(2,1)S(1)}, bf16[128,128]{1,0:T(8,128)(2,1)}, u32[]{:S(2)}) copy-start(bf16[128,128]{1,0:T(8,128)(2,1)} %get-tuple-element.44.high_ref) | copy-start | bytes 98308
  39.6 14.2 %copy-start.1 = (bf16[128,128]{1,0:T(8,128)(2,1)S(1)}, bf16[128,128]{1,0:T(8,128)(2,1)}, u32[]{:S(2)}) copy-start(bf16[128,128]{1,0:T(8,128)(2,1)} %get-tuple-element.45.low_ref) | copy-start | bytes 98308

commit v12 on v11

--- a/solution.py
+++ b/solution.py
@@ -341,10 +341,8 @@
     positions_ref,
     queries_hbm,
     w_uv_hbm,
-    own_near,
-    own_far,
-    core_near,
-    core_far,
+    own_keys,
+    core_keys,
     out_ref,
     keys,
     queries,
@@ -361,14 +359,12 @@
     w_uv_copy = pltpu.make_async_copy(w_uv_hbm, w_uv, semaphores.at[2])
     for copy in (query_copies[0], w_uv_copy, query_copies[1]):
         copy.start()
-    blocks = own_near.shape[0]
+    blocks = own_keys.shape[0]
     my_ctx, my_ep = own_ref[0], ep_ref[0]
-    flips = gather_order(2 * blocks)
-    sources = ((own_near, 0, 0), (own_far, 0, 1), (core_near, 1, 0), (core_far, 1, 1))
-    for source, flip, last in sources:
+    for flip, source in enumerate((own_keys, core_keys)):
         for block in range(blocks):
-            source_ctx = my_ctx ^ flips[-1] if last else my_ctx
-            for bit, step in enumerate(flips[:-1]):
+            source_ctx = my_ctx
+            for bit, step in enumerate(gather_order(blocks)):
                 if block >> bit & 1:
                     source_ctx = source_ctx ^ step
             start = source_ctx * (2 * HALF) + ((my_ep % 2) ^ flip) * HALF
@@ -488,7 +484,7 @@
     return pl.pallas_call(
         attention_kernel,
         out_shape=jax.ShapeDtypeStruct((2 * HALF, columns), jnp.bfloat16),
-        in_specs=[SMEM_SPEC] * 3 + [HBM_SPEC] * 2 + [VMEM_SPEC] * 4,
+        in_specs=[SMEM_SPEC] * 3 + [HBM_SPEC] * 2 + [VMEM_SPEC] * 2,
         out_specs=VMEM_SPEC,
         scratch_shapes=[
             VMEM((key_count, width), jnp.bfloat16),
@@ -578,9 +574,11 @@
     sent, far_keys = lax.optimization_barrier((sent, far_keys))
     received = over(sent, "core")
     kept = expert_step(kept_kernel, "kept_pieces", pieces, hidden, down)
-    own_keys, far_keys, received = lax.optimization_barrier((own_keys, far_keys, received))
+    own_keys, far_keys, received, kept = lax.optimization_barrier(
+        (own_keys, far_keys, received, kept)
+    )
+    own_keys = jnp.concatenate([own_keys, far_keys], axis=0)
     core_keys = over(own_keys, "core")
-    core_far_keys = over(far_keys, "core")
     returning = sum_cores(ep, kept, received, ctx)
     returned = lax.all_to_all(
         returning.reshape(2 * ctx, CAP, returning.shape[3]),
@@ -589,9 +587,7 @@
         concat_axis=0,
         tiled=True,
     )
-    attention = attend(
-        me, ep, positions, queries, w_uv, own_keys, far_keys, core_keys, core_far_keys
-    )
+    attention = attend(me, ep, positions, queries, w_uv, own_keys, core_keys)
     moe_out = combine(high, low, returned.reshape(2 * ctx * CAP, returned.shape[2]))
     return (attention, moe_out)
 

time: 55.4 us -> 55 us (level)
    ppermute x6 -> x5, waiting for transfers between devices: 3.02 us -> 2.56 us  [over(): return lax.ppermute(value, axis, [(0, 1), (1, 0)])]
    ppermute x6 -> x5, starting transfers between devices: 2.14 us -> 1.83 us  [over(): return lax.ppermute(value, axis, [(0, 1), (1, 0)])]
  transfers between devices with their start and end apart: 11 -> 10, of which waited for: 7 -> 7; matrix products, arithmetic and copies ran while one was open for 2% -> 2% of each run, Pallas kernels for 39% -> 39%
where the time goes in v12:
time: 55 us; the launch traced here: 54.5 us
  Pallas kernels  24.8 us (45%)
  starting transfers between devices  18.4 us (33%)
  waiting for transfers between devices  9.45 us (17%)
  other arithmetic  0.97 us (2%)
  between operations  0.75 us (1%)
    pallas_call x1, Pallas kernels, attend(): pl.pallas_call(attention_kernel, out_shape=jax.ShapeDtypeStruct((2 * HALF...  9.72 us
    ppermute x3, starting transfers between devices, over_ctx(): return lax.ppermute(value, 'ctx', [(i, i ^ flip) for i in range(ctx)])  7.71 us
    all_to_all x1, starting transfers between devices, shards(): lax.all_to_all(returning.reshape(2 * ctx, CAP, returning.shape[3]), ('ctx...  5.09 us
    pallas_call x1, Pallas kernels, fold(): pl.pallas_call(fold_kernel, out_shape=jax.ShapeDtypeStruct((2, 2, heads /...  4.66 us
    all_to_all x1, waiting for transfers between devices, shards(): lax.all_to_all(returning.reshape(2 * ctx, CAP, returning.shape[3]), ('ctx...  4.57 us
    pallas_call x1, Pallas kernels, near_experts(): pl.pallas_call(near_kernel, out_shape=[jax.ShapeDtypeStruct((slots, 2 * u...  4.39 us
    all_to_all x1, starting transfers between devices, shards(): lax.all_to_all(outgoing, 'ctx', split_axis=0, concat_axis=0, tiled=True)  3.81 us
    ppermute x5, waiting for transfers between devices, over(): return lax.ppermute(value, axis, [(0, 1), (1, 0)])  2.56 us
  transfers between devices with their start and end apart: 10, of which 7 were waited for; matrix products, arithmetic and copies ran while one was open for 2% of the time, Pallas kernels for 39%

profile of v12, /device:TPU:0, one launch (start us, length us, event | category | flops | bytes accessed | tf_op | source)
XLA Modules:
  0.0 54.5 jit_solution(2371385692516667502)
XLA Ops:
  0.6 2.2 %route.1 = (bf16[8,8,1792]{2,1,0:T(8,128)(2,1)}, bf16[128,128]{1,0:T(8,128)(2,1)}, bf16[128,128]{1,0:T(8,128)(2,1)}, bf16[64,576]{1,0:T(8,128)(2,1)}) custom-call(s32[1]{0:T(128)} %bitcast.1.ep_ref, s32[8,128]{1,0:T(8,128)} %bitcast.19, f32[8,128]{1,0:T(8,128)} %bitcast.20, bf16[64,128]{1,0:T(8,128)(2,1)} %bitcast.18, bf16[128,1792]{1,0:T(8,128)(2,1)} %rows_ref.1, ...), custom_call_target="tpu_custom_call" | custom-call | flops 29360128 | bytes 1048576 | tf_op jit(solution)/shard_map/route/pallas_call | solution.py:88
  2.9 4.0 %collective-permute-start = (bf16[1,64,576]{2,1,0:T(8,128)(2,1)}, bf16[1,64,576]{2,1,0:T(8,128)(2,1)S(1)}, u32[]{:S(2)}, u32[]{:S(2)}) collective-permute-start(bf16[1,64,576]{2,1,0:T(8,128)(2,1)} %bitcast.15), channel_id=1, source_target_pairs={{0,16},{4,20},{8,24},{12,28},{16,0},{20,4},{24,8},{28,12},{1,17},{... | collective-permute-start | bytes 221192 | tf_op jit(solution)/shard_map/ppermute | solution.py:528
  6.9 3.8 %all-to-all-start = ((bf16[8,8,1792]{2,1,0:T(8,128)(2,1)}), bf16[8,8,1792]{2,1,0:T(8,128)(2,1)S(1)}, u32[]{:S(2)}, u32[]{:S(2)}) async-start(bf16[8,8,1792]{2,1,0:T(8,128)(2,1)} %get-tuple-element.26), calls=%async_computation | async-start | bytes 458752 | tf_op jit(solution)/shard_map/all_to_all | solution.py:536
  10.7 0.6 %collective-permute-done = bf16[1,64,576]{2,1,0:T(8,128)(2,1)S(1)} collective-permute-done((bf16[1,64,576]{2,1,0:T(8,128)(2,1)}, bf16[1,64,576]{2,1,0:T(8,128)(2,1)S(1)}, u32[]{:S(2)}, u32[]{:S(2)}) %collective-permute-start) | collective-permute-done | bytes 73760 | tf_op jit(solution)/shard_map/ppermute | solution.py:528
  11.3 0.9 %pad_maximum_fusion.1 = bf16[2,64,576]{2,1,0:T(8,128)(2,1)S(1)} fusion(bf16[1,64,576]{2,1,0:T(8,128)(2,1)S(1)} %collective-permute-done, bf16[1,64,576]{2,1,0:T(8,128)(2,1)} %bitcast.16), kind=kLoop, calls=%fused_computation.1 | loop fusion | flops 73728 | bytes 294912 | tf_op jit(solution)/shard_map/concatenate | solution.py:541
  12.2 1.8 %collective-permute-start.1 = (bf16[2,64,576]{2,1,0:T(8,128)(2,1)S(1)}, bf16[2,64,576]{2,1,0:T(8,128)(2,1)S(1)}, u32[]{:S(2)}, u32[]{:S(2)}) collective-permute-start(bf16[2,64,576]{2,1,0:T(8,128)(2,1)S(1)} %pad_maximum_fusion.1), channel_id=1, source_target_pairs={{0,4},{4,0},{8,12},{12,8},{16,20},{20,16},{24,28},{28,24},{1,5},{5... | collective-permute-start | bytes 442376 | tf_op jit(solution)/shard_map/ppermute | solution.py:528
  14.0 0.0 copy-start.3
  14.0 4.7 %fold.1 = bf16[2,2,512,576]{3,2,1,0:T(8,128)(2,1)} custom-call(s32[1]{0:T(128)} %bitcast.own_ref, s32[1024]{0:T(1024)} %positions_ref.3, bf16[128,2048]{1,0:T(8,128)(2,1)} %q_nope_ref, bf16[128,1024]{1,0:T(8,128)(2,1)} %q_rope_ref.1, bf16[512,2048]{1,0:T(8,128)(2,1)} %w_uk_ref.1), custom_call_target="tpu_custom_call" | custom-call | flops 268435456 | bytes 6291456 | tf_op jit(solution)/shard_map/fold/pallas_call | solution.py:313
  18.7 0.6 %collective-permute-done.1 = bf16[2,64,576]{2,1,0:T(8,128)(2,1)S(1)} collective-permute-done((bf16[2,64,576]{2,1,0:T(8,128)(2,1)S(1)}, bf16[2,64,576]{2,1,0:T(8,128)(2,1)S(1)}, u32[]{:S(2)}, u32[]{:S(2)}) %collective-permute-start.1) | collective-permute-done | bytes 147488 | tf_op jit(solution)/shard_map/ppermute | solution.py:528
  19.2 0.0 copy-done.3
  19.2 0.1 pad_maximum_fusion
  19.3 0.0 all-to-all-done
  19.3 0.1 collective-permute-start.3
  19.4 1.6 %collective-permute-start.2 = (bf16[64,1792]{1,0:T(8,128)(2,1)S(1)}, bf16[64,1792]{1,0:T(8,128)(2,1)S(1)}, u32[]{:S(2)}, u32[]{:S(2)}) collective-permute-start(bf16[64,1792]{1,0:T(8,128)(2,1)S(1)} %bitcast.12), channel_id=1, source_target_pairs={{0,2},{2,0},{1,3},{3,1},{4,6},{6,4},{5,7},{7,5},{8,10},{10,8},{9,1... | collective-permute-start | bytes 688136 | tf_op jit(solution)/shard_map/ppermute | solution.py:531
  20.9 1.9 %collective-permute-start.5 = (bf16[4,64,576]{2,1,0:T(8,128)(2,1)S(1)}, bf16[4,64,576]{2,1,0:T(8,128)(2,1)S(1)}, u32[]{:S(2)}, u32[]{:S(2)}) collective-permute-start(bf16[4,64,576]{2,1,0:T(8,128)(2,1)S(1)} %pad_maximum_fusion), channel_id=1, source_target_pairs={{0,8},{4,12},{8,0},{12,4},{16,24},{20,28},{24,16},{28,20},{1,9},{5... | collective-permute-start | bytes 884744 | tf_op jit(solution)/shard_map/ppermute | solution.py:528
  22.9 0.0 collective-permute-done.3.core_ref
  22.9 4.4 %near_experts.1 = (f32[64,512]{1,0:T(8,128)S(1)}, bf16[2,1792,256]{2,1,0:T(8,128)(2,1)S(1)}, bf16[2,1792,256]{2,1,0:T(8,128)(2,1)S(1)}, bf16[4,256,1792]{2,1,0:T(8,128)(2,1)S(1)}) custom-call(s32[1]{0:T(128)} %bitcast.1.ep_ref, bf16[64,1792]{1,0:T(8,128)(2,1)S(1)} %bitcast.13, bf16[64,1792]{1,0:T(8,128)(2,1)S(1)} %collective-permute-done.3.core_ref, ...), custom_call_target="tpu_custom_call" | custom-call | flops 234881024 | bytes 11010048 | tf_op jit(solution)/shard_map/near_experts/pallas_call | solution.py:166
  27.3 0.2 collective-permute-done.2.far_ref
  27.4 0.0 collective-permute-start.4
  27.4 0.4 far_rows.1.sums_ref
  27.9 1.0 %collective-permute-done.4.core_far_ref = bf16[64,1792]{1,0:T(8,128)(2,1)S(1)} collective-permute-done((bf16[64,1792]{1,0:T(8,128)(2,1)S(1)}, bf16[64,1792]{1,0:T(8,128)(2,1)S(1)}, u32[]{:S(2)}, u32[]{:S(2)}) %collective-permute-start.4) | collective-permute-done | bytes 229408 | tf_op jit(solution)/shard_map/ppermute | solution.py:531
  28.9 0.9 %sent_pieces.1 = (bf16[64,256]{1,0:T(8,128)(2,1)S(1)}, bf16[2,64,1792]{2,1,0:T(8,128)(2,1)S(1)}) custom-call(bf16[64,1792]{1,0:T(8,128)(2,1)S(1)} %collective-permute-done.4.core_far_ref, f32[64,512]{1,0:T(8,128)S(1)} %far_rows.1.sums_ref, bf16[2,1792,256]{2,1,0:T(8,128)(2,1)S(1)} %get-tuple-element.37.gate, bf16[2,1792,256]{2,1,0:T(8,128)(2,1)S(1)} %get-tuple-element.38.up, ...), custom_call_target="tpu_custom_call" | custom-call | flops 268435456 | bytes 2097152 | tf_op jit(solution)/shard_map/sent_pieces/pallas_call | solution.py:225
  29.8 1.1 %collective-permute-done.5 = bf16[4,64,576]{2,1,0:T(8,128)(2,1)S(1)} collective-permute-done((bf16[4,64,576]{2,1,0:T(8,128)(2,1)S(1)}, bf16[4,64,576]{2,1,0:T(8,128)(2,1)S(1)}, u32[]{:S(2)}, u32[]{:S(2)}) %collective-permute-start.5) | collective-permute-done | bytes 294944 | tf_op jit(solution)/shard_map/ppermute | solution.py:528
  30.9 0.0 collective-permute-start.6
  30.9 0.4 kept_pieces.1.kept_ref
  31.3 0.0 copy-start.2
  31.3 1.4 %collective-permute-done.6.received_ref = bf16[2,64,1792]{2,1,0:T(8,128)(2,1)S(1)} collective-permute-done((bf16[2,64,1792]{2,1,0:T(8,128)(2,1)S(1)}, bf16[2,64,1792]{2,1,0:T(8,128)(2,1)S(1)}, u32[]{:S(2)}, u32[]{:S(2)}) %collective-permute-start.6) | collective-permute-done | bytes 458784 | tf_op jit(solution)/shard_map/ppermute | solution.py:531
  32.8 0.2 collective-permute-start.7
  33.0 0.9 %sum_cores.1 = bf16[8,2,8,1792]{3,2,1,0:T(8,128)(2,1)} custom-call(s32[1]{0:T(128)} %bitcast.1.ep_ref, bf16[2,64,1792]{2,1,0:T(8,128)(2,1)S(1)} %kept_pieces.1.kept_ref, bf16[2,64,1792]{2,1,0:T(8,128)(2,1)S(1)} %collective-permute-done.6.received_ref), custom_call_target="tpu_custom_call" | custom-call | bytes 1048576 | tf_op jit(solution)/shard_map/sum_cores/pallas_call | solution.py:249
  33.9 5.1 %all-to-all-start.1 = ((bf16[16,8,1792]{2,1,0:T(8,128)(2,1)}), bf16[16,8,1792]{2,1,0:T(8,128)(2,1)S(1)}, u32[]{:S(2)}, u32[]{:S(2)}) async-start(bf16[16,8,1792]{2,1,0:T(8,128)(2,1)} %bitcast.8), calls=%async_computation.1 | async-start | bytes 917504 | tf_op jit(solution)/shard_map/all_to_all | solution.py:583
  39.0 0.0 copy-start
  39.0 0.0 copy-start.1
  39.0 0.0 collective-permute-done.7.core_keys
  39.0 0.0 copy-done.2
  39.0 9.7 %attention.1 = bf16[128,2048]{1,0:T(8,128)(2,1)} custom-call(s32[1]{0:T(128)} %bitcast.own_ref, s32[1]{0:T(128)} %bitcast.1.ep_ref, s32[1024]{0:T(1024)S(1)} %copy-done.2, bf16[2,1024,576]{2,1,0:T(8,128)(2,1)} %bitcast.14, bf16[512,2048]{1,0:T(8,128)(2,1)} %w_uv_hbm.1, bf16[8,64,576]{2,1,0:T(8,128)(2,1)S(1)} %constant_dynamic-update-slice_fusion.own_keys, ...), custom_call_target="tpu_custom_call" | custom-call | flops 14495514624 | bytes 8388608 | tf_op jit(solution)/shard_map/attention/pallas_call | solution.py:484
  48.7 4.6 %all-to-all-done.1 = bf16[16,8,1792]{2,1,0:T(8,128)(2,1)S(1)} async-done(((bf16[16,8,1792]{2,1,0:T(8,128)(2,1)}), bf16[16,8,1792]{2,1,0:T(8,128)(2,1)S(1)}, u32[]{:S(2)}, u32[]{:S(2)}) %all-to-all-start.1) | async-done | bytes 458784 | tf_op jit(solution)/shard_map/all_to_all | solution.py:583
  53.3 0.0 copy-done
  53.3 0.0 copy-done.1
  53.3 1.2 %combine.1 = bf16[128,1792]{1,0:T(8,128)(2,1)} custom-call(bf16[128,128]{1,0:T(8,128)(2,1)S(1)} %copy-done, bf16[128,128]{1,0:T(8,128)(2,1)S(1)} %copy-done.1, bf16[128,1792]{1,0:T(8,128)(2,1)S(1)} %bitcast.10), custom_call_target="tpu_custom_call" | custom-call | flops 117440512 | bytes 1048576 | tf_op jit(solution)/shard_map/combine/pallas_call | solution.py:272
  (2 shorter events, 0.1 us)
Async XLA Ops:
  2.9 8.4 %collective-permute-start = (bf16[1,64,576]{2,1,0:T(8,128)(2,1)}, bf16[1,64,576]{2,1,0:T(8,128)(2,1)S(1)}, u32[]{:S(2)}, u32[]{:S(2)}) collective-permute-start(bf16[1,64,576]{2,1,0:T(8,128)(2,1)} %bitcast.15), channel_id=1, source_target_pairs={{0,16},{4,20},{8,24},{12,28},{16,0},{20,4},{24,8},{28,12},{1,17},{... | collective-permute-start | bytes 221192 | tf_op jit(solution)/shard_map/ppermute | solution.py:528
  6.9 12.4 %all-to-all-start = ((bf16[8,8,1792]{2,1,0:T(8,128)(2,1)}), bf16[8,8,1792]{2,1,0:T(8,128)(2,1)S(1)}, u32[]{:S(2)}, u32[]{:S(2)}) async-start(bf16[8,8,1792]{2,1,0:T(8,128)(2,1)} %get-tuple-element.26), calls=%async_computation | async-start | bytes 458752 | tf_op jit(solution)/shard_map/all_to_all | solution.py:536
  12.2 7.0 %collective-permute-start.1 = (bf16[2,64,576]{2,1,0:T(8,128)(2,1)S(1)}, bf16[2,64,576]{2,1,0:T(8,128)(2,1)S(1)}, u32[]{:S(2)}, u32[]{:S(2)}) collective-permute-start(bf16[2,64,576]{2,1,0:T(8,128)(2,1)S(1)} %pad_maximum_fusion.1), channel_id=1, source_target_pairs={{0,4},{4,0},{8,12},{12,8},{16,20},{20,16},{24,28},{28,24},{1,5},{5... | collective-permute-start | bytes 442376 | tf_op jit(solution)/shard_map/ppermute | solution.py:528
  14.0 5.2 %copy-start.3 = (bf16[64,576]{1,0:T(8,128)(2,1)S(1)}, bf16[64,576]{1,0:T(8,128)(2,1)}, u32[]{:S(2)}) copy-start(bf16[64,576]{1,0:T(8,128)(2,1)} %get-tuple-element.28) | copy-start | bytes 221188
  19.3 3.5 %collective-permute-start.3 = (bf16[64,1792]{1,0:T(8,128)(2,1)S(1)}, bf16[64,1792]{1,0:T(8,128)(2,1)S(1)}, u32[]{:S(2)}, u32[]{:S(2)}) collective-permute-start(bf16[64,1792]{1,0:T(8,128)(2,1)S(1)} %bitcast.11), channel_id=1, source_target_pairs={{0,1},{1,0},{2,3},{3,2},{4,5},{5,4},{6,7},{7,6},{8,9},{9,8},{10,11... | collective-permute-start | bytes 688136 | tf_op jit(solution)/shard_map/ppermute | solution.py:531
  19.4 8.0 %collective-permute-start.2 = (bf16[64,1792]{1,0:T(8,128)(2,1)S(1)}, bf16[64,1792]{1,0:T(8,128)(2,1)S(1)}, u32[]{:S(2)}, u32[]{:S(2)}) collective-permute-start(bf16[64,1792]{1,0:T(8,128)(2,1)S(1)} %bitcast.12), channel_id=1, source_target_pairs={{0,2},{2,0},{1,3},{3,1},{4,6},{6,4},{5,7},{7,5},{8,10},{10,8},{9,1... | collective-permute-start | bytes 688136 | tf_op jit(solution)/shard_map/ppermute | solution.py:531
  20.9 9.9 %collective-permute-start.5 = (bf16[4,64,576]{2,1,0:T(8,128)(2,1)S(1)}, bf16[4,64,576]{2,1,0:T(8,128)(2,1)S(1)}, u32[]{:S(2)}, u32[]{:S(2)}) collective-permute-start(bf16[4,64,576]{2,1,0:T(8,128)(2,1)S(1)} %pad_maximum_fusion), channel_id=1, source_target_pairs={{0,8},{4,12},{8,0},{12,4},{16,24},{20,28},{24,16},{28,20},{1,9},{5... | collective-permute-start | bytes 884744 | tf_op jit(solution)/shard_map/ppermute | solution.py:528
  27.4 1.5 %collective-permute-start.4 = (bf16[64,1792]{1,0:T(8,128)(2,1)S(1)}, bf16[64,1792]{1,0:T(8,128)(2,1)S(1)}, u32[]{:S(2)}, u32[]{:S(2)}) collective-permute-start(bf16[64,1792]{1,0:T(8,128)(2,1)S(1)} %collective-permute-done.2.far_ref), channel_id=1, source_target_pairs={{0,1},{1,0},{2,3},{3,2},{4,5},{5,4},{6,7},{7,6},{8,9},{9,8},{10,11... | collective-permute-start | bytes 688136 | tf_op jit(solution)/shard_map/ppermute | solution.py:531
  30.9 1.8 %collective-permute-start.6 = (bf16[2,64,1792]{2,1,0:T(8,128)(2,1)S(1)}, bf16[2,64,1792]{2,1,0:T(8,128)(2,1)S(1)}, u32[]{:S(2)}, u32[]{:S(2)}) collective-permute-start(bf16[2,64,1792]{2,1,0:T(8,128)(2,1)S(1)} %get-tuple-element.42), channel_id=1, source_target_pairs={{0,1},{1,0},{2,3},{3,2},{4,5},{5,4},{6,7},{7,6},{8,9},{9,8},{10,11... | collective-permute-start | bytes 1376264 | tf_op jit(solution)/shard_map/ppermute | solution.py:531
  31.3 7.7 %copy-start.2 = (s32[1024]{0:T(1024)S(1)}, s32[1024]{0:T(1024)}, u32[]{:S(2)}) copy-start(s32[1024]{0:T(1024)} %positions_ref.3) | copy-start | bytes 12292
  32.8 6.2 %collective-permute-start.7 = (bf16[8,64,576]{2,1,0:T(8,128)(2,1)S(1)}, bf16[8,64,576]{2,1,0:T(8,128)(2,1)S(1)}, u32[]{:S(2)}, u32[]{:S(2)}) collective-permute-start(bf16[8,64,576]{2,1,0:T(8,128)(2,1)S(1)} %constant_dynamic-update-slice_fusion.own_keys), channel_id=1, source_target_pairs={{0,1},{1,0},{2,3},{3,2},{4,5},{5,4},{6,7},{7,6},{8,9},{9,8},{10,11... | collective-permute-start | bytes 1769480 | tf_op jit(solution)/shard_map/ppermute | solution.py:531
  33.9 19.4 %all-to-all-start.1 = ((bf16[16,8,1792]{2,1,0:T(8,128)(2,1)}), bf16[16,8,1792]{2,1,0:T(8,128)(2,1)S(1)}, u32[]{:S(2)}, u32[]{:S(2)}) async-start(bf16[16,8,1792]{2,1,0:T(8,128)(2,1)} %bitcast.8), calls=%async_computation.1 | async-start | bytes 917504 | tf_op jit(solution)/shard_map/all_to_all | solution.py:583
  39.0 14.3 %copy-start = (bf16[128,128]{1,0:T(8,128)(2,1)S(1)}, bf16[128,128]{1,0:T(8,128)(2,1)}, u32[]{:S(2)}) copy-start(bf16[128,128]{1,0:T(8,128)(2,1)} %get-tuple-element.46.high_ref) | copy-start | bytes 98308
  39.0 14.3 %copy-start.1 = (bf16[128,128]{1,0:T(8,128)(2,1)S(1)}, bf16[128,128]{1,0:T(8,128)(2,1)}, u32[]{:S(2)}) copy-start(bf16[128,128]{1,0:T(8,128)(2,1)} %get-tuple-element.47.low_ref) | copy-start | bytes 98308

commit v13 on v12

--- a/solution.py
+++ b/solution.py
@@ -538,8 +538,11 @@
     received = over_ctx(packed[None], flips[0])
     high, q_nope, received = lax.optimization_barrier((high, q_nope, received))
     queries = fold(me, positions, q_nope, q_rope, w_uk)
-    own_keys = jnp.concatenate([packed[None], received], axis=0)
-    for flip in flips[1:-1]:
+    packed, received = lax.optimization_barrier((packed, received))
+    blocks = [packed[None], received]
+    blocks = blocks + [over_ctx(block, flips[1]) for block in blocks]
+    own_keys = jnp.concatenate(blocks, axis=0)
+    for flip in flips[2:-1]:
         own_keys = jnp.concatenate([own_keys, over_ctx(own_keys, flip)], axis=0)
     arrived, queries, own_keys = lax.optimization_barrier((arrived, queries, own_keys))
 

time: 55 us -> 62.8 us (1.14)
  waiting for transfers between devices: 9.45 us -> 18.8 us
  other arithmetic: 0.97 us -> 0.07 us
    ppermute x3 -> x4, waiting for transfers between devices: 2.31 us -> 9.79 us  [over_ctx(): return lax.ppermute(value, 'ctx', [(i, i ^ flip) for i in range(ctx)])]
    all_to_all x1, starting transfers between devices: 3.81 us -> 7.28 us  [shards(): lax.all_to_all(outgoing, 'ctx', split_axis=0, concat_axis=0, tiled=True)]
    ppermute x3 -> x4, starting transfers between devices: 7.71 us -> 4.95 us  [over_ctx(): return lax.ppermute(value, 'ctx', [(i, i ^ flip) for i in range(ctx)])]
    ppermute x5, waiting for transfers between devices: 2.56 us -> 4.46 us  [over(): return lax.ppermute(value, axis, [(0, 1), (1, 0)])]
    all_to_all x1, starting transfers between devices: 5.09 us -> 3.74 us  [shards(): lax.all_to_all(returning.reshape(2 * ctx, CAP, returning.shape[3]), ('ctx...]
    concatenate x2 -> x1, other arithmetic: 0.97 us -> 0.07 us  [shards(): own_keys = jnp.concatenate(blocks, axis=0)]
  transfers between devices with their start and end apart: 10 -> 11, of which waited for: 7 -> 6; matrix products, arithmetic and copies ran while one was open for 2% -> 0% of each run, Pallas kernels for 39% -> 34%
where the time goes in v13:
time: 62.8 us; the launch traced here: 62.3 us
  Pallas kernels  24.8 us (39%)
  waiting for transfers between devices  18.8 us (30%)
  starting transfers between devices  17.8 us (28%)
  between operations  0.76 us (1%)
    ppermute x4, waiting for transfers between devices, over_ctx(): return lax.ppermute(value, 'ctx', [(i, i ^ flip) for i in range(ctx)])  9.79 us
    pallas_call x1, Pallas kernels, attend(): pl.pallas_call(attention_kernel, out_shape=jax.ShapeDtypeStruct((2 * HALF...  9.71 us
    all_to_all x1, starting transfers between devices, shards(): lax.all_to_all(outgoing, 'ctx', split_axis=0, concat_axis=0, tiled=True)  7.28 us
    ppermute x4, starting transfers between devices, over_ctx(): return lax.ppermute(value, 'ctx', [(i, i ^ flip) for i in range(ctx)])  4.95 us
    pallas_call x1, Pallas kernels, fold(): pl.pallas_call(fold_kernel, out_shape=jax.ShapeDtypeStruct((2, 2, heads /...  4.66 us
    all_to_all x1, waiting for transfers between devices, shards(): lax.all_to_all(returning.reshape(2 * ctx, CAP, returning.shape[3]), ('ctx...  4.56 us
    ppermute x5, waiting for transfers between devices, over(): return lax.ppermute(value, axis, [(0, 1), (1, 0)])  4.46 us
    pallas_call x1, Pallas kernels, near_experts(): pl.pallas_call(near_kernel, out_shape=[jax.ShapeDtypeStruct((slots, 2 * u...  4.4 us
  transfers between devices with their start and end apart: 11, of which 6 were waited for; matrix products, arithmetic and copies ran while one was open for 0% of the time, Pallas kernels for 34%

profile of v13, /device:TPU:0, one launch (start us, length us, event | category | flops | bytes accessed | tf_op | source)
XLA Modules:
  0.0 62.3 jit_solution(14417049830734751844)
XLA Ops:
  0.6 2.2 %route.1 = (bf16[8,8,1792]{2,1,0:T(8,128)(2,1)}, bf16[128,128]{1,0:T(8,128)(2,1)}, bf16[128,128]{1,0:T(8,128)(2,1)}, bf16[64,576]{1,0:T(8,128)(2,1)}) custom-call(s32[1]{0:T(128)} %bitcast.1.ep_ref, s32[8,128]{1,0:T(8,128)} %bitcast.20, f32[8,128]{1,0:T(8,128)} %bitcast.21, bf16[64,128]{1,0:T(8,128)(2,1)} %bitcast.19, bf16[128,1792]{1,0:T(8,128)(2,1)} %rows_ref.1, ...), custom_call_target="tpu_custom_call" | custom-call | flops 29360128 | bytes 1048576 | tf_op jit(solution)/shard_map/route/pallas_call | solution.py:88
  2.9 7.3 %all-to-all-start = ((bf16[8,8,1792]{2,1,0:T(8,128)(2,1)}), bf16[8,8,1792]{2,1,0:T(8,128)(2,1)S(1)}, u32[]{:S(2)}, u32[]{:S(2)}) async-start(bf16[8,8,1792]{2,1,0:T(8,128)(2,1)} %get-tuple-element.28), calls=%async_computation | async-start | bytes 458752 | tf_op jit(solution)/shard_map/all_to_all | solution.py:536
  10.1 2.9 %collective-permute-start = (bf16[1,64,576]{2,1,0:T(8,128)(2,1)}, bf16[1,64,576]{2,1,0:T(8,128)(2,1)S(1)}, u32[]{:S(2)}, u32[]{:S(2)}) collective-permute-start(bf16[1,64,576]{2,1,0:T(8,128)(2,1)} %bitcast.16), channel_id=1, source_target_pairs={{0,16},{4,20},{8,24},{12,28},{16,0},{20,4},{24,8},{28,12},{1,17},{... | collective-permute-start | bytes 221192 | tf_op jit(solution)/shard_map/ppermute | solution.py:528
  13.1 8.8 %collective-permute-done = bf16[1,64,576]{2,1,0:T(8,128)(2,1)S(1)} collective-permute-done((bf16[1,64,576]{2,1,0:T(8,128)(2,1)}, bf16[1,64,576]{2,1,0:T(8,128)(2,1)S(1)}, u32[]{:S(2)}, u32[]{:S(2)}) %collective-permute-start) | collective-permute-done | bytes 73760 | tf_op jit(solution)/shard_map/ppermute | solution.py:528
  21.9 1.4 %collective-permute-start.2 = (bf16[1,64,576]{2,1,0:T(8,128)(2,1)S(1)}, bf16[1,64,576]{2,1,0:T(8,128)(2,1)S(1)}, u32[]{:S(2)}, u32[]{:S(2)}) collective-permute-start(bf16[1,64,576]{2,1,0:T(8,128)(2,1)S(1)} %collective-permute-done), channel_id=1, source_target_pairs={{0,4},{4,0},{8,12},{12,8},{16,20},{20,16},{24,28},{28,24},{1,5},{5... | collective-permute-start | bytes 221192 | tf_op jit(solution)/shard_map/ppermute | solution.py:528
  23.3 0.6 collective-permute-start.1
  23.9 0.0 copy-start.3
  23.9 4.7 %fold.1 = bf16[2,2,512,576]{3,2,1,0:T(8,128)(2,1)} custom-call(s32[1]{0:T(128)} %bitcast.own_ref, s32[1024]{0:T(1024)} %positions_ref.3, bf16[128,2048]{1,0:T(8,128)(2,1)} %q_nope_ref, bf16[128,1024]{1,0:T(8,128)(2,1)} %q_rope_ref.1, bf16[512,2048]{1,0:T(8,128)(2,1)} %w_uk_ref.1), custom_call_target="tpu_custom_call" | custom-call | flops 268435456 | bytes 6291456 | tf_op jit(solution)/shard_map/fold/pallas_call | solution.py:313
  28.6 0.0 collective-permute-done.2
  28.6 0.0 collective-permute-done.1
  28.6 0.0 copy-done.3
  28.6 0.1 pad_maximum_fusion
  28.7 0.0 all-to-all-done
  28.7 0.1 collective-permute-start.4
  28.8 1.6 %collective-permute-start.3 = (bf16[64,1792]{1,0:T(8,128)(2,1)S(1)}, bf16[64,1792]{1,0:T(8,128)(2,1)S(1)}, u32[]{:S(2)}, u32[]{:S(2)}) collective-permute-start(bf16[64,1792]{1,0:T(8,128)(2,1)S(1)} %bitcast.13), channel_id=1, source_target_pairs={{0,2},{2,0},{1,3},{3,1},{4,6},{6,4},{5,7},{7,5},{8,10},{10,8},{9,1... | collective-permute-start | bytes 688136 | tf_op jit(solution)/shard_map/ppermute | solution.py:531
  30.3 0.0 collective-permute-start.6
  30.3 0.0 collective-permute-done.4.core_ref
  30.3 4.4 %near_experts.1 = (f32[64,512]{1,0:T(8,128)S(1)}, bf16[2,1792,256]{2,1,0:T(8,128)(2,1)S(1)}, bf16[2,1792,256]{2,1,0:T(8,128)(2,1)S(1)}, bf16[4,256,1792]{2,1,0:T(8,128)(2,1)S(1)}) custom-call(s32[1]{0:T(128)} %bitcast.1.ep_ref, bf16[64,1792]{1,0:T(8,128)(2,1)S(1)} %bitcast.14, bf16[64,1792]{1,0:T(8,128)(2,1)S(1)} %collective-permute-done.4.core_ref, ...), custom_call_target="tpu_custom_call" | custom-call | flops 234881024 | bytes 11010048 | tf_op jit(solution)/shard_map/near_experts/pallas_call | solution.py:166
  34.7 2.1 %collective-permute-done.3.far_ref = bf16[64,1792]{1,0:T(8,128)(2,1)S(1)} collective-permute-done((bf16[64,1792]{1,0:T(8,128)(2,1)S(1)}, bf16[64,1792]{1,0:T(8,128)(2,1)S(1)}, u32[]{:S(2)}, u32[]{:S(2)}) %collective-permute-start.3) | collective-permute-done | bytes 229408 | tf_op jit(solution)/shard_map/ppermute | solution.py:531
  36.8 0.0 collective-permute-start.5
  36.8 0.4 far_rows.1.sums_ref
  37.2 1.0 %collective-permute-done.5.core_far_ref = bf16[64,1792]{1,0:T(8,128)(2,1)S(1)} collective-permute-done((bf16[64,1792]{1,0:T(8,128)(2,1)S(1)}, bf16[64,1792]{1,0:T(8,128)(2,1)S(1)}, u32[]{:S(2)}, u32[]{:S(2)}) %collective-permute-start.5) | collective-permute-done | bytes 229408 | tf_op jit(solution)/shard_map/ppermute | solution.py:531
  38.3 0.9 %sent_pieces.1 = (bf16[64,256]{1,0:T(8,128)(2,1)S(1)}, bf16[2,64,1792]{2,1,0:T(8,128)(2,1)S(1)}) custom-call(bf16[64,1792]{1,0:T(8,128)(2,1)S(1)} %collective-permute-done.5.core_far_ref, f32[64,512]{1,0:T(8,128)S(1)} %far_rows.1.sums_ref, bf16[2,1792,256]{2,1,0:T(8,128)(2,1)S(1)} %get-tuple-element.41.gate, bf16[2,1792,256]{2,1,0:T(8,128)(2,1)S(1)} %get-tuple-element.42.up, ...), custom_call_target="tpu_custom_call" | custom-call | flops 268435456 | bytes 2097152 | tf_op jit(solution)/shard_map/sent_pieces/pallas_call | solution.py:225
  39.1 1.0 %collective-permute-done.6 = bf16[4,64,576]{2,1,0:T(8,128)(2,1)S(1)} collective-permute-done((bf16[4,64,576]{2,1,0:T(8,128)(2,1)S(1)}, bf16[4,64,576]{2,1,0:T(8,128)(2,1)S(1)}, u32[]{:S(2)}, u32[]{:S(2)}) %collective-permute-start.6) | collective-permute-done | bytes 294944 | tf_op jit(solution)/shard_map/ppermute | solution.py:528
  40.1 0.0 collective-permute-start.7
  40.1 0.4 kept_pieces.1.kept_ref
  40.5 0.0 copy-start.2
  40.5 1.4 %collective-permute-done.7.received_ref = bf16[2,64,1792]{2,1,0:T(8,128)(2,1)S(1)} collective-permute-done((bf16[2,64,1792]{2,1,0:T(8,128)(2,1)S(1)}, bf16[2,64,1792]{2,1,0:T(8,128)(2,1)S(1)}, u32[]{:S(2)}, u32[]{:S(2)}) %collective-permute-start.7) | collective-permute-done | bytes 458784 | tf_op jit(solution)/shard_map/ppermute | solution.py:531
  42.0 0.2 collective-permute-start.8
  42.2 0.9 %sum_cores.1 = bf16[8,2,8,1792]{3,2,1,0:T(8,128)(2,1)} custom-call(s32[1]{0:T(128)} %bitcast.1.ep_ref, bf16[2,64,1792]{2,1,0:T(8,128)(2,1)S(1)} %kept_pieces.1.kept_ref, bf16[2,64,1792]{2,1,0:T(8,128)(2,1)S(1)} %collective-permute-done.7.received_ref), custom_call_target="tpu_custom_call" | custom-call | bytes 1048576 | tf_op jit(solution)/shard_map/sum_cores/pallas_call | solution.py:249
  43.1 3.7 %all-to-all-start.1 = ((bf16[16,8,1792]{2,1,0:T(8,128)(2,1)}), bf16[16,8,1792]{2,1,0:T(8,128)(2,1)S(1)}, u32[]{:S(2)}, u32[]{:S(2)}) async-start(bf16[16,8,1792]{2,1,0:T(8,128)(2,1)} %bitcast.9), calls=%async_computation.1 | async-start | bytes 917504 | tf_op jit(solution)/shard_map/all_to_all | solution.py:586
  46.8 0.0 copy-start
  46.8 0.0 copy-start.1
  46.8 0.0 collective-permute-done.8.core_keys
  46.8 0.0 copy-done.2
  46.9 9.7 %attention.1 = bf16[128,2048]{1,0:T(8,128)(2,1)} custom-call(s32[1]{0:T(128)} %bitcast.own_ref, s32[1]{0:T(128)} %bitcast.1.ep_ref, s32[1024]{0:T(1024)S(1)} %copy-done.2, bf16[2,1024,576]{2,1,0:T(8,128)(2,1)} %bitcast.15, bf16[512,2048]{1,0:T(8,128)(2,1)} %w_uv_hbm.1, bf16[8,64,576]{2,1,0:T(8,128)(2,1)S(1)} %constant_dynamic-update-slice_fusion.own_keys, ...), custom_call_target="tpu_custom_call" | custom-call | flops 14495514624 | bytes 8388608 | tf_op jit(solution)/shard_map/attention/pallas_call | solution.py:484
  56.6 4.6 %all-to-all-done.1 = bf16[16,8,1792]{2,1,0:T(8,128)(2,1)S(1)} async-done(((bf16[16,8,1792]{2,1,0:T(8,128)(2,1)}), bf16[16,8,1792]{2,1,0:T(8,128)(2,1)S(1)}, u32[]{:S(2)}, u32[]{:S(2)}) %all-to-all-start.1) | async-done | bytes 458784 | tf_op jit(solution)/shard_map/all_to_all | solution.py:586
  61.1 0.0 copy-done
  61.1 0.0 copy-done.1
  61.1 1.2 %combine.1 = bf16[128,1792]{1,0:T(8,128)(2,1)} custom-call(bf16[128,128]{1,0:T(8,128)(2,1)S(1)} %copy-done, bf16[128,128]{1,0:T(8,128)(2,1)S(1)} %copy-done.1, bf16[128,1792]{1,0:T(8,128)(2,1)S(1)} %bitcast.11), custom_call_target="tpu_custom_call" | custom-call | flops 117440512 | bytes 1048576 | tf_op jit(solution)/shard_map/combine/pallas_call | solution.py:272
  (2 shorter events, 0.1 us)
Async XLA Ops:
  2.9 25.8 %all-to-all-start = ((bf16[8,8,1792]{2,1,0:T(8,128)(2,1)}), bf16[8,8,1792]{2,1,0:T(8,128)(2,1)S(1)}, u32[]{:S(2)}, u32[]{:S(2)}) async-start(bf16[8,8,1792]{2,1,0:T(8,128)(2,1)} %get-tuple-element.28), calls=%async_computation | async-start | bytes 458752 | tf_op jit(solution)/shard_map/all_to_all | solution.py:536
  10.1 11.7 %collective-permute-start = (bf16[1,64,576]{2,1,0:T(8,128)(2,1)}, bf16[1,64,576]{2,1,0:T(8,128)(2,1)S(1)}, u32[]{:S(2)}, u32[]{:S(2)}) collective-permute-start(bf16[1,64,576]{2,1,0:T(8,128)(2,1)} %bitcast.16), channel_id=1, source_target_pairs={{0,16},{4,20},{8,24},{12,28},{16,0},{20,4},{24,8},{28,12},{1,17},{... | collective-permute-start | bytes 221192 | tf_op jit(solution)/shard_map/ppermute | solution.py:528
  21.9 6.7 %collective-permute-start.2 = (bf16[1,64,576]{2,1,0:T(8,128)(2,1)S(1)}, bf16[1,64,576]{2,1,0:T(8,128)(2,1)S(1)}, u32[]{:S(2)}, u32[]{:S(2)}) collective-permute-start(bf16[1,64,576]{2,1,0:T(8,128)(2,1)S(1)} %collective-permute-done), channel_id=1, source_target_pairs={{0,4},{4,0},{8,12},{12,8},{16,20},{20,16},{24,28},{28,24},{1,5},{5... | collective-permute-start | bytes 221192 | tf_op jit(solution)/shard_map/ppermute | solution.py:528
  23.3 5.3 %collective-permute-start.1 = (bf16[1,64,576]{2,1,0:T(8,128)(2,1)}, bf16[1,64,576]{2,1,0:T(8,128)(2,1)S(1)}, u32[]{:S(2)}, u32[]{:S(2)}) collective-permute-start(bf16[1,64,576]{2,1,0:T(8,128)(2,1)} %bitcast.17), channel_id=1, source_target_pairs={{0,4},{4,0},{8,12},{12,8},{16,20},{20,16},{24,28},{28,24},{1,5},{5... | collective-permute-start | bytes 221192 | tf_op jit(solution)/shard_map/ppermute | solution.py:528
  23.9 4.7 %copy-start.3 = (bf16[64,576]{1,0:T(8,128)(2,1)S(1)}, bf16[64,576]{1,0:T(8,128)(2,1)}, u32[]{:S(2)}) copy-start(bf16[64,576]{1,0:T(8,128)(2,1)} %get-tuple-element.33) | copy-start | bytes 221188
  28.7 1.6 %collective-permute-start.4 = (bf16[64,1792]{1,0:T(8,128)(2,1)S(1)}, bf16[64,1792]{1,0:T(8,128)(2,1)S(1)}, u32[]{:S(2)}, u32[]{:S(2)}) collective-permute-start(bf16[64,1792]{1,0:T(8,128)(2,1)S(1)} %bitcast.12), channel_id=1, source_target_pairs={{0,1},{1,0},{2,3},{3,2},{4,5},{5,4},{6,7},{7,6},{8,9},{9,8},{10,11... | collective-permute-start | bytes 688136 | tf_op jit(solution)/shard_map/ppermute | solution.py:531
  28.8 8.0 %collective-permute-start.3 = (bf16[64,1792]{1,0:T(8,128)(2,1)S(1)}, bf16[64,1792]{1,0:T(8,128)(2,1)S(1)}, u32[]{:S(2)}, u32[]{:S(2)}) collective-permute-start(bf16[64,1792]{1,0:T(8,128)(2,1)S(1)} %bitcast.13), channel_id=1, source_target_pairs={{0,2},{2,0},{1,3},{3,1},{4,6},{6,4},{5,7},{7,5},{8,10},{10,8},{9,1... | collective-permute-start | bytes 688136 | tf_op jit(solution)/shard_map/ppermute | solution.py:531
  30.3 9.8 %collective-permute-start.6 = (bf16[4,64,576]{2,1,0:T(8,128)(2,1)S(1)}, bf16[4,64,576]{2,1,0:T(8,128)(2,1)S(1)}, u32[]{:S(2)}, u32[]{:S(2)}) collective-permute-start(bf16[4,64,576]{2,1,0:T(8,128)(2,1)S(1)} %pad_maximum_fusion), channel_id=1, source_target_pairs={{0,8},{4,12},{8,0},{12,4},{16,24},{20,28},{24,16},{28,20},{1,9},{5... | collective-permute-start | bytes 884744 | tf_op jit(solution)/shard_map/ppermute | solution.py:528
  36.8 1.5 %collective-permute-start.5 = (bf16[64,1792]{1,0:T(8,128)(2,1)S(1)}, bf16[64,1792]{1,0:T(8,128)(2,1)S(1)}, u32[]{:S(2)}, u32[]{:S(2)}) collective-permute-start(bf16[64,1792]{1,0:T(8,128)(2,1)S(1)} %collective-permute-done.3.far_ref), channel_id=1, source_target_pairs={{0,1},{1,0},{2,3},{3,2},{4,5},{5,4},{6,7},{7,6},{8,9},{9,8},{10,11... | collective-permute-start | bytes 688136 | tf_op jit(solution)/shard_map/ppermute | solution.py:531
  40.1 1.8 %collective-permute-start.7 = (bf16[2,64,1792]{2,1,0:T(8,128)(2,1)S(1)}, bf16[2,64,1792]{2,1,0:T(8,128)(2,1)S(1)}, u32[]{:S(2)}, u32[]{:S(2)}) collective-permute-start(bf16[2,64,1792]{2,1,0:T(8,128)(2,1)S(1)} %get-tuple-element.46), channel_id=1, source_target_pairs={{0,1},{1,0},{2,3},{3,2},{4,5},{5,4},{6,7},{7,6},{8,9},{9,8},{10,11... | collective-permute-start | bytes 1376264 | tf_op jit(solution)/shard_map/ppermute | solution.py:531
  40.5 6.3 %copy-start.2 = (s32[1024]{0:T(1024)S(1)}, s32[1024]{0:T(1024)}, u32[]{:S(2)}) copy-start(s32[1024]{0:T(1024)} %positions_ref.3) | copy-start | bytes 12292
  42.0 4.8 %collective-permute-start.8 = (bf16[8,64,576]{2,1,0:T(8,128)(2,1)S(1)}, bf16[8,64,576]{2,1,0:T(8,128)(2,1)S(1)}, u32[]{:S(2)}, u32[]{:S(2)}) collective-permute-start(bf16[8,64,576]{2,1,0:T(8,128)(2,1)S(1)} %constant_dynamic-update-slice_fusion.own_keys), channel_id=1, source_target_pairs={{0,1},{1,0},{2,3},{3,2},{4,5},{5,4},{6,7},{7,6},{8,9},{9,8},{10,11... | collective-permute-start | bytes 1769480 | tf_op jit(solution)/shard_map/ppermute | solution.py:531
  43.1 18.1 %all-to-all-start.1 = ((bf16[16,8,1792]{2,1,0:T(8,128)(2,1)}), bf16[16,8,1792]{2,1,0:T(8,128)(2,1)S(1)}, u32[]{:S(2)}, u32[]{:S(2)}) async-start(bf16[16,8,1792]{2,1,0:T(8,128)(2,1)} %bitcast.9), calls=%async_computation.1 | async-start | bytes 917504 | tf_op jit(solution)/shard_map/all_to_all | solution.py:586
  46.8 14.3 %copy-start = (bf16[128,128]{1,0:T(8,128)(2,1)S(1)}, bf16[128,128]{1,0:T(8,128)(2,1)}, u32[]{:S(2)}) copy-start(bf16[128,128]{1,0:T(8,128)(2,1)} %get-tuple-element.50.high_ref) | copy-start | bytes 98308
  46.8 14.3 %copy-start.1 = (bf16[128,128]{1,0:T(8,128)(2,1)S(1)}, bf16[128,128]{1,0:T(8,128)(2,1)}, u32[]{:S(2)}) copy-start(bf16[128,128]{1,0:T(8,128)(2,1)} %get-tuple-element.51.low_ref) | copy-start | bytes 98308
